TPU v7x, 32 devices: a whole 2x2x4 slice. The times are simulated.
32 devices in a mesh: groups: 2 (over y), tile: 4 (over z), shot: 4 (over x, core).
Axes of the slice: x: 2, y: 2, z: 4, core: 2. Of those that a mesh axis runs over, the one named last changes fastest.
Arguments:
- src_prev: float32 [8, 8, 64, 128], P(('groups', 'shot'), None, 'tile'), parts along dimension 0, may hold values from -6 to 6
- src_now: float32 [8, 8, 64, 128], P(('groups', 'shot'), None, 'tile'), parts along dimension 0, may hold values from -6 to 6
- rec_prev: float32 [8, 8, 64, 128], P(('groups', 'shot'), None, 'tile'), parts along dimension 0, may hold values from -6 to 6
- rec_now: float32 [8, 8, 64, 128], P(('groups', 'shot'), None, 'tile'), parts along dimension 0, may hold values from -6 to 6
- speed_table: float32 [32], P('groups'), parts along dimension 0, may hold values from 0.05 to 0.2
- region_ids: int32 [8, 128, 128], P(None, ('groups', 'tile')), parts along dimension 1, may hold values from 0 to 15
- source_cell: int32 [8], P(('groups', 'shot')), parts along dimension 0, may hold values from 0 to 65535
- wavelet: float32 [8, 2], P(('groups', 'shot')), parts along dimension 0, may hold values from -12 to 12
- receiver_cell: int32 [8, 128], P(('groups', 'shot'), 'tile'), parts along dimension 0, may hold values from 0 to 2047
- receiver_data: float32 [8, 2, 128], P(('groups', 'shot'), None, 'tile'), parts along dimension 0, may hold values from -12 to 12
Outputs:
- src_next: float32 [8, 8, 64, 128], P(('groups', 'shot'), None, 'tile'), parts along dimension 0
- rec_next: float32 [8, 8, 64, 128], P(('groups', 'shot'), None, 'tile'), parts along dimension 0
- offset_image: float32 [33, 8, 128, 128], P(None, 'shot', ('groups', 'tile')), parts along dimension 2
There are 2 independent parts, one for each index of `groups`. A program takes and returns all parts, laid end to end along the dimension named above; each array names one. Nothing has to cross between parts.
Inputs may be any that keep to these rules, and one draw needn't show every extreme that they name: `receiver_cell`: receivers may share a cell; their traces then add.
All inputs are finite; a program needn't handle non-finite values.
Results may differ from a plain program's by a relative error of at most 0.0001.
Values sent between devices are 32-bit elements; how exact they have to be, the bound alone decides.
No kernel may reach another device: no remote copies, remote signals or barrier semaphores. Data moves between devices by JAX's collectives and lax.ppermute only.
A program may use at most 64 MiB of HBM per device.

v0:
```python
import jax
import jax.numpy as jnp
from jax import lax
from jax.sharding import PartitionSpec as P

OFFS = 33


COEFS = (-205.0 / 72.0, 8.0 / 5.0, -1.0 / 5.0, 8.0 / 315.0, -1.0 / 560.0)


def padded_2(block, sides, width):
    for axis, dim in sides:
        count = lax.axis_size(axis)
        forward = [(i, i + 1) for i in range(count - 1)]
        backward = [(target, source) for source, target in forward]
        low = lax.ppermute(
            lax.slice_in_dim(block, block.shape[dim] - width, None, axis=dim), axis, forward
        )
        high = lax.ppermute(lax.slice_in_dim(block, 0, width, axis=dim), axis, backward)
        block = jnp.concatenate([low, block, high], axis=dim)
    return block


def laplace(extended):
    leading = extended.ndim - 3
    levels = extended.shape[leading]
    extent = extended.shape[leading + 1] - 8
    across = extended.shape[leading + 2]
    padded = jnp.pad(extended, [(0, 0)] * leading + [(4, 4), (0, 0), (4, 4)])
    centre = extended[..., 4 : 4 + extent, :]
    total = 3.0 * COEFS[0] * centre
    for stride in range(1, 5):
        beside = (
            padded[..., 4 + stride : 4 + stride + levels, 4 : 4 + extent, 4 : 4 + across]
            + padded[..., 4 - stride : 4 - stride + levels, 4 : 4 + extent, 4 : 4 + across]
        )
        beside = (
            beside
            + padded[..., 4 : 4 + levels, 4 + stride : 4 + stride + extent, 4 : 4 + across]
            + padded[..., 4 : 4 + levels, 4 - stride : 4 - stride + extent, 4 : 4 + across]
        )
        beside = (
            beside
            + padded[..., 4 : 4 + levels, 4 : 4 + extent, 4 + stride : 4 + stride + across]
            + padded[..., 4 : 4 + levels, 4 : 4 + extent, 4 - stride : 4 - stride + across]
        )
        total = total + COEFS[stride] * beside
    return total


def source_term(cells, amps, first_x, extent, levels, across, width_all):
    level_of = cells // (width_all * across)
    column_of = cells // across % width_all
    row_of = cells % across
    level_iota = lax.broadcasted_iota(jnp.int32, (1, levels, extent, across), 1)
    column_iota = lax.broadcasted_iota(jnp.int32, (1, levels, extent, across), 2) + first_x
    row_iota = lax.broadcasted_iota(jnp.int32, (1, levels, extent, across), 3)
    hit = (
        (level_iota == level_of[:, None, None, None])
        & (column_iota == column_of[:, None, None, None])
        & (row_iota == row_of[:, None, None, None])
    )
    return jnp.where(hit, amps[:, None, None, None], 0.0)


def receiver_plane(cells, values, extent, across):
    shot_count = cells.shape[0]
    shot_rows = jnp.broadcast_to(jnp.arange(shot_count)[:, None], cells.shape)
    flat = jnp.zeros((shot_count, extent * across), jnp.float32).at[shot_rows, cells].add(values)
    return flat.reshape(shot_count, extent, across)


def offset_products(fields, extent):
    reach = OFFS // 2
    outer = padded_2(fields, (("tile", 3),), reach)
    gathers = []
    for offset in range(OFFS):
        product = (
            outer[0, :, :, 2 * reach - offset : 2 * reach - offset + extent]
            * outer[1, :, :, offset : offset + extent]
        )
        gathers.append(jnp.sum(product, axis=0))
    return jnp.stack(gathers)


def per_device(
    src_prev,
    src_now,
    rec_prev,
    rec_now,
    speed_table,
    region_ids,
    source_cell,
    wavelet,
    receiver_cell,
    receiver_data,
):
    shot_count, levels, extent, across = src_now.shape
    width_all = extent * lax.axis_size("tile")
    first = lax.axis_index("tile") * extent
    regions = speed_table.shape[0]
    region_iota = lax.broadcasted_iota(jnp.int32, (regions, 1, 1, 1), 0)
    coef = jnp.sum(
        jnp.where(region_ids[None] == region_iota, speed_table[:, None, None, None], 0.0), axis=0
    )
    plane_first = receiver_plane(receiver_cell, receiver_data[:, 0], extent, across)
    plane_second = receiver_plane(receiver_cell, receiver_data[:, 1], extent, across)

    def finish(base, first_x, amps, plane):
        source_part = base[0] + source_term(
            source_cell, amps, first_x, base.shape[3], levels, across, width_all
        )
        receiver_part = base[1].at[:, 0].add(plane)
        return jnp.stack([source_part, receiver_part])

    previous = jnp.stack([src_prev, rec_prev])
    current = jnp.stack([src_now, rec_now])

    def advance(older, newer, amps, plane):
        widened = padded_2(newer, (("tile", 3),), 4)
        base = 2.0 * newer - older + coef * laplace(widened)
        return finish(base, first, amps, plane)

    middle = advance(previous, current, wavelet[:, 0], plane_first)
    final = advance(current, middle, wavelet[:, 1], plane_second)
    weight = 1.0 / (shot_count * lax.axis_size("shot"))
    products = offset_products(final, extent) * weight
    summed = lax.psum(products, "shot")
    share = levels // lax.axis_size("shot")
    offset_image = lax.dynamic_slice_in_dim(summed, lax.axis_index("shot") * share, share, 1)
    return (final[0], final[1], offset_image)


def solution(mesh):
    return jax.shard_map(
        per_device,
        mesh=mesh,
        in_specs=(
            P(("groups", "shot"), None, "tile", None),
            P(("groups", "shot"), None, "tile", None),
            P(("groups", "shot"), None, "tile", None),
            P(("groups", "shot"), None, "tile", None),
            P("groups"),
            P(None, ("groups", "tile"), None),
            P(("groups", "shot")),
            P(("groups", "shot"), None),
            P(("groups", "shot"), "tile"),
            P(("groups", "shot"), None, "tile"),
        ),
        out_specs=(
            P(("groups", "shot"), None, "tile", None),
            P(("groups", "shot"), None, "tile", None),
            P(None, "shot", ("groups", "tile"), None),
        ),
        check_vma=False,
    )
```

profile of v0, /device:TPU:0, one launch (start us, length us, event | category | flops | bytes accessed | tf_op | source)
XLA Modules:
  0.0 110.7 jit_solution(4538726725366144693)
XLA Ops:
  7.2 0.0 all-reduce.5.cloned.1.call-start
  7.2 0.8 fusion.61
  8.0 4.9 %collective-permute-start = (f32[2,1,8,4,128]{4,3,2,1,0:T(4,128)S(1)}, f32[2,1,8,4,128]{4,3,2,1,0:T(4,128)S(1)}, u32[]{:S(2)}, u32[]{:S(2)}) collective-permute-start(f32[2,1,8,4,128]{4,3,2,1,0:T(4,128)S(1)} %get-tuple-element.41), channel_id=1, source_target_pairs={{0,4},{4,8},{8,12},{1,5},{5,9},{9,13},{2,6},{6,10},{10,14},{3,7},{... | collective-permute-start | bytes 98312 | tf_op jit(solution)/shard_map/ppermute | solution.py:17
  13.0 1.3 %collective-permute-start.1 = (f32[2,1,8,4,128]{4,3,2,1,0:T(4,128)S(1)}, f32[2,1,8,4,128]{4,3,2,1,0:T(4,128)S(1)}, u32[]{:S(2)}, u32[]{:S(2)}) collective-permute-start(f32[2,1,8,4,128]{4,3,2,1,0:T(4,128)S(1)} %get-tuple-element.42), channel_id=1, source_target_pairs={{4,0},{8,4},{12,8},{5,1},{9,5},{13,9},{6,2},{10,6},{14,10},{7,3},{... | collective-permute-start | bytes 98312 | tf_op jit(solution)/shard_map/ppermute | solution.py:20
  15.0 0.7 fusion.71
  15.6 1.3 %fusion.73 = (f32[1,1]{1,0:T(1,128)}, f32[1,1]{1,0:T(1,128)}) fusion(f32[1,2]{1,0:T(1,128)} %param.21), kind=kLoop, calls=%fused_computation.228 | loop fusion | bytes 16 | tf_op jit(solution)/shard_map/slice | solution.py:126
  17.0 0.8 slice_bitcast_fusion.2
  17.7 1.0 select_reduce_fusion
  18.8 0.7 scatter_custom_fusion
  19.5 0.0 collective-permute-done
  19.6 0.0 collective-permute-done.1
  19.6 1.0 pad_maximum_fusion.1
  20.5 1.1 %select_maximum_fusion.3 = f32[2,1,16,24,136]{4,3,2,1,0:T(8,128)S(1)} fusion(f32[2,1,8,4,128]{4,3,2,1,0:T(4,128)S(1)} %collective-permute-done.1, f32[2,1,8,4,128]{4,3,2,1,0:T(4,128)S(1)} %collective-permute-done, f32[1,1,8,16,128]{4,3,2,1,0:T(8,128)} %bitcast.170, f32[1,1,8,16,128]{4,3,2,1,0:T(8,128)} %bitcast.165), kind=kLoop, calls=%fused_computation.12 | loop fusion | flops 1880064 | bytes 614400 | tf_op jit(solution)/shard_map/concatenate | solution.py:21
  21.7 0.0 copy-start
  21.7 0.0 copy-start.1
  21.7 1.5 %fusion.16 = f32[2,1,8,16,128]{4,3,2,1,0:T(8,128)S(1)} fusion(f32[2,1,16,24,136]{4,3,2,1,0:T(8,128)S(1)} %select_maximum_fusion.3, f32[2,1,8,20,128]{4,3,2,1,0:T(8,128)S(1)} %get-tuple-element.40, f32[2,1,8,20,128]{4,3,2,1,0:T(8,128)S(1)} %get-tuple-element.39, f32[1,1,8,16,128]{4,3,2,1,0:T(8,128)} %bitcast.175, f32[1,1,8,16,128]{4,3,2,1,0:T(8,128)} %bitcast.176, ...), kind=kLoop, calls=%fused_computation.68 | loop fusion | flops 1146880 | bytes 3604480 | tf_op jit(solution)/shard_map/add | solution.py:122
  23.3 0.7 fusion.72
  24.0 4.6 %collective-permute-start.2 = (f32[2,1,8,4,128]{4,3,2,1,0:T(4,128)S(1)}, f32[2,1,8,4,128]{4,3,2,1,0:T(4,128)S(1)}, u32[]{:S(2)}, u32[]{:S(2)}) collective-permute-start(f32[2,1,8,4,128]{4,3,2,1,0:T(4,128)S(1)} %get-tuple-element.35), channel_id=1, source_target_pairs={{0,4},{4,8},{8,12},{1,5},{5,9},{9,13},{2,6},{6,10},{10,14},{3,7},{... | collective-permute-start | bytes 98312 | tf_op jit(solution)/shard_map/ppermute | solution.py:17
  28.6 1.3 %collective-permute-start.3 = (f32[2,1,8,4,128]{4,3,2,1,0:T(4,128)S(1)}, f32[2,1,8,4,128]{4,3,2,1,0:T(4,128)S(1)}, u32[]{:S(2)}, u32[]{:S(2)}) collective-permute-start(f32[2,1,8,4,128]{4,3,2,1,0:T(4,128)S(1)} %get-tuple-element.36), channel_id=1, source_target_pairs={{4,0},{8,4},{12,8},{5,1},{9,5},{13,9},{6,2},{10,6},{14,10},{7,3},{... | collective-permute-start | bytes 98312 | tf_op jit(solution)/shard_map/ppermute | solution.py:20
  29.9 0.7 scatter_custom_fusion.1
  30.6 0.0 collective-permute-done.2
  30.6 3.8 %collective-permute-done.3 = f32[2,1,8,4,128]{4,3,2,1,0:T(4,128)S(1)} collective-permute-done((f32[2,1,8,4,128]{4,3,2,1,0:T(4,128)S(1)}, f32[2,1,8,4,128]{4,3,2,1,0:T(4,128)S(1)}, u32[]{:S(2)}, u32[]{:S(2)}) %collective-permute-start.3) | collective-permute-done | bytes 32800 | tf_op jit(solution)/shard_map/ppermute | solution.py:20
  34.4 0.2 select_maximum_fusion
  34.7 0.0 copy-done
  34.7 0.0 copy-done.1
  34.7 0.6 fusion.6
  35.3 0.7 select_add_fusion
  36.0 0.0 copy-start.2
  36.1 3.5 %collective-permute-start.5 = (f32[2,1,8,16,128]{4,3,2,1,0:T(8,128)S(1)}, f32[2,1,8,16,128]{4,3,2,1,0:T(8,128)S(1)}, u32[]{:S(2)}, u32[]{:S(2)}) collective-permute-start(f32[2,1,8,16,128]{4,3,2,1,0:T(8,128)S(1)} %pad_maximum_fusion.5), channel_id=1, source_target_pairs={{0,4},{4,8},{8,12},{1,5},{5,9},{9,13},{2,6},{6,10},{10,14},{3,7},{... | collective-permute-start | bytes 393224 | tf_op jit(solution)/shard_map/ppermute | solution.py:17
  39.6 1.3 %collective-permute-start.4 = (f32[2,1,8,16,128]{4,3,2,1,0:T(8,128)S(1)}, f32[2,1,8,16,128]{4,3,2,1,0:T(8,128)S(1)}, u32[]{:S(2)}, u32[]{:S(2)}) collective-permute-start(f32[2,1,8,16,128]{4,3,2,1,0:T(8,128)S(1)} %pad_maximum_fusion.5), channel_id=1, source_target_pairs={{4,0},{8,4},{12,8},{5,1},{9,5},{13,9},{6,2},{10,6},{14,10},{7,3},{... | collective-permute-start | bytes 393224 | tf_op jit(solution)/shard_map/ppermute | solution.py:20
  40.9 1.2 %collective-permute-done.5 = f32[2,1,8,16,128]{4,3,2,1,0:T(8,128)S(1)} collective-permute-done((f32[2,1,8,16,128]{4,3,2,1,0:T(8,128)S(1)}, f32[2,1,8,16,128]{4,3,2,1,0:T(8,128)S(1)}, u32[]{:S(2)}, u32[]{:S(2)}) %collective-permute-start.5) | collective-permute-done | bytes 131104 | tf_op jit(solution)/shard_map/ppermute | solution.py:17
  42.1 4.4 %collective-permute-done.4 = f32[2,1,8,16,128]{4,3,2,1,0:T(8,128)S(1)} collective-permute-done((f32[2,1,8,16,128]{4,3,2,1,0:T(8,128)S(1)}, f32[2,1,8,16,128]{4,3,2,1,0:T(8,128)S(1)}, u32[]{:S(2)}, u32[]{:S(2)}) %collective-permute-start.4) | collective-permute-done | bytes 131104 | tf_op jit(solution)/shard_map/ppermute | solution.py:20
  46.9 0.0 copy-done.2
  46.9 1.4 %constant_dynamic-update-slice_fusion.16 = (f32[33,8,16,128]{3,2,1,0:T(8,128)S(1)}, f32[1,8,16,128]{3,2,1,0:T(8,128)}) fusion(f32[33,8,16,128]{3,2,1,0:T(8,128)S(1)} %constant_dynamic-update-slice_fusion.17, f32[1,8,16,128]{3,2,1,0:T(8,128)S(1)} %fusion.64, f32[]{:T(128)} %bitcast.14, s32[]{:T(128)} %bitcast.6, pred[16]{0:T(512)(128)(4,1)S(1)} %add_compare_fusion, ...), kind=kLoop, calls=%fused_computation.112 | loop fusion | flops 114688 | bytes 262668
  48.6 1.5 %broadcast_multiply_fusion = f32[33,8,16,128]{3,2,1,0:T(8,128)} fusion(f32[33,8,16,128]{3,2,1,0:T(8,128)S(1)} %constant_dynamic-update-slice_fusion), kind=kLoop, calls=%fused_computation.6 | loop fusion | flops 540672 | bytes 4325376 | tf_op jit(solution)/shard_map/mul | solution.py:128
  50.1 0.0 all-reduce.5.cloned.1.call-update
  50.2 51.8 %all-reduce.5.cloned.1.call-done = f32[33,8,16,128]{3,2,1,0:T(8,128)} async-done(((f32[33,8,16,128]{3,2,1,0:T(8,128)}), f32[33,8,16,128]{3,2,1,0:T(8,128)}) %all-reduce.5.cloned.1.call-update) | async-done | bytes 2162704 | tf_op jit(solution)/shard_map/psum | solution.py:129
  102.0 1.9 %constant_dynamic-slice_fusion = f32[33,2,16,128]{3,2,1,0:T(8,128)} fusion(f32[33,8,16,128]{3,2,1,0:T(8,128)} %all-reduce.5.cloned.1.call-done, s32[]{:T(128)S(6)} %select_n.78), kind=kLoop, calls=%fused_computation.221 | loop fusion | bytes 1081348 | tf_op jit(solution)/shard_map/dynamic_slice | solution.py:131
  (41 shorter events, 0.7 us)
Async XLA Ops:
  7.2 94.8 %all-reduce.5.cloned.1.call-start = ((), (), s32[]{:S(2)}) async-start(), calls=%async_computation | async-start | bytes 4325376 | tf_op jit(solution)/shard_map/psum | solution.py:129
  8.0 11.5 %collective-permute-start = (f32[2,1,8,4,128]{4,3,2,1,0:T(4,128)S(1)}, f32[2,1,8,4,128]{4,3,2,1,0:T(4,128)S(1)}, u32[]{:S(2)}, u32[]{:S(2)}) collective-permute-start(f32[2,1,8,4,128]{4,3,2,1,0:T(4,128)S(1)} %get-tuple-element.41), channel_id=1, source_target_pairs={{0,4},{4,8},{8,12},{1,5},{5,9},{9,13},{2,6},{6,10},{10,14},{3,7},{... | collective-permute-start | bytes 98312 | tf_op jit(solution)/shard_map/ppermute | solution.py:17
  13.0 6.6 %collective-permute-start.1 = (f32[2,1,8,4,128]{4,3,2,1,0:T(4,128)S(1)}, f32[2,1,8,4,128]{4,3,2,1,0:T(4,128)S(1)}, u32[]{:S(2)}, u32[]{:S(2)}) collective-permute-start(f32[2,1,8,4,128]{4,3,2,1,0:T(4,128)S(1)} %get-tuple-element.42), channel_id=1, source_target_pairs={{4,0},{8,4},{12,8},{5,1},{9,5},{13,9},{6,2},{10,6},{14,10},{7,3},{... | collective-permute-start | bytes 98312 | tf_op jit(solution)/shard_map/ppermute | solution.py:20
  21.7 13.0 %copy-start = (f32[1,8,16,128]{3,2,1,0:T(8,128)S(1)}, f32[1,8,16,128]{3,2,1,0:T(8,128)}, u32[]{:S(2)}) copy-start(f32[1,8,16,128]{3,2,1,0:T(8,128)} %param.15) | copy-start | bytes 196612
  21.7 13.0 %copy-start.1 = (f32[1,8,16,128]{3,2,1,0:T(8,128)S(1)}, f32[1,8,16,128]{3,2,1,0:T(8,128)}, u32[]{:S(2)}) copy-start(f32[1,8,16,128]{3,2,1,0:T(8,128)} %param.17) | copy-start | bytes 196612
  24.0 6.6 %collective-permute-start.2 = (f32[2,1,8,4,128]{4,3,2,1,0:T(4,128)S(1)}, f32[2,1,8,4,128]{4,3,2,1,0:T(4,128)S(1)}, u32[]{:S(2)}, u32[]{:S(2)}) collective-permute-start(f32[2,1,8,4,128]{4,3,2,1,0:T(4,128)S(1)} %get-tuple-element.35), channel_id=1, source_target_pairs={{0,4},{4,8},{8,12},{1,5},{5,9},{9,13},{2,6},{6,10},{10,14},{3,7},{... | collective-permute-start | bytes 98312 | tf_op jit(solution)/shard_map/ppermute | solution.py:17
  28.6 5.8 %collective-permute-start.3 = (f32[2,1,8,4,128]{4,3,2,1,0:T(4,128)S(1)}, f32[2,1,8,4,128]{4,3,2,1,0:T(4,128)S(1)}, u32[]{:S(2)}, u32[]{:S(2)}) collective-permute-start(f32[2,1,8,4,128]{4,3,2,1,0:T(4,128)S(1)} %get-tuple-element.36), channel_id=1, source_target_pairs={{4,0},{8,4},{12,8},{5,1},{9,5},{13,9},{6,2},{10,6},{14,10},{7,3},{... | collective-permute-start | bytes 98312 | tf_op jit(solution)/shard_map/ppermute | solution.py:20
  36.0 10.8 %copy-start.2 = (f32[1,8,16,128]{3,2,1,0:T(8,128)}, f32[1,8,16,128]{3,2,1,0:T(8,128)S(1)}, u32[]{:S(2)}) copy-start(f32[1,8,16,128]{3,2,1,0:T(8,128)S(1)} %fusion.64) | copy-start | bytes 196612
  36.1 6.0 %collective-permute-start.5 = (f32[2,1,8,16,128]{4,3,2,1,0:T(8,128)S(1)}, f32[2,1,8,16,128]{4,3,2,1,0:T(8,128)S(1)}, u32[]{:S(2)}, u32[]{:S(2)}) collective-permute-start(f32[2,1,8,16,128]{4,3,2,1,0:T(8,128)S(1)} %pad_maximum_fusion.5), channel_id=1, source_target_pairs={{0,4},{4,8},{8,12},{1,5},{5,9},{9,13},{2,6},{6,10},{10,14},{3,7},{... | collective-permute-start | bytes 393224 | tf_op jit(solution)/shard_map/ppermute | solution.py:17
  39.6 6.9 %collective-permute-start.4 = (f32[2,1,8,16,128]{4,3,2,1,0:T(8,128)S(1)}, f32[2,1,8,16,128]{4,3,2,1,0:T(8,128)S(1)}, u32[]{:S(2)}, u32[]{:S(2)}) collective-permute-start(f32[2,1,8,16,128]{4,3,2,1,0:T(8,128)S(1)} %pad_maximum_fusion.5), channel_id=1, source_target_pairs={{4,0},{8,4},{12,8},{5,1},{9,5},{13,9},{6,2},{10,6},{14,10},{7,3},{... | collective-permute-start | bytes 393224 | tf_op jit(solution)/shard_map/ppermute | solution.py:20
Sparse Core Ops, SparseCore 0:
  50.3 51.6 all-reduce.4
where the time goes:
time: 111 us
  waiting for transfers between devices  61.1 us (55%)
  starting transfers between devices  16.9 us (15%)
  between operations  15.2 us (14%)
  other arithmetic  13.4 us (12%)
  local copies, waits for them, and re-layouts  3.98 us (4%)
    psum x1, waiting for transfers between devices, per_device(): summed = lax.psum(products, 'shot')  51.8 us
    ppermute x3, starting transfers between devices, padded_2(): lax.ppermute(lax.slice_in_dim(block, block.shape[dim] - width, None, axis...  13 us
    ppermute x3, waiting for transfers between devices, padded_2(): lax.ppermute(lax.slice_in_dim(block, 0, width, axis=dim), axis, backward)  8.12 us
    ppermute x3, starting transfers between devices, padded_2(): lax.ppermute(lax.slice_in_dim(block, 0, width, axis=dim), axis, backward)  3.88 us
    concatenate x5, other arithmetic, padded_2(): block = jnp.concatenate([low, block, high], axis=dim)  2.42 us
  transfers between devices with their start and end apart: 7, of which 4 were waited for; matrix products, arithmetic and copies ran while one was open for 5% of the time, Pallas kernels for 0%

commit v1 on v0

v1 whole, which is shorter than its diff:
```python
import functools

import jax
import jax.numpy as jnp
from jax import lax
from jax.experimental import pallas as pl
from jax.experimental.pallas import tpu as pltpu
from jax.sharding import PartitionSpec as P

OFFS = 33
REACH = OFFS // 2
HALO = 4
LEAD = 8

COEFS = (-205.0 / 72.0, 8.0 / 5.0, -1.0 / 5.0, 8.0 / 315.0, -1.0 / 560.0)

VMEM = pl.BlockSpec(memory_space=pltpu.VMEM)
SMEM = pl.BlockSpec(memory_space=pltpu.SMEM)
LIMIT = 16 * 1024 * 1024


def lane_weights(shape):
    lane = lax.broadcasted_iota(jnp.int32, shape, 1)
    across = shape[1]
    after = [jnp.where(lane < across - k, COEFS[k], 0.0) for k in range(1, HALO + 1)]
    before = [jnp.where(lane >= k, COEFS[k], 0.0) for k in range(1, HALO + 1)]
    return after, before


def laplace_level(wide, field, level, levels, extent, weights):
    after, before = weights
    centre = wide[field, level, LEAD : LEAD + extent, :]
    across = centre.shape[1]
    total = 3.0 * COEFS[0] * centre
    for k in range(1, HALO + 1):
        beside = (
            wide[field, level, LEAD + k : LEAD + k + extent, :]
            + wide[field, level, LEAD - k : LEAD - k + extent, :]
        )
        if level + k < levels:
            beside = beside + wide[field, level + k, LEAD : LEAD + extent, :]
        if level - k >= 0:
            beside = beside + wide[field, level - k, LEAD : LEAD + extent, :]
        total = total + COEFS[k] * beside
        total = total + after[k - 1] * pltpu.roll(centre, across - k, 1)
        total = total + before[k - 1] * pltpu.roll(centre, k, 1)
    return total


def source_hit(cell, level, width, first, shape):
    across = shape[1]
    flat = lax.broadcasted_iota(jnp.int32, shape, 0) * across + lax.broadcasted_iota(
        jnp.int32, shape, 1
    )
    return flat == cell - (level * width + first) * across


def own_part(
    width,
    first_ref,
    cell_ref,
    amps_ref,
    src_prev,
    src_now,
    rec_prev,
    rec_now,
    table_ref,
    ids_ref,
    spots_ref,
    traces_ref,
    part_ref,
    coef_ref,
    plane_ref,
    low_ref,
    high_ref,
    wide,
    table,
):
    levels, extent, across = src_now.shape[1:]
    shape = (extent, across)
    regions = table_ref.shape[1]

    table[...] = jnp.zeros_like(table)
    table[0:1, 0:regions] = table_ref[...]
    speeds = jnp.broadcast_to(table[0:1, :], (8, across))
    for level in range(levels):
        for row in range(0, extent, 8):
            ids = ids_ref[level, row : row + 8, :]
            coef_ref[level, row : row + 8, :] = jnp.take_along_axis(
                speeds, ids, axis=1, mode="promise_in_bounds"
            )

    spots = spots_ref[...]
    column = lax.broadcasted_iota(jnp.int32, (extent, spots.shape[1]), 0) * across
    in_column = (spots >= column) & (spots < column + across)
    lane = lax.broadcasted_iota(jnp.int32, (across, spots.shape[1]), 0)
    in_row = jnp.where(lax.rem(spots, across) == lane, 1.0, 0.0)
    traces = jnp.concatenate(
        [jnp.where(in_column, traces_ref[0, t : t + 1, :], 0.0) for t in range(2)], axis=0
    )
    planes = lax.dot_general(
        traces,
        in_row,
        (((1,), (1,)), ((), ())),
        precision=lax.Precision.HIGHEST,
        preferred_element_type=jnp.float32,
    )
    plane_ref[...] = planes[extent:, :]

    first = first_ref[0]
    for field, now in enumerate((src_now, rec_now)):
        for level in range(levels):
            zeros = jnp.zeros((LEAD, across), jnp.float32)
            wide[field, level, 0:LEAD, :] = zeros
            wide[field, level, LEAD + extent : 2 * LEAD + extent, :] = zeros
            wide[field, level, LEAD : LEAD + extent, :] = now[0, level]
    weights = lane_weights(shape)
    for field, (prev, now) in enumerate(((src_prev, src_now), (rec_prev, rec_now))):
        for level in range(levels):
            total = laplace_level(wide, field, level, levels, extent, weights)
            value = 2.0 * now[0, level] - prev[0, level] + coef_ref[level] * total
            if field == 0:
                hit = source_hit(cell_ref[0], level, width, first, shape)
                value = value + jnp.where(hit, amps_ref[0, 0], 0.0)
            elif level == 0:
                value = value + planes[:extent, :]
            part_ref[field, level] = value
            place = field * levels + level
            low_ref[place, 0:HALO, :] = now[0, level, 0:HALO, :]
            low_ref[place, HALO : 2 * HALO, :] = value[0:HALO, :]
            high_ref[place, 0:HALO, :] = now[0, level, extent - HALO : extent, :]
            high_ref[place, HALO : 2 * HALO, :] = value[extent - HALO : extent, :]
    for level in range(levels):
        place = 2 * levels + level // 2
        rows = pl.ds(level % 2 * HALO, HALO)
        low_ref[place, rows, :] = coef_ref[level, 0:HALO, :]
        high_ref[place, rows, :] = coef_ref[level, extent - HALO : extent, :]


def both_steps(
    width,
    first_ref,
    cell_ref,
    amps_ref,
    src_now,
    rec_now,
    part_ref,
    coef_ref,
    plane_ref,
    low_ref,
    high_ref,
    src_next,
    rec_next,
    packed_ref,
    own,
    other,
    middle,
):
    levels, extent, across = src_now.shape[1:]
    shape = (extent, across)
    share = packed_ref.shape[2]
    zeros = jnp.zeros((LEAD, across), jnp.float32)
    end = LEAD + extent
    for field, now in enumerate((src_now, rec_now)):
        for level in range(levels):
            place = field * levels + level
            own[field, level, 0:LEAD, :] = zeros
            own[field, level, end : end + LEAD, :] = zeros
            own[field, level, LEAD:end, :] = now[0, level]
            other[field, level, LEAD:end, :] = jnp.zeros(shape, jnp.float32)
            other[field, level, LEAD - HALO : LEAD, :] = low_ref[place, 0:HALO, :]
            other[field, level, end : end + HALO, :] = high_ref[place, 0:HALO, :]
    for field in range(2):
        for level in range(levels):
            place = field * levels + level
            pair = 2 * levels + level // 2
            rows = pl.ds(level % 2 * HALO, HALO)
            below = jnp.zeros((HALO, across), jnp.float32)
            above = jnp.zeros((HALO, across), jnp.float32)
            left = jnp.zeros((8, across), jnp.float32)
            right = jnp.zeros((8, across), jnp.float32)
            for k in range(1, HALO + 1):
                begin = LEAD - HALO + k
                below = below + COEFS[k] * own[field, level, begin : begin + HALO, :]
                above = above + COEFS[k] * own[field, level, end - k : end - k + HALO, :]
                left = left + COEFS[k] * other[field, level, LEAD - k : LEAD - k + 8, :]
                right = right + COEFS[k] * other[field, level, end - 8 + k : end + k, :]
            middle[field, level, LEAD - HALO : LEAD, :] = (
                low_ref[place, HALO : 2 * HALO, :] + low_ref[pair, rows, :] * below
            )
            middle[field, level, end : end + HALO, :] = (
                high_ref[place, HALO : 2 * HALO, :] + high_ref[pair, rows, :] * above
            )
            middle[field, level, LEAD : LEAD + 8, :] = (
                part_ref[field, level, 0:8, :] + coef_ref[level, 0:8, :] * left
            )
            middle[field, level, end - 8 : end, :] = (
                part_ref[field, level, extent - 8 : extent, :]
                + coef_ref[level, extent - 8 : extent, :] * right
            )
    first = first_ref[0]
    weights = lane_weights(shape)
    for field, (now, after) in enumerate(((src_now, src_next), (rec_now, rec_next))):
        for level in range(levels):
            total = laplace_level(middle, field, level, levels, extent, weights)
            value = 2.0 * middle[field, level, LEAD:end, :] - now[0, level]
            value = value + coef_ref[level] * total
            if field == 0:
                hit = source_hit(cell_ref[0], level, width, first, shape)
                value = value + jnp.where(hit, amps_ref[0, 1], 0.0)
            elif level == 0:
                value = value + plane_ref[...]
            after[0, level] = value
            packed_ref[level // share, field, level % share] = value


def image_products(weight, mine_ref, low_ref, high_ref, image_ref, wide):
    shots, _, share, extent, across = mine_ref.shape
    for shot in range(shots):
        for field in range(2):
            for level in range(share):
                scale = weight if field == 0 else 1.0
                wide[shot, field, level, 0:REACH, :] = (
                    scale * low_ref[shot, field, level, extent - REACH : extent, :]
                )
                wide[shot, field, level, REACH : REACH + extent, :] = (
                    scale * mine_ref[shot, field, level]
                )
                wide[shot, field, level, REACH + extent : 2 * REACH + extent, :] = (
                    scale * high_ref[shot, field, level, 0:REACH, :]
                )
    for level in range(share):
        for offset in range(OFFS):
            total = jnp.zeros((extent, across), jnp.float32)
            for shot in range(shots):
                begin = 2 * REACH - offset
                total = total + (
                    wide[shot, 0, level, begin : begin + extent, :]
                    * wide[shot, 1, level, offset : offset + extent, :]
                )
            image_ref[offset, level] = total


def swap_sides(low, high):
    count = lax.axis_size("tile")
    forward = [(i, i + 1) for i in range(count - 1)]
    backward = [(target, source) for source, target in forward]
    return lax.ppermute(high, "tile", forward), lax.ppermute(low, "tile", backward)


def per_device(
    src_prev,
    src_now,
    rec_prev,
    rec_now,
    speed_table,
    region_ids,
    source_cell,
    wavelet,
    receiver_cell,
    receiver_data,
):
    _, levels, extent, across = src_now.shape
    width = extent * lax.axis_size("tile")
    shots = lax.axis_size("shot")
    share = levels // shots
    first = (lax.axis_index("tile") * extent).reshape(1)
    params = pltpu.CompilerParams(vmem_limit_bytes=LIMIT)

    def struct(*shape):
        return jax.ShapeDtypeStruct(shape, jnp.float32)

    wide = pltpu.VMEM((2, levels, extent + 2 * LEAD, across), jnp.float32)
    message = struct(2 * levels + levels // 2, 2 * HALO, across)
    part, coef, plane, low, high = pl.pallas_call(
        functools.partial(own_part, width),
        out_shape=(
            struct(2, levels, extent, across),
            struct(levels, extent, across),
            struct(extent, across),
            message,
            message,
        ),
        in_specs=[SMEM] * 3 + [VMEM] * 8,
        out_specs=[VMEM] * 5,
        scratch_shapes=[wide, pltpu.VMEM((8, across), jnp.float32)],
        compiler_params=params,
        name="own_part",
    )(
        first,
        source_cell,
        wavelet,
        src_prev,
        src_now,
        rec_prev,
        rec_now,
        speed_table.reshape(1, -1),
        region_ids,
        receiver_cell,
        receiver_data,
    )
    from_low, from_high = swap_sides(low, high)
    src_next, rec_next, packed = pl.pallas_call(
        functools.partial(both_steps, width),
        out_shape=(
            struct(1, levels, extent, across),
            struct(1, levels, extent, across),
            struct(shots, 2, share, extent, across),
        ),
        in_specs=[SMEM] * 3 + [VMEM] * 7,
        out_specs=[VMEM] * 3,
        scratch_shapes=[wide, wide, wide],
        compiler_params=params,
        name="both_steps",
    )(first, source_cell, wavelet, src_now, rec_now, part, coef, plane, from_low, from_high)
    mine = lax.all_to_all(packed, "shot", 0, 0, tiled=True)
    low_fields, high_fields = swap_sides(mine, mine)
    image = pl.pallas_call(
        functools.partial(image_products, 1.0 / shots),
        out_shape=struct(OFFS, share, extent, across),
        in_specs=[VMEM] * 3,
        out_specs=VMEM,
        scratch_shapes=[pltpu.VMEM((shots, 2, share, extent + 2 * REACH, across), jnp.float32)],
        compiler_params=params,
        name="image_products",
    )(mine, low_fields, high_fields)
    return src_next, rec_next, image


def solution(mesh):
    field = P(("groups", "shot"), None, "tile", None)
    return jax.shard_map(
        per_device,
        mesh=mesh,
        in_specs=(
            field,
            field,
            field,
            field,
            P("groups"),
            P(None, ("groups", "tile"), None),
            P(("groups", "shot")),
            P(("groups", "shot"), None),
            P(("groups", "shot"), "tile"),
            P(("groups", "shot"), None, "tile"),
        ),
        out_specs=(field, field, P(None, "shot", ("groups", "tile"), None)),
        check_vma=False,
    )
```

time: 111 us -> 37.1 us (0.33)
  waiting for transfers between devices: 61.1 us -> 7.53 us
  between operations: 15.2 us -> 1.37 us
  other arithmetic: 13.4 us -> 0 us
  blocking collectives: 0 us -> 7.18 us
  starting transfers between devices: 16.9 us -> 12.1 us
  Pallas kernels: 0 us -> 3.61 us
    psum x1 -> x0, waiting for transfers between devices: 51.8 us -> none  [per_device(): summed = lax.psum(products, 'shot')]
    all_to_all x0 -> x1, blocking collectives: none -> 7.18 us  [per_device(): mine = lax.all_to_all(packed, 'shot', 0, 0, tiled=True)]
    unnamed x6 -> x22, local copies, waits for them, and re-layouts: 0.02 us -> 4.9 us
    ppermute x6 -> x4, starting transfers between devices: 16.9 us -> 12.1 us  [the longest x2 9.49 us: swap_sides(): lax.ppermute(high, 'tile', forward)]
    pallas_call x0 -> x3, Pallas kernels: none -> 3.61 us  [the longest x1 1.59 us: per_device(): pl.pallas_call(functools.partial(both_steps, width), out_shape=(struct(1,...]
    add x3 -> x0, other arithmetic: 2.86 us -> none  [the longest x2 2.13 us: advance(): base = 2.0 * newer - older + coef * laplace(widened)]
    concatenate x6 -> x0, other arithmetic: 2.42 us -> none  [the longest x5 2.42 us: padded_2(): block = jnp.concatenate([low, block, high], axis=dim)]
    dynamic_slice x1 -> x0, local copies, waits for them, and re-layouts: 1.88 us -> none  [per_device(): lax.dynamic_slice_in_dim(summed, lax.axis_index('shot') * share, share, 1)]
  transfers between devices with their start and end apart: 7 -> 4, of which waited for: 4 -> 4; matrix products, arithmetic and copies ran while one was open for 5% -> 0% of each run, Pallas kernels for 0% -> 0%
where the time goes in v1:
time: 37.1 us; the launch traced here: 36.6 us
  starting transfers between devices  12.1 us (33%)
  waiting for transfers between devices  7.53 us (20%)
  blocking collectives  7.18 us (19%)
  local copies, waits for them, and re-layouts  4.9 us (13%)
  Pallas kernels  3.61 us (10%)
  between operations  1.37 us (4%)
    ppermute x2, starting transfers between devices, swap_sides(): lax.ppermute(high, 'tile', forward)  9.49 us
    all_to_all x1, blocking collectives, per_device(): mine = lax.all_to_all(packed, 'shot', 0, 0, tiled=True)  7.18 us
    ppermute x2, waiting for transfers between devices, swap_sides(): lax.ppermute(low, 'tile', backward)  5.3 us
    unnamed x22, local copies, waits for them, and re-layouts  4.9 us
    ppermute x2, starting transfers between devices, swap_sides(): lax.ppermute(low, 'tile', backward)  2.57 us
    ppermute x2, waiting for transfers between devices, swap_sides(): lax.ppermute(high, 'tile', forward)  2.23 us
    pallas_call x1, Pallas kernels, per_device(): pl.pallas_call(functools.partial(both_steps, width), out_shape=(struct(1,...  1.59 us
    pallas_call x1, Pallas kernels, per_device(): pl.pallas_call(functools.partial(image_products, 1.0 / shots), out_shape=...  1.05 us
  transfers between devices with their start and end apart: 4, of which 4 were waited for; matrix products, arithmetic and copies ran while one was open for 0% of the time, Pallas kernels for 0%

profile of v1, /device:TPU:0, one launch (start us, length us, event | category | flops | bytes accessed | tf_op | source)
XLA Modules:
  0.0 36.6 jit_solution(3640504439622861391)
XLA Ops:
  1.3 0.0 copy-start.9
  1.3 0.0 copy-start.10
  1.3 0.0 copy-start.7
  1.3 0.0 copy-start.8
  1.3 0.6 %copy-done.9 = f32[16]{0:T(128)S(1)} copy-done((f32[16]{0:T(128)S(1)}, f32[16]{0:T(128)}, u32[]{:S(2)}) %copy-start.9) | copy-done | bytes 88
  1.9 0.0 copy-done.10
  2.0 0.0 copy-done.7
  2.0 0.0 copy-done.8
  2.0 0.0 copy-start
  2.0 0.8 %copy-done = f32[1,8,16,128]{3,2,1,0:T(8,128)S(1)} copy-done((f32[1,8,16,128]{3,2,1,0:T(8,128)S(1)}, f32[1,8,16,128]{3,2,1,0:T(8,128)}, u32[]{:S(2)}) %copy-start) | copy-done | bytes 65560
  2.9 0.0 copy-start.2
  2.9 0.8 %copy-done.2 = f32[1,8,16,128]{3,2,1,0:T(8,128)S(1)} copy-done((f32[1,8,16,128]{3,2,1,0:T(8,128)S(1)}, f32[1,8,16,128]{3,2,1,0:T(8,128)}, u32[]{:S(2)}) %copy-start.2) | copy-done | bytes 65560
  3.7 0.0 copy-start.4
  3.7 0.8 %copy-done.4 = f32[1,8,16,128]{3,2,1,0:T(8,128)S(1)} copy-done((f32[1,8,16,128]{3,2,1,0:T(8,128)S(1)}, f32[1,8,16,128]{3,2,1,0:T(8,128)}, u32[]{:S(2)}) %copy-start.4) | copy-done | bytes 65560
  4.5 0.0 copy-start.5
  4.5 0.8 %copy-done.5 = f32[1,8,16,128]{3,2,1,0:T(8,128)S(1)} copy-done((f32[1,8,16,128]{3,2,1,0:T(8,128)S(1)}, f32[1,8,16,128]{3,2,1,0:T(8,128)}, u32[]{:S(2)}) %copy-start.5) | copy-done | bytes 65560
  5.4 0.0 copy-start.6
  5.4 0.8 %copy-done.6 = s32[8,16,128]{2,1,0:T(8,128)S(1)} copy-done((s32[8,16,128]{2,1,0:T(8,128)S(1)}, s32[8,16,128]{2,1,0:T(8,128)}, u32[]{:S(2)}) %copy-start.6) | copy-done | bytes 65560
  6.2 0.0 copy-start.1
  6.2 0.0 copy-start.3
  6.2 1.0 %own_part.1 = (f32[2,8,16,128]{3,2,1,0:T(8,128)S(1)}, f32[8,16,128]{2,1,0:T(8,128)S(1)}, f32[16,128]{1,0:T(8,128)S(1)}, f32[20,8,128]{2,1,0:T(8,128)S(1)}, f32[20,8,128]{2,1,0:T(8,128)S(1)}) custom-call(s32[1]{0:T(128)} %bitcast.first_ref, s32[1]{0:T(128)S(6)} %copy.13.cell_ref, f32[1,2]{1,0:T(1,128)S(1)} %copy-done.7, f32[1,8,16,128]{3,2,1,0:T(8,128)S(1)} %copy-done.4, ...), custom_call_target="tpu_custom_call" | custom-call | tf_op jit(solution)/shard_map/own_part/pallas_call | solution.py:275
  7.2 4.9 %collective-permute-start = (f32[20,8,128]{2,1,0:T(8,128)S(1)}, f32[20,8,128]{2,1,0:T(8,128)S(1)}, u32[]{:S(2)}, u32[]{:S(2)}) collective-permute-start(f32[20,8,128]{2,1,0:T(8,128)S(1)} %get-tuple-element.14), channel_id=1, source_target_pairs={{0,4},{4,8},{8,12},{1,5},{5,9},{9,13},{2,6},{6,10},{10,14},{3,7},{... | collective-permute-start | bytes 245768 | tf_op jit(solution)/shard_map/ppermute | solution.py:248
  12.1 1.3 %collective-permute-start.1 = (f32[20,8,128]{2,1,0:T(8,128)S(1)}, f32[20,8,128]{2,1,0:T(8,128)S(1)}, u32[]{:S(2)}, u32[]{:S(2)}) collective-permute-start(f32[20,8,128]{2,1,0:T(8,128)S(1)} %get-tuple-element.15), channel_id=1, source_target_pairs={{4,0},{8,4},{12,8},{5,1},{9,5},{13,9},{6,2},{10,6},{14,10},{7,3},{... | collective-permute-start | bytes 245768 | tf_op jit(solution)/shard_map/ppermute | solution.py:248
  13.4 0.7 %collective-permute-done.low_ref = f32[20,8,128]{2,1,0:T(8,128)S(1)} collective-permute-done((f32[20,8,128]{2,1,0:T(8,128)S(1)}, f32[20,8,128]{2,1,0:T(8,128)S(1)}, u32[]{:S(2)}, u32[]{:S(2)}) %collective-permute-start) | collective-permute-done | bytes 81952 | tf_op jit(solution)/shard_map/ppermute | solution.py:248
  14.2 4.3 %collective-permute-done.1.high_ref = f32[20,8,128]{2,1,0:T(8,128)S(1)} collective-permute-done((f32[20,8,128]{2,1,0:T(8,128)S(1)}, f32[20,8,128]{2,1,0:T(8,128)S(1)}, u32[]{:S(2)}, u32[]{:S(2)}) %collective-permute-start.1) | collective-permute-done | bytes 81952 | tf_op jit(solution)/shard_map/ppermute | solution.py:248
  18.5 0.0 copy-done.1
  18.5 0.0 copy-done.3
  18.5 1.6 %both_steps.1 = (f32[1,8,16,128]{3,2,1,0:T(8,128)}, f32[1,8,16,128]{3,2,1,0:T(8,128)}, f32[4,2,2,16,128]{4,3,2,1,0:T(8,128)S(1)}) custom-call(s32[1]{0:T(128)} %bitcast.first_ref, s32[1]{0:T(128)S(6)} %copy.13.cell_ref, f32[1,2]{1,0:T(1,128)S(1)} %copy-done.7, f32[1,8,16,128]{3,2,1,0:T(8,128)S(1)} %copy-done.1, f32[1,8,16,128]{3,2,1,0:T(8,128)S(1)} %copy-done.3, ...), custom_call_target="tpu_custom_call" | custom-call | tf_op jit(solution)/shard_map/both_steps/pallas_call | solution.py:303
  20.1 7.2 %all_to_all.5.mine_ref = f32[4,2,2,16,128]{4,3,2,1,0:T(8,128)S(1)} all-to-all(f32[4,2,2,16,128]{4,3,2,1,0:T(8,128)S(1)} %get-tuple-element.18), channel_id=1, replica_groups=mesh['groups'=2,'tile'=4,'shot'=4] {'shot'}, dimensions={0} | all-to-all | bytes 262144 | tf_op jit(solution)/shard_map/all_to_all | solution.py:316
  27.2 1.3 %collective-permute-start.3 = (f32[4,2,2,16,128]{4,3,2,1,0:T(8,128)S(1)}, f32[4,2,2,16,128]{4,3,2,1,0:T(8,128)S(1)}, u32[]{:S(2)}, u32[]{:S(2)}) collective-permute-start(f32[4,2,2,16,128]{4,3,2,1,0:T(8,128)S(1)} %all_to_all.5.mine_ref), channel_id=1, source_target_pairs={{4,0},{8,4},{12,8},{5,1},{9,5},{13,9},{6,2},{10,6},{14,10},{7,3},{... | collective-permute-start | bytes 393224 | tf_op jit(solution)/shard_map/ppermute | solution.py:248
  28.5 4.6 %collective-permute-start.2 = (f32[4,2,2,16,128]{4,3,2,1,0:T(8,128)S(1)}, f32[4,2,2,16,128]{4,3,2,1,0:T(8,128)S(1)}, u32[]{:S(2)}, u32[]{:S(2)}) collective-permute-start(f32[4,2,2,16,128]{4,3,2,1,0:T(8,128)S(1)} %all_to_all.5.mine_ref), channel_id=1, source_target_pairs={{0,4},{4,8},{8,12},{1,5},{5,9},{9,13},{2,6},{6,10},{10,14},{3,7},{... | collective-permute-start | bytes 393224 | tf_op jit(solution)/shard_map/ppermute | solution.py:248
  33.1 1.0 %collective-permute-done.3.high_ref = f32[4,2,2,16,128]{4,3,2,1,0:T(8,128)S(1)} collective-permute-done((f32[4,2,2,16,128]{4,3,2,1,0:T(8,128)S(1)}, f32[4,2,2,16,128]{4,3,2,1,0:T(8,128)S(1)}, u32[]{:S(2)}, u32[]{:S(2)}) %collective-permute-start.3) | collective-permute-done | bytes 131104 | tf_op jit(solution)/shard_map/ppermute | solution.py:248
  34.1 1.5 %collective-permute-done.2.low_ref = f32[4,2,2,16,128]{4,3,2,1,0:T(8,128)S(1)} collective-permute-done((f32[4,2,2,16,128]{4,3,2,1,0:T(8,128)S(1)}, f32[4,2,2,16,128]{4,3,2,1,0:T(8,128)S(1)}, u32[]{:S(2)}, u32[]{:S(2)}) %collective-permute-start.2) | collective-permute-done | bytes 131104 | tf_op jit(solution)/shard_map/ppermute | solution.py:248
  35.6 1.1 %image_products.1 = f32[33,2,16,128]{3,2,1,0:T(8,128)} custom-call(f32[4,2,2,16,128]{4,3,2,1,0:T(8,128)S(1)} %all_to_all.5.mine_ref, f32[4,2,2,16,128]{4,3,2,1,0:T(8,128)S(1)} %collective-permute-done.2.low_ref, f32[4,2,2,16,128]{4,3,2,1,0:T(8,128)S(1)} %collective-permute-done.3.high_ref), custom_call_target="tpu_custom_call" | custom-call | tf_op jit(solution)/shard_map/image_products/pallas_call | solution.py:318
Async XLA Ops:
  1.3 0.7 %copy-start.9 = (f32[16]{0:T(128)S(1)}, f32[16]{0:T(128)}, u32[]{:S(2)}) copy-start(f32[16]{0:T(128)} %param.14) | copy-start | bytes 196
  1.3 0.7 %copy-start.10 = (s32[1,32]{1,0:T(1,128)S(1)}, s32[1,32]{1,0:T(1,128)}, u32[]{:S(2)}) copy-start(s32[1,32]{1,0:T(1,128)} %spots_ref.1) | copy-start | bytes 388
  1.3 0.7 %copy-start.7 = (f32[1,2]{1,0:T(1,128)S(1)}, f32[1,2]{1,0:T(1,128)}, u32[]{:S(2)}) copy-start(f32[1,2]{1,0:T(1,128)} %amps_ref.3) | copy-start | bytes 28
  1.3 0.7 %copy-start.8 = (f32[1,2,32]{2,1,0:T(2,128)S(1)}, f32[1,2,32]{2,1,0:T(2,128)}, u32[]{:S(2)}) copy-start(f32[1,2,32]{2,1,0:T(2,128)} %traces_ref.1) | copy-start | bytes 772
  2.0 0.8 %copy-start = (f32[1,8,16,128]{3,2,1,0:T(8,128)S(1)}, f32[1,8,16,128]{3,2,1,0:T(8,128)}, u32[]{:S(2)}) copy-start(f32[1,8,16,128]{3,2,1,0:T(8,128)} %src_now.3) | copy-start | bytes 196612
  2.9 0.8 %copy-start.2 = (f32[1,8,16,128]{3,2,1,0:T(8,128)S(1)}, f32[1,8,16,128]{3,2,1,0:T(8,128)}, u32[]{:S(2)}) copy-start(f32[1,8,16,128]{3,2,1,0:T(8,128)} %rec_now.3) | copy-start | bytes 196612
  3.7 0.8 %copy-start.4 = (f32[1,8,16,128]{3,2,1,0:T(8,128)S(1)}, f32[1,8,16,128]{3,2,1,0:T(8,128)}, u32[]{:S(2)}) copy-start(f32[1,8,16,128]{3,2,1,0:T(8,128)} %src_prev.1) | copy-start | bytes 196612
  4.5 0.8 %copy-start.5 = (f32[1,8,16,128]{3,2,1,0:T(8,128)S(1)}, f32[1,8,16,128]{3,2,1,0:T(8,128)}, u32[]{:S(2)}) copy-start(f32[1,8,16,128]{3,2,1,0:T(8,128)} %rec_prev.1) | copy-start | bytes 196612
  5.4 0.8 %copy-start.6 = (s32[8,16,128]{2,1,0:T(8,128)S(1)}, s32[8,16,128]{2,1,0:T(8,128)}, u32[]{:S(2)}) copy-start(s32[8,16,128]{2,1,0:T(8,128)} %ids_ref.1) | copy-start | bytes 196612
  6.2 12.2 %copy-start.1 = (f32[1,8,16,128]{3,2,1,0:T(8,128)S(1)}, f32[1,8,16,128]{3,2,1,0:T(8,128)}, u32[]{:S(2)}) copy-start(f32[1,8,16,128]{3,2,1,0:T(8,128)} %src_now.3) | copy-start | bytes 196612
  6.2 12.2 %copy-start.3 = (f32[1,8,16,128]{3,2,1,0:T(8,128)S(1)}, f32[1,8,16,128]{3,2,1,0:T(8,128)}, u32[]{:S(2)}) copy-start(f32[1,8,16,128]{3,2,1,0:T(8,128)} %rec_now.3) | copy-start | bytes 196612
  7.2 7.0 %collective-permute-start = (f32[20,8,128]{2,1,0:T(8,128)S(1)}, f32[20,8,128]{2,1,0:T(8,128)S(1)}, u32[]{:S(2)}, u32[]{:S(2)}) collective-permute-start(f32[20,8,128]{2,1,0:T(8,128)S(1)} %get-tuple-element.14), channel_id=1, source_target_pairs={{0,4},{4,8},{8,12},{1,5},{5,9},{9,13},{2,6},{6,10},{10,14},{3,7},{... | collective-permute-start | bytes 245768 | tf_op jit(solution)/shard_map/ppermute | solution.py:248
  12.1 6.3 %collective-permute-start.1 = (f32[20,8,128]{2,1,0:T(8,128)S(1)}, f32[20,8,128]{2,1,0:T(8,128)S(1)}, u32[]{:S(2)}, u32[]{:S(2)}) collective-permute-start(f32[20,8,128]{2,1,0:T(8,128)S(1)} %get-tuple-element.15), channel_id=1, source_target_pairs={{4,0},{8,4},{12,8},{5,1},{9,5},{13,9},{6,2},{10,6},{14,10},{7,3},{... | collective-permute-start | bytes 245768 | tf_op jit(solution)/shard_map/ppermute | solution.py:248
  27.2 6.8 %collective-permute-start.3 = (f32[4,2,2,16,128]{4,3,2,1,0:T(8,128)S(1)}, f32[4,2,2,16,128]{4,3,2,1,0:T(8,128)S(1)}, u32[]{:S(2)}, u32[]{:S(2)}) collective-permute-start(f32[4,2,2,16,128]{4,3,2,1,0:T(8,128)S(1)} %all_to_all.5.mine_ref), channel_id=1, source_target_pairs={{4,0},{8,4},{12,8},{5,1},{9,5},{13,9},{6,2},{10,6},{14,10},{7,3},{... | collective-permute-start | bytes 393224 | tf_op jit(solution)/shard_map/ppermute | solution.py:248
  28.5 7.1 %collective-permute-start.2 = (f32[4,2,2,16,128]{4,3,2,1,0:T(8,128)S(1)}, f32[4,2,2,16,128]{4,3,2,1,0:T(8,128)S(1)}, u32[]{:S(2)}, u32[]{:S(2)}) collective-permute-start(f32[4,2,2,16,128]{4,3,2,1,0:T(8,128)S(1)} %all_to_all.5.mine_ref), channel_id=1, source_target_pairs={{0,4},{4,8},{8,12},{1,5},{5,9},{9,13},{2,6},{6,10},{10,14},{3,7},{... | collective-permute-start | bytes 393224 | tf_op jit(solution)/shard_map/ppermute | solution.py:248

commit v2 on v1

v2 whole, which is shorter than its diff:
```python
import functools

import jax
import jax.numpy as jnp
from jax import lax
from jax.experimental import pallas as pl
from jax.experimental.pallas import tpu as pltpu
from jax.sharding import PartitionSpec as P

OFFS = 33
REACH = OFFS // 2
HALO = 4
LEAD = 8

COEFS = (-205.0 / 72.0, 8.0 / 5.0, -1.0 / 5.0, 8.0 / 315.0, -1.0 / 560.0)

VMEM = pl.BlockSpec(memory_space=pltpu.VMEM)
HBM = pl.BlockSpec(memory_space=pltpu.HBM)
LIMIT = 16 * 1024 * 1024


def lane_weights(shape):
    lane = lax.broadcasted_iota(jnp.int32, shape, 1)
    across = shape[1]
    after = [jnp.where(lane < across - k, COEFS[k], 0.0) for k in range(1, HALO + 1)]
    before = [jnp.where(lane >= k, COEFS[k], 0.0) for k in range(1, HALO + 1)]
    return after, before


def laplace_level(wide, field, level, levels, extent, weights):
    after, before = weights
    centre = wide[field, level, LEAD : LEAD + extent, :]
    across = centre.shape[1]
    total = 3.0 * COEFS[0] * centre
    for k in range(1, HALO + 1):
        beside = (
            wide[field, level, LEAD + k : LEAD + k + extent, :]
            + wide[field, level, LEAD - k : LEAD - k + extent, :]
        )
        if level + k < levels:
            beside = beside + wide[field, level + k, LEAD : LEAD + extent, :]
        if level - k >= 0:
            beside = beside + wide[field, level - k, LEAD : LEAD + extent, :]
        total = total + COEFS[k] * beside
        total = total + after[k - 1] * pltpu.roll(centre, across - k, 1)
        total = total + before[k - 1] * pltpu.roll(centre, k, 1)
    return total


def source_hit(cell, level, width, first, shape):
    across = shape[1]
    flat = lax.broadcasted_iota(jnp.int32, shape, 0) * across + lax.broadcasted_iota(
        jnp.int32, shape, 1
    )
    return flat == cell - (level * width + first) * across


def own_part(
    width,
    table_hbm,
    spots_hbm,
    traces_hbm,
    cell_hbm,
    amps_hbm,
    ids_hbm,
    src_now,
    rec_now,
    src_prev,
    rec_prev,
    wide,
    part_ref,
    later_ref,
    coef_ref,
    low_ref,
    high_ref,
    table,
    spots_ref,
    traces_ref,
    cell_ref,
    amps_ref,
    ids_ref,
    prev_ref,
    sems,
):
    levels, extent, across = ids_ref.shape
    shape = (extent, across)
    regions = table_hbm.shape[1]
    end = LEAD + extent
    moves = (
        (table_hbm, table),
        (ids_hbm, ids_ref),
        (spots_hbm, spots_ref),
        (traces_hbm, traces_ref),
        (cell_hbm, cell_ref),
        (amps_hbm, amps_ref),
        (src_now.at[0], wide.at[0, :, pl.ds(LEAD, extent), :]),
        (src_prev.at[0], prev_ref.at[0]),
        (rec_now.at[0], wide.at[1, :, pl.ds(LEAD, extent), :]),
        (rec_prev.at[0], prev_ref.at[1]),
    )
    copies = [
        pltpu.make_async_copy(here, there, sems.at[i]) for i, (here, there) in enumerate(moves)
    ]
    for copy in copies:
        copy.start()
    zeros = jnp.zeros((LEAD, across), jnp.float32)
    for field in range(2):
        for level in range(levels):
            wide[field, level, 0:LEAD, :] = zeros
            wide[field, level, end : end + LEAD, :] = zeros
    weights = lane_weights(shape)

    for copy in copies[2:4]:
        copy.wait()
    spots = spots_ref[...]
    column = lax.broadcasted_iota(jnp.int32, (extent, spots.shape[1]), 0) * across
    in_column = (spots >= column) & (spots < column + across)
    lane = lax.broadcasted_iota(jnp.int32, (across, spots.shape[1]), 0)
    in_row = jnp.where(lax.rem(spots, across) == lane, 1.0, 0.0)
    traces = jnp.concatenate(
        [jnp.where(in_column, traces_ref[0, t : t + 1, :], 0.0) for t in range(2)], axis=0
    )
    planes = lax.dot_general(
        traces,
        in_row,
        (((1,), (1,)), ((), ())),
        precision=lax.Precision.HIGHEST,
        preferred_element_type=jnp.float32,
    )

    copies[0].wait()
    copies[1].wait()
    speeds = jnp.concatenate(
        [table[...], jnp.zeros((1, across - regions), jnp.float32)], axis=1
    )
    speeds = jnp.broadcast_to(speeds, (8, across))
    for level in range(levels):
        for row in range(0, extent, 8):
            ids = ids_ref[level, row : row + 8, :]
            coef_ref[level, row : row + 8, :] = jnp.take_along_axis(
                speeds, ids, axis=1, mode="promise_in_bounds"
            )
        place = 2 * levels + level // 2
        rows = pl.ds(level % 2 * HALO, HALO)
        low_ref[place, rows, :] = coef_ref[level, 0:HALO, :]
        high_ref[place, rows, :] = coef_ref[level, extent - HALO : extent, :]

    copies[4].wait()
    copies[5].wait()
    first = lax.axis_index("tile") * extent
    for field in range(2):
        copies[6 + 2 * field].wait()
        copies[7 + 2 * field].wait()
        for level in range(levels):
            total = laplace_level(wide, field, level, levels, extent, weights)
            now = wide[field, level, LEAD:end, :]
            value = 2.0 * now - prev_ref[field, level] + coef_ref[level] * total
            later = -now
            if field == 0:
                hit = source_hit(cell_ref[0], level, width, first, shape)
                value = value + jnp.where(hit, amps_ref[0, 0], 0.0)
                later = later + jnp.where(hit, amps_ref[0, 1], 0.0)
            elif level == 0:
                value = value + planes[:extent, :]
                later = later + planes[extent:, :]
            part_ref[field, level] = value
            later_ref[field, level] = later
            place = field * levels + level
            low_ref[place, 0:HALO, :] = now[0:HALO, :]
            low_ref[place, HALO : 2 * HALO, :] = value[0:HALO, :]
            high_ref[place, 0:HALO, :] = now[extent - HALO : extent, :]
            high_ref[place, HALO : 2 * HALO, :] = value[extent - HALO : extent, :]


def both_steps(
    own,
    part_ref,
    later_ref,
    coef_ref,
    low_ref,
    high_ref,
    packed_ref,
    other,
    middle,
):
    levels, extent, across = coef_ref.shape
    shape = (extent, across)
    share = packed_ref.shape[2]
    end = LEAD + extent
    for field in range(2):
        for level in range(levels):
            place = field * levels + level
            other[field, level, LEAD:end, :] = jnp.zeros(shape, jnp.float32)
            other[field, level, LEAD - HALO : LEAD, :] = low_ref[place, 0:HALO, :]
            other[field, level, end : end + HALO, :] = high_ref[place, 0:HALO, :]
    for field in range(2):
        for level in range(levels):
            place = field * levels + level
            pair = 2 * levels + level // 2
            rows = pl.ds(level % 2 * HALO, HALO)
            below = jnp.zeros((HALO, across), jnp.float32)
            above = jnp.zeros((HALO, across), jnp.float32)
            left = jnp.zeros((8, across), jnp.float32)
            right = jnp.zeros((8, across), jnp.float32)
            for k in range(1, HALO + 1):
                begin = LEAD - HALO + k
                below = below + COEFS[k] * own[field, level, begin : begin + HALO, :]
                above = above + COEFS[k] * own[field, level, end - k : end - k + HALO, :]
                left = left + COEFS[k] * other[field, level, LEAD - k : LEAD - k + 8, :]
                right = right + COEFS[k] * other[field, level, end - 8 + k : end + k, :]
            middle[field, level, LEAD - HALO : LEAD, :] = (
                low_ref[place, HALO : 2 * HALO, :] + low_ref[pair, rows, :] * below
            )
            middle[field, level, end : end + HALO, :] = (
                high_ref[place, HALO : 2 * HALO, :] + high_ref[pair, rows, :] * above
            )
            middle[field, level, LEAD : LEAD + 8, :] = (
                part_ref[field, level, 0:8, :] + coef_ref[level, 0:8, :] * left
            )
            middle[field, level, end - 8 : end, :] = (
                part_ref[field, level, extent - 8 : extent, :]
                + coef_ref[level, extent - 8 : extent, :] * right
            )
    weights = lane_weights(shape)
    for field in range(2):
        for level in range(levels):
            total = laplace_level(middle, field, level, levels, extent, weights)
            value = 2.0 * middle[field, level, LEAD:end, :] + later_ref[field, level]
            packed_ref[level // share, field, level % share] = value + coef_ref[level] * total


def image_products(
    weight,
    final_ref,
    mine_ref,
    low_ref,
    high_ref,
    src_hbm,
    rec_hbm,
    image_hbm,
    wide,
    image_ref,
    field_sems,
    image_sems,
):
    shots, _, share, extent, across = mine_ref.shape
    copies = []
    for field, out in enumerate((src_hbm, rec_hbm)):
        for shot in range(shots):
            copies.append(
                pltpu.make_async_copy(
                    final_ref.at[shot, field],
                    out.at[0, pl.ds(shot * share, share)],
                    field_sems.at[field, shot],
                )
            )
    for copy in copies:
        copy.start()
    for shot in range(shots):
        for field in range(2):
            for level in range(share):
                scale = weight if field == 0 else 1.0
                wide[shot, field, level, 0:REACH, :] = (
                    scale * low_ref[shot, field, level, extent - REACH : extent, :]
                )
                wide[shot, field, level, REACH : REACH + extent, :] = (
                    scale * mine_ref[shot, field, level]
                )
                wide[shot, field, level, REACH + extent : 2 * REACH + extent, :] = (
                    scale * high_ref[shot, field, level, 0:REACH, :]
                )
    parts = image_sems.shape[0]
    for piece in range(parts):
        offsets = range(piece * OFFS // parts, (piece + 1) * OFFS // parts)
        for offset in offsets:
            for level in range(share):
                total = jnp.zeros((extent, across), jnp.float32)
                for shot in range(shots):
                    begin = 2 * REACH - offset
                    total = total + (
                        wide[shot, 0, level, begin : begin + extent, :]
                        * wide[shot, 1, level, offset : offset + extent, :]
                    )
                image_ref[offset, level] = total
        rows = pl.ds(offsets[0], len(offsets))
        copy = pltpu.make_async_copy(image_ref.at[rows], image_hbm.at[rows], image_sems.at[piece])
        copy.start()
        copies.append(copy)
    for copy in copies:
        copy.wait()


def swap_sides(low, high):
    count = lax.axis_size("tile")
    forward = [(i, i + 1) for i in range(count - 1)]
    backward = [(target, source) for source, target in forward]
    return lax.ppermute(high, "tile", forward), lax.ppermute(low, "tile", backward)


def per_device(
    src_prev,
    src_now,
    rec_prev,
    rec_now,
    speed_table,
    region_ids,
    source_cell,
    wavelet,
    receiver_cell,
    receiver_data,
):
    _, levels, extent, across = src_now.shape
    width = extent * lax.axis_size("tile")
    shots = lax.axis_size("shot")
    share = levels // shots
    params = pltpu.CompilerParams(vmem_limit_bytes=LIMIT)

    def struct(*shape):
        return jax.ShapeDtypeStruct(shape, jnp.float32)

    def scratch(*shape, dtype=jnp.float32):
        return pltpu.VMEM(shape, dtype)

    wide_shape = (2, levels, extent + 2 * LEAD, across)
    message = struct(2 * levels + levels // 2, 2 * HALO, across)
    own, part, later, coef, low, high = pl.pallas_call(
        functools.partial(own_part, width),
        out_shape=(
            struct(*wide_shape),
            struct(2, levels, extent, across),
            struct(2, levels, extent, across),
            struct(levels, extent, across),
            message,
            message,
        ),
        in_specs=[HBM] * 10,
        out_specs=[VMEM] * 6,
        scratch_shapes=[
            scratch(1, speed_table.shape[0]),
            scratch(*receiver_cell.shape, dtype=jnp.int32),
            scratch(*receiver_data.shape),
            pltpu.SMEM(source_cell.shape, jnp.int32),
            pltpu.SMEM(wavelet.shape, jnp.float32),
            scratch(levels, extent, across, dtype=jnp.int32),
            scratch(2, levels, extent, across),
            pltpu.SemaphoreType.DMA((10,)),
        ],
        compiler_params=params,
        name="own_part",
    )(
        speed_table.reshape(1, -1),
        receiver_cell,
        receiver_data,
        source_cell,
        wavelet,
        region_ids,
        src_now,
        rec_now,
        src_prev,
        rec_prev,
    )
    from_low, from_high = swap_sides(low, high)
    packed = pl.pallas_call(
        both_steps,
        out_shape=struct(shots, 2, share, extent, across),
        in_specs=[VMEM] * 6,
        out_specs=VMEM,
        scratch_shapes=[scratch(*wide_shape), scratch(*wide_shape)],
        compiler_params=params,
        name="both_steps",
    )(own, part, later, coef, from_low, from_high)
    mine = lax.all_to_all(packed, "shot", 0, 0, tiled=True)
    low_fields, high_fields = swap_sides(mine, mine)
    return pl.pallas_call(
        functools.partial(image_products, 1.0 / shots),
        out_shape=(
            struct(1, levels, extent, across),
            struct(1, levels, extent, across),
            struct(OFFS, share, extent, across),
        ),
        in_specs=[VMEM] * 4,
        out_specs=[HBM] * 3,
        scratch_shapes=[
            scratch(shots, 2, share, extent + 2 * REACH, across),
            scratch(OFFS, share, extent, across),
            pltpu.SemaphoreType.DMA((2, shots)),
            pltpu.SemaphoreType.DMA((3,)),
        ],
        compiler_params=params,
        name="image_products",
    )(packed, mine, low_fields, high_fields)


def solution(mesh):
    field = P(("groups", "shot"), None, "tile", None)
    return jax.shard_map(
        per_device,
        mesh=mesh,
        in_specs=(
            field,
            field,
            field,
            field,
            P("groups"),
            P(None, ("groups", "tile"), None),
            P(("groups", "shot")),
            P(("groups", "shot"), None),
            P(("groups", "shot"), "tile"),
            P(("groups", "shot"), None, "tile"),
        ),
        out_specs=(field, field, P(None, "shot", ("groups", "tile"), None)),
        check_vma=False,
    )
```

time: 37.1 us -> 36 us (0.970)
  Pallas kernels: 3.61 us -> 2.52 us
    pallas_call x2, Pallas kernels: 2.56 us -> 1.54 us  [the longest x1 1.16 us: per_device(): pl.pallas_call(functools.partial(own_part, width), out_shape=(struct(*wid...]
    unnamed x22 -> x18, local copies, waits for them, and re-layouts: 4.9 us -> 4.85 us
where the time goes in v2:
time: 36 us; the launch traced here: 35.6 us
  starting transfers between devices  12.1 us (34%)
  waiting for transfers between devices  7.53 us (21%)
  blocking collectives  7.19 us (20%)
  local copies, waits for them, and re-layouts  4.85 us (13%)
  Pallas kernels  2.52 us (7%)
  between operations  1.4 us (4%)
    ppermute x2, starting transfers between devices, swap_sides(): lax.ppermute(high, 'tile', forward)  9.49 us
    all_to_all x1, blocking collectives, per_device(): mine = lax.all_to_all(packed, 'shot', 0, 0, tiled=True)  7.19 us
    ppermute x2, waiting for transfers between devices, swap_sides(): lax.ppermute(low, 'tile', backward)  5.3 us
    unnamed x18, local copies, waits for them, and re-layouts  4.85 us
    ppermute x2, starting transfers between devices, swap_sides(): lax.ppermute(low, 'tile', backward)  2.57 us
    ppermute x2, waiting for transfers between devices, swap_sides(): lax.ppermute(high, 'tile', forward)  2.23 us
    pallas_call x1, Pallas kernels, per_device(): pl.pallas_call(functools.partial(own_part, width), out_shape=(struct(*wid...  1.16 us
    pallas_call x1, Pallas kernels, per_device(): pl.pallas_call(functools.partial(image_products, 1.0 / shots), out_shape=...  0.98 us
  transfers between devices with their start and end apart: 4, of which 4 were waited for; matrix products, arithmetic and copies ran while one was open for 0% of the time, Pallas kernels for 0%

profile of v2, /device:TPU:0, one launch (start us, length us, event | category | flops | bytes accessed | tf_op | source)
XLA Modules:
  0.0 35.6 jit_solution(11541865704600427108)
XLA Ops:
  0.6 0.0 copy-start.7
  0.6 0.0 copy-start.8
  1.3 0.0 copy-start.5
  1.3 0.0 copy-start.6
  1.3 0.0 copy-done.7
  1.3 0.0 copy-done.8
  1.4 0.6 %copy-done.5 = f32[1,2,32]{2,1,0:T(2,128)S(1)} copy-done((f32[1,2,32]{2,1,0:T(2,128)S(1)}, f32[1,2,32]{2,1,0:T(2,128)}, u32[]{:S(2)}) %copy-start.5) | copy-done | bytes 280
  2.0 0.0 copy-done.6
  2.0 0.0 copy-start
  2.0 0.8 %copy-done = s32[8,16,128]{2,1,0:T(8,128)S(1)} copy-done((s32[8,16,128]{2,1,0:T(8,128)S(1)}, s32[8,16,128]{2,1,0:T(8,128)}, u32[]{:S(2)}) %copy-start) | copy-done | bytes 65560
  2.8 0.0 copy-start.1
  2.8 0.8 %copy-done.1 = f32[1,8,16,128]{3,2,1,0:T(8,128)S(1)} copy-done((f32[1,8,16,128]{3,2,1,0:T(8,128)S(1)}, f32[1,8,16,128]{3,2,1,0:T(8,128)}, u32[]{:S(2)}) %copy-start.1) | copy-done | bytes 65560
  3.7 0.0 copy-start.2
  3.7 0.8 %copy-done.2 = f32[1,8,16,128]{3,2,1,0:T(8,128)S(1)} copy-done((f32[1,8,16,128]{3,2,1,0:T(8,128)S(1)}, f32[1,8,16,128]{3,2,1,0:T(8,128)}, u32[]{:S(2)}) %copy-start.2) | copy-done | bytes 65560
  4.5 0.0 copy-start.3
  4.5 0.8 %copy-done.3 = f32[1,8,16,128]{3,2,1,0:T(8,128)S(1)} copy-done((f32[1,8,16,128]{3,2,1,0:T(8,128)S(1)}, f32[1,8,16,128]{3,2,1,0:T(8,128)}, u32[]{:S(2)}) %copy-start.3) | copy-done | bytes 65560
  5.4 0.0 copy-start.4
  5.4 0.8 %copy-done.4 = f32[1,8,16,128]{3,2,1,0:T(8,128)S(1)} copy-done((f32[1,8,16,128]{3,2,1,0:T(8,128)S(1)}, f32[1,8,16,128]{3,2,1,0:T(8,128)}, u32[]{:S(2)}) %copy-start.4) | copy-done | bytes 65560
  6.2 1.2 %own_part.1 = (f32[2,8,32,128]{3,2,1,0:T(8,128)S(1)}, f32[2,8,16,128]{3,2,1,0:T(8,128)S(1)}, f32[2,8,16,128]{3,2,1,0:T(8,128)S(1)}, f32[8,16,128]{2,1,0:T(8,128)...) custom-call(f32[1,16]{1,0:T(1,128)S(1)} %bitcast.1, s32[1,32]{1,0:T(1,128)S(1)} %copy-done.7, ...), custom_call_target="tpu_custom_call" | custom-call | tf_op jit(solution)/shard_map/own_part/pallas_call | solution.py:326
  7.4 4.9 %collective-permute-start = (f32[20,8,128]{2,1,0:T(8,128)S(1)}, f32[20,8,128]{2,1,0:T(8,128)S(1)}, u32[]{:S(2)}, u32[]{:S(2)}) collective-permute-start(f32[20,8,128]{2,1,0:T(8,128)S(1)} %get-tuple-element.13), channel_id=1, source_target_pairs={{0,4},{4,8},{8,12},{1,5},{5,9},{9,13},{2,6},{6,10},{10,14},{3,7},{... | collective-permute-start | bytes 245768 | tf_op jit(solution)/shard_map/ppermute | solution.py:297
  12.3 1.3 %collective-permute-start.1 = (f32[20,8,128]{2,1,0:T(8,128)S(1)}, f32[20,8,128]{2,1,0:T(8,128)S(1)}, u32[]{:S(2)}, u32[]{:S(2)}) collective-permute-start(f32[20,8,128]{2,1,0:T(8,128)S(1)} %get-tuple-element.14), channel_id=1, source_target_pairs={{4,0},{8,4},{12,8},{5,1},{9,5},{13,9},{6,2},{10,6},{14,10},{7,3},{... | collective-permute-start | bytes 245768 | tf_op jit(solution)/shard_map/ppermute | solution.py:297
  13.6 0.7 %collective-permute-done.low_ref = f32[20,8,128]{2,1,0:T(8,128)S(1)} collective-permute-done((f32[20,8,128]{2,1,0:T(8,128)S(1)}, f32[20,8,128]{2,1,0:T(8,128)S(1)}, u32[]{:S(2)}, u32[]{:S(2)}) %collective-permute-start) | collective-permute-done | bytes 81952 | tf_op jit(solution)/shard_map/ppermute | solution.py:297
  14.3 4.3 %collective-permute-done.1.high_ref = f32[20,8,128]{2,1,0:T(8,128)S(1)} collective-permute-done((f32[20,8,128]{2,1,0:T(8,128)S(1)}, f32[20,8,128]{2,1,0:T(8,128)S(1)}, u32[]{:S(2)}, u32[]{:S(2)}) %collective-permute-start.1) | collective-permute-done | bytes 81952 | tf_op jit(solution)/shard_map/ppermute | solution.py:297
  18.6 0.4 %both_steps.1.final_ref = f32[4,2,2,16,128]{4,3,2,1,0:T(8,128)S(1)} custom-call(f32[2,8,32,128]{3,2,1,0:T(8,128)S(1)} %get-tuple-element.9.own, f32[2,8,16,128]{3,2,1,0:T(8,128)S(1)} %get-tuple-element.10.part_ref, f32[2,8,16,128]{3,2,1,0:T(8,128)S(1)} %get-tuple-element.11.later_ref, f32[8,16,128]{2,1,0:T(8,128)S(1)} %get-tuple-element.12.coef_ref, ...), custom_call_target="tpu_custom_call" | custom-call | tf_op jit(solution)/shard_map/both_steps/pallas_call | solution.py:363
  19.0 7.2 %all_to_all.5.mine_ref = f32[4,2,2,16,128]{4,3,2,1,0:T(8,128)S(1)} all-to-all(f32[4,2,2,16,128]{4,3,2,1,0:T(8,128)S(1)} %both_steps.1.final_ref), channel_id=1, replica_groups=mesh['groups'=2,'tile'=4,'shot'=4] {'shot'}, dimensions={0} | all-to-all | bytes 262144 | tf_op jit(solution)/shard_map/all_to_all | solution.py:372
  26.2 1.3 %collective-permute-start.3 = (f32[4,2,2,16,128]{4,3,2,1,0:T(8,128)S(1)}, f32[4,2,2,16,128]{4,3,2,1,0:T(8,128)S(1)}, u32[]{:S(2)}, u32[]{:S(2)}) collective-permute-start(f32[4,2,2,16,128]{4,3,2,1,0:T(8,128)S(1)} %all_to_all.5.mine_ref), channel_id=1, source_target_pairs={{4,0},{8,4},{12,8},{5,1},{9,5},{13,9},{6,2},{10,6},{14,10},{7,3},{... | collective-permute-start | bytes 393224 | tf_op jit(solution)/shard_map/ppermute | solution.py:297
  27.5 4.6 %collective-permute-start.2 = (f32[4,2,2,16,128]{4,3,2,1,0:T(8,128)S(1)}, f32[4,2,2,16,128]{4,3,2,1,0:T(8,128)S(1)}, u32[]{:S(2)}, u32[]{:S(2)}) collective-permute-start(f32[4,2,2,16,128]{4,3,2,1,0:T(8,128)S(1)} %all_to_all.5.mine_ref), channel_id=1, source_target_pairs={{0,4},{4,8},{8,12},{1,5},{5,9},{9,13},{2,6},{6,10},{10,14},{3,7},{... | collective-permute-start | bytes 393224 | tf_op jit(solution)/shard_map/ppermute | solution.py:297
  32.1 1.0 %collective-permute-done.3.high_ref = f32[4,2,2,16,128]{4,3,2,1,0:T(8,128)S(1)} collective-permute-done((f32[4,2,2,16,128]{4,3,2,1,0:T(8,128)S(1)}, f32[4,2,2,16,128]{4,3,2,1,0:T(8,128)S(1)}, u32[]{:S(2)}, u32[]{:S(2)}) %collective-permute-start.3) | collective-permute-done | bytes 131104 | tf_op jit(solution)/shard_map/ppermute | solution.py:297
  33.1 1.5 %collective-permute-done.2.low_ref = f32[4,2,2,16,128]{4,3,2,1,0:T(8,128)S(1)} collective-permute-done((f32[4,2,2,16,128]{4,3,2,1,0:T(8,128)S(1)}, f32[4,2,2,16,128]{4,3,2,1,0:T(8,128)S(1)}, u32[]{:S(2)}, u32[]{:S(2)}) %collective-permute-start.2) | collective-permute-done | bytes 131104 | tf_op jit(solution)/shard_map/ppermute | solution.py:297
  34.6 1.0 %image_products.1 = (f32[1,8,16,128]{3,2,1,0:T(8,128)}, f32[1,8,16,128]{3,2,1,0:T(8,128)}, f32[33,2,16,128]{3,2,1,0:T(8,128)}) custom-call(f32[4,2,2,16,128]{4,3,2,1,0:T(8,128)S(1)} %both_steps.1.final_ref, f32[4,2,2,16,128]{4,3,2,1,0:T(8,128)S(1)} %all_to_all.5.mine_ref, f32[4,2,2,16,128]{4,3,2,1,0:T(8,128)S(1)} %collective-permute-done.2.low_ref, ...), custom_call_target="tpu_custom_call" | custom-call | tf_op jit(solution)/shard_map/image_products/pallas_call | solution.py:374
Async XLA Ops:
  0.6 0.7 %copy-start.7 = (s32[1,32]{1,0:T(1,128)S(1)}, s32[1,32]{1,0:T(1,128)}, u32[]{:S(2)}) copy-start(s32[1,32]{1,0:T(1,128)} %spots_hbm.1) | copy-start | bytes 388
  0.6 0.7 %copy-start.8 = (f32[1,2]{1,0:T(1,128)S(1)}, f32[1,2]{1,0:T(1,128)}, u32[]{:S(2)}) copy-start(f32[1,2]{1,0:T(1,128)} %amps_hbm.1) | copy-start | bytes 28
  1.3 0.7 %copy-start.5 = (f32[1,2,32]{2,1,0:T(2,128)S(1)}, f32[1,2,32]{2,1,0:T(2,128)}, u32[]{:S(2)}) copy-start(f32[1,2,32]{2,1,0:T(2,128)} %traces_hbm.1) | copy-start | bytes 772
  1.3 0.7 %copy-start.6 = (f32[16]{0:T(128)S(1)}, f32[16]{0:T(128)}, u32[]{:S(2)}) copy-start(f32[16]{0:T(128)} %param.14) | copy-start | bytes 196
  2.0 0.8 %copy-start = (s32[8,16,128]{2,1,0:T(8,128)S(1)}, s32[8,16,128]{2,1,0:T(8,128)}, u32[]{:S(2)}) copy-start(s32[8,16,128]{2,1,0:T(8,128)} %ids_hbm.1) | copy-start | bytes 196612
  2.8 0.8 %copy-start.1 = (f32[1,8,16,128]{3,2,1,0:T(8,128)S(1)}, f32[1,8,16,128]{3,2,1,0:T(8,128)}, u32[]{:S(2)}) copy-start(f32[1,8,16,128]{3,2,1,0:T(8,128)} %src_now.1) | copy-start | bytes 196612
  3.7 0.8 %copy-start.2 = (f32[1,8,16,128]{3,2,1,0:T(8,128)S(1)}, f32[1,8,16,128]{3,2,1,0:T(8,128)}, u32[]{:S(2)}) copy-start(f32[1,8,16,128]{3,2,1,0:T(8,128)} %rec_now.1) | copy-start | bytes 196612
  4.5 0.8 %copy-start.3 = (f32[1,8,16,128]{3,2,1,0:T(8,128)S(1)}, f32[1,8,16,128]{3,2,1,0:T(8,128)}, u32[]{:S(2)}) copy-start(f32[1,8,16,128]{3,2,1,0:T(8,128)} %src_prev.1) | copy-start | bytes 196612
  5.4 0.8 %copy-start.4 = (f32[1,8,16,128]{3,2,1,0:T(8,128)S(1)}, f32[1,8,16,128]{3,2,1,0:T(8,128)}, u32[]{:S(2)}) copy-start(f32[1,8,16,128]{3,2,1,0:T(8,128)} %rec_prev.1) | copy-start | bytes 196612
  7.4 7.0 %collective-permute-start = (f32[20,8,128]{2,1,0:T(8,128)S(1)}, f32[20,8,128]{2,1,0:T(8,128)S(1)}, u32[]{:S(2)}, u32[]{:S(2)}) collective-permute-start(f32[20,8,128]{2,1,0:T(8,128)S(1)} %get-tuple-element.13), channel_id=1, source_target_pairs={{0,4},{4,8},{8,12},{1,5},{5,9},{9,13},{2,6},{6,10},{10,14},{3,7},{... | collective-permute-start | bytes 245768 | tf_op jit(solution)/shard_map/ppermute | solution.py:297
  12.3 6.3 %collective-permute-start.1 = (f32[20,8,128]{2,1,0:T(8,128)S(1)}, f32[20,8,128]{2,1,0:T(8,128)S(1)}, u32[]{:S(2)}, u32[]{:S(2)}) collective-permute-start(f32[20,8,128]{2,1,0:T(8,128)S(1)} %get-tuple-element.14), channel_id=1, source_target_pairs={{4,0},{8,4},{12,8},{5,1},{9,5},{13,9},{6,2},{10,6},{14,10},{7,3},{... | collective-permute-start | bytes 245768 | tf_op jit(solution)/shard_map/ppermute | solution.py:297
  26.2 6.8 %collective-permute-start.3 = (f32[4,2,2,16,128]{4,3,2,1,0:T(8,128)S(1)}, f32[4,2,2,16,128]{4,3,2,1,0:T(8,128)S(1)}, u32[]{:S(2)}, u32[]{:S(2)}) collective-permute-start(f32[4,2,2,16,128]{4,3,2,1,0:T(8,128)S(1)} %all_to_all.5.mine_ref), channel_id=1, source_target_pairs={{4,0},{8,4},{12,8},{5,1},{9,5},{13,9},{6,2},{10,6},{14,10},{7,3},{... | collective-permute-start | bytes 393224 | tf_op jit(solution)/shard_map/ppermute | solution.py:297
  27.5 7.1 %collective-permute-start.2 = (f32[4,2,2,16,128]{4,3,2,1,0:T(8,128)S(1)}, f32[4,2,2,16,128]{4,3,2,1,0:T(8,128)S(1)}, u32[]{:S(2)}, u32[]{:S(2)}) collective-permute-start(f32[4,2,2,16,128]{4,3,2,1,0:T(8,128)S(1)} %all_to_all.5.mine_ref), channel_id=1, source_target_pairs={{0,4},{4,8},{8,12},{1,5},{5,9},{9,13},{2,6},{6,10},{10,14},{3,7},{... | collective-permute-start | bytes 393224 | tf_op jit(solution)/shard_map/ppermute | solution.py:297

commit v3 on v2

--- a/solution.py
+++ b/solution.py
@@ -16,6 +16,7 @@
 
 VMEM = pl.BlockSpec(memory_space=pltpu.VMEM)
 HBM = pl.BlockSpec(memory_space=pltpu.HBM)
+SMEM = pl.BlockSpec(memory_space=pltpu.SMEM)
 LIMIT = 16 * 1024 * 1024
 
 
@@ -47,26 +48,17 @@
     return total
 
 
-def source_hit(cell, level, width, first, shape):
-    across = shape[1]
-    flat = lax.broadcasted_iota(jnp.int32, shape, 0) * across + lax.broadcasted_iota(
-        jnp.int32, shape, 1
-    )
-    return flat == cell - (level * width + first) * across
-
-
 def own_part(
-    width,
     table_hbm,
     spots_hbm,
     traces_hbm,
-    cell_hbm,
     amps_hbm,
     ids_hbm,
     src_now,
     rec_now,
     src_prev,
     rec_prev,
+    amps_ref,
     wide,
     part_ref,
     later_ref,
@@ -76,8 +68,6 @@
     table,
     spots_ref,
     traces_ref,
-    cell_ref,
-    amps_ref,
     ids_ref,
     prev_ref,
     sems,
@@ -91,12 +81,11 @@
         (ids_hbm, ids_ref),
         (spots_hbm, spots_ref),
         (traces_hbm, traces_ref),
-        (cell_hbm, cell_ref),
-        (amps_hbm, amps_ref),
         (src_now.at[0], wide.at[0, :, pl.ds(LEAD, extent), :]),
         (src_prev.at[0], prev_ref.at[0]),
         (rec_now.at[0], wide.at[1, :, pl.ds(LEAD, extent), :]),
         (rec_prev.at[0], prev_ref.at[1]),
+        (amps_hbm, amps_ref),
     )
     copies = [
         pltpu.make_async_copy(here, there, sems.at[i]) for i, (here, there) in enumerate(moves)
@@ -145,22 +134,15 @@
         low_ref[place, rows, :] = coef_ref[level, 0:HALO, :]
         high_ref[place, rows, :] = coef_ref[level, extent - HALO : extent, :]
 
-    copies[4].wait()
-    copies[5].wait()
-    first = lax.axis_index("tile") * extent
     for field in range(2):
-        copies[6 + 2 * field].wait()
-        copies[7 + 2 * field].wait()
+        copies[4 + 2 * field].wait()
+        copies[5 + 2 * field].wait()
         for level in range(levels):
             total = laplace_level(wide, field, level, levels, extent, weights)
             now = wide[field, level, LEAD:end, :]
             value = 2.0 * now - prev_ref[field, level] + coef_ref[level] * total
             later = -now
-            if field == 0:
-                hit = source_hit(cell_ref[0], level, width, first, shape)
-                value = value + jnp.where(hit, amps_ref[0, 0], 0.0)
-                later = later + jnp.where(hit, amps_ref[0, 1], 0.0)
-            elif level == 0:
+            if field == 1 and level == 0:
                 value = value + planes[:extent, :]
                 later = later + planes[extent:, :]
             part_ref[field, level] = value
@@ -170,9 +152,13 @@
             low_ref[place, HALO : 2 * HALO, :] = value[0:HALO, :]
             high_ref[place, 0:HALO, :] = now[extent - HALO : extent, :]
             high_ref[place, HALO : 2 * HALO, :] = value[extent - HALO : extent, :]
+    copies[8].wait()
 
 
 def both_steps(
+    width,
+    cell_ref,
+    amps_ref,
     own,
     part_ref,
     later_ref,
@@ -185,7 +171,7 @@
 ):
     levels, extent, across = coef_ref.shape
     shape = (extent, across)
-    share = packed_ref.shape[2]
+    shots, share = packed_ref.shape[0] // 2, packed_ref.shape[2]
     end = LEAD + extent
     for field in range(2):
         for level in range(levels):
@@ -221,20 +207,38 @@
                 part_ref[field, level, extent - 8 : extent, :]
                 + coef_ref[level, extent - 8 : extent, :] * right
             )
+    cell = cell_ref[0]
+    deep = lax.div(cell, width * across)
+    row = lax.rem(lax.div(cell, across), width) - lax.axis_index("tile") * extent
+    lane = lax.broadcasted_iota(jnp.int32, (1, across), 1)
+    at_cell = lane == lax.rem(cell, across)
+    inject = [jnp.where(at_cell, amps_ref[0:1, t : t + 1], 0.0) for t in range(2)]
+
+    @pl.when((row >= -HALO) & (row < extent + HALO))
+    def _():
+        middle[0, deep, pl.ds(row + LEAD, 1), :] += inject[0]
+
     weights = lane_weights(shape)
     for field in range(2):
         for level in range(levels):
             total = laplace_level(middle, field, level, levels, extent, weights)
             value = 2.0 * middle[field, level, LEAD:end, :] + later_ref[field, level]
-            packed_ref[level // share, field, level % share] = value + coef_ref[level] * total
+            value = value + coef_ref[level] * total
+            for half in range(2):
+                packed_ref[half * shots + level // share, field, level % share] = value
+
+    @pl.when((row >= 0) & (row < extent))
+    def _():
+        for half in range(2):
+            place = half * shots + lax.div(deep, share)
+            packed_ref[place, 0, lax.rem(deep, share), pl.ds(row, 1), :] += inject[1]
 
 
 def image_products(
     weight,
     final_ref,
-    mine_ref,
-    low_ref,
-    high_ref,
+    pair_ref,
+    beyond_ref,
     src_hbm,
     rec_hbm,
     image_hbm,
@@ -243,7 +247,7 @@
     field_sems,
     image_sems,
 ):
-    shots, _, share, extent, across = mine_ref.shape
+    shots, _, share, extent, across = beyond_ref.shape
     copies = []
     for field, out in enumerate((src_hbm, rec_hbm)):
         for shot in range(shots):
@@ -256,18 +260,19 @@
             )
     for copy in copies:
         copy.start()
+    odd = lax.rem(lax.axis_index("tile"), 2)
+    places = [pl.multiple_of((1 - odd + half) * extent, extent) for half in range(2)]
+    outside = pl.multiple_of(odd * 2 * extent, extent)
     for shot in range(shots):
         for field in range(2):
             for level in range(share):
                 scale = weight if field == 0 else 1.0
-                wide[shot, field, level, 0:REACH, :] = (
-                    scale * low_ref[shot, field, level, extent - REACH : extent, :]
-                )
-                wide[shot, field, level, REACH : REACH + extent, :] = (
-                    scale * mine_ref[shot, field, level]
-                )
-                wide[shot, field, level, REACH + extent : 2 * REACH + extent, :] = (
-                    scale * high_ref[shot, field, level, 0:REACH, :]
+                for half in range(2):
+                    wide[shot, field, level, pl.ds(places[half], extent), :] = (
+                        scale * pair_ref[half * shots + shot, field, level]
+                    )
+                wide[shot, field, level, pl.ds(outside, extent), :] = (
+                    scale * beyond_ref[shot, field, level]
                 )
     parts = image_sems.shape[0]
     for piece in range(parts):
@@ -276,10 +281,11 @@
             for level in range(share):
                 total = jnp.zeros((extent, across), jnp.float32)
                 for shot in range(shots):
-                    begin = 2 * REACH - offset
+                    lower = extent + REACH - offset
+                    upper = extent - REACH + offset
                     total = total + (
-                        wide[shot, 0, level, begin : begin + extent, :]
-                        * wide[shot, 1, level, offset : offset + extent, :]
+                        wide[shot, 0, level, lower : lower + extent, :]
+                        * wide[shot, 1, level, upper : upper + extent, :]
                     )
                 image_ref[offset, level] = total
         rows = pl.ds(offsets[0], len(offsets))
@@ -310,7 +316,8 @@
     receiver_data,
 ):
     _, levels, extent, across = src_now.shape
-    width = extent * lax.axis_size("tile")
+    tiles = lax.axis_size("tile")
+    width = extent * tiles
     shots = lax.axis_size("shot")
     share = levels // shots
     params = pltpu.CompilerParams(vmem_limit_bytes=LIMIT)
@@ -323,9 +330,10 @@
 
     wide_shape = (2, levels, extent + 2 * LEAD, across)
     message = struct(2 * levels + levels // 2, 2 * HALO, across)
-    own, part, later, coef, low, high = pl.pallas_call(
-        functools.partial(own_part, width),
+    amps, own, part, later, coef, low, high = pl.pallas_call(
+        own_part,
         out_shape=(
+            struct(*wavelet.shape),
             struct(*wide_shape),
             struct(2, levels, extent, across),
             struct(2, levels, extent, across),
@@ -333,44 +341,54 @@
             message,
             message,
         ),
-        in_specs=[HBM] * 10,
-        out_specs=[VMEM] * 6,
+        in_specs=[HBM] * 9,
+        out_specs=[VMEM] * 7,
         scratch_shapes=[
             scratch(1, speed_table.shape[0]),
             scratch(*receiver_cell.shape, dtype=jnp.int32),
             scratch(*receiver_data.shape),
-            pltpu.SMEM(source_cell.shape, jnp.int32),
-            pltpu.SMEM(wavelet.shape, jnp.float32),
             scratch(levels, extent, across, dtype=jnp.int32),
             scratch(2, levels, extent, across),
-            pltpu.SemaphoreType.DMA((10,)),
+            pltpu.SemaphoreType.DMA((9,)),
         ],
         compiler_params=params,
         name="own_part",
     )(
-        speed_table.reshape(1, -1),
-        receiver_cell,
-        receiver_data,
-        source_cell,
-        wavelet,
-        region_ids,
-        src_now,
-        rec_now,
-        src_prev,
-        rec_prev,
+        *(
+            pltpu.with_memory_space_constraint(array, pltpu.HBM)
+            for array in (
+                speed_table.reshape(1, -1),
+                receiver_cell,
+                receiver_data,
+                wavelet,
+                region_ids,
+                src_now,
+                rec_now,
+                src_prev,
+                rec_prev,
+            )
+        )
     )
     from_low, from_high = swap_sides(low, high)
     packed = pl.pallas_call(
-        both_steps,
-        out_shape=struct(shots, 2, share, extent, across),
-        in_specs=[VMEM] * 6,
+        functools.partial(both_steps, width),
+        out_shape=struct(2 * shots, 2, share, extent, across),
+        in_specs=[SMEM] + [VMEM] * 7,
         out_specs=VMEM,
         scratch_shapes=[scratch(*wide_shape), scratch(*wide_shape)],
         compiler_params=params,
         name="both_steps",
-    )(own, part, later, coef, from_low, from_high)
-    mine = lax.all_to_all(packed, "shot", 0, 0, tiled=True)
-    low_fields, high_fields = swap_sides(mine, mine)
+    )(source_cell, amps, own, part, later, coef, from_low, from_high)
+    groups = [
+        [tile * shots + shot for tile in (first, first + 1) for shot in range(shots)]
+        for first in range(0, tiles, 2)
+    ]
+    pair = lax.all_to_all(
+        packed, ("tile", "shot"), 0, 0, axis_index_groups=groups, tiled=True
+    )
+    mine = lax.dynamic_slice_in_dim(pair, lax.axis_index("tile") % 2 * shots, shots, 0)
+    across_pairs = [(i, i + 1) for i in range(1, tiles - 1, 2)]
+    beyond = lax.ppermute(mine, "tile", across_pairs + [(b, a) for a, b in across_pairs])
     return pl.pallas_call(
         functools.partial(image_products, 1.0 / shots),
         out_shape=(
@@ -378,17 +396,17 @@
             struct(1, levels, extent, across),
             struct(OFFS, share, extent, across),
         ),
-        in_specs=[VMEM] * 4,
+        in_specs=[VMEM] * 3,
         out_specs=[HBM] * 3,
         scratch_shapes=[
-            scratch(shots, 2, share, extent + 2 * REACH, across),
+            scratch(shots, 2, share, 3 * extent, across),
             scratch(OFFS, share, extent, across),
             pltpu.SemaphoreType.DMA((2, shots)),
             pltpu.SemaphoreType.DMA((3,)),
         ],
         compiler_params=params,
         name="image_products",
-    )(packed, mine, low_fields, high_fields)
+    )(packed, pair, beyond)
 
 
 def solution(mesh):

time: 36 us -> 32.3 us (0.90)
  the two profiles are of different devices: /device:TPU:0 before, /device:TPU:8 now
where the time goes in v3:
time: 32.3 us; the launch traced here: 32 us
  starting transfers between devices  13.2 us (41%)
  waiting for transfers between devices  12.6 us (39%)
  Pallas kernels  4.75 us (15%)
  between operations  1.33 us (4%)
    all_to_all x1, waiting for transfers between devices, per_device(): lax.all_to_all(packed, ('tile', 'shot'), 0, 0, axis_index_groups=groups,...  5.48 us
    all_to_all x1, starting transfers between devices, per_device(): lax.all_to_all(packed, ('tile', 'shot'), 0, 0, axis_index_groups=groups,...  4.23 us
    ppermute x1, waiting for transfers between devices, per_device(): lax.ppermute(mine, 'tile', across_pairs + [(b, a) for a, b in across_pairs])  3.84 us
    ppermute x1, starting transfers between devices, swap_sides(): lax.ppermute(high, 'tile', forward)  3.48 us
    ppermute x1, waiting for transfers between devices, swap_sides(): lax.ppermute(low, 'tile', backward)  3.31 us
    ppermute x1, starting transfers between devices, per_device(): lax.ppermute(mine, 'tile', across_pairs + [(b, a) for a, b in across_pairs])  3.18 us
    ppermute x1, starting transfers between devices, swap_sides(): lax.ppermute(low, 'tile', backward)  2.36 us
    pallas_call x1, Pallas kernels, per_device(): pl.pallas_call(functools.partial(image_products, 1.0 / shots), out_shape=...  1.96 us
  transfers between devices with their start and end apart: 4, of which 3 were waited for; matrix products, arithmetic and copies ran while one was open for 0% of the time, Pallas kernels for 0%

profile of v3, /device:TPU:8, one launch (start us, length us, event | category | flops | bytes accessed | tf_op | source)
XLA Modules:
  0.0 32.0 jit_solution(6712615725303292558)
XLA Ops:
  0.6 1.6 %own_part.1 = (f32[1,2]{1,0:T(1,128)S(1)}, f32[2,8,32,128]{3,2,1,0:T(8,128)S(1)}, f32[2,8,16,128]{3,2,1,0:T(8,128)S(1)}, f32[2,8,16,128]{3,2,1,0:T(8,128)S(1)}, ...) custom-call(f32[1,16]{1,0:T(1,128)} %bitcast.1, s32[1,32]{1,0:T(1,128)} %spots_hbm.1, ...), custom_call_target="tpu_custom_call" | custom-call | tf_op jit(solution)/shard_map/own_part/pallas_call | solution.py:333
  2.2 3.5 %collective-permute-start = (f32[20,8,128]{2,1,0:T(8,128)S(1)}, f32[20,8,128]{2,1,0:T(8,128)S(1)}, u32[]{:S(2)}, u32[]{:S(2)}) collective-permute-start(f32[20,8,128]{2,1,0:T(8,128)S(1)} %get-tuple-element.15), channel_id=1, source_target_pairs={{0,4},{4,8},{8,12},{1,5},{5,9},{9,13},{2,6},{6,10},{10,14},{3,7},{... | collective-permute-start | bytes 245768 | tf_op jit(solution)/shard_map/ppermute | solution.py:303
  5.7 2.4 %collective-permute-start.1 = (f32[20,8,128]{2,1,0:T(8,128)S(1)}, f32[20,8,128]{2,1,0:T(8,128)S(1)}, u32[]{:S(2)}, u32[]{:S(2)}) collective-permute-start(f32[20,8,128]{2,1,0:T(8,128)S(1)} %get-tuple-element.16), channel_id=1, source_target_pairs={{4,0},{8,4},{12,8},{5,1},{9,5},{13,9},{6,2},{10,6},{14,10},{7,3},{... | collective-permute-start | bytes 245768 | tf_op jit(solution)/shard_map/ppermute | solution.py:303
  8.8 0.0 collective-permute-done.low_ref
  8.8 3.3 %collective-permute-done.1.high_ref = f32[20,8,128]{2,1,0:T(8,128)S(1)} collective-permute-done((f32[20,8,128]{2,1,0:T(8,128)S(1)}, f32[20,8,128]{2,1,0:T(8,128)S(1)}, u32[]{:S(2)}, u32[]{:S(2)}) %collective-permute-start.1) | collective-permute-done | bytes 81952 | tf_op jit(solution)/shard_map/ppermute | solution.py:303
  12.1 1.2 %both_steps.1.final_ref = f32[8,2,2,16,128]{4,3,2,1,0:T(8,128)} custom-call(s32[1]{0:T(128)S(6)} %copy.13.cell_ref, f32[1,2]{1,0:T(1,128)S(1)} %get-tuple-element.10.amps_ref, f32[2,8,32,128]{3,2,1,0:T(8,128)S(1)} %get-tuple-element.11.own, f32[2,8,16,128]{3,2,1,0:T(8,128)S(1)} %get-tuple-element.12.part_ref, ...), custom_call_target="tpu_custom_call" | custom-call | tf_op jit(solution)/shard_map/both_steps/pallas_call | solution.py:373
  13.3 4.2 %all-to-all-start = ((f32[8,2,2,16,128]{4,3,2,1,0:T(8,128)}), f32[8,2,2,16,128]{4,3,2,1,0:T(8,128)S(1)}, u32[]{:S(2)}, u32[]{:S(2)}) async-start(f32[8,2,2,16,128]{4,3,2,1,0:T(8,128)} %both_steps.1.final_ref), calls=%async_computation | async-start | bytes 524288 | tf_op jit(solution)/shard_map/all_to_all | solution.py:386
  17.5 5.5 %all-to-all-done.pair_ref = f32[8,2,2,16,128]{4,3,2,1,0:T(8,128)S(1)} async-done(((f32[8,2,2,16,128]{4,3,2,1,0:T(8,128)}), f32[8,2,2,16,128]{4,3,2,1,0:T(8,128)S(1)}, u32[]{:S(2)}, u32[]{:S(2)}) %all-to-all-start) | async-done | bytes 262176 | tf_op jit(solution)/shard_map/all_to_all | solution.py:386
  23.0 3.2 %collective-permute-start.2 = (f32[4,2,2,16,128]{4,3,2,1,0:T(8,128)S(1)}, f32[4,2,2,16,128]{4,3,2,1,0:T(8,128)S(1)}, u32[]{:S(2)}, u32[]{:S(2)}) collective-permute-start(f32[4,2,2,16,128]{4,3,2,1,0:T(8,128)S(1)} %constant_dynamic-slice_fusion), channel_id=1, source_target_pairs={{4,8},{8,4},{5,9},{9,5},{6,10},{10,6},{7,11},{11,7},{20,24},{24,20... | collective-permute-start | bytes 393224 | tf_op jit(solution)/shard_map/ppermute | solution.py:391
  26.2 3.8 %collective-permute-done.2.beyond_ref = f32[4,2,2,16,128]{4,3,2,1,0:T(8,128)S(1)} collective-permute-done((f32[4,2,2,16,128]{4,3,2,1,0:T(8,128)S(1)}, f32[4,2,2,16,128]{4,3,2,1,0:T(8,128)S(1)}, u32[]{:S(2)}, u32[]{:S(2)}) %collective-permute-start.2) | collective-permute-done | bytes 131104 | tf_op jit(solution)/shard_map/ppermute | solution.py:391
  30.0 2.0 %image_products.1 = (f32[1,8,16,128]{3,2,1,0:T(8,128)}, f32[1,8,16,128]{3,2,1,0:T(8,128)}, f32[33,2,16,128]{3,2,1,0:T(8,128)}) custom-call(f32[8,2,2,16,128]{4,3,2,1,0:T(8,128)} %both_steps.1.final_ref, f32[8,2,2,16,128]{4,3,2,1,0:T(8,128)S(1)} %all-to-all-done.pair_ref, f32[4,2,2,16,128]{4,3,2,1,0:T(8,128)S(1)} %collective-permute-done.2.beyond_ref), custom_call_target="tpu_custom_call" | custom-call | tf_op jit(solution)/shard_map/image_products/pallas_call | solution.py:392
  (1 shorter events, 0.0 us)
Async XLA Ops:
  2.2 6.5 %collective-permute-start = (f32[20,8,128]{2,1,0:T(8,128)S(1)}, f32[20,8,128]{2,1,0:T(8,128)S(1)}, u32[]{:S(2)}, u32[]{:S(2)}) collective-permute-start(f32[20,8,128]{2,1,0:T(8,128)S(1)} %get-tuple-element.15), channel_id=1, source_target_pairs={{0,4},{4,8},{8,12},{1,5},{5,9},{9,13},{2,6},{6,10},{10,14},{3,7},{... | collective-permute-start | bytes 245768 | tf_op jit(solution)/shard_map/ppermute | solution.py:303
  5.7 6.3 %collective-permute-start.1 = (f32[20,8,128]{2,1,0:T(8,128)S(1)}, f32[20,8,128]{2,1,0:T(8,128)S(1)}, u32[]{:S(2)}, u32[]{:S(2)}) collective-permute-start(f32[20,8,128]{2,1,0:T(8,128)S(1)} %get-tuple-element.16), channel_id=1, source_target_pairs={{4,0},{8,4},{12,8},{5,1},{9,5},{13,9},{6,2},{10,6},{14,10},{7,3},{... | collective-permute-start | bytes 245768 | tf_op jit(solution)/shard_map/ppermute | solution.py:303
  13.3 9.7 %all-to-all-start = ((f32[8,2,2,16,128]{4,3,2,1,0:T(8,128)}), f32[8,2,2,16,128]{4,3,2,1,0:T(8,128)S(1)}, u32[]{:S(2)}, u32[]{:S(2)}) async-start(f32[8,2,2,16,128]{4,3,2,1,0:T(8,128)} %both_steps.1.final_ref), calls=%async_computation | async-start | bytes 524288 | tf_op jit(solution)/shard_map/all_to_all | solution.py:386
  23.0 7.0 %collective-permute-start.2 = (f32[4,2,2,16,128]{4,3,2,1,0:T(8,128)S(1)}, f32[4,2,2,16,128]{4,3,2,1,0:T(8,128)S(1)}, u32[]{:S(2)}, u32[]{:S(2)}) collective-permute-start(f32[4,2,2,16,128]{4,3,2,1,0:T(8,128)S(1)} %constant_dynamic-slice_fusion), channel_id=1, source_target_pairs={{4,8},{8,4},{5,9},{9,5},{6,10},{10,6},{7,11},{11,7},{20,24},{24,20... | collective-permute-start | bytes 393224 | tf_op jit(solution)/shard_map/ppermute | solution.py:391

commit v4 on v3

--- a/solution.py
+++ b/solution.py
@@ -48,6 +48,32 @@
     return total
 
 
+def goes_up_first():
+    return lax.rem(lax.axis_index("tile") + lax.axis_index("shot"), 2) == 0
+
+
+def source_and_order(
+    width, cell_ref, amps_ref, later_ref, source_ref, source_later_ref, up_first_ref
+):
+    levels, extent, across = source_later_ref.shape
+    cell = cell_ref[0]
+    deep = lax.div(cell, width * across)
+    row = lax.rem(lax.div(cell, across), width) - lax.axis_index("tile") * extent + LEAD
+    shape = (extent + 2 * LEAD, across)
+    rows = lax.broadcasted_iota(jnp.int32, shape, 0)
+    lanes = lax.broadcasted_iota(jnp.int32, shape, 1)
+    hit = jnp.where((rows == row) & (lanes == lax.rem(cell, across)), 1.0, 0.0)
+    for level in range(levels):
+        here = hit * jnp.where(deep == level, 1.0, 0.0)
+        source_ref[level] = here * amps_ref[0:1, 0:1]
+        source_later_ref[level] = (
+            later_ref[0, level] + here[LEAD : LEAD + extent, :] * amps_ref[0:1, 1:2]
+        )
+    up_first_ref[...] = jnp.full(
+        up_first_ref.shape, jnp.where(goes_up_first(), 1, 0), dtype=jnp.int32
+    )
+
+
 def own_part(
     table_hbm,
     spots_hbm,
@@ -63,8 +89,8 @@
     part_ref,
     later_ref,
     coef_ref,
-    low_ref,
-    high_ref,
+    sent_first_ref,
+    sent_last_ref,
     table,
     spots_ref,
     traces_ref,
@@ -117,6 +143,14 @@
         preferred_element_type=jnp.float32,
     )
 
+    up_first = goes_up_first()
+
+    def send(place, rows, value):
+        low = value[0:HALO, :]
+        high = value[extent - HALO : extent, :]
+        sent_first_ref[place, rows, :] = jnp.where(up_first, high, low)
+        sent_last_ref[place, rows, :] = jnp.where(up_first, low, high)
+
     copies[0].wait()
     copies[1].wait()
     speeds = jnp.concatenate(
@@ -129,10 +163,7 @@
             coef_ref[level, row : row + 8, :] = jnp.take_along_axis(
                 speeds, ids, axis=1, mode="promise_in_bounds"
             )
-        place = 2 * levels + level // 2
-        rows = pl.ds(level % 2 * HALO, HALO)
-        low_ref[place, rows, :] = coef_ref[level, 0:HALO, :]
-        high_ref[place, rows, :] = coef_ref[level, extent - HALO : extent, :]
+        send(2 * levels + level // 2, pl.ds(level % 2 * HALO, HALO), coef_ref[level])
 
     for field in range(2):
         copies[4 + 2 * field].wait()
@@ -148,42 +179,44 @@
             part_ref[field, level] = value
             later_ref[field, level] = later
             place = field * levels + level
-            low_ref[place, 0:HALO, :] = now[0:HALO, :]
-            low_ref[place, HALO : 2 * HALO, :] = value[0:HALO, :]
-            high_ref[place, 0:HALO, :] = now[extent - HALO : extent, :]
-            high_ref[place, HALO : 2 * HALO, :] = value[extent - HALO : extent, :]
+            send(place, pl.ds(0, HALO), now)
+            send(place, pl.ds(HALO, HALO), value)
     copies[8].wait()
 
 
 def both_steps(
-    width,
-    cell_ref,
-    amps_ref,
+    up_first_ref,
     own,
     part_ref,
     later_ref,
+    source_ref,
+    source_later_ref,
     coef_ref,
-    low_ref,
-    high_ref,
+    came_first_ref,
+    came_last_ref,
     packed_ref,
     other,
     middle,
 ):
     levels, extent, across = coef_ref.shape
     shape = (extent, across)
-    shots, share = packed_ref.shape[0] // 2, packed_ref.shape[2]
+    share = packed_ref.shape[2]
     end = LEAD + extent
+    up_first = up_first_ref[0:HALO, :] != 0
+
+    def received(place, rows):
+        first = came_first_ref[place, rows, :]
+        last = came_last_ref[place, rows, :]
+        return jnp.where(up_first, last, first), jnp.where(up_first, first, last)
+
     for field in range(2):
         for level in range(levels):
-            place = field * levels + level
+            low, high = received(field * levels + level, pl.ds(0, HALO))
             other[field, level, LEAD:end, :] = jnp.zeros(shape, jnp.float32)
-            other[field, level, LEAD - HALO : LEAD, :] = low_ref[place, 0:HALO, :]
-            other[field, level, end : end + HALO, :] = high_ref[place, 0:HALO, :]
+            other[field, level, LEAD - HALO : LEAD, :] = low
+            other[field, level, end : end + HALO, :] = high
     for field in range(2):
         for level in range(levels):
-            place = field * levels + level
-            pair = 2 * levels + level // 2
-            rows = pl.ds(level % 2 * HALO, HALO)
             below = jnp.zeros((HALO, across), jnp.float32)
             above = jnp.zeros((HALO, across), jnp.float32)
             left = jnp.zeros((8, across), jnp.float32)
@@ -194,51 +227,42 @@
                 above = above + COEFS[k] * own[field, level, end - k : end - k + HALO, :]
                 left = left + COEFS[k] * other[field, level, LEAD - k : LEAD - k + 8, :]
                 right = right + COEFS[k] * other[field, level, end - 8 + k : end + k, :]
-            middle[field, level, LEAD - HALO : LEAD, :] = (
-                low_ref[place, HALO : 2 * HALO, :] + low_ref[pair, rows, :] * below
+            low, high = received(field * levels + level, pl.ds(HALO, HALO))
+            low_coef, high_coef = received(
+                2 * levels + level // 2, pl.ds(level % 2 * HALO, HALO)
             )
-            middle[field, level, end : end + HALO, :] = (
-                high_ref[place, HALO : 2 * HALO, :] + high_ref[pair, rows, :] * above
-            )
-            middle[field, level, LEAD : LEAD + 8, :] = (
-                part_ref[field, level, 0:8, :] + coef_ref[level, 0:8, :] * left
-            )
-            middle[field, level, end - 8 : end, :] = (
+            low = low + low_coef * below
+            high = high + high_coef * above
+            left = part_ref[field, level, 0:8, :] + coef_ref[level, 0:8, :] * left
+            right = (
                 part_ref[field, level, extent - 8 : extent, :]
                 + coef_ref[level, extent - 8 : extent, :] * right
             )
-    cell = cell_ref[0]
-    deep = lax.div(cell, width * across)
-    row = lax.rem(lax.div(cell, across), width) - lax.axis_index("tile") * extent
-    lane = lax.broadcasted_iota(jnp.int32, (1, across), 1)
-    at_cell = lane == lax.rem(cell, across)
-    inject = [jnp.where(at_cell, amps_ref[0:1, t : t + 1], 0.0) for t in range(2)]
-
-    @pl.when((row >= -HALO) & (row < extent + HALO))
-    def _():
-        middle[0, deep, pl.ds(row + LEAD, 1), :] += inject[0]
-
+            if field == 0:
+                low = low + source_ref[level, LEAD - HALO : LEAD, :]
+                left = left + source_ref[level, LEAD : LEAD + 8, :]
+                right = right + source_ref[level, end - 8 : end, :]
+                high = high + source_ref[level, end : end + HALO, :]
+            middle[field, level, LEAD - HALO : LEAD, :] = low
+            middle[field, level, LEAD : LEAD + 8, :] = left
+            middle[field, level, end - 8 : end, :] = right
+            middle[field, level, end : end + HALO, :] = high
     weights = lane_weights(shape)
     for field in range(2):
         for level in range(levels):
             total = laplace_level(middle, field, level, levels, extent, weights)
-            value = 2.0 * middle[field, level, LEAD:end, :] + later_ref[field, level]
-            value = value + coef_ref[level] * total
-            for half in range(2):
-                packed_ref[half * shots + level // share, field, level % share] = value
-
-    @pl.when((row >= 0) & (row < extent))
-    def _():
-        for half in range(2):
-            place = half * shots + lax.div(deep, share)
-            packed_ref[place, 0, lax.rem(deep, share), pl.ds(row, 1), :] += inject[1]
+            later = source_later_ref[level] if field == 0 else later_ref[field, level]
+            value = 2.0 * middle[field, level, LEAD:end, :] + later
+            packed_ref[level // share, field, level % share] = value + coef_ref[level] * total
 
 
 def image_products(
     weight,
+    up_first_ref,
     final_ref,
-    pair_ref,
-    beyond_ref,
+    mine_ref,
+    came_first_ref,
+    came_last_ref,
     src_hbm,
     rec_hbm,
     image_hbm,
@@ -247,7 +271,7 @@
     field_sems,
     image_sems,
 ):
-    shots, _, share, extent, across = beyond_ref.shape
+    shots, _, share, extent, across = mine_ref.shape
     copies = []
     for field, out in enumerate((src_hbm, rec_hbm)):
         for shot in range(shots):
@@ -260,19 +284,19 @@
             )
     for copy in copies:
         copy.start()
-    odd = lax.rem(lax.axis_index("tile"), 2)
-    places = [pl.multiple_of((1 - odd + half) * extent, extent) for half in range(2)]
-    outside = pl.multiple_of(odd * 2 * extent, extent)
+    up_first = jnp.concatenate([up_first_ref[...]] * (extent // 8), axis=0) != 0
     for shot in range(shots):
         for field in range(2):
             for level in range(share):
                 scale = weight if field == 0 else 1.0
-                for half in range(2):
-                    wide[shot, field, level, pl.ds(places[half], extent), :] = (
-                        scale * pair_ref[half * shots + shot, field, level]
-                    )
-                wide[shot, field, level, pl.ds(outside, extent), :] = (
-                    scale * beyond_ref[shot, field, level]
+                first = scale * came_first_ref[shot, field, level]
+                last = scale * came_last_ref[shot, field, level]
+                wide[shot, field, level, 0:extent, :] = jnp.where(up_first, last, first)
+                wide[shot, field, level, extent : 2 * extent, :] = (
+                    scale * mine_ref[shot, field, level]
+                )
+                wide[shot, field, level, 2 * extent : 3 * extent, :] = jnp.where(
+                    up_first, first, last
                 )
     parts = image_sems.shape[0]
     for piece in range(parts):
@@ -296,11 +320,15 @@
         copy.wait()
 
 
-def swap_sides(low, high):
-    count = lax.axis_size("tile")
-    forward = [(i, i + 1) for i in range(count - 1)]
-    backward = [(target, source) for source, target in forward]
-    return lax.ppermute(high, "tile", forward), lax.ppermute(low, "tile", backward)
+def swap_sides(first, last):
+    tiles, shots = lax.axis_size("tile"), lax.axis_size("shot")
+    rounds = [[], []]
+    for tile in range(tiles - 1):
+        for shot in range(shots):
+            here, there = tile * shots + shot, (tile + 1) * shots + shot
+            rounds[(tile + shot) % 2] += [(here, there), (there, here)]
+    axes = ("tile", "shot")
+    return lax.ppermute(first, axes, rounds[0]), lax.ppermute(last, axes, rounds[1])
 
 
 def per_device(
@@ -330,7 +358,7 @@
 
     wide_shape = (2, levels, extent + 2 * LEAD, across)
     message = struct(2 * levels + levels // 2, 2 * HALO, across)
-    amps, own, part, later, coef, low, high = pl.pallas_call(
+    amps, own, part, later, coef, first, last = pl.pallas_call(
         own_part,
         out_shape=(
             struct(*wavelet.shape),
@@ -369,26 +397,30 @@
             )
         )
     )
-    from_low, from_high = swap_sides(low, high)
+    came_first, came_last = swap_sides(first, last)
+    source, source_later, up_first = pl.pallas_call(
+        functools.partial(source_and_order, width),
+        out_shape=(
+            struct(levels, extent + 2 * LEAD, across),
+            struct(levels, extent, across),
+            jax.ShapeDtypeStruct((8, across), jnp.int32),
+        ),
+        in_specs=[SMEM] + [VMEM] * 2,
+        out_specs=[VMEM] * 3,
+        compiler_params=params,
+        name="source_and_order",
+    )(source_cell, amps, later)
     packed = pl.pallas_call(
-        functools.partial(both_steps, width),
-        out_shape=struct(2 * shots, 2, share, extent, across),
-        in_specs=[SMEM] + [VMEM] * 7,
+        both_steps,
+        out_shape=struct(shots, 2, share, extent, across),
+        in_specs=[VMEM] * 9,
         out_specs=VMEM,
         scratch_shapes=[scratch(*wide_shape), scratch(*wide_shape)],
         compiler_params=params,
         name="both_steps",
-    )(source_cell, amps, own, part, later, coef, from_low, from_high)
-    groups = [
-        [tile * shots + shot for tile in (first, first + 1) for shot in range(shots)]
-        for first in range(0, tiles, 2)
-    ]
-    pair = lax.all_to_all(
-        packed, ("tile", "shot"), 0, 0, axis_index_groups=groups, tiled=True
-    )
-    mine = lax.dynamic_slice_in_dim(pair, lax.axis_index("tile") % 2 * shots, shots, 0)
-    across_pairs = [(i, i + 1) for i in range(1, tiles - 1, 2)]
-    beyond = lax.ppermute(mine, "tile", across_pairs + [(b, a) for a, b in across_pairs])
+    )(up_first, own, part, later, source, source_later, coef, came_first, came_last)
+    mine = lax.all_to_all(packed, "shot", 0, 0, tiled=True)
+    fields_first, fields_last = swap_sides(mine, mine)
     return pl.pallas_call(
         functools.partial(image_products, 1.0 / shots),
         out_shape=(
@@ -396,7 +428,7 @@
             struct(1, levels, extent, across),
             struct(OFFS, share, extent, across),
         ),
-        in_specs=[VMEM] * 3,
+        in_specs=[VMEM] * 5,
         out_specs=[HBM] * 3,
         scratch_shapes=[
             scratch(shots, 2, share, 3 * extent, across),
@@ -406,7 +438,7 @@
         ],
         compiler_params=params,
         name="image_products",
-    )(packed, pair, beyond)
+    )(up_first, packed, mine, fields_first, fields_last)
 
 
 def solution(mesh):

time: 32.3 us -> 32.3 us (level)
  the two profiles are of different devices: /device:TPU:8 before, /device:TPU:0 now
where the time goes in v4:
time: 32.3 us; the launch traced here: 32 us
  starting transfers between devices  14.7 us (46%)
  blocking collectives  8.97 us (28%)
  waiting for transfers between devices  3.92 us (12%)
  Pallas kernels  3.07 us (10%)
  between operations  1.34 us (4%)
    ppermute x2, starting transfers between devices, swap_sides(): lax.ppermute(first, axes, rounds[0])  13.4 us
    all_to_all x1, blocking collectives, per_device(): mine = lax.all_to_all(packed, 'shot', 0, 0, tiled=True)  8.97 us
    ppermute x2, waiting for transfers between devices, swap_sides(): lax.ppermute(first, axes, rounds[0])  3.91 us
    pallas_call x1, Pallas kernels, per_device(): pl.pallas_call(own_part, out_shape=(struct(*wavelet.shape), struct(*wide_...  1.59 us
    ppermute x2, starting transfers between devices, swap_sides(): lax.ppermute(last, axes, rounds[1])  1.32 us
    pallas_call x1, Pallas kernels, per_device(): pl.pallas_call(functools.partial(image_products, 1.0 / shots), out_shape=...  0.98 us
  transfers between devices with their start and end apart: 4, of which 2 were waited for; matrix products, arithmetic and copies ran while one was open for 0% of the time, Pallas kernels for 0%

profile of v4, /device:TPU:0, one launch (start us, length us, event | category | flops | bytes accessed | tf_op | source)
XLA Modules:
  0.0 32.0 jit_solution(12825558348618214043)
XLA Ops:
  0.6 1.6 %own_part.1 = (f32[1,2]{1,0:T(1,128)S(1)}, f32[2,8,32,128]{3,2,1,0:T(8,128)S(1)}, f32[2,8,16,128]{3,2,1,0:T(8,128)S(1)}, f32[2,8,16,128]{3,2,1,0:T(8,128)S(1)}, ...) custom-call(f32[1,16]{1,0:T(1,128)} %bitcast.1, s32[1,32]{1,0:T(1,128)} %spots_hbm.1, ...), custom_call_target="tpu_custom_call" | custom-call | tf_op jit(solution)/shard_map/own_part/pallas_call | solution.py:361
  2.2 4.9 %collective-permute-start = (f32[20,8,128]{2,1,0:T(8,128)S(1)}, f32[20,8,128]{2,1,0:T(8,128)S(1)}, u32[]{:S(2)}, u32[]{:S(2)}) collective-permute-start(f32[20,8,128]{2,1,0:T(8,128)S(1)} %get-tuple-element.21), channel_id=1, source_target_pairs={{0,4},{4,0},{2,6},{6,2},{5,9},{9,5},{7,11},{11,7},{8,12},{12,8},{1... | collective-permute-start | bytes 245768 | tf_op jit(solution)/shard_map/ppermute | solution.py:331
  7.2 0.7 %collective-permute-start.1 = (f32[20,8,128]{2,1,0:T(8,128)S(1)}, f32[20,8,128]{2,1,0:T(8,128)S(1)}, u32[]{:S(2)}, u32[]{:S(2)}) collective-permute-start(f32[20,8,128]{2,1,0:T(8,128)S(1)} %get-tuple-element.22), channel_id=1, source_target_pairs={{1,5},{5,1},{3,7},{7,3},{4,8},{8,4},{6,10},{10,6},{9,13},{13,9},{1... | collective-permute-start | bytes 245768 | tf_op jit(solution)/shard_map/ppermute | solution.py:331
  8.5 0.1 source_and_order.1
  8.6 1.0 %collective-permute-done.came_first_ref = f32[20,8,128]{2,1,0:T(8,128)S(1)} collective-permute-done((f32[20,8,128]{2,1,0:T(8,128)S(1)}, f32[20,8,128]{2,1,0:T(8,128)S(1)}, u32[]{:S(2)}, u32[]{:S(2)}) %collective-permute-start) | collective-permute-done | bytes 81952 | tf_op jit(solution)/shard_map/ppermute | solution.py:331
  9.6 0.0 collective-permute-done.1.came_last_ref
  9.6 0.4 %both_steps.1.final_ref = f32[4,2,2,16,128]{4,3,2,1,0:T(8,128)S(1)} custom-call(s32[8,128]{1,0:T(8,128)S(1)} %get-tuple-element.15.up_first_ref, f32[2,8,32,128]{3,2,1,0:T(8,128)S(1)} %get-tuple-element.16.own, f32[2,8,16,128]{3,2,1,0:T(8,128)S(1)} %get-tuple-element.17.part_ref, f32[2,8,16,128]{3,2,1,0:T(8,128)S(1)} %get-tuple-element.14.later_ref, ...), custom_call_target="tpu_custom_call" | custom-call | tf_op jit(solution)/shard_map/both_steps/pallas_call | solution.py:413
  10.0 9.0 %all_to_all.5.mine_ref = f32[4,2,2,16,128]{4,3,2,1,0:T(8,128)S(1)} all-to-all(f32[4,2,2,16,128]{4,3,2,1,0:T(8,128)S(1)} %both_steps.1.final_ref), channel_id=1, replica_groups=mesh['groups'=2,'tile'=4,'shot'=4] {'shot'}, dimensions={0} | all-to-all | bytes 262144 | tf_op jit(solution)/shard_map/all_to_all | solution.py:422
  19.0 0.7 %collective-permute-start.3 = (f32[4,2,2,16,128]{4,3,2,1,0:T(8,128)S(1)}, f32[4,2,2,16,128]{4,3,2,1,0:T(8,128)S(1)}, u32[]{:S(2)}, u32[]{:S(2)}) collective-permute-start(f32[4,2,2,16,128]{4,3,2,1,0:T(8,128)S(1)} %all_to_all.5.mine_ref), channel_id=1, source_target_pairs={{1,5},{5,1},{3,7},{7,3},{4,8},{8,4},{6,10},{10,6},{9,13},{13,9},{1... | collective-permute-start | bytes 393224 | tf_op jit(solution)/shard_map/ppermute | solution.py:331
  19.6 8.4 %collective-permute-start.2 = (f32[4,2,2,16,128]{4,3,2,1,0:T(8,128)S(1)}, f32[4,2,2,16,128]{4,3,2,1,0:T(8,128)S(1)}, u32[]{:S(2)}, u32[]{:S(2)}) collective-permute-start(f32[4,2,2,16,128]{4,3,2,1,0:T(8,128)S(1)} %all_to_all.5.mine_ref), channel_id=1, source_target_pairs={{0,4},{4,0},{2,6},{6,2},{5,9},{9,5},{7,11},{11,7},{8,12},{12,8},{1... | collective-permute-start | bytes 393224 | tf_op jit(solution)/shard_map/ppermute | solution.py:331
  28.1 0.0 collective-permute-done.3.came_last_ref
  28.1 2.9 %collective-permute-done.2.came_first_ref = f32[4,2,2,16,128]{4,3,2,1,0:T(8,128)S(1)} collective-permute-done((f32[4,2,2,16,128]{4,3,2,1,0:T(8,128)S(1)}, f32[4,2,2,16,128]{4,3,2,1,0:T(8,128)S(1)}, u32[]{:S(2)}, u32[]{:S(2)}) %collective-permute-start.2) | collective-permute-done | bytes 131104 | tf_op jit(solution)/shard_map/ppermute | solution.py:331
  31.0 1.0 %image_products.1 = (f32[1,8,16,128]{3,2,1,0:T(8,128)}, f32[1,8,16,128]{3,2,1,0:T(8,128)}, f32[33,2,16,128]{3,2,1,0:T(8,128)}) custom-call(s32[8,128]{1,0:T(8,128)S(1)} %get-tuple-element.15.up_first_ref, f32[4,2,2,16,128]{4,3,2,1,0:T(8,128)S(1)} %both_steps.1.final_ref, f32[4,2,2,16,128]{4,3,2,1,0:T(8,128)S(1)} %all_to_all.5.mine_ref, ...), custom_call_target="tpu_custom_call" | custom-call | tf_op jit(solution)/shard_map/image_products/pallas_call | solution.py:424
Async XLA Ops:
  2.2 7.3 %collective-permute-start = (f32[20,8,128]{2,1,0:T(8,128)S(1)}, f32[20,8,128]{2,1,0:T(8,128)S(1)}, u32[]{:S(2)}, u32[]{:S(2)}) collective-permute-start(f32[20,8,128]{2,1,0:T(8,128)S(1)} %get-tuple-element.21), channel_id=1, source_target_pairs={{0,4},{4,0},{2,6},{6,2},{5,9},{9,5},{7,11},{11,7},{8,12},{12,8},{1... | collective-permute-start | bytes 245768 | tf_op jit(solution)/shard_map/ppermute | solution.py:331
  7.2 2.4 %collective-permute-start.1 = (f32[20,8,128]{2,1,0:T(8,128)S(1)}, f32[20,8,128]{2,1,0:T(8,128)S(1)}, u32[]{:S(2)}, u32[]{:S(2)}) collective-permute-start(f32[20,8,128]{2,1,0:T(8,128)S(1)} %get-tuple-element.22), channel_id=1, source_target_pairs={{1,5},{5,1},{3,7},{7,3},{4,8},{8,4},{6,10},{10,6},{9,13},{13,9},{1... | collective-permute-start | bytes 245768 | tf_op jit(solution)/shard_map/ppermute | solution.py:331
  19.0 9.1 %collective-permute-start.3 = (f32[4,2,2,16,128]{4,3,2,1,0:T(8,128)S(1)}, f32[4,2,2,16,128]{4,3,2,1,0:T(8,128)S(1)}, u32[]{:S(2)}, u32[]{:S(2)}) collective-permute-start(f32[4,2,2,16,128]{4,3,2,1,0:T(8,128)S(1)} %all_to_all.5.mine_ref), channel_id=1, source_target_pairs={{1,5},{5,1},{3,7},{7,3},{4,8},{8,4},{6,10},{10,6},{9,13},{13,9},{1... | collective-permute-start | bytes 393224 | tf_op jit(solution)/shard_map/ppermute | solution.py:331
  19.6 11.4 %collective-permute-start.2 = (f32[4,2,2,16,128]{4,3,2,1,0:T(8,128)S(1)}, f32[4,2,2,16,128]{4,3,2,1,0:T(8,128)S(1)}, u32[]{:S(2)}, u32[]{:S(2)}) collective-permute-start(f32[4,2,2,16,128]{4,3,2,1,0:T(8,128)S(1)} %all_to_all.5.mine_ref), channel_id=1, source_target_pairs={{0,4},{4,0},{2,6},{6,2},{5,9},{9,5},{7,11},{11,7},{8,12},{12,8},{1... | collective-permute-start | bytes 393224 | tf_op jit(solution)/shard_map/ppermute | solution.py:331

commit v5 on v4

--- a/solution.py
+++ b/solution.py
@@ -49,7 +49,7 @@
 
 
 def goes_up_first():
-    return lax.rem(lax.axis_index("tile") + lax.axis_index("shot"), 2) == 0
+    return lax.rem(lax.axis_index("tile"), 2) == 0
 
 
 def source_and_order(
@@ -261,8 +261,8 @@
     up_first_ref,
     final_ref,
     mine_ref,
+    came_last_ref,
     came_first_ref,
-    came_last_ref,
     src_hbm,
     rec_hbm,
     image_hbm,
@@ -321,14 +321,17 @@
 
 
 def swap_sides(first, last):
-    tiles, shots = lax.axis_size("tile"), lax.axis_size("shot")
-    rounds = [[], []]
-    for tile in range(tiles - 1):
-        for shot in range(shots):
-            here, there = tile * shots + shot, (tile + 1) * shots + shot
-            rounds[(tile + shot) % 2] += [(here, there), (there, here)]
-    axes = ("tile", "shot")
-    return lax.ppermute(first, axes, rounds[0]), lax.ppermute(last, axes, rounds[1])
+    rounds = [
+        [pair for here in range(begin, lax.axis_size("tile") - 1, 2) for pair in both_ways(here)]
+        for begin in range(2)
+    ]
+    came_last = lax.ppermute(last, "tile", rounds[1])
+    came_first = lax.ppermute(first, "tile", rounds[0])
+    return came_first, came_last
+
+
+def both_ways(tile):
+    return (tile, tile + 1), (tile + 1, tile)
 
 
 def per_device(
@@ -438,7 +441,7 @@
         ],
         compiler_params=params,
         name="image_products",
-    )(up_first, packed, mine, fields_first, fields_last)
+    )(up_first, packed, mine, fields_last, fields_first)
 
 
 def solution(mesh):

time: 32.3 us -> 25.9 us (0.80)
  the two profiles are of different devices: /device:TPU:0 before, /device:TPU:16 now
where the time goes in v5:
time: 25.9 us; the launch traced here: 25.6 us
  waiting for transfers between devices  8.6 us (33%)
  blocking collectives  7.19 us (28%)
  starting transfers between devices  5.46 us (21%)
  Pallas kernels  3.07 us (12%)
  between operations  1.32 us (5%)
    all_to_all x1, blocking collectives, per_device(): mine = lax.all_to_all(packed, 'shot', 0, 0, tiled=True)  7.19 us
    ppermute x2, waiting for transfers between devices, swap_sides(): came_last = lax.ppermute(last, 'tile', rounds[1])  5.34 us
    ppermute x2, starting transfers between devices, swap_sides(): came_last = lax.ppermute(last, 'tile', rounds[1])  3.82 us
    ppermute x2, waiting for transfers between devices, swap_sides(): came_first = lax.ppermute(first, 'tile', rounds[0])  3.26 us
    ppermute x2, starting transfers between devices, swap_sides(): came_first = lax.ppermute(first, 'tile', rounds[0])  1.64 us
    pallas_call x1, Pallas kernels, per_device(): pl.pallas_call(own_part, out_shape=(struct(*wavelet.shape), struct(*wide_...  1.59 us
    pallas_call x1, Pallas kernels, per_device(): pl.pallas_call(functools.partial(image_products, 1.0 / shots), out_shape=...  0.98 us
  transfers between devices with their start and end apart: 4, of which 4 were waited for; matrix products, arithmetic and copies ran while one was open for 0% of the time, Pallas kernels for 0%

profile of v5, /device:TPU:16, one launch (start us, length us, event | category | flops | bytes accessed | tf_op | source)
XLA Modules:
  0.0 25.6 jit_solution(18116149464401570597)
XLA Ops:
  0.6 1.6 %own_part.1 = (f32[1,2]{1,0:T(1,128)S(1)}, f32[2,8,32,128]{3,2,1,0:T(8,128)S(1)}, f32[2,8,16,128]{3,2,1,0:T(8,128)S(1)}, f32[2,8,16,128]{3,2,1,0:T(8,128)S(1)}, ...) custom-call(f32[1,16]{1,0:T(1,128)} %bitcast.1, s32[1,32]{1,0:T(1,128)} %spots_hbm.1, ...), custom_call_target="tpu_custom_call" | custom-call | tf_op jit(solution)/shard_map/own_part/pallas_call | solution.py:364
  2.2 1.6 %collective-permute-start = (f32[20,8,128]{2,1,0:T(8,128)S(1)}, f32[20,8,128]{2,1,0:T(8,128)S(1)}, u32[]{:S(2)}, u32[]{:S(2)}) collective-permute-start(f32[20,8,128]{2,1,0:T(8,128)S(1)} %get-tuple-element.21), channel_id=1, source_target_pairs={{0,4},{4,0},{8,12},{12,8},{1,5},{5,1},{9,13},{13,9},{2,6},{6,2},{1... | collective-permute-start | bytes 245768 | tf_op jit(solution)/shard_map/ppermute | solution.py:329
  3.9 1.9 %collective-permute-start.1 = (f32[20,8,128]{2,1,0:T(8,128)S(1)}, f32[20,8,128]{2,1,0:T(8,128)S(1)}, u32[]{:S(2)}, u32[]{:S(2)}) collective-permute-start(f32[20,8,128]{2,1,0:T(8,128)S(1)} %get-tuple-element.22), channel_id=1, source_target_pairs={{4,8},{8,4},{5,9},{9,5},{6,10},{10,6},{7,11},{11,7},{20,24},{24,20... | collective-permute-start | bytes 245768 | tf_op jit(solution)/shard_map/ppermute | solution.py:328
  6.4 0.1 source_and_order.1
  6.5 0.2 collective-permute-done.came_first_ref
  6.7 3.5 %collective-permute-done.1.came_last_ref = f32[20,8,128]{2,1,0:T(8,128)S(1)} collective-permute-done((f32[20,8,128]{2,1,0:T(8,128)S(1)}, f32[20,8,128]{2,1,0:T(8,128)S(1)}, u32[]{:S(2)}, u32[]{:S(2)}) %collective-permute-start.1) | collective-permute-done | bytes 81952 | tf_op jit(solution)/shard_map/ppermute | solution.py:328
  10.2 0.4 %both_steps.1.final_ref = f32[4,2,2,16,128]{4,3,2,1,0:T(8,128)S(1)} custom-call(s32[8,128]{1,0:T(8,128)S(1)} %get-tuple-element.15.up_first_ref, f32[2,8,32,128]{3,2,1,0:T(8,128)S(1)} %get-tuple-element.16.own, f32[2,8,16,128]{3,2,1,0:T(8,128)S(1)} %get-tuple-element.17.part_ref, f32[2,8,16,128]{3,2,1,0:T(8,128)S(1)} %get-tuple-element.14.later_ref, ...), custom_call_target="tpu_custom_call" | custom-call | tf_op jit(solution)/shard_map/both_steps/pallas_call | solution.py:416
  10.6 7.2 %all_to_all.5.mine_ref = f32[4,2,2,16,128]{4,3,2,1,0:T(8,128)S(1)} all-to-all(f32[4,2,2,16,128]{4,3,2,1,0:T(8,128)S(1)} %both_steps.1.final_ref), channel_id=1, replica_groups=mesh['groups'=2,'tile'=4,'shot'=4] {'shot'}, dimensions={0} | all-to-all | bytes 262144 | tf_op jit(solution)/shard_map/all_to_all | solution.py:425
  17.8 0.0 collective-permute-start.3
  17.8 1.9 %collective-permute-start.2 = (f32[4,2,2,16,128]{4,3,2,1,0:T(8,128)S(1)}, f32[4,2,2,16,128]{4,3,2,1,0:T(8,128)S(1)}, u32[]{:S(2)}, u32[]{:S(2)}) collective-permute-start(f32[4,2,2,16,128]{4,3,2,1,0:T(8,128)S(1)} %all_to_all.5.mine_ref), channel_id=1, source_target_pairs={{4,8},{8,4},{5,9},{9,5},{6,10},{10,6},{7,11},{11,7},{20,24},{24,20... | collective-permute-start | bytes 393224 | tf_op jit(solution)/shard_map/ppermute | solution.py:328
  19.7 3.0 %collective-permute-done.3.came_first_ref = f32[4,2,2,16,128]{4,3,2,1,0:T(8,128)S(1)} collective-permute-done((f32[4,2,2,16,128]{4,3,2,1,0:T(8,128)S(1)}, f32[4,2,2,16,128]{4,3,2,1,0:T(8,128)S(1)}, u32[]{:S(2)}, u32[]{:S(2)}) %collective-permute-start.3) | collective-permute-done | bytes 131104 | tf_op jit(solution)/shard_map/ppermute | solution.py:329
  22.8 1.9 %collective-permute-done.2.came_last_ref = f32[4,2,2,16,128]{4,3,2,1,0:T(8,128)S(1)} collective-permute-done((f32[4,2,2,16,128]{4,3,2,1,0:T(8,128)S(1)}, f32[4,2,2,16,128]{4,3,2,1,0:T(8,128)S(1)}, u32[]{:S(2)}, u32[]{:S(2)}) %collective-permute-start.2) | collective-permute-done | bytes 131104 | tf_op jit(solution)/shard_map/ppermute | solution.py:328
  24.7 1.0 %image_products.1 = (f32[1,8,16,128]{3,2,1,0:T(8,128)}, f32[1,8,16,128]{3,2,1,0:T(8,128)}, f32[33,2,16,128]{3,2,1,0:T(8,128)}) custom-call(s32[8,128]{1,0:T(8,128)S(1)} %get-tuple-element.15.up_first_ref, f32[4,2,2,16,128]{4,3,2,1,0:T(8,128)S(1)} %both_steps.1.final_ref, f32[4,2,2,16,128]{4,3,2,1,0:T(8,128)S(1)} %all_to_all.5.mine_ref, ...), custom_call_target="tpu_custom_call" | custom-call | tf_op jit(solution)/shard_map/image_products/pallas_call | solution.py:427
Async XLA Ops:
  2.2 4.5 %collective-permute-start = (f32[20,8,128]{2,1,0:T(8,128)S(1)}, f32[20,8,128]{2,1,0:T(8,128)S(1)}, u32[]{:S(2)}, u32[]{:S(2)}) collective-permute-start(f32[20,8,128]{2,1,0:T(8,128)S(1)} %get-tuple-element.21), channel_id=1, source_target_pairs={{0,4},{4,0},{8,12},{12,8},{1,5},{5,1},{9,13},{13,9},{2,6},{6,2},{1... | collective-permute-start | bytes 245768 | tf_op jit(solution)/shard_map/ppermute | solution.py:329
  3.9 6.3 %collective-permute-start.1 = (f32[20,8,128]{2,1,0:T(8,128)S(1)}, f32[20,8,128]{2,1,0:T(8,128)S(1)}, u32[]{:S(2)}, u32[]{:S(2)}) collective-permute-start(f32[20,8,128]{2,1,0:T(8,128)S(1)} %get-tuple-element.22), channel_id=1, source_target_pairs={{4,8},{8,4},{5,9},{9,5},{6,10},{10,6},{7,11},{11,7},{20,24},{24,20... | collective-permute-start | bytes 245768 | tf_op jit(solution)/shard_map/ppermute | solution.py:328
  17.8 5.0 %collective-permute-start.3 = (f32[4,2,2,16,128]{4,3,2,1,0:T(8,128)S(1)}, f32[4,2,2,16,128]{4,3,2,1,0:T(8,128)S(1)}, u32[]{:S(2)}, u32[]{:S(2)}) collective-permute-start(f32[4,2,2,16,128]{4,3,2,1,0:T(8,128)S(1)} %all_to_all.5.mine_ref), channel_id=1, source_target_pairs={{0,4},{4,0},{8,12},{12,8},{1,5},{5,1},{9,13},{13,9},{2,6},{6,2},{1... | collective-permute-start | bytes 393224 | tf_op jit(solution)/shard_map/ppermute | solution.py:329
  17.8 6.9 %collective-permute-start.2 = (f32[4,2,2,16,128]{4,3,2,1,0:T(8,128)S(1)}, f32[4,2,2,16,128]{4,3,2,1,0:T(8,128)S(1)}, u32[]{:S(2)}, u32[]{:S(2)}) collective-permute-start(f32[4,2,2,16,128]{4,3,2,1,0:T(8,128)S(1)} %all_to_all.5.mine_ref), channel_id=1, source_target_pairs={{4,8},{8,4},{5,9},{9,5},{6,10},{10,6},{7,11},{11,7},{20,24},{24,20... | collective-permute-start | bytes 393224 | tf_op jit(solution)/shard_map/ppermute | solution.py:328

commit v6 on v5

--- a/solution.py
+++ b/solution.py
@@ -53,7 +53,7 @@
 
 
 def source_and_order(
-    width, cell_ref, amps_ref, later_ref, source_ref, source_later_ref, up_first_ref
+    width, cell_ref, amps_ref, later_ref, source_ref, source_later_ref, up_first_ref, inside_ref
 ):
     levels, extent, across = source_later_ref.shape
     cell = cell_ref[0]
@@ -72,6 +72,9 @@
     up_first_ref[...] = jnp.full(
         up_first_ref.shape, jnp.where(goes_up_first(), 1, 0), dtype=jnp.int32
     )
+    tile = lax.axis_index("tile")
+    inside = (tile > 0) & (tile < lax.axis_size("tile") - 1)
+    inside_ref[...] = jnp.full(inside_ref.shape, jnp.where(inside, 1, 0), dtype=jnp.int32)
 
 
 def own_part(
@@ -186,6 +189,7 @@
 
 def both_steps(
     up_first_ref,
+    inside_ref,
     own,
     part_ref,
     later_ref,
@@ -203,10 +207,11 @@
     share = packed_ref.shape[2]
     end = LEAD + extent
     up_first = up_first_ref[0:HALO, :] != 0
+    inside = inside_ref[0:HALO, :] != 0
 
     def received(place, rows):
         first = came_first_ref[place, rows, :]
-        last = came_last_ref[place, rows, :]
+        last = jnp.where(inside, came_last_ref[place, rows, :], 0.0)
         return jnp.where(up_first, last, first), jnp.where(up_first, first, last)
 
     for field in range(2):
@@ -259,6 +264,7 @@
 def image_products(
     weight,
     up_first_ref,
+    inside_ref,
     final_ref,
     mine_ref,
     came_last_ref,
@@ -285,12 +291,13 @@
     for copy in copies:
         copy.start()
     up_first = jnp.concatenate([up_first_ref[...]] * (extent // 8), axis=0) != 0
+    inside = jnp.concatenate([inside_ref[...]] * (extent // 8), axis=0) != 0
     for shot in range(shots):
         for field in range(2):
             for level in range(share):
                 scale = weight if field == 0 else 1.0
                 first = scale * came_first_ref[shot, field, level]
-                last = scale * came_last_ref[shot, field, level]
+                last = jnp.where(inside, scale * came_last_ref[shot, field, level], 0.0)
                 wide[shot, field, level, 0:extent, :] = jnp.where(up_first, last, first)
                 wide[shot, field, level, extent : 2 * extent, :] = (
                     scale * mine_ref[shot, field, level]
@@ -321,17 +328,16 @@
 
 
 def swap_sides(first, last):
-    rounds = [
-        [pair for here in range(begin, lax.axis_size("tile") - 1, 2) for pair in both_ways(here)]
-        for begin in range(2)
-    ]
-    came_last = lax.ppermute(last, "tile", rounds[1])
-    came_first = lax.ppermute(first, "tile", rounds[0])
-    return came_first, came_last
-
-
-def both_ways(tile):
-    return (tile, tile + 1), (tile + 1, tile)
+    tiles = lax.axis_size("tile")
+
+    def swap(value, begin):
+        partner = list(range(tiles))
+        for tile in range(begin, tiles - 1, 2):
+            partner[tile], partner[tile + 1] = tile + 1, tile
+        return lax.ppermute(value, "tile", list(enumerate(partner)))
+
+    came_last = swap(last, 1)
+    return swap(first, 0), came_last
 
 
 def per_device(
@@ -401,27 +407,28 @@
         )
     )
     came_first, came_last = swap_sides(first, last)
-    source, source_later, up_first = pl.pallas_call(
+    source, source_later, up_first, inside = pl.pallas_call(
         functools.partial(source_and_order, width),
         out_shape=(
             struct(levels, extent + 2 * LEAD, across),
             struct(levels, extent, across),
             jax.ShapeDtypeStruct((8, across), jnp.int32),
+            jax.ShapeDtypeStruct((8, across), jnp.int32),
         ),
         in_specs=[SMEM] + [VMEM] * 2,
-        out_specs=[VMEM] * 3,
+        out_specs=[VMEM] * 4,
         compiler_params=params,
         name="source_and_order",
     )(source_cell, amps, later)
     packed = pl.pallas_call(
         both_steps,
         out_shape=struct(shots, 2, share, extent, across),
-        in_specs=[VMEM] * 9,
+        in_specs=[VMEM] * 10,
         out_specs=VMEM,
         scratch_shapes=[scratch(*wide_shape), scratch(*wide_shape)],
         compiler_params=params,
         name="both_steps",
-    )(up_first, own, part, later, source, source_later, coef, came_first, came_last)
+    )(up_first, inside, own, part, later, source, source_later, coef, came_first, came_last)
     mine = lax.all_to_all(packed, "shot", 0, 0, tiled=True)
     fields_first, fields_last = swap_sides(mine, mine)
     return pl.pallas_call(
@@ -431,7 +438,7 @@
             struct(1, levels, extent, across),
             struct(OFFS, share, extent, across),
         ),
-        in_specs=[VMEM] * 5,
+        in_specs=[VMEM] * 6,
         out_specs=[HBM] * 3,
         scratch_shapes=[
             scratch(shots, 2, share, 3 * extent, across),
@@ -441,7 +448,7 @@
         ],
         compiler_params=params,
         name="image_products",
-    )(up_first, packed, mine, fields_last, fields_first)
+    )(up_first, inside, packed, mine, fields_last, fields_first)
 
 
 def solution(mesh):

time: 25.9 us -> 25.9 us (level)
  no operation moved by 1% of the time
where the time goes in v6:
time: 25.9 us; the launch traced here: 25.7 us
  waiting for transfers between devices  8.6 us (33%)
  blocking collectives  7.19 us (28%)
  starting transfers between devices  5.46 us (21%)
  Pallas kernels  3.09 us (12%)
  between operations  1.32 us (5%)
    ppermute x4, waiting for transfers between devices, swap(): return lax.ppermute(value, 'tile', list(enumerate(partner)))  8.6 us
    all_to_all x1, blocking collectives, per_device(): mine = lax.all_to_all(packed, 'shot', 0, 0, tiled=True)  7.19 us
    ppermute x4, starting transfers between devices, swap(): return lax.ppermute(value, 'tile', list(enumerate(partner)))  5.46 us
    pallas_call x1, Pallas kernels, per_device(): pl.pallas_call(own_part, out_shape=(struct(*wavelet.shape), struct(*wide_...  1.59 us
    pallas_call x1, Pallas kernels, per_device(): pl.pallas_call(functools.partial(image_products, 1.0 / shots), out_shape=...  0.98 us
  transfers between devices with their start and end apart: 4, of which 4 were waited for; matrix products, arithmetic and copies ran while one was open for 0% of the time, Pallas kernels for 0%

profile of v6, /device:TPU:16, one launch (start us, length us, event | category | flops | bytes accessed | tf_op | source)
XLA Modules:
  0.0 25.7 jit_solution(18398848355956930743)
XLA Ops:
  0.6 1.6 %own_part.1 = (f32[1,2]{1,0:T(1,128)S(1)}, f32[2,8,32,128]{3,2,1,0:T(8,128)S(1)}, f32[2,8,16,128]{3,2,1,0:T(8,128)S(1)}, f32[2,8,16,128]{3,2,1,0:T(8,128)S(1)}, ...) custom-call(f32[1,16]{1,0:T(1,128)} %bitcast.1, s32[1,32]{1,0:T(1,128)} %spots_hbm.1, ...), custom_call_target="tpu_custom_call" | custom-call | tf_op jit(solution)/shard_map/own_part/pallas_call | solution.py:370
  2.2 1.6 %collective-permute-start = (f32[20,8,128]{2,1,0:T(8,128)S(1)}, f32[20,8,128]{2,1,0:T(8,128)S(1)}, u32[]{:S(2)}, u32[]{:S(2)}) collective-permute-start(f32[20,8,128]{2,1,0:T(8,128)S(1)} %get-tuple-element.23), channel_id=1, source_target_pairs={{0,4},{4,0},{8,12},{12,8},{1,5},{5,1},{9,13},{13,9},{2,6},{6,2},{1... | collective-permute-start | bytes 245768 | tf_op jit(solution)/shard_map/ppermute | solution.py:337
  3.9 1.9 %collective-permute-start.1 = (f32[20,8,128]{2,1,0:T(8,128)S(1)}, f32[20,8,128]{2,1,0:T(8,128)S(1)}, u32[]{:S(2)}, u32[]{:S(2)}) collective-permute-start(f32[20,8,128]{2,1,0:T(8,128)S(1)} %get-tuple-element.24), channel_id=1, source_target_pairs={{0,0},{4,8},{8,4},{12,12},{1,1},{5,9},{9,5},{13,13},{2,2},{6,10},{... | collective-permute-start | bytes 245768 | tf_op jit(solution)/shard_map/ppermute | solution.py:337
  6.4 0.1 source_and_order.1
  6.5 0.2 collective-permute-done.came_first_ref
  6.7 3.5 %collective-permute-done.1.came_last_ref = f32[20,8,128]{2,1,0:T(8,128)S(1)} collective-permute-done((f32[20,8,128]{2,1,0:T(8,128)S(1)}, f32[20,8,128]{2,1,0:T(8,128)S(1)}, u32[]{:S(2)}, u32[]{:S(2)}) %collective-permute-start.1) | collective-permute-done | bytes 81952 | tf_op jit(solution)/shard_map/ppermute | solution.py:337
  10.2 0.4 %both_steps.1.final_ref = f32[4,2,2,16,128]{4,3,2,1,0:T(8,128)S(1)} custom-call(s32[8,128]{1,0:T(8,128)S(1)} %get-tuple-element.16.up_first_ref, s32[8,128]{1,0:T(8,128)S(1)} %get-tuple-element.17.inside_ref, f32[2,8,32,128]{3,2,1,0:T(8,128)S(1)} %get-tuple-element.18.own, f32[2,8,16,128]{3,2,1,0:T(8,128)S(1)} %get-tuple-element.19.part_ref, ...), custom_call_target="tpu_custom_call" | custom-call | tf_op jit(solution)/shard_map/both_steps/pallas_call | solution.py:423
  10.6 7.2 %all_to_all.5.mine_ref = f32[4,2,2,16,128]{4,3,2,1,0:T(8,128)S(1)} all-to-all(f32[4,2,2,16,128]{4,3,2,1,0:T(8,128)S(1)} %both_steps.1.final_ref), channel_id=1, replica_groups=mesh['groups'=2,'tile'=4,'shot'=4] {'shot'}, dimensions={0} | all-to-all | bytes 262144 | tf_op jit(solution)/shard_map/all_to_all | solution.py:432
  17.8 0.0 collective-permute-start.3
  17.8 1.9 %collective-permute-start.2 = (f32[4,2,2,16,128]{4,3,2,1,0:T(8,128)S(1)}, f32[4,2,2,16,128]{4,3,2,1,0:T(8,128)S(1)}, u32[]{:S(2)}, u32[]{:S(2)}) collective-permute-start(f32[4,2,2,16,128]{4,3,2,1,0:T(8,128)S(1)} %all_to_all.5.mine_ref), channel_id=1, source_target_pairs={{0,0},{4,8},{8,4},{12,12},{1,1},{5,9},{9,5},{13,13},{2,2},{6,10},{... | collective-permute-start | bytes 393224 | tf_op jit(solution)/shard_map/ppermute | solution.py:337
  19.7 3.0 %collective-permute-done.3.came_first_ref = f32[4,2,2,16,128]{4,3,2,1,0:T(8,128)S(1)} collective-permute-done((f32[4,2,2,16,128]{4,3,2,1,0:T(8,128)S(1)}, f32[4,2,2,16,128]{4,3,2,1,0:T(8,128)S(1)}, u32[]{:S(2)}, u32[]{:S(2)}) %collective-permute-start.3) | collective-permute-done | bytes 131104 | tf_op jit(solution)/shard_map/ppermute | solution.py:337
  22.8 1.9 %collective-permute-done.2.came_last_ref = f32[4,2,2,16,128]{4,3,2,1,0:T(8,128)S(1)} collective-permute-done((f32[4,2,2,16,128]{4,3,2,1,0:T(8,128)S(1)}, f32[4,2,2,16,128]{4,3,2,1,0:T(8,128)S(1)}, u32[]{:S(2)}, u32[]{:S(2)}) %collective-permute-start.2) | collective-permute-done | bytes 131104 | tf_op jit(solution)/shard_map/ppermute | solution.py:337
  24.7 1.0 %image_products.1 = (f32[1,8,16,128]{3,2,1,0:T(8,128)}, f32[1,8,16,128]{3,2,1,0:T(8,128)}, f32[33,2,16,128]{3,2,1,0:T(8,128)}) custom-call(s32[8,128]{1,0:T(8,128)S(1)} %get-tuple-element.16.up_first_ref, s32[8,128]{1,0:T(8,128)S(1)} %get-tuple-element.17.inside_ref, f32[4,2,2,16,128]{4,3,2,1,0:T(8,128)S(1)} %both_steps.1.final_ref, ...), custom_call_target="tpu_custom_call" | custom-call | tf_op jit(solution)/shard_map/image_products/pallas_call | solution.py:434
Async XLA Ops:
  2.2 4.5 %collective-permute-start = (f32[20,8,128]{2,1,0:T(8,128)S(1)}, f32[20,8,128]{2,1,0:T(8,128)S(1)}, u32[]{:S(2)}, u32[]{:S(2)}) collective-permute-start(f32[20,8,128]{2,1,0:T(8,128)S(1)} %get-tuple-element.23), channel_id=1, source_target_pairs={{0,4},{4,0},{8,12},{12,8},{1,5},{5,1},{9,13},{13,9},{2,6},{6,2},{1... | collective-permute-start | bytes 245768 | tf_op jit(solution)/shard_map/ppermute | solution.py:337
  3.9 6.3 %collective-permute-start.1 = (f32[20,8,128]{2,1,0:T(8,128)S(1)}, f32[20,8,128]{2,1,0:T(8,128)S(1)}, u32[]{:S(2)}, u32[]{:S(2)}) collective-permute-start(f32[20,8,128]{2,1,0:T(8,128)S(1)} %get-tuple-element.24), channel_id=1, source_target_pairs={{0,0},{4,8},{8,4},{12,12},{1,1},{5,9},{9,5},{13,13},{2,2},{6,10},{... | collective-permute-start | bytes 245768 | tf_op jit(solution)/shard_map/ppermute | solution.py:337
  17.8 5.0 %collective-permute-start.3 = (f32[4,2,2,16,128]{4,3,2,1,0:T(8,128)S(1)}, f32[4,2,2,16,128]{4,3,2,1,0:T(8,128)S(1)}, u32[]{:S(2)}, u32[]{:S(2)}) collective-permute-start(f32[4,2,2,16,128]{4,3,2,1,0:T(8,128)S(1)} %all_to_all.5.mine_ref), channel_id=1, source_target_pairs={{0,4},{4,0},{8,12},{12,8},{1,5},{5,1},{9,13},{13,9},{2,6},{6,2},{1... | collective-permute-start | bytes 393224 | tf_op jit(solution)/shard_map/ppermute | solution.py:337
  17.8 6.9 %collective-permute-start.2 = (f32[4,2,2,16,128]{4,3,2,1,0:T(8,128)S(1)}, f32[4,2,2,16,128]{4,3,2,1,0:T(8,128)S(1)}, u32[]{:S(2)}, u32[]{:S(2)}) collective-permute-start(f32[4,2,2,16,128]{4,3,2,1,0:T(8,128)S(1)} %all_to_all.5.mine_ref), channel_id=1, source_target_pairs={{0,0},{4,8},{8,4},{12,12},{1,1},{5,9},{9,5},{13,13},{2,2},{6,10},{... | collective-permute-start | bytes 393224 | tf_op jit(solution)/shard_map/ppermute | solution.py:337

commit v7 on v6

--- a/solution.py
+++ b/solution.py
@@ -53,7 +53,7 @@
 
 
 def source_and_order(
-    width, cell_ref, amps_ref, later_ref, source_ref, source_later_ref, up_first_ref, inside_ref
+    width, cell_ref, amps_ref, later_ref, source_ref, source_later_ref, up_first_ref, inside_ref, bits_ref
 ):
     levels, extent, across = source_later_ref.shape
     cell = cell_ref[0]
@@ -75,6 +75,9 @@
     tile = lax.axis_index("tile")
     inside = (tile > 0) & (tile < lax.axis_size("tile") - 1)
     inside_ref[...] = jnp.full(inside_ref.shape, jnp.where(inside, 1, 0), dtype=jnp.int32)
+    shot = jnp.full(bits_ref.shape[1:], lax.axis_index("shot"), dtype=jnp.int32)
+    for bit in range(bits_ref.shape[0]):
+        bits_ref[bit] = shot & (1 << bit)
 
 
 def own_part(
@@ -190,6 +193,7 @@
 def both_steps(
     up_first_ref,
     inside_ref,
+    bits_ref,
     own,
     part_ref,
     later_ref,
@@ -198,13 +202,15 @@
     coef_ref,
     came_first_ref,
     came_last_ref,
-    packed_ref,
-    other,
-    middle,
+    final_ref,
+    mine_ref,
+    *rest,
 ):
+    *theirs, other, middle = rest
+    blocks = [mine_ref, *theirs]
     levels, extent, across = coef_ref.shape
     shape = (extent, across)
-    share = packed_ref.shape[2]
+    share = mine_ref.shape[1]
     end = LEAD + extent
     up_first = up_first_ref[0:HALO, :] != 0
     inside = inside_ref[0:HALO, :] != 0
@@ -258,7 +264,21 @@
             total = laplace_level(middle, field, level, levels, extent, weights)
             later = source_later_ref[level] if field == 0 else later_ref[field, level]
             value = 2.0 * middle[field, level, LEAD:end, :] + later
-            packed_ref[level // share, field, level % share] = value + coef_ref[level] * total
+            final_ref[field, level] = value + coef_ref[level] * total
+    masks = [
+        jnp.concatenate([bits_ref[bit]] * (extent // 8), axis=0) != 0
+        for bit in range(bits_ref.shape[0])
+    ]
+    for field in range(2):
+        for level in range(share):
+            parts = [final_ref[field, place * share + level] for place in range(len(blocks))]
+            for bit, mask in enumerate(masks):
+                parts = [
+                    jnp.where(mask, parts[place ^ (1 << bit)], parts[place])
+                    for place in range(len(blocks))
+                ]
+            for block, part in zip(blocks, parts):
+                block[field, level] = part
 
 
 def image_products(
@@ -280,14 +300,9 @@
     shots, _, share, extent, across = mine_ref.shape
     copies = []
     for field, out in enumerate((src_hbm, rec_hbm)):
-        for shot in range(shots):
-            copies.append(
-                pltpu.make_async_copy(
-                    final_ref.at[shot, field],
-                    out.at[0, pl.ds(shot * share, share)],
-                    field_sems.at[field, shot],
-                )
-            )
+        copies.append(
+            pltpu.make_async_copy(final_ref.at[field], out.at[0], field_sems.at[field])
+        )
     for copy in copies:
         copy.start()
     up_first = jnp.concatenate([up_first_ref[...]] * (extent // 8), axis=0) != 0
@@ -332,8 +347,9 @@
 
     def swap(value, begin):
         partner = list(range(tiles))
-        for tile in range(begin, tiles - 1, 2):
-            partner[tile], partner[tile + 1] = tile + 1, tile
+        for tile in range(begin, tiles - 1 + begin, 2):
+            after = (tile + 1) % tiles
+            partner[tile], partner[after] = after, tile
         return lax.ppermute(value, "tile", list(enumerate(partner)))
 
     came_last = swap(last, 1)
@@ -407,29 +423,35 @@
         )
     )
     came_first, came_last = swap_sides(first, last)
-    source, source_later, up_first, inside = pl.pallas_call(
+    source, source_later, up_first, inside, bits = pl.pallas_call(
         functools.partial(source_and_order, width),
         out_shape=(
             struct(levels, extent + 2 * LEAD, across),
             struct(levels, extent, across),
             jax.ShapeDtypeStruct((8, across), jnp.int32),
             jax.ShapeDtypeStruct((8, across), jnp.int32),
+            jax.ShapeDtypeStruct((shots.bit_length() - 1, 8, across), jnp.int32),
         ),
         in_specs=[SMEM] + [VMEM] * 2,
-        out_specs=[VMEM] * 4,
+        out_specs=[VMEM] * 5,
         compiler_params=params,
         name="source_and_order",
     )(source_cell, amps, later)
-    packed = pl.pallas_call(
+    block = struct(2, share, extent, across)
+    final, own_block, *blocks = pl.pallas_call(
         both_steps,
-        out_shape=struct(shots, 2, share, extent, across),
-        in_specs=[VMEM] * 10,
-        out_specs=VMEM,
+        out_shape=(struct(2, levels, extent, across), *([block] * shots)),
+        in_specs=[VMEM] * 11,
+        out_specs=[VMEM] * (1 + shots),
         scratch_shapes=[scratch(*wide_shape), scratch(*wide_shape)],
         compiler_params=params,
         name="both_steps",
-    )(up_first, inside, own, part, later, source, source_later, coef, came_first, came_last)
-    mine = lax.all_to_all(packed, "shot", 0, 0, tiled=True)
+    )(up_first, inside, bits, own, part, later, source, source_later, coef, came_first, came_last)
+    came = [
+        lax.ppermute(sent, "shot", [(shot, shot ^ (1 + i)) for shot in range(shots)])
+        for i, sent in enumerate(blocks)
+    ]
+    mine = jnp.stack([own_block, *came])
     fields_first, fields_last = swap_sides(mine, mine)
     return pl.pallas_call(
         functools.partial(image_products, 1.0 / shots),
@@ -443,12 +465,12 @@
         scratch_shapes=[
             scratch(shots, 2, share, 3 * extent, across),
             scratch(OFFS, share, extent, across),
-            pltpu.SemaphoreType.DMA((2, shots)),
+            pltpu.SemaphoreType.DMA((2,)),
             pltpu.SemaphoreType.DMA((3,)),
         ],
         compiler_params=params,
         name="image_products",
-    )(up_first, inside, packed, mine, fields_last, fields_first)
+    )(up_first, inside, final, mine, fields_last, fields_first)
 
 
 def solution(mesh):

time: 25.9 us -> 28 us (1.081)
  the two profiles are of different devices: /device:TPU:16 before, /device:TPU:0 now
where the time goes in v7:
time: 28 us; the launch traced here: 27.9 us
  waiting for transfers between devices  12.9 us (46%)
  starting transfers between devices  10.6 us (38%)
  Pallas kernels  3 us (11%)
  between operations  1.34 us (5%)
    ppermute x4, waiting for transfers between devices, swap(): return lax.ppermute(value, 'tile', list(enumerate(partner)))  9.87 us
    ppermute x4, starting transfers between devices, swap(): return lax.ppermute(value, 'tile', list(enumerate(partner)))  8.69 us
    ppermute x3, waiting for transfers between devices, per_device(): lax.ppermute(sent, 'shot', [(shot, shot ^ 1 + i) for shot in range(shots)])  3.04 us
    ppermute x3, starting transfers between devices, per_device(): lax.ppermute(sent, 'shot', [(shot, shot ^ 1 + i) for shot in range(shots)])  1.93 us
    pallas_call x1, Pallas kernels, per_device(): pl.pallas_call(own_part, out_shape=(struct(*wavelet.shape), struct(*wide_...  1.59 us
    pallas_call x1, Pallas kernels, per_device(): pl.pallas_call(functools.partial(image_products, 1.0 / shots), out_shape=...  0.93 us
  transfers between devices with their start and end apart: 7, of which 5 were waited for; matrix products, arithmetic and copies ran while one was open for 0% of the time, Pallas kernels for 0%

profile of v7, /device:TPU:0, one launch (start us, length us, event | category | flops | bytes accessed | tf_op | source)
XLA Modules:
  0.0 27.9 jit_solution(6620421068480092882)
XLA Ops:
  0.6 1.6 %own_part.1 = (f32[1,2]{1,0:T(1,128)S(1)}, f32[2,8,32,128]{3,2,1,0:T(8,128)S(1)}, f32[2,8,16,128]{3,2,1,0:T(8,128)S(1)}, f32[2,8,16,128]{3,2,1,0:T(8,128)S(1)}, ...) custom-call(f32[1,16]{1,0:T(1,128)} %bitcast.9, s32[1,32]{1,0:T(1,128)} %spots_hbm.1, ...), custom_call_target="tpu_custom_call" | custom-call | tf_op jit(solution)/shard_map/own_part/pallas_call | solution.py:386
  2.2 3.1 %collective-permute-start = (f32[20,8,128]{2,1,0:T(8,128)S(1)}, f32[20,8,128]{2,1,0:T(8,128)S(1)}, u32[]{:S(2)}, u32[]{:S(2)}) collective-permute-start(f32[20,8,128]{2,1,0:T(8,128)S(1)} %get-tuple-element.30), channel_id=1, source_target_pairs={{0,4},{4,0},{8,12},{12,8},{1,5},{5,1},{9,13},{13,9},{2,6},{6,2},{1... | collective-permute-start | bytes 245768 | tf_op jit(solution)/shard_map/ppermute | solution.py:353
  5.3 2.5 %collective-permute-start.1 = (f32[20,8,128]{2,1,0:T(8,128)S(1)}, f32[20,8,128]{2,1,0:T(8,128)S(1)}, u32[]{:S(2)}, u32[]{:S(2)}) collective-permute-start(f32[20,8,128]{2,1,0:T(8,128)S(1)} %get-tuple-element.31), channel_id=1, source_target_pairs={{0,12},{4,8},{8,4},{12,0},{1,13},{5,9},{9,5},{13,1},{2,14},{6,10},... | collective-permute-start | bytes 245768 | tf_op jit(solution)/shard_map/ppermute | solution.py:353
  8.4 0.1 source_and_order.1
  8.5 0.0 collective-permute-done.came_first_ref
  8.5 3.4 %collective-permute-done.1.came_last_ref = f32[20,8,128]{2,1,0:T(8,128)S(1)} collective-permute-done((f32[20,8,128]{2,1,0:T(8,128)S(1)}, f32[20,8,128]{2,1,0:T(8,128)S(1)}, u32[]{:S(2)}, u32[]{:S(2)}) %collective-permute-start.1) | collective-permute-done | bytes 81952 | tf_op jit(solution)/shard_map/ppermute | solution.py:353
  12.0 0.4 %both_steps.1 = (f32[2,8,16,128]{3,2,1,0:T(8,128)S(1)}, f32[2,2,16,128]{3,2,1,0:T(8,128)S(1)}, f32[2,2,16,128]{3,2,1,0:T(8,128)S(1)}, f32[2,2,16,128]{3,2,1,0:T(8,128)S(1)}, f32[2,2,16,128]{3,2,1,0:T(8,128)S(1)}) custom-call(s32[8,128]{1,0:T(8,128)S(1)} %get-tuple-element.22.up_first_ref, s32[8,128]{1,0:T(8,128)S(1)} %get-tuple-element.23.inside_ref, ...), custom_call_target="tpu_custom_call" | custom-call | tf_op jit(solution)/shard_map/both_steps/pallas_call | solution.py:441
  12.4 0.1 collective-permute-start.2
  12.4 1.6 %collective-permute-start.3 = (f32[2,2,16,128]{3,2,1,0:T(8,128)S(1)}, f32[2,2,16,128]{3,2,1,0:T(8,128)S(1)}, u32[]{:S(2)}, u32[]{:S(2)}) collective-permute-start(f32[2,2,16,128]{3,2,1,0:T(8,128)S(1)} %get-tuple-element.35), channel_id=1, source_target_pairs={{0,2},{1,3},{2,0},{3,1},{4,6},{5,7},{6,4},{7,5},{8,10},{9,11},{10,... | collective-permute-start | bytes 98312 | tf_op jit(solution)/shard_map/ppermute | solution.py:451
  14.0 0.3 %collective-permute-start.4 = (f32[2,2,16,128]{3,2,1,0:T(8,128)S(1)}, f32[2,2,16,128]{3,2,1,0:T(8,128)S(1)}, u32[]{:S(2)}, u32[]{:S(2)}) collective-permute-start(f32[2,2,16,128]{3,2,1,0:T(8,128)S(1)} %get-tuple-element.36), channel_id=1, source_target_pairs={{0,3},{1,2},{2,1},{3,0},{4,7},{5,6},{6,5},{7,4},{8,11},{9,10},{10,... | collective-permute-start | bytes 98312 | tf_op jit(solution)/shard_map/ppermute | solution.py:451
  14.3 0.0 collective-permute-done.2
  14.3 2.1 %collective-permute-done.3 = f32[2,2,16,128]{3,2,1,0:T(8,128)S(1)} collective-permute-done((f32[2,2,16,128]{3,2,1,0:T(8,128)S(1)}, f32[2,2,16,128]{3,2,1,0:T(8,128)S(1)}, u32[]{:S(2)}, u32[]{:S(2)}) %collective-permute-start.3) | collective-permute-done | bytes 32800 | tf_op jit(solution)/shard_map/ppermute | solution.py:451
  16.4 0.9 %collective-permute-done.4 = f32[2,2,16,128]{3,2,1,0:T(8,128)S(1)} collective-permute-done((f32[2,2,16,128]{3,2,1,0:T(8,128)S(1)}, f32[2,2,16,128]{3,2,1,0:T(8,128)S(1)}, u32[]{:S(2)}, u32[]{:S(2)}) %collective-permute-start.4) | collective-permute-done | bytes 32800 | tf_op jit(solution)/shard_map/ppermute | solution.py:451
  17.4 0.1 collective-permute-start.6
  17.4 3.1 %collective-permute-start.5 = (f32[4,2,2,16,128]{4,3,2,1,0:T(8,128)S(1)}, f32[4,2,2,16,128]{4,3,2,1,0:T(8,128)S(1)}, u32[]{:S(2)}, u32[]{:S(2)}) collective-permute-start(f32[4,2,2,16,128]{4,3,2,1,0:T(8,128)S(1)} %pad_maximum_fusion.mine_ref), channel_id=1, source_target_pairs={{0,12},{4,8},{8,4},{12,0},{1,13},{5,9},{9,5},{13,1},{2,14},{6,10},... | collective-permute-start | bytes 393224 | tf_op jit(solution)/shard_map/ppermute | solution.py:353
  20.5 2.5 %collective-permute-done.6.came_first_ref = f32[4,2,2,16,128]{4,3,2,1,0:T(8,128)S(1)} collective-permute-done((f32[4,2,2,16,128]{4,3,2,1,0:T(8,128)S(1)}, f32[4,2,2,16,128]{4,3,2,1,0:T(8,128)S(1)}, u32[]{:S(2)}, u32[]{:S(2)}) %collective-permute-start.6) | collective-permute-done | bytes 131104 | tf_op jit(solution)/shard_map/ppermute | solution.py:353
  23.0 4.0 %collective-permute-done.5.came_last_ref = f32[4,2,2,16,128]{4,3,2,1,0:T(8,128)S(1)} collective-permute-done((f32[4,2,2,16,128]{4,3,2,1,0:T(8,128)S(1)}, f32[4,2,2,16,128]{4,3,2,1,0:T(8,128)S(1)}, u32[]{:S(2)}, u32[]{:S(2)}) %collective-permute-start.5) | collective-permute-done | bytes 131104 | tf_op jit(solution)/shard_map/ppermute | solution.py:353
  27.0 0.9 %image_products.1 = (f32[1,8,16,128]{3,2,1,0:T(8,128)}, f32[1,8,16,128]{3,2,1,0:T(8,128)}, f32[33,2,16,128]{3,2,1,0:T(8,128)}) custom-call(s32[8,128]{1,0:T(8,128)S(1)} %get-tuple-element.22.up_first_ref, s32[8,128]{1,0:T(8,128)S(1)} %get-tuple-element.23.inside_ref, f32[2,8,16,128]{3,2,1,0:T(8,128)S(1)} %get-tuple-element.32.final_ref, ...), custom_call_target="tpu_custom_call" | custom-call | tf_op jit(solution)/shard_map/image_products/pallas_call | solution.py:456
  (1 shorter events, 0.0 us)
Async XLA Ops:
  2.2 6.3 %collective-permute-start = (f32[20,8,128]{2,1,0:T(8,128)S(1)}, f32[20,8,128]{2,1,0:T(8,128)S(1)}, u32[]{:S(2)}, u32[]{:S(2)}) collective-permute-start(f32[20,8,128]{2,1,0:T(8,128)S(1)} %get-tuple-element.30), channel_id=1, source_target_pairs={{0,4},{4,0},{8,12},{12,8},{1,5},{5,1},{9,13},{13,9},{2,6},{6,2},{1... | collective-permute-start | bytes 245768 | tf_op jit(solution)/shard_map/ppermute | solution.py:353
  5.3 6.6 %collective-permute-start.1 = (f32[20,8,128]{2,1,0:T(8,128)S(1)}, f32[20,8,128]{2,1,0:T(8,128)S(1)}, u32[]{:S(2)}, u32[]{:S(2)}) collective-permute-start(f32[20,8,128]{2,1,0:T(8,128)S(1)} %get-tuple-element.31), channel_id=1, source_target_pairs={{0,12},{4,8},{8,4},{12,0},{1,13},{5,9},{9,5},{13,1},{2,14},{6,10},... | collective-permute-start | bytes 245768 | tf_op jit(solution)/shard_map/ppermute | solution.py:353
  12.4 1.9 %collective-permute-start.2 = (f32[2,2,16,128]{3,2,1,0:T(8,128)S(1)}, f32[2,2,16,128]{3,2,1,0:T(8,128)S(1)}, u32[]{:S(2)}, u32[]{:S(2)}) collective-permute-start(f32[2,2,16,128]{3,2,1,0:T(8,128)S(1)} %get-tuple-element.34), channel_id=1, source_target_pairs={{0,1},{1,0},{2,3},{3,2},{4,5},{5,4},{6,7},{7,6},{8,9},{9,8},{10,11... | collective-permute-start | bytes 98312 | tf_op jit(solution)/shard_map/ppermute | solution.py:451
  12.4 4.0 %collective-permute-start.3 = (f32[2,2,16,128]{3,2,1,0:T(8,128)S(1)}, f32[2,2,16,128]{3,2,1,0:T(8,128)S(1)}, u32[]{:S(2)}, u32[]{:S(2)}) collective-permute-start(f32[2,2,16,128]{3,2,1,0:T(8,128)S(1)} %get-tuple-element.35), channel_id=1, source_target_pairs={{0,2},{1,3},{2,0},{3,1},{4,6},{5,7},{6,4},{7,5},{8,10},{9,11},{10,... | collective-permute-start | bytes 98312 | tf_op jit(solution)/shard_map/ppermute | solution.py:451
  14.0 3.3 %collective-permute-start.4 = (f32[2,2,16,128]{3,2,1,0:T(8,128)S(1)}, f32[2,2,16,128]{3,2,1,0:T(8,128)S(1)}, u32[]{:S(2)}, u32[]{:S(2)}) collective-permute-start(f32[2,2,16,128]{3,2,1,0:T(8,128)S(1)} %get-tuple-element.36), channel_id=1, source_target_pairs={{0,3},{1,2},{2,1},{3,0},{4,7},{5,6},{6,5},{7,4},{8,11},{9,10},{10,... | collective-permute-start | bytes 98312 | tf_op jit(solution)/shard_map/ppermute | solution.py:451
  17.4 5.6 %collective-permute-start.6 = (f32[4,2,2,16,128]{4,3,2,1,0:T(8,128)S(1)}, f32[4,2,2,16,128]{4,3,2,1,0:T(8,128)S(1)}, u32[]{:S(2)}, u32[]{:S(2)}) collective-permute-start(f32[4,2,2,16,128]{4,3,2,1,0:T(8,128)S(1)} %pad_maximum_fusion.mine_ref), channel_id=1, source_target_pairs={{0,4},{4,0},{8,12},{12,8},{1,5},{5,1},{9,13},{13,9},{2,6},{6,2},{1... | collective-permute-start | bytes 393224 | tf_op jit(solution)/shard_map/ppermute | solution.py:353
  17.4 9.5 %collective-permute-start.5 = (f32[4,2,2,16,128]{4,3,2,1,0:T(8,128)S(1)}, f32[4,2,2,16,128]{4,3,2,1,0:T(8,128)S(1)}, u32[]{:S(2)}, u32[]{:S(2)}) collective-permute-start(f32[4,2,2,16,128]{4,3,2,1,0:T(8,128)S(1)} %pad_maximum_fusion.mine_ref), channel_id=1, source_target_pairs={{0,12},{4,8},{8,4},{12,0},{1,13},{5,9},{9,5},{13,1},{2,14},{6,10},... | collective-permute-start | bytes 393224 | tf_op jit(solution)/shard_map/ppermute | solution.py:353

commit v8 on v7

--- a/solution.py
+++ b/solution.py
@@ -343,14 +343,17 @@
 
 
 def swap_sides(first, last):
-    tiles = lax.axis_size("tile")
+    tiles, shots = lax.axis_size("tile"), lax.axis_size("shot")
 
     def swap(value, begin):
-        partner = list(range(tiles))
-        for tile in range(begin, tiles - 1 + begin, 2):
-            after = (tile + 1) % tiles
-            partner[tile], partner[after] = after, tile
-        return lax.ppermute(value, "tile", list(enumerate(partner)))
+        pairs = []
+        for tile in range(tiles):
+            partner = tile + 1 if (tile - begin) % 2 == 0 else tile - 1
+            inside = 0 <= partner < tiles
+            for shot in range(shots):
+                target = partner * shots + shot if inside else tile * shots + (shot ^ 1)
+                pairs.append((tile * shots + shot, target))
+        return lax.ppermute(value, ("tile", "shot"), pairs)
 
     came_last = swap(last, 1)
     return swap(first, 0), came_last

time: 28 us -> 21.3 us (0.76)
  waiting for transfers between devices: 12.9 us -> 8.8 us
  starting transfers between devices: 10.6 us -> 7.98 us
    ppermute x4, waiting for transfers between devices: 9.87 us -> 5.53 us  [swap(): return lax.ppermute(value, ('tile', 'shot'), pairs)]
    ppermute x4, starting transfers between devices: 8.69 us -> 5.86 us  [swap(): return lax.ppermute(value, ('tile', 'shot'), pairs)]
  transfers between devices with their start and end apart: 7 -> 7, of which waited for: 5 -> 4; matrix products, arithmetic and copies ran while one was open for 0% -> 0% of each run, Pallas kernels for 0% -> 0%
where the time goes in v8:
time: 21.3 us; the launch traced here: 21.1 us
  waiting for transfers between devices  8.8 us (41%)
  starting transfers between devices  7.98 us (37%)
  Pallas kernels  3 us (14%)
  between operations  1.32 us (6%)
    ppermute x4, starting transfers between devices, swap(): return lax.ppermute(value, ('tile', 'shot'), pairs)  5.86 us
    ppermute x4, waiting for transfers between devices, swap(): return lax.ppermute(value, ('tile', 'shot'), pairs)  5.53 us
    ppermute x3, waiting for transfers between devices, per_device(): lax.ppermute(sent, 'shot', [(shot, shot ^ 1 + i) for shot in range(shots)])  3.27 us
    ppermute x3, starting transfers between devices, per_device(): lax.ppermute(sent, 'shot', [(shot, shot ^ 1 + i) for shot in range(shots)])  2.12 us
    pallas_call x1, Pallas kernels, per_device(): pl.pallas_call(own_part, out_shape=(struct(*wavelet.shape), struct(*wide_...  1.59 us
    pallas_call x1, Pallas kernels, per_device(): pl.pallas_call(functools.partial(image_products, 1.0 / shots), out_shape=...  0.93 us
  transfers between devices with their start and end apart: 7, of which 4 were waited for; matrix products, arithmetic and copies ran while one was open for 0% of the time, Pallas kernels for 0%

profile of v8, /device:TPU:0, one launch (start us, length us, event | category | flops | bytes accessed | tf_op | source)
XLA Modules:
  0.0 21.1 jit_solution(15070403839594314851)
XLA Ops:
  0.6 1.6 %own_part.1 = (f32[1,2]{1,0:T(1,128)S(1)}, f32[2,8,32,128]{3,2,1,0:T(8,128)S(1)}, f32[2,8,16,128]{3,2,1,0:T(8,128)S(1)}, f32[2,8,16,128]{3,2,1,0:T(8,128)S(1)}, ...) custom-call(f32[1,16]{1,0:T(1,128)} %bitcast.9, s32[1,32]{1,0:T(1,128)} %spots_hbm.1, ...), custom_call_target="tpu_custom_call" | custom-call | tf_op jit(solution)/shard_map/own_part/pallas_call | solution.py:389
  2.2 3.1 %collective-permute-start = (f32[20,8,128]{2,1,0:T(8,128)S(1)}, f32[20,8,128]{2,1,0:T(8,128)S(1)}, u32[]{:S(2)}, u32[]{:S(2)}) collective-permute-start(f32[20,8,128]{2,1,0:T(8,128)S(1)} %get-tuple-element.30), channel_id=1, source_target_pairs={{0,4},{1,5},{2,6},{3,7},{4,0},{5,1},{6,2},{7,3},{8,12},{9,13},{10,... | collective-permute-start | bytes 245768 | tf_op jit(solution)/shard_map/ppermute | solution.py:356
  5.3 0.0 collective-permute-start.1
  6.0 0.1 source_and_order.1
  6.1 1.7 %collective-permute-done.came_first_ref = f32[20,8,128]{2,1,0:T(8,128)S(1)} collective-permute-done((f32[20,8,128]{2,1,0:T(8,128)S(1)}, f32[20,8,128]{2,1,0:T(8,128)S(1)}, u32[]{:S(2)}, u32[]{:S(2)}) %collective-permute-start) | collective-permute-done | bytes 81952 | tf_op jit(solution)/shard_map/ppermute | solution.py:356
  7.8 0.0 collective-permute-done.1.came_last_ref
  7.8 0.4 %both_steps.1 = (f32[2,8,16,128]{3,2,1,0:T(8,128)S(1)}, f32[2,2,16,128]{3,2,1,0:T(8,128)S(1)}, f32[2,2,16,128]{3,2,1,0:T(8,128)S(1)}, f32[2,2,16,128]{3,2,1,0:T(8,128)S(1)}, f32[2,2,16,128]{3,2,1,0:T(8,128)S(1)}) custom-call(s32[8,128]{1,0:T(8,128)S(1)} %get-tuple-element.22.up_first_ref, s32[8,128]{1,0:T(8,128)S(1)} %get-tuple-element.23.inside_ref, ...), custom_call_target="tpu_custom_call" | custom-call | tf_op jit(solution)/shard_map/both_steps/pallas_call | solution.py:444
  8.2 0.1 collective-permute-start.2
  8.3 2.0 %collective-permute-start.3 = (f32[2,2,16,128]{3,2,1,0:T(8,128)S(1)}, f32[2,2,16,128]{3,2,1,0:T(8,128)S(1)}, u32[]{:S(2)}, u32[]{:S(2)}) collective-permute-start(f32[2,2,16,128]{3,2,1,0:T(8,128)S(1)} %get-tuple-element.35), channel_id=1, source_target_pairs={{0,2},{1,3},{2,0},{3,1},{4,6},{5,7},{6,4},{7,5},{8,10},{9,11},{10,... | collective-permute-start | bytes 98312 | tf_op jit(solution)/shard_map/ppermute | solution.py:454
  10.2 0.1 collective-permute-start.4
  10.3 0.0 collective-permute-done.2
  10.3 1.9 %collective-permute-done.3 = f32[2,2,16,128]{3,2,1,0:T(8,128)S(1)} collective-permute-done((f32[2,2,16,128]{3,2,1,0:T(8,128)S(1)}, f32[2,2,16,128]{3,2,1,0:T(8,128)S(1)}, u32[]{:S(2)}, u32[]{:S(2)}) %collective-permute-start.3) | collective-permute-done | bytes 32800 | tf_op jit(solution)/shard_map/ppermute | solution.py:454
  12.2 1.3 %collective-permute-done.4 = f32[2,2,16,128]{3,2,1,0:T(8,128)S(1)} collective-permute-done((f32[2,2,16,128]{3,2,1,0:T(8,128)S(1)}, f32[2,2,16,128]{3,2,1,0:T(8,128)S(1)}, u32[]{:S(2)}, u32[]{:S(2)}) %collective-permute-start.4) | collective-permute-done | bytes 32800 | tf_op jit(solution)/shard_map/ppermute | solution.py:454
  13.6 2.8 %collective-permute-start.6 = (f32[4,2,2,16,128]{4,3,2,1,0:T(8,128)S(1)}, f32[4,2,2,16,128]{4,3,2,1,0:T(8,128)S(1)}, u32[]{:S(2)}, u32[]{:S(2)}) collective-permute-start(f32[4,2,2,16,128]{4,3,2,1,0:T(8,128)S(1)} %pad_maximum_fusion.mine_ref), channel_id=1, source_target_pairs={{0,4},{1,5},{2,6},{3,7},{4,0},{5,1},{6,2},{7,3},{8,12},{9,13},{10,... | collective-permute-start | bytes 393224 | tf_op jit(solution)/shard_map/ppermute | solution.py:356
  16.4 0.0 collective-permute-start.5
  16.4 3.8 %collective-permute-done.6.came_first_ref = f32[4,2,2,16,128]{4,3,2,1,0:T(8,128)S(1)} collective-permute-done((f32[4,2,2,16,128]{4,3,2,1,0:T(8,128)S(1)}, f32[4,2,2,16,128]{4,3,2,1,0:T(8,128)S(1)}, u32[]{:S(2)}, u32[]{:S(2)}) %collective-permute-start.6) | collective-permute-done | bytes 131104 | tf_op jit(solution)/shard_map/ppermute | solution.py:356
  20.2 0.0 collective-permute-done.5.came_last_ref
  20.2 0.9 %image_products.1 = (f32[1,8,16,128]{3,2,1,0:T(8,128)}, f32[1,8,16,128]{3,2,1,0:T(8,128)}, f32[33,2,16,128]{3,2,1,0:T(8,128)}) custom-call(s32[8,128]{1,0:T(8,128)S(1)} %get-tuple-element.22.up_first_ref, s32[8,128]{1,0:T(8,128)S(1)} %get-tuple-element.23.inside_ref, f32[2,8,16,128]{3,2,1,0:T(8,128)S(1)} %get-tuple-element.32.final_ref, ...), custom_call_target="tpu_custom_call" | custom-call | tf_op jit(solution)/shard_map/image_products/pallas_call | solution.py:459
  (1 shorter events, 0.0 us)
Async XLA Ops:
  2.2 5.5 %collective-permute-start = (f32[20,8,128]{2,1,0:T(8,128)S(1)}, f32[20,8,128]{2,1,0:T(8,128)S(1)}, u32[]{:S(2)}, u32[]{:S(2)}) collective-permute-start(f32[20,8,128]{2,1,0:T(8,128)S(1)} %get-tuple-element.30), channel_id=1, source_target_pairs={{0,4},{1,5},{2,6},{3,7},{4,0},{5,1},{6,2},{7,3},{8,12},{9,13},{10,... | collective-permute-start | bytes 245768 | tf_op jit(solution)/shard_map/ppermute | solution.py:356
  5.3 2.4 %collective-permute-start.1 = (f32[20,8,128]{2,1,0:T(8,128)S(1)}, f32[20,8,128]{2,1,0:T(8,128)S(1)}, u32[]{:S(2)}, u32[]{:S(2)}) collective-permute-start(f32[20,8,128]{2,1,0:T(8,128)S(1)} %get-tuple-element.31), channel_id=1, source_target_pairs={{0,1},{1,0},{2,3},{3,2},{4,8},{5,9},{6,10},{7,11},{8,4},{9,5},{10,... | collective-permute-start | bytes 245768 | tf_op jit(solution)/shard_map/ppermute | solution.py:356
  8.2 2.1 %collective-permute-start.2 = (f32[2,2,16,128]{3,2,1,0:T(8,128)S(1)}, f32[2,2,16,128]{3,2,1,0:T(8,128)S(1)}, u32[]{:S(2)}, u32[]{:S(2)}) collective-permute-start(f32[2,2,16,128]{3,2,1,0:T(8,128)S(1)} %get-tuple-element.34), channel_id=1, source_target_pairs={{0,1},{1,0},{2,3},{3,2},{4,5},{5,4},{6,7},{7,6},{8,9},{9,8},{10,11... | collective-permute-start | bytes 98312 | tf_op jit(solution)/shard_map/ppermute | solution.py:454
  8.3 4.0 %collective-permute-start.3 = (f32[2,2,16,128]{3,2,1,0:T(8,128)S(1)}, f32[2,2,16,128]{3,2,1,0:T(8,128)S(1)}, u32[]{:S(2)}, u32[]{:S(2)}) collective-permute-start(f32[2,2,16,128]{3,2,1,0:T(8,128)S(1)} %get-tuple-element.35), channel_id=1, source_target_pairs={{0,2},{1,3},{2,0},{3,1},{4,6},{5,7},{6,4},{7,5},{8,10},{9,11},{10,... | collective-permute-start | bytes 98312 | tf_op jit(solution)/shard_map/ppermute | solution.py:454
  10.2 3.3 %collective-permute-start.4 = (f32[2,2,16,128]{3,2,1,0:T(8,128)S(1)}, f32[2,2,16,128]{3,2,1,0:T(8,128)S(1)}, u32[]{:S(2)}, u32[]{:S(2)}) collective-permute-start(f32[2,2,16,128]{3,2,1,0:T(8,128)S(1)} %get-tuple-element.36), channel_id=1, source_target_pairs={{0,3},{1,2},{2,1},{3,0},{4,7},{5,6},{6,5},{7,4},{8,11},{9,10},{10,... | collective-permute-start | bytes 98312 | tf_op jit(solution)/shard_map/ppermute | solution.py:454
  13.6 6.6 %collective-permute-start.6 = (f32[4,2,2,16,128]{4,3,2,1,0:T(8,128)S(1)}, f32[4,2,2,16,128]{4,3,2,1,0:T(8,128)S(1)}, u32[]{:S(2)}, u32[]{:S(2)}) collective-permute-start(f32[4,2,2,16,128]{4,3,2,1,0:T(8,128)S(1)} %pad_maximum_fusion.mine_ref), channel_id=1, source_target_pairs={{0,4},{1,5},{2,6},{3,7},{4,0},{5,1},{6,2},{7,3},{8,12},{9,13},{10,... | collective-permute-start | bytes 393224 | tf_op jit(solution)/shard_map/ppermute | solution.py:356
  16.4 3.8 %collective-permute-start.5 = (f32[4,2,2,16,128]{4,3,2,1,0:T(8,128)S(1)}, f32[4,2,2,16,128]{4,3,2,1,0:T(8,128)S(1)}, u32[]{:S(2)}, u32[]{:S(2)}) collective-permute-start(f32[4,2,2,16,128]{4,3,2,1,0:T(8,128)S(1)} %pad_maximum_fusion.mine_ref), channel_id=1, source_target_pairs={{0,1},{1,0},{2,3},{3,2},{4,8},{5,9},{6,10},{7,11},{8,4},{9,5},{10,... | collective-permute-start | bytes 393224 | tf_op jit(solution)/shard_map/ppermute | solution.py:356

commit v9 on v8

--- a/solution.py
+++ b/solution.py
@@ -281,32 +281,12 @@
                 block[field, level] = part
 
 
-def image_products(
-    weight,
-    up_first_ref,
-    inside_ref,
-    final_ref,
-    mine_ref,
-    came_last_ref,
-    came_first_ref,
-    src_hbm,
-    rec_hbm,
-    image_hbm,
-    wide,
-    image_ref,
-    field_sems,
-    image_sems,
-):
-    shots, _, share, extent, across = mine_ref.shape
-    copies = []
-    for field, out in enumerate((src_hbm, rec_hbm)):
-        copies.append(
-            pltpu.make_async_copy(final_ref.at[field], out.at[0], field_sems.at[field])
-        )
-    for copy in copies:
-        copy.start()
-    up_first = jnp.concatenate([up_first_ref[...]] * (extent // 8), axis=0) != 0
-    inside = jnp.concatenate([inside_ref[...]] * (extent // 8), axis=0) != 0
+def widen(weight, masks, blocks, wide):
+    mine_ref, came_last_ref, came_first_ref = blocks
+    shots, _, share, extent, _ = mine_ref.shape
+    up_first, inside = (
+        jnp.concatenate([mask[...]] * (extent // 8), axis=0) != 0 for mask in masks
+    )
     for shot in range(shots):
         for field in range(2):
             for level in range(share):
@@ -320,20 +300,72 @@
                 wide[shot, field, level, 2 * extent : 3 * extent, :] = jnp.where(
                     up_first, first, last
                 )
+
+
+def offset_product(wide, offset, level, total):
+    extent = wide.shape[3] // 3
+    lower = extent + REACH - offset
+    upper = extent - REACH + offset
+    for shot in range(wide.shape[0]):
+        product = (
+            wide[shot, 0, level, lower : lower + extent, :]
+            * wide[shot, 1, level, upper : upper + extent, :]
+        )
+        total = product if total is None else total + product
+    return total
+
+
+def stack(count, *refs):
+    for place in range(count):
+        refs[-1][place] = refs[place][...]
+
+
+def own_products(
+    weight, up_first_ref, inside_ref, mine_ref, came_last_ref, came_first_ref, image_ref, wide
+):
+    widen(
+        weight, (up_first_ref, inside_ref), (mine_ref, came_last_ref, came_first_ref), wide
+    )
+    for offset in range(OFFS):
+        for level in range(wide.shape[2]):
+            image_ref[offset, level] = offset_product(wide, offset, level, None)
+
+
+def image_products(
+    weight,
+    up_first_ref,
+    inside_ref,
+    mine_ref,
+    came_last_ref,
+    came_first_ref,
+    before_ref,
+    final_ref,
+    src_hbm,
+    rec_hbm,
+    image_hbm,
+    wide,
+    image_ref,
+    field_sems,
+    image_sems,
+):
+    copies = []
+    for field, out in enumerate((src_hbm, rec_hbm)):
+        copies.append(
+            pltpu.make_async_copy(final_ref.at[field], out.at[0], field_sems.at[field])
+        )
+    for copy in copies:
+        copy.start()
+    widen(
+        weight, (up_first_ref, inside_ref), (mine_ref, came_last_ref, came_first_ref), wide
+    )
     parts = image_sems.shape[0]
     for piece in range(parts):
         offsets = range(piece * OFFS // parts, (piece + 1) * OFFS // parts)
         for offset in offsets:
-            for level in range(share):
-                total = jnp.zeros((extent, across), jnp.float32)
-                for shot in range(shots):
-                    lower = extent + REACH - offset
-                    upper = extent - REACH + offset
-                    total = total + (
-                        wide[shot, 0, level, lower : lower + extent, :]
-                        * wide[shot, 1, level, upper : upper + extent, :]
-                    )
-                image_ref[offset, level] = total
+            for level in range(wide.shape[2]):
+                image_ref[offset, level] = offset_product(
+                    wide, offset, level, before_ref[offset, level]
+                )
         rows = pl.ds(offsets[0], len(offsets))
         copy = pltpu.make_async_copy(image_ref.at[rows], image_hbm.at[rows], image_sems.at[piece])
         copy.start()
@@ -454,26 +486,54 @@
         lax.ppermute(sent, "shot", [(shot, shot ^ (1 + i)) for shot in range(shots)])
         for i, sent in enumerate(blocks)
     ]
-    mine = jnp.stack([own_block, *came])
+    weight = 1.0 / shots
+    image_shape = (OFFS, share, extent, across)
+
+    def wide_scratch(blocks):
+        return scratch(blocks.shape[0], 2, share, 3 * extent, across)
+
+    mine = own_block[None]
     fields_first, fields_last = swap_sides(mine, mine)
+    others = pl.pallas_call(
+        functools.partial(stack, len(came)),
+        out_shape=struct(len(came), *own_block.shape),
+        in_specs=[VMEM] * (len(came) + 2),
+        out_specs=VMEM,
+        compiler_params=params,
+        name="stack",
+    )(*came, fields_last, fields_first)
+    products = OFFS * share * extent * across
+    before = pl.pallas_call(
+        functools.partial(own_products, weight),
+        out_shape=struct(*image_shape),
+        in_specs=[VMEM] * 5,
+        out_specs=VMEM,
+        scratch_shapes=[wide_scratch(mine)],
+        compiler_params=params,
+        cost_estimate=pl.CostEstimate(
+            flops=2 * products, bytes_accessed=8 * products, transcendentals=0
+        ),
+        name="own_products",
+    )(up_first, inside, mine, fields_last, fields_first)
+    fields_first, fields_last = swap_sides(others, others)
     return pl.pallas_call(
-        functools.partial(image_products, 1.0 / shots),
+        functools.partial(image_products, weight),
         out_shape=(
             struct(1, levels, extent, across),
             struct(1, levels, extent, across),
-            struct(OFFS, share, extent, across),
+            struct(*image_shape),
         ),
-        in_specs=[VMEM] * 6,
+        in_specs=[VMEM] * 7,
         out_specs=[HBM] * 3,
         scratch_shapes=[
-            scratch(shots, 2, share, 3 * extent, across),
-            scratch(OFFS, share, extent, across),
+            wide_scratch(others),
+            scratch(*image_shape),
             pltpu.SemaphoreType.DMA((2,)),
             pltpu.SemaphoreType.DMA((3,)),
         ],
         compiler_params=params,
         name="image_products",
-    )(up_first, inside, final, mine, fields_last, fields_first)
+    )(up_first, inside, others, fields_last, fields_first, before, final)
 
 
 def solution(mesh):

time: 21.3 us -> 21.1 us (level)
  waiting for transfers between devices: 8.8 us -> 6.2 us
  starting transfers between devices: 7.98 us -> 10.3 us
    ppermute x3, waiting for transfers between devices: 3.27 us -> 0.27 us  [per_device(): lax.ppermute(sent, 'shot', [(shot, shot ^ 1 + i) for shot in range(shots)])]
    ppermute x4 -> x6, starting transfers between devices: 5.86 us -> 8.18 us  [swap(): return lax.ppermute(value, ('tile', 'shot'), pairs)]
    ppermute x4 -> x6, waiting for transfers between devices: 5.53 us -> 5.93 us  [swap(): return lax.ppermute(value, ('tile', 'shot'), pairs)]
    pallas_call x1 -> x3, Pallas kernels: 0.93 us -> 1.01 us  [the longest x1 0.95 us: per_device(): pl.pallas_call(functools.partial(image_products, weight), out_shape=(stru...]
  transfers between devices with their start and end apart: 7 -> 9, of which waited for: 4 -> 4; matrix products, arithmetic and copies ran while one was open for 0% -> 0% of each run, Pallas kernels for 0% -> 1%
where the time goes in v9:
time: 21.1 us; the launch traced here: 20.9 us
  starting transfers between devices  10.3 us (49%)
  waiting for transfers between devices  6.2 us (29%)
  Pallas kernels  3.09 us (15%)
  between operations  1.33 us (6%)
    ppermute x6, starting transfers between devices, swap(): return lax.ppermute(value, ('tile', 'shot'), pairs)  8.18 us
    ppermute x6, waiting for transfers between devices, swap(): return lax.ppermute(value, ('tile', 'shot'), pairs)  5.93 us
    ppermute x3, starting transfers between devices, per_device(): lax.ppermute(sent, 'shot', [(shot, shot ^ 1 + i) for shot in range(shots)])  2.12 us
    pallas_call x1, Pallas kernels, per_device(): pl.pallas_call(own_part, out_shape=(struct(*wavelet.shape), struct(*wide_...  1.59 us
    pallas_call x1, Pallas kernels, per_device(): pl.pallas_call(functools.partial(image_products, weight), out_shape=(stru...  0.95 us
  transfers between devices with their start and end apart: 9, of which 4 were waited for; matrix products, arithmetic and copies ran while one was open for 0% of the time, Pallas kernels for 1%

profile of v9, /device:TPU:0, one launch (start us, length us, event | category | flops | bytes accessed | tf_op | source)
XLA Modules:
  0.0 20.9 jit_solution(1824994970665086685)
XLA Ops:
  0.6 1.6 %own_part.1 = (f32[1,2]{1,0:T(1,128)S(1)}, f32[2,8,32,128]{3,2,1,0:T(8,128)S(1)}, f32[2,8,16,128]{3,2,1,0:T(8,128)S(1)}, f32[2,8,16,128]{3,2,1,0:T(8,128)S(1)}, ...) custom-call(f32[1,16]{1,0:T(1,128)} %bitcast.5, s32[1,32]{1,0:T(1,128)} %spots_hbm.1, ...), custom_call_target="tpu_custom_call" | custom-call | tf_op jit(solution)/shard_map/own_part/pallas_call | solution.py:421
  2.2 3.1 %collective-permute-start = (f32[20,8,128]{2,1,0:T(8,128)S(1)}, f32[20,8,128]{2,1,0:T(8,128)S(1)}, u32[]{:S(2)}, u32[]{:S(2)}) collective-permute-start(f32[20,8,128]{2,1,0:T(8,128)S(1)} %get-tuple-element.30), channel_id=1, source_target_pairs={{0,4},{1,5},{2,6},{3,7},{4,0},{5,1},{6,2},{7,3},{8,12},{9,13},{10,... | collective-permute-start | bytes 245768 | tf_op jit(solution)/shard_map/ppermute | solution.py:388
  5.3 0.0 collective-permute-start.1
  6.0 0.1 source_and_order.1
  6.1 1.7 %collective-permute-done.came_first_ref = f32[20,8,128]{2,1,0:T(8,128)S(1)} collective-permute-done((f32[20,8,128]{2,1,0:T(8,128)S(1)}, f32[20,8,128]{2,1,0:T(8,128)S(1)}, u32[]{:S(2)}, u32[]{:S(2)}) %collective-permute-start) | collective-permute-done | bytes 81952 | tf_op jit(solution)/shard_map/ppermute | solution.py:388
  7.8 0.0 collective-permute-done.1.came_last_ref
  7.8 0.4 %both_steps.1 = (f32[2,8,16,128]{3,2,1,0:T(8,128)S(1)}, f32[2,2,16,128]{3,2,1,0:T(8,128)S(1)}, f32[2,2,16,128]{3,2,1,0:T(8,128)S(1)}, f32[2,2,16,128]{3,2,1,0:T(8,128)S(1)}, f32[2,2,16,128]{3,2,1,0:T(8,128)S(1)}) custom-call(s32[8,128]{1,0:T(8,128)S(1)} %get-tuple-element.22.up_first_ref, s32[8,128]{1,0:T(8,128)S(1)} %get-tuple-element.23.inside_ref, ...), custom_call_target="tpu_custom_call" | custom-call | tf_op jit(solution)/shard_map/both_steps/pallas_call | solution.py:476
  8.2 0.1 collective-permute-start.2
  8.3 2.0 %collective-permute-start.3 = (f32[2,2,16,128]{3,2,1,0:T(8,128)S(1)}, f32[2,2,16,128]{3,2,1,0:T(8,128)S(1)}, u32[]{:S(2)}, u32[]{:S(2)}) collective-permute-start(f32[2,2,16,128]{3,2,1,0:T(8,128)S(1)} %get-tuple-element.33), channel_id=1, source_target_pairs={{0,2},{1,3},{2,0},{3,1},{4,6},{5,7},{6,4},{7,5},{8,10},{9,11},{10,... | collective-permute-start | bytes 98312 | tf_op jit(solution)/shard_map/ppermute | solution.py:486
  10.2 0.1 collective-permute-start.4
  10.3 2.9 %collective-permute-start.6 = (f32[1,2,2,16,128]{4,3,2,1,0:T(8,128)S(1)}, f32[1,2,2,16,128]{4,3,2,1,0:T(8,128)S(1)}, u32[]{:S(2)}, u32[]{:S(2)}) collective-permute-start(f32[1,2,2,16,128]{4,3,2,1,0:T(8,128)S(1)} %bitcast.2), channel_id=1, source_target_pairs={{0,4},{1,5},{2,6},{3,7},{4,0},{5,1},{6,2},{7,3},{8,12},{9,13},{10,... | collective-permute-start | bytes 98312 | tf_op jit(solution)/shard_map/ppermute | solution.py:388
  13.2 0.1 collective-permute-start.5
  13.3 0.0 collective-permute-done.2.refs_0_
  13.3 0.0 collective-permute-done.3.refs_1_
  13.3 0.3 %collective-permute-done.4.refs_2_ = f32[2,2,16,128]{3,2,1,0:T(8,128)S(1)} collective-permute-done((f32[2,2,16,128]{3,2,1,0:T(8,128)S(1)}, f32[2,2,16,128]{3,2,1,0:T(8,128)S(1)}, u32[]{:S(2)}, u32[]{:S(2)}) %collective-permute-start.4) | collective-permute-done | bytes 32800 | tf_op jit(solution)/shard_map/ppermute | solution.py:486
  13.6 1.6 %collective-permute-done.6.refs_4_.came_first_ref = f32[1,2,2,16,128]{4,3,2,1,0:T(8,128)S(1)} collective-permute-done((f32[1,2,2,16,128]{4,3,2,1,0:T(8,128)S(1)}, f32[1,2,2,16,128]{4,3,2,1,0:T(8,128)S(1)}, u32[]{:S(2)}, u32[]{:S(2)}) %collective-permute-start.6) | collective-permute-done | bytes 32800 | tf_op jit(solution)/shard_map/ppermute | solution.py:388
  15.1 0.0 collective-permute-done.5.refs_3_.came_last_ref
  15.1 2.1 %collective-permute-start.8 = (f32[3,2,2,16,128]{4,3,2,1,0:T(8,128)S(1)}, f32[3,2,2,16,128]{4,3,2,1,0:T(8,128)S(1)}, u32[]{:S(2)}, u32[]{:S(2)}) collective-permute-start(f32[3,2,2,16,128]{4,3,2,1,0:T(8,128)S(1)} %stack.1.mine_ref), channel_id=1, source_target_pairs={{0,4},{1,5},{2,6},{3,7},{4,0},{5,1},{6,2},{7,3},{8,12},{9,13},{10,... | collective-permute-start | bytes 294920 | tf_op jit(solution)/shard_map/ppermute | solution.py:388
  17.2 0.0 collective-permute-start.7
  17.2 0.1 own_products.1.before_ref
  17.3 2.7 %collective-permute-done.8.came_first_ref = f32[3,2,2,16,128]{4,3,2,1,0:T(8,128)S(1)} collective-permute-done((f32[3,2,2,16,128]{4,3,2,1,0:T(8,128)S(1)}, f32[3,2,2,16,128]{4,3,2,1,0:T(8,128)S(1)}, u32[]{:S(2)}, u32[]{:S(2)}) %collective-permute-start.8) | collective-permute-done | bytes 98336 | tf_op jit(solution)/shard_map/ppermute | solution.py:388
  20.0 0.0 collective-permute-done.7.came_last_ref
  20.0 1.0 %image_products.1 = (f32[1,8,16,128]{3,2,1,0:T(8,128)}, f32[1,8,16,128]{3,2,1,0:T(8,128)}, f32[33,2,16,128]{3,2,1,0:T(8,128)}) custom-call(s32[8,128]{1,0:T(8,128)S(1)} %get-tuple-element.22.up_first_ref, s32[8,128]{1,0:T(8,128)S(1)} %get-tuple-element.23.inside_ref, f32[3,2,2,16,128]{4,3,2,1,0:T(8,128)S(1)} %stack.1.mine_ref, ...), custom_call_target="tpu_custom_call" | custom-call | tf_op jit(solution)/shard_map/image_products/pallas_call | solution.py:519
  (1 shorter events, 0.0 us)
Async XLA Ops:
  2.2 5.5 %collective-permute-start = (f32[20,8,128]{2,1,0:T(8,128)S(1)}, f32[20,8,128]{2,1,0:T(8,128)S(1)}, u32[]{:S(2)}, u32[]{:S(2)}) collective-permute-start(f32[20,8,128]{2,1,0:T(8,128)S(1)} %get-tuple-element.30), channel_id=1, source_target_pairs={{0,4},{1,5},{2,6},{3,7},{4,0},{5,1},{6,2},{7,3},{8,12},{9,13},{10,... | collective-permute-start | bytes 245768 | tf_op jit(solution)/shard_map/ppermute | solution.py:388
  5.3 2.4 %collective-permute-start.1 = (f32[20,8,128]{2,1,0:T(8,128)S(1)}, f32[20,8,128]{2,1,0:T(8,128)S(1)}, u32[]{:S(2)}, u32[]{:S(2)}) collective-permute-start(f32[20,8,128]{2,1,0:T(8,128)S(1)} %get-tuple-element.31), channel_id=1, source_target_pairs={{0,1},{1,0},{2,3},{3,2},{4,8},{5,9},{6,10},{7,11},{8,4},{9,5},{10,... | collective-permute-start | bytes 245768 | tf_op jit(solution)/shard_map/ppermute | solution.py:388
  8.2 5.1 %collective-permute-start.2 = (f32[2,2,16,128]{3,2,1,0:T(8,128)S(1)}, f32[2,2,16,128]{3,2,1,0:T(8,128)S(1)}, u32[]{:S(2)}, u32[]{:S(2)}) collective-permute-start(f32[2,2,16,128]{3,2,1,0:T(8,128)S(1)} %get-tuple-element.32), channel_id=1, source_target_pairs={{0,1},{1,0},{2,3},{3,2},{4,5},{5,4},{6,7},{7,6},{8,9},{9,8},{10,11... | collective-permute-start | bytes 98312 | tf_op jit(solution)/shard_map/ppermute | solution.py:486
  8.3 5.1 %collective-permute-start.3 = (f32[2,2,16,128]{3,2,1,0:T(8,128)S(1)}, f32[2,2,16,128]{3,2,1,0:T(8,128)S(1)}, u32[]{:S(2)}, u32[]{:S(2)}) collective-permute-start(f32[2,2,16,128]{3,2,1,0:T(8,128)S(1)} %get-tuple-element.33), channel_id=1, source_target_pairs={{0,2},{1,3},{2,0},{3,1},{4,6},{5,7},{6,4},{7,5},{8,10},{9,11},{10,... | collective-permute-start | bytes 98312 | tf_op jit(solution)/shard_map/ppermute | solution.py:486
  10.2 3.3 %collective-permute-start.4 = (f32[2,2,16,128]{3,2,1,0:T(8,128)S(1)}, f32[2,2,16,128]{3,2,1,0:T(8,128)S(1)}, u32[]{:S(2)}, u32[]{:S(2)}) collective-permute-start(f32[2,2,16,128]{3,2,1,0:T(8,128)S(1)} %get-tuple-element.34), channel_id=1, source_target_pairs={{0,3},{1,2},{2,1},{3,0},{4,7},{5,6},{6,5},{7,4},{8,11},{9,10},{10,... | collective-permute-start | bytes 98312 | tf_op jit(solution)/shard_map/ppermute | solution.py:486
  10.3 4.8 %collective-permute-start.6 = (f32[1,2,2,16,128]{4,3,2,1,0:T(8,128)S(1)}, f32[1,2,2,16,128]{4,3,2,1,0:T(8,128)S(1)}, u32[]{:S(2)}, u32[]{:S(2)}) collective-permute-start(f32[1,2,2,16,128]{4,3,2,1,0:T(8,128)S(1)} %bitcast.2), channel_id=1, source_target_pairs={{0,4},{1,5},{2,6},{3,7},{4,0},{5,1},{6,2},{7,3},{8,12},{9,13},{10,... | collective-permute-start | bytes 98312 | tf_op jit(solution)/shard_map/ppermute | solution.py:388
  13.2 1.9 %collective-permute-start.5 = (f32[1,2,2,16,128]{4,3,2,1,0:T(8,128)S(1)}, f32[1,2,2,16,128]{4,3,2,1,0:T(8,128)S(1)}, u32[]{:S(2)}, u32[]{:S(2)}) collective-permute-start(f32[1,2,2,16,128]{4,3,2,1,0:T(8,128)S(1)} %bitcast.3), channel_id=1, source_target_pairs={{0,1},{1,0},{2,3},{3,2},{4,8},{5,9},{6,10},{7,11},{8,4},{9,5},{10,... | collective-permute-start | bytes 98312 | tf_op jit(solution)/shard_map/ppermute | solution.py:388
  15.1 4.8 %collective-permute-start.8 = (f32[3,2,2,16,128]{4,3,2,1,0:T(8,128)S(1)}, f32[3,2,2,16,128]{4,3,2,1,0:T(8,128)S(1)}, u32[]{:S(2)}, u32[]{:S(2)}) collective-permute-start(f32[3,2,2,16,128]{4,3,2,1,0:T(8,128)S(1)} %stack.1.mine_ref), channel_id=1, source_target_pairs={{0,4},{1,5},{2,6},{3,7},{4,0},{5,1},{6,2},{7,3},{8,12},{9,13},{10,... | collective-permute-start | bytes 294920 | tf_op jit(solution)/shard_map/ppermute | solution.py:388
  17.2 2.7 %collective-permute-start.7 = (f32[3,2,2,16,128]{4,3,2,1,0:T(8,128)S(1)}, f32[3,2,2,16,128]{4,3,2,1,0:T(8,128)S(1)}, u32[]{:S(2)}, u32[]{:S(2)}) collective-permute-start(f32[3,2,2,16,128]{4,3,2,1,0:T(8,128)S(1)} %stack.1.mine_ref), channel_id=1, source_target_pairs={{0,1},{1,0},{2,3},{3,2},{4,8},{5,9},{6,10},{7,11},{8,4},{9,5},{10,... | collective-permute-start | bytes 294920 | tf_op jit(solution)/shard_map/ppermute | solution.py:388

commit v10 on v9

--- a/solution.py
+++ b/solution.py
@@ -108,17 +108,18 @@
     shape = (extent, across)
     regions = table_hbm.shape[1]
     end = LEAD + extent
-    moves = (
-        (table_hbm, table),
-        (ids_hbm, ids_ref),
-        (spots_hbm, spots_ref),
-        (traces_hbm, traces_ref),
-        (src_now.at[0], wide.at[0, :, pl.ds(LEAD, extent), :]),
-        (src_prev.at[0], prev_ref.at[0]),
-        (rec_now.at[0], wide.at[1, :, pl.ds(LEAD, extent), :]),
-        (rec_prev.at[0], prev_ref.at[1]),
-        (amps_hbm, amps_ref),
-    )
+    rows = pl.ds(LEAD, extent)
+    moves = [(table_hbm, table), (spots_hbm, spots_ref), (traces_hbm, traces_ref)]
+    for begin in range(0, levels, levels // 2):
+        part = pl.ds(begin, levels // 2)
+        moves += [
+            (src_now.at[0, part], wide.at[0, part, rows, :]),
+            (rec_now.at[0, part], wide.at[1, part, rows, :]),
+            (ids_hbm.at[part], ids_ref.at[part]),
+            (src_prev.at[0, part], prev_ref.at[0, part]),
+            (rec_prev.at[0, part], prev_ref.at[1, part]),
+        ]
+    moves.append((amps_hbm, amps_ref))
     copies = [
         pltpu.make_async_copy(here, there, sems.at[i]) for i, (here, there) in enumerate(moves)
     ]
@@ -130,9 +131,16 @@
             wide[field, level, 0:LEAD, :] = zeros
             wide[field, level, end : end + LEAD, :] = zeros
     weights = lane_weights(shape)
-
-    for copy in copies[2:4]:
+    up_first = goes_up_first()
+    for copy in copies:
         copy.wait()
+
+    def send(place, rows, value):
+        low = value[0:HALO, :]
+        high = value[extent - HALO : extent, :]
+        sent_first_ref[place, rows, :] = jnp.where(up_first, high, low)
+        sent_last_ref[place, rows, :] = jnp.where(up_first, low, high)
+
     spots = spots_ref[...]
     column = lax.broadcasted_iota(jnp.int32, (extent, spots.shape[1]), 0) * across
     in_column = (spots >= column) & (spots < column + across)
@@ -149,16 +157,6 @@
         preferred_element_type=jnp.float32,
     )
 
-    up_first = goes_up_first()
-
-    def send(place, rows, value):
-        low = value[0:HALO, :]
-        high = value[extent - HALO : extent, :]
-        sent_first_ref[place, rows, :] = jnp.where(up_first, high, low)
-        sent_last_ref[place, rows, :] = jnp.where(up_first, low, high)
-
-    copies[0].wait()
-    copies[1].wait()
     speeds = jnp.concatenate(
         [table[...], jnp.zeros((1, across - regions), jnp.float32)], axis=1
     )
@@ -172,8 +170,6 @@
         send(2 * levels + level // 2, pl.ds(level % 2 * HALO, HALO), coef_ref[level])
 
     for field in range(2):
-        copies[4 + 2 * field].wait()
-        copies[5 + 2 * field].wait()
         for level in range(levels):
             total = laplace_level(wide, field, level, levels, extent, weights)
             now = wide[field, level, LEAD:end, :]
@@ -187,7 +183,6 @@
             place = field * levels + level
             send(place, pl.ds(0, HALO), now)
             send(place, pl.ds(HALO, HALO), value)
-    copies[8].wait()
 
 
 def both_steps(
@@ -200,8 +195,8 @@
     source_ref,
     source_later_ref,
     coef_ref,
+    came_last_ref,
     came_first_ref,
-    came_last_ref,
     final_ref,
     mine_ref,
     *rest,
@@ -321,14 +316,33 @@
 
 
 def own_products(
-    weight, up_first_ref, inside_ref, mine_ref, came_last_ref, came_first_ref, image_ref, wide
+    weight,
+    up_first_ref,
+    inside_ref,
+    mine_ref,
+    came_last_ref,
+    came_first_ref,
+    final_ref,
+    src_hbm,
+    rec_hbm,
+    image_ref,
+    wide,
+    sems,
 ):
+    copies = [
+        pltpu.make_async_copy(final_ref.at[field], out.at[0], sems.at[field])
+        for field, out in enumerate((src_hbm, rec_hbm))
+    ]
+    for copy in copies:
+        copy.start()
     widen(
         weight, (up_first_ref, inside_ref), (mine_ref, came_last_ref, came_first_ref), wide
     )
     for offset in range(OFFS):
         for level in range(wide.shape[2]):
             image_ref[offset, level] = offset_product(wide, offset, level, None)
+    for copy in copies:
+        copy.wait()
 
 
 def image_products(
@@ -339,26 +353,16 @@
     came_last_ref,
     came_first_ref,
     before_ref,
-    final_ref,
-    src_hbm,
-    rec_hbm,
     image_hbm,
     wide,
     image_ref,
-    field_sems,
-    image_sems,
+    sems,
 ):
-    copies = []
-    for field, out in enumerate((src_hbm, rec_hbm)):
-        copies.append(
-            pltpu.make_async_copy(final_ref.at[field], out.at[0], field_sems.at[field])
-        )
-    for copy in copies:
-        copy.start()
     widen(
         weight, (up_first_ref, inside_ref), (mine_ref, came_last_ref, came_first_ref), wide
     )
-    parts = image_sems.shape[0]
+    parts = sems.shape[0]
+    copies = []
     for piece in range(parts):
         offsets = range(piece * OFFS // parts, (piece + 1) * OFFS // parts)
         for offset in offsets:
@@ -367,7 +371,7 @@
                     wide, offset, level, before_ref[offset, level]
                 )
         rows = pl.ds(offsets[0], len(offsets))
-        copy = pltpu.make_async_copy(image_ref.at[rows], image_hbm.at[rows], image_sems.at[piece])
+        copy = pltpu.make_async_copy(image_ref.at[rows], image_hbm.at[rows], sems.at[piece])
         copy.start()
         copies.append(copy)
     for copy in copies:
@@ -437,7 +441,7 @@
             scratch(*receiver_data.shape),
             scratch(levels, extent, across, dtype=jnp.int32),
             scratch(2, levels, extent, across),
-            pltpu.SemaphoreType.DMA((9,)),
+            pltpu.SemaphoreType.DMA((14,)),
         ],
         compiler_params=params,
         name="own_part",
@@ -481,7 +485,7 @@
         scratch_shapes=[scratch(*wide_shape), scratch(*wide_shape)],
         compiler_params=params,
         name="both_steps",
-    )(up_first, inside, bits, own, part, later, source, source_later, coef, came_first, came_last)
+    )(up_first, inside, bits, own, part, later, source, source_later, coef, came_last, came_first)
     came = [
         lax.ppermute(sent, "shot", [(shot, shot ^ (1 + i)) for shot in range(shots)])
         for i, sent in enumerate(blocks)
@@ -503,37 +507,37 @@
         name="stack",
     )(*came, fields_last, fields_first)
     products = OFFS * share * extent * across
-    before = pl.pallas_call(
+    src_next, rec_next, before = pl.pallas_call(
         functools.partial(own_products, weight),
-        out_shape=struct(*image_shape),
-        in_specs=[VMEM] * 5,
-        out_specs=VMEM,
-        scratch_shapes=[wide_scratch(mine)],
+        out_shape=(
+            struct(1, levels, extent, across),
+            struct(1, levels, extent, across),
+            struct(*image_shape),
+        ),
+        in_specs=[VMEM] * 6,
+        out_specs=[HBM, HBM, VMEM],
+        scratch_shapes=[wide_scratch(mine), pltpu.SemaphoreType.DMA((2,))],
         compiler_params=params,
         cost_estimate=pl.CostEstimate(
             flops=2 * products, bytes_accessed=8 * products, transcendentals=0
         ),
         name="own_products",
-    )(up_first, inside, mine, fields_last, fields_first)
+    )(up_first, inside, mine, fields_last, fields_first, final)
     fields_first, fields_last = swap_sides(others, others)
-    return pl.pallas_call(
+    image = pl.pallas_call(
         functools.partial(image_products, weight),
-        out_shape=(
-            struct(1, levels, extent, across),
-            struct(1, levels, extent, across),
-            struct(*image_shape),
-        ),
-        in_specs=[VMEM] * 7,
-        out_specs=[HBM] * 3,
+        out_shape=struct(*image_shape),
+        in_specs=[VMEM] * 6,
+        out_specs=HBM,
         scratch_shapes=[
             wide_scratch(others),
             scratch(*image_shape),
-            pltpu.SemaphoreType.DMA((2,)),
-            pltpu.SemaphoreType.DMA((3,)),
+            pltpu.SemaphoreType.DMA((11,)),
         ],
         compiler_params=params,
         name="image_products",
-    )(up_first, inside, others, fields_last, fields_first, before, final)
+    )(up_first, inside, others, fields_last, fields_first, before)
+    return src_next, rec_next, image
 
 
 def solution(mesh):

time: 21.1 us -> 23.2 us (1.100)
  waiting for transfers between devices: 6.2 us -> 8.03 us
  Pallas kernels: 3.09 us -> 3.59 us
    ppermute x3, waiting for transfers between devices: 0.27 us -> 3.57 us  [per_device(): lax.ppermute(sent, 'shot', [(shot, shot ^ 1 + i) for shot in range(shots)])]
    ppermute x6, waiting for transfers between devices: 5.93 us -> 4.46 us  [swap(): return lax.ppermute(value, ('tile', 'shot'), pairs)]
    pallas_call x2, Pallas kernels: 1 us -> 1.63 us  [the longest x1 0.96 us: per_device(): pl.pallas_call(functools.partial(image_products, weight), out_shape=struc...]
  transfers between devices with their start and end apart: 9 -> 9, of which waited for: 4 -> 4; matrix products, arithmetic and copies ran while one was open for 0% -> 0% of each run, Pallas kernels for 1% -> 3%
where the time goes in v10:
time: 23.2 us; the launch traced here: 23 us
  starting transfers between devices  10.1 us (44%)
  waiting for transfers between devices  8.03 us (35%)
  Pallas kernels  3.59 us (15%)
  between operations  1.34 us (6%)
    ppermute x6, starting transfers between devices, swap(): return lax.ppermute(value, ('tile', 'shot'), pairs)  8.07 us
    ppermute x6, waiting for transfers between devices, swap(): return lax.ppermute(value, ('tile', 'shot'), pairs)  4.46 us
    ppermute x3, waiting for transfers between devices, per_device(): lax.ppermute(sent, 'shot', [(shot, shot ^ 1 + i) for shot in range(shots)])  3.57 us
    ppermute x3, starting transfers between devices, per_device(): lax.ppermute(sent, 'shot', [(shot, shot ^ 1 + i) for shot in range(shots)])  2 us
    pallas_call x1, Pallas kernels, per_device(): pl.pallas_call(own_part, out_shape=(struct(*wavelet.shape), struct(*wide_...  1.46 us
    pallas_call x1, Pallas kernels, per_device(): pl.pallas_call(functools.partial(image_products, weight), out_shape=struc...  0.96 us
    pallas_call x1, Pallas kernels, per_device(): pl.pallas_call(functools.partial(own_products, weight), out_shape=(struct...  0.67 us
  transfers between devices with their start and end apart: 9, of which 4 were waited for; matrix products, arithmetic and copies ran while one was open for 0% of the time, Pallas kernels for 3%

profile of v10, /device:TPU:0, one launch (start us, length us, event | category | flops | bytes accessed | tf_op | source)
XLA Modules:
  0.0 23.0 jit_solution(12098127707629602803)
XLA Ops:
  0.6 1.5 %own_part.1 = (f32[1,2]{1,0:T(1,128)S(1)}, f32[2,8,32,128]{3,2,1,0:T(8,128)S(1)}, f32[2,8,16,128]{3,2,1,0:T(8,128)S(1)}, f32[2,8,16,128]{3,2,1,0:T(8,128)S(1)}, ...) custom-call(f32[1,16]{1,0:T(1,128)} %bitcast.5, s32[1,32]{1,0:T(1,128)} %spots_hbm.1, ...), custom_call_target="tpu_custom_call" | custom-call | tf_op jit(solution)/shard_map/own_part/pallas_call | solution.py:425
  2.1 0.5 %collective-permute-start = (f32[20,8,128]{2,1,0:T(8,128)S(1)}, f32[20,8,128]{2,1,0:T(8,128)S(1)}, u32[]{:S(2)}, u32[]{:S(2)}) collective-permute-start(f32[20,8,128]{2,1,0:T(8,128)S(1)} %get-tuple-element.33), channel_id=1, source_target_pairs={{0,1},{1,0},{2,3},{3,2},{4,8},{5,9},{6,10},{7,11},{8,4},{9,5},{10,... | collective-permute-start | bytes 245768 | tf_op jit(solution)/shard_map/ppermute | solution.py:392
  2.6 4.1 %collective-permute-start.1 = (f32[20,8,128]{2,1,0:T(8,128)S(1)}, f32[20,8,128]{2,1,0:T(8,128)S(1)}, u32[]{:S(2)}, u32[]{:S(2)}) collective-permute-start(f32[20,8,128]{2,1,0:T(8,128)S(1)} %get-tuple-element.34), channel_id=1, source_target_pairs={{0,4},{1,5},{2,6},{3,7},{4,0},{5,1},{6,2},{7,3},{8,12},{9,13},{10,... | collective-permute-start | bytes 245768 | tf_op jit(solution)/shard_map/ppermute | solution.py:392
  7.4 0.1 source_and_order.1
  7.5 0.0 collective-permute-done.came_last_ref
  7.5 1.7 %collective-permute-done.1.came_first_ref = f32[20,8,128]{2,1,0:T(8,128)S(1)} collective-permute-done((f32[20,8,128]{2,1,0:T(8,128)S(1)}, f32[20,8,128]{2,1,0:T(8,128)S(1)}, u32[]{:S(2)}, u32[]{:S(2)}) %collective-permute-start.1) | collective-permute-done | bytes 81952 | tf_op jit(solution)/shard_map/ppermute | solution.py:392
  9.2 0.4 %both_steps.1 = (f32[2,8,16,128]{3,2,1,0:T(8,128)S(1)}, f32[2,2,16,128]{3,2,1,0:T(8,128)S(1)}, f32[2,2,16,128]{3,2,1,0:T(8,128)S(1)}, f32[2,2,16,128]{3,2,1,0:T(8,128)S(1)}, f32[2,2,16,128]{3,2,1,0:T(8,128)S(1)}) custom-call(s32[8,128]{1,0:T(8,128)S(1)} %get-tuple-element.25.up_first_ref, s32[8,128]{1,0:T(8,128)S(1)} %get-tuple-element.26.inside_ref, ...), custom_call_target="tpu_custom_call" | custom-call | tf_op jit(solution)/shard_map/both_steps/pallas_call | solution.py:480
  9.6 2.1 %collective-permute-start.3 = (f32[1,2,2,16,128]{4,3,2,1,0:T(8,128)S(1)}, f32[1,2,2,16,128]{4,3,2,1,0:T(8,128)S(1)}, u32[]{:S(2)}, u32[]{:S(2)}) collective-permute-start(f32[1,2,2,16,128]{4,3,2,1,0:T(8,128)S(1)} %bitcast.2), channel_id=1, source_target_pairs={{0,4},{1,5},{2,6},{3,7},{4,0},{5,1},{6,2},{7,3},{8,12},{9,13},{10,... | collective-permute-start | bytes 98312 | tf_op jit(solution)/shard_map/ppermute | solution.py:392
  11.7 0.0 collective-permute-start.2
  11.7 0.5 %collective-permute-start.4 = (f32[2,2,16,128]{3,2,1,0:T(8,128)S(1)}, f32[2,2,16,128]{3,2,1,0:T(8,128)S(1)}, u32[]{:S(2)}, u32[]{:S(2)}) collective-permute-start(f32[2,2,16,128]{3,2,1,0:T(8,128)S(1)} %get-tuple-element.39), channel_id=1, source_target_pairs={{0,1},{1,0},{2,3},{3,2},{4,5},{5,4},{6,7},{7,6},{8,9},{9,8},{10,11... | collective-permute-start | bytes 98312 | tf_op jit(solution)/shard_map/ppermute | solution.py:490
  12.2 1.5 %collective-permute-start.5 = (f32[2,2,16,128]{3,2,1,0:T(8,128)S(1)}, f32[2,2,16,128]{3,2,1,0:T(8,128)S(1)}, u32[]{:S(2)}, u32[]{:S(2)}) collective-permute-start(f32[2,2,16,128]{3,2,1,0:T(8,128)S(1)} %get-tuple-element.40), channel_id=1, source_target_pairs={{0,2},{1,3},{2,0},{3,1},{4,6},{5,7},{6,4},{7,5},{8,10},{9,11},{10,... | collective-permute-start | bytes 98312 | tf_op jit(solution)/shard_map/ppermute | solution.py:490
  13.7 0.0 collective-permute-start.6
  13.7 0.0 collective-permute-done.3.came_first_ref.refs_4_
  13.7 0.0 collective-permute-done.2.came_last_ref.refs_3_
  13.7 0.0 collective-permute-done.4.refs_0_
  13.7 2.4 %collective-permute-done.5.refs_1_ = f32[2,2,16,128]{3,2,1,0:T(8,128)S(1)} collective-permute-done((f32[2,2,16,128]{3,2,1,0:T(8,128)S(1)}, f32[2,2,16,128]{3,2,1,0:T(8,128)S(1)}, u32[]{:S(2)}, u32[]{:S(2)}) %collective-permute-start.5) | collective-permute-done | bytes 32800 | tf_op jit(solution)/shard_map/ppermute | solution.py:490
  16.1 1.2 %collective-permute-done.6.refs_2_ = f32[2,2,16,128]{3,2,1,0:T(8,128)S(1)} collective-permute-done((f32[2,2,16,128]{3,2,1,0:T(8,128)S(1)}, f32[2,2,16,128]{3,2,1,0:T(8,128)S(1)}, u32[]{:S(2)}, u32[]{:S(2)}) %collective-permute-start.6) | collective-permute-done | bytes 32800 | tf_op jit(solution)/shard_map/ppermute | solution.py:490
  17.3 1.3 %collective-permute-start.8 = (f32[3,2,2,16,128]{4,3,2,1,0:T(8,128)S(1)}, f32[3,2,2,16,128]{4,3,2,1,0:T(8,128)S(1)}, u32[]{:S(2)}, u32[]{:S(2)}) collective-permute-start(f32[3,2,2,16,128]{4,3,2,1,0:T(8,128)S(1)} %stack.1.mine_ref), channel_id=1, source_target_pairs={{0,4},{1,5},{2,6},{3,7},{4,0},{5,1},{6,2},{7,3},{8,12},{9,13},{10,... | collective-permute-start | bytes 294920 | tf_op jit(solution)/shard_map/ppermute | solution.py:392
  18.6 0.0 collective-permute-start.7
  18.6 0.7 %own_products.1 = (f32[1,8,16,128]{3,2,1,0:T(8,128)}, f32[1,8,16,128]{3,2,1,0:T(8,128)}, f32[33,2,16,128]{3,2,1,0:T(8,128)S(1)}) custom-call(s32[8,128]{1,0:T(8,128)S(1)} %get-tuple-element.25.up_first_ref, s32[8,128]{1,0:T(8,128)S(1)} %get-tuple-element.26.inside_ref, f32[1,2,2,16,128]{4,3,2,1,0:T(8,128)S(1)} %bitcast.4, ...), custom_call_target="tpu_custom_call" | custom-call | flops 270336 | bytes 1081344 | tf_op jit(solution)/shard_map/own_products/pallas_call | solution.py:510
  19.3 2.8 %collective-permute-done.8.came_first_ref = f32[3,2,2,16,128]{4,3,2,1,0:T(8,128)S(1)} collective-permute-done((f32[3,2,2,16,128]{4,3,2,1,0:T(8,128)S(1)}, f32[3,2,2,16,128]{4,3,2,1,0:T(8,128)S(1)}, u32[]{:S(2)}, u32[]{:S(2)}) %collective-permute-start.8) | collective-permute-done | bytes 98336 | tf_op jit(solution)/shard_map/ppermute | solution.py:392
  22.1 0.0 collective-permute-done.7.came_last_ref
  22.1 1.0 %image_products.1 = f32[33,2,16,128]{3,2,1,0:T(8,128)} custom-call(s32[8,128]{1,0:T(8,128)S(1)} %get-tuple-element.25.up_first_ref, s32[8,128]{1,0:T(8,128)S(1)} %get-tuple-element.26.inside_ref, f32[3,2,2,16,128]{4,3,2,1,0:T(8,128)S(1)} %stack.1.mine_ref, f32[3,2,2,16,128]{4,3,2,1,0:T(8,128)S(1)} %collective-permute-done.7.came_last_ref, ...), custom_call_target="tpu_custom_call" | custom-call | tf_op jit(solution)/shard_map/image_products/pallas_call | solution.py:527
  (1 shorter events, 0.0 us)
Async XLA Ops:
  2.1 5.4 %collective-permute-start = (f32[20,8,128]{2,1,0:T(8,128)S(1)}, f32[20,8,128]{2,1,0:T(8,128)S(1)}, u32[]{:S(2)}, u32[]{:S(2)}) collective-permute-start(f32[20,8,128]{2,1,0:T(8,128)S(1)} %get-tuple-element.33), channel_id=1, source_target_pairs={{0,1},{1,0},{2,3},{3,2},{4,8},{5,9},{6,10},{7,11},{8,4},{9,5},{10,... | collective-permute-start | bytes 245768 | tf_op jit(solution)/shard_map/ppermute | solution.py:392
  2.6 6.6 %collective-permute-start.1 = (f32[20,8,128]{2,1,0:T(8,128)S(1)}, f32[20,8,128]{2,1,0:T(8,128)S(1)}, u32[]{:S(2)}, u32[]{:S(2)}) collective-permute-start(f32[20,8,128]{2,1,0:T(8,128)S(1)} %get-tuple-element.34), channel_id=1, source_target_pairs={{0,4},{1,5},{2,6},{3,7},{4,0},{5,1},{6,2},{7,3},{8,12},{9,13},{10,... | collective-permute-start | bytes 245768 | tf_op jit(solution)/shard_map/ppermute | solution.py:392
  9.6 4.1 %collective-permute-start.3 = (f32[1,2,2,16,128]{4,3,2,1,0:T(8,128)S(1)}, f32[1,2,2,16,128]{4,3,2,1,0:T(8,128)S(1)}, u32[]{:S(2)}, u32[]{:S(2)}) collective-permute-start(f32[1,2,2,16,128]{4,3,2,1,0:T(8,128)S(1)} %bitcast.2), channel_id=1, source_target_pairs={{0,4},{1,5},{2,6},{3,7},{4,0},{5,1},{6,2},{7,3},{8,12},{9,13},{10,... | collective-permute-start | bytes 98312 | tf_op jit(solution)/shard_map/ppermute | solution.py:392
  11.7 2.0 %collective-permute-start.2 = (f32[1,2,2,16,128]{4,3,2,1,0:T(8,128)S(1)}, f32[1,2,2,16,128]{4,3,2,1,0:T(8,128)S(1)}, u32[]{:S(2)}, u32[]{:S(2)}) collective-permute-start(f32[1,2,2,16,128]{4,3,2,1,0:T(8,128)S(1)} %bitcast.3), channel_id=1, source_target_pairs={{0,1},{1,0},{2,3},{3,2},{4,8},{5,9},{6,10},{7,11},{8,4},{9,5},{10,... | collective-permute-start | bytes 98312 | tf_op jit(solution)/shard_map/ppermute | solution.py:392
  11.7 2.0 %collective-permute-start.4 = (f32[2,2,16,128]{3,2,1,0:T(8,128)S(1)}, f32[2,2,16,128]{3,2,1,0:T(8,128)S(1)}, u32[]{:S(2)}, u32[]{:S(2)}) collective-permute-start(f32[2,2,16,128]{3,2,1,0:T(8,128)S(1)} %get-tuple-element.39), channel_id=1, source_target_pairs={{0,1},{1,0},{2,3},{3,2},{4,5},{5,4},{6,7},{7,6},{8,9},{9,8},{10,11... | collective-permute-start | bytes 98312 | tf_op jit(solution)/shard_map/ppermute | solution.py:490
  12.2 3.9 %collective-permute-start.5 = (f32[2,2,16,128]{3,2,1,0:T(8,128)S(1)}, f32[2,2,16,128]{3,2,1,0:T(8,128)S(1)}, u32[]{:S(2)}, u32[]{:S(2)}) collective-permute-start(f32[2,2,16,128]{3,2,1,0:T(8,128)S(1)} %get-tuple-element.40), channel_id=1, source_target_pairs={{0,2},{1,3},{2,0},{3,1},{4,6},{5,7},{6,4},{7,5},{8,10},{9,11},{10,... | collective-permute-start | bytes 98312 | tf_op jit(solution)/shard_map/ppermute | solution.py:490
  13.7 3.6 %collective-permute-start.6 = (f32[2,2,16,128]{3,2,1,0:T(8,128)S(1)}, f32[2,2,16,128]{3,2,1,0:T(8,128)S(1)}, u32[]{:S(2)}, u32[]{:S(2)}) collective-permute-start(f32[2,2,16,128]{3,2,1,0:T(8,128)S(1)} %get-tuple-element.41), channel_id=1, source_target_pairs={{0,3},{1,2},{2,1},{3,0},{4,7},{5,6},{6,5},{7,4},{8,11},{9,10},{10,... | collective-permute-start | bytes 98312 | tf_op jit(solution)/shard_map/ppermute | solution.py:490
  17.3 4.8 %collective-permute-start.8 = (f32[3,2,2,16,128]{4,3,2,1,0:T(8,128)S(1)}, f32[3,2,2,16,128]{4,3,2,1,0:T(8,128)S(1)}, u32[]{:S(2)}, u32[]{:S(2)}) collective-permute-start(f32[3,2,2,16,128]{4,3,2,1,0:T(8,128)S(1)} %stack.1.mine_ref), channel_id=1, source_target_pairs={{0,4},{1,5},{2,6},{3,7},{4,0},{5,1},{6,2},{7,3},{8,12},{9,13},{10,... | collective-permute-start | bytes 294920 | tf_op jit(solution)/shard_map/ppermute | solution.py:392
  18.6 3.5 %collective-permute-start.7 = (f32[3,2,2,16,128]{4,3,2,1,0:T(8,128)S(1)}, f32[3,2,2,16,128]{4,3,2,1,0:T(8,128)S(1)}, u32[]{:S(2)}, u32[]{:S(2)}) collective-permute-start(f32[3,2,2,16,128]{4,3,2,1,0:T(8,128)S(1)} %stack.1.mine_ref), channel_id=1, source_target_pairs={{0,1},{1,0},{2,3},{3,2},{4,8},{5,9},{6,10},{7,11},{8,4},{9,5},{10,... | collective-permute-start | bytes 294920 | tf_op jit(solution)/shard_map/ppermute | solution.py:392

commit v11 on v10

--- a/solution.py
+++ b/solution.py
@@ -310,66 +310,36 @@
     return total
 
 
-def stack(count, *refs):
-    for place in range(count):
+def stack(*refs):
+    for place in range(len(refs) - 1):
         refs[-1][place] = refs[place][...]
 
 
-def own_products(
-    weight,
-    up_first_ref,
-    inside_ref,
-    mine_ref,
-    came_last_ref,
-    came_first_ref,
-    final_ref,
-    src_hbm,
-    rec_hbm,
-    image_ref,
-    wide,
-    sems,
-):
+def write_fields(final_ref, src_hbm, rec_hbm, sems):
     copies = [
         pltpu.make_async_copy(final_ref.at[field], out.at[0], sems.at[field])
         for field, out in enumerate((src_hbm, rec_hbm))
     ]
     for copy in copies:
         copy.start()
-    widen(
-        weight, (up_first_ref, inside_ref), (mine_ref, came_last_ref, came_first_ref), wide
-    )
-    for offset in range(OFFS):
-        for level in range(wide.shape[2]):
-            image_ref[offset, level] = offset_product(wide, offset, level, None)
     for copy in copies:
         copy.wait()
 
 
-def image_products(
-    weight,
-    up_first_ref,
-    inside_ref,
-    mine_ref,
-    came_last_ref,
-    came_first_ref,
-    before_ref,
-    image_hbm,
-    wide,
-    image_ref,
-    sems,
-):
-    widen(
-        weight, (up_first_ref, inside_ref), (mine_ref, came_last_ref, came_first_ref), wide
-    )
+def image_products(weight, up_first_ref, inside_ref, *rest):
+    groups, (image_hbm, *wides, image_ref, sems) = (rest[0:3], rest[3:6]), rest[6:]
+    for blocks, wide in zip(groups, wides):
+        widen(weight, (up_first_ref, inside_ref), blocks, wide)
     parts = sems.shape[0]
     copies = []
     for piece in range(parts):
         offsets = range(piece * OFFS // parts, (piece + 1) * OFFS // parts)
         for offset in offsets:
-            for level in range(wide.shape[2]):
-                image_ref[offset, level] = offset_product(
-                    wide, offset, level, before_ref[offset, level]
-                )
+            for level in range(image_ref.shape[1]):
+                total = None
+                for wide in wides:
+                    total = offset_product(wide, offset, level, total)
+                image_ref[offset, level] = total
         rows = pl.ds(offsets[0], len(offsets))
         copy = pltpu.make_async_copy(image_ref.at[rows], image_hbm.at[rows], sems.at[piece])
         copy.start()
@@ -496,47 +466,37 @@
     def wide_scratch(blocks):
         return scratch(blocks.shape[0], 2, share, 3 * extent, across)
 
-    mine = own_block[None]
-    fields_first, fields_last = swap_sides(mine, mine)
-    others = pl.pallas_call(
-        functools.partial(stack, len(came)),
-        out_shape=struct(len(came), *own_block.shape),
-        in_specs=[VMEM] * (len(came) + 2),
-        out_specs=VMEM,
+    src_next, rec_next = pl.pallas_call(
+        write_fields,
+        out_shape=(struct(1, levels, extent, across), struct(1, levels, extent, across)),
+        in_specs=[VMEM],
+        out_specs=[HBM, HBM],
+        scratch_shapes=[pltpu.SemaphoreType.DMA((2,))],
         compiler_params=params,
-        name="stack",
-    )(*came, fields_last, fields_first)
-    products = OFFS * share * extent * across
-    src_next, rec_next, before = pl.pallas_call(
-        functools.partial(own_products, weight),
-        out_shape=(
-            struct(1, levels, extent, across),
-            struct(1, levels, extent, across),
-            struct(*image_shape),
-        ),
-        in_specs=[VMEM] * 6,
-        out_specs=[HBM, HBM, VMEM],
-        scratch_shapes=[wide_scratch(mine), pltpu.SemaphoreType.DMA((2,))],
-        compiler_params=params,
-        cost_estimate=pl.CostEstimate(
-            flops=2 * products, bytes_accessed=8 * products, transcendentals=0
-        ),
-        name="own_products",
-    )(up_first, inside, mine, fields_last, fields_first, final)
-    fields_first, fields_last = swap_sides(others, others)
+        name="write_fields",
+    )(final)
+    operands, wides = [], []
+    for blocks in ([own_block, came[0]], came[1:]):
+        group = pl.pallas_call(
+            stack,
+            out_shape=struct(len(blocks), *own_block.shape),
+            in_specs=[VMEM] * len(blocks),
+            out_specs=VMEM,
+            compiler_params=params,
+            name="stack",
+        )(*blocks)
+        fields_first, fields_last = swap_sides(group, group)
+        operands = [group, fields_last, fields_first, *operands]
+        wides.insert(0, wide_scratch(group))
     image = pl.pallas_call(
         functools.partial(image_products, weight),
         out_shape=struct(*image_shape),
-        in_specs=[VMEM] * 6,
+        in_specs=[VMEM] * (2 + len(operands)),
         out_specs=HBM,
-        scratch_shapes=[
-            wide_scratch(others),
-            scratch(*image_shape),
-            pltpu.SemaphoreType.DMA((11,)),
-        ],
+        scratch_shapes=[*wides, scratch(*image_shape), pltpu.SemaphoreType.DMA((11,))],
         compiler_params=params,
         name="image_products",
-    )(up_first, inside, others, fields_last, fields_first, before)
+    )(up_first, inside, *operands)
     return src_next, rec_next, image
 
 

time: 23.2 us -> 20.2 us (0.87)
  waiting for transfers between devices: 8.03 us -> 4.27 us
  starting transfers between devices: 10.1 us -> 10.8 us
    ppermute x3, waiting for transfers between devices: 3.57 us -> 0.88 us  [per_device(): lax.ppermute(sent, 'shot', [(shot, shot ^ 1 + i) for shot in range(shots)])]
    ppermute x6, waiting for transfers between devices: 4.46 us -> 3.4 us  [swap(): return lax.ppermute(value, ('tile', 'shot'), pairs)]
    ppermute x6, starting transfers between devices: 8.07 us -> 8.84 us  [swap(): return lax.ppermute(value, ('tile', 'shot'), pairs)]
    pallas_call x2 -> x3, Pallas kernels: 0.68 us -> 0.68 us  [the longest x1 0.67 us: per_device(): pl.pallas_call(write_fields, out_shape=(struct(1, levels, extent, across)...]
  transfers between devices with their start and end apart: 9 -> 9, of which waited for: 4 -> 3; matrix products, arithmetic and copies ran while one was open for 0% -> 0% of each run, Pallas kernels for 3% -> 4%
where the time goes in v11:
time: 20.2 us; the launch traced here: 20 us
  starting transfers between devices  10.8 us (53%)
  waiting for transfers between devices  4.27 us (21%)
  Pallas kernels  3.57 us (18%)
  between operations  1.35 us (7%)
    ppermute x6, starting transfers between devices, swap(): return lax.ppermute(value, ('tile', 'shot'), pairs)  8.84 us
    ppermute x6, waiting for transfers between devices, swap(): return lax.ppermute(value, ('tile', 'shot'), pairs)  3.4 us
    ppermute x3, starting transfers between devices, per_device(): lax.ppermute(sent, 'shot', [(shot, shot ^ 1 + i) for shot in range(shots)])  1.93 us
    pallas_call x1, Pallas kernels, per_device(): pl.pallas_call(own_part, out_shape=(struct(*wavelet.shape), struct(*wide_...  1.46 us
    pallas_call x1, Pallas kernels, per_device(): pl.pallas_call(functools.partial(image_products, weight), out_shape=struc...  0.94 us
    ppermute x3, waiting for transfers between devices, per_device(): lax.ppermute(sent, 'shot', [(shot, shot ^ 1 + i) for shot in range(shots)])  0.88 us
    pallas_call x1, Pallas kernels, per_device(): pl.pallas_call(write_fields, out_shape=(struct(1, levels, extent, across)...  0.67 us
  transfers between devices with their start and end apart: 9, of which 3 were waited for; matrix products, arithmetic and copies ran while one was open for 0% of the time, Pallas kernels for 4%

profile of v11, /device:TPU:0, one launch (start us, length us, event | category | flops | bytes accessed | tf_op | source)
XLA Modules:
  0.0 20.0 jit_solution(11233488457278221243)
XLA Ops:
  0.6 1.5 %own_part.1 = (f32[1,2]{1,0:T(1,128)S(1)}, f32[2,8,32,128]{3,2,1,0:T(8,128)S(1)}, f32[2,8,16,128]{3,2,1,0:T(8,128)S(1)}, f32[2,8,16,128]{3,2,1,0:T(8,128)S(1)}, ...) custom-call(f32[1,16]{1,0:T(1,128)} %bitcast.1, s32[1,32]{1,0:T(1,128)} %spots_hbm.1, ...), custom_call_target="tpu_custom_call" | custom-call | tf_op jit(solution)/shard_map/own_part/pallas_call | solution.py:395
  2.1 0.5 %collective-permute-start = (f32[20,8,128]{2,1,0:T(8,128)S(1)}, f32[20,8,128]{2,1,0:T(8,128)S(1)}, u32[]{:S(2)}, u32[]{:S(2)}) collective-permute-start(f32[20,8,128]{2,1,0:T(8,128)S(1)} %get-tuple-element.32), channel_id=1, source_target_pairs={{0,1},{1,0},{2,3},{3,2},{4,8},{5,9},{6,10},{7,11},{8,4},{9,5},{10,... | collective-permute-start | bytes 245768 | tf_op jit(solution)/shard_map/ppermute | solution.py:362
  2.6 4.1 %collective-permute-start.1 = (f32[20,8,128]{2,1,0:T(8,128)S(1)}, f32[20,8,128]{2,1,0:T(8,128)S(1)}, u32[]{:S(2)}, u32[]{:S(2)}) collective-permute-start(f32[20,8,128]{2,1,0:T(8,128)S(1)} %get-tuple-element.33), channel_id=1, source_target_pairs={{0,4},{1,5},{2,6},{3,7},{4,0},{5,1},{6,2},{7,3},{8,12},{9,13},{10,... | collective-permute-start | bytes 245768 | tf_op jit(solution)/shard_map/ppermute | solution.py:362
  7.4 0.1 source_and_order.1
  7.5 0.0 collective-permute-done.came_last_ref
  7.5 1.7 %collective-permute-done.1.came_first_ref = f32[20,8,128]{2,1,0:T(8,128)S(1)} collective-permute-done((f32[20,8,128]{2,1,0:T(8,128)S(1)}, f32[20,8,128]{2,1,0:T(8,128)S(1)}, u32[]{:S(2)}, u32[]{:S(2)}) %collective-permute-start.1) | collective-permute-done | bytes 81952 | tf_op jit(solution)/shard_map/ppermute | solution.py:362
  9.2 0.4 %both_steps.1 = (f32[2,8,16,128]{3,2,1,0:T(8,128)S(1)}, f32[2,2,16,128]{3,2,1,0:T(8,128)S(1)}, f32[2,2,16,128]{3,2,1,0:T(8,128)S(1)}, f32[2,2,16,128]{3,2,1,0:T(8,128)S(1)}, f32[2,2,16,128]{3,2,1,0:T(8,128)S(1)}) custom-call(s32[8,128]{1,0:T(8,128)S(1)} %get-tuple-element.24.up_first_ref, s32[8,128]{1,0:T(8,128)S(1)} %get-tuple-element.25.inside_ref, ...), custom_call_target="tpu_custom_call" | custom-call | tf_op jit(solution)/shard_map/both_steps/pallas_call | solution.py:450
  9.6 0.1 collective-permute-start.6
  9.7 1.6 %collective-permute-start.2 = (f32[2,2,16,128]{3,2,1,0:T(8,128)S(1)}, f32[2,2,16,128]{3,2,1,0:T(8,128)S(1)}, u32[]{:S(2)}, u32[]{:S(2)}) collective-permute-start(f32[2,2,16,128]{3,2,1,0:T(8,128)S(1)} %get-tuple-element.37), channel_id=1, source_target_pairs={{0,2},{1,3},{2,0},{3,1},{4,6},{5,7},{6,4},{7,5},{8,10},{9,11},{10,... | collective-permute-start | bytes 98312 | tf_op jit(solution)/shard_map/ppermute | solution.py:460
  11.2 0.3 %collective-permute-start.3 = (f32[2,2,16,128]{3,2,1,0:T(8,128)S(1)}, f32[2,2,16,128]{3,2,1,0:T(8,128)S(1)}, u32[]{:S(2)}, u32[]{:S(2)}) collective-permute-start(f32[2,2,16,128]{3,2,1,0:T(8,128)S(1)} %get-tuple-element.38), channel_id=1, source_target_pairs={{0,3},{1,2},{2,1},{3,0},{4,7},{5,6},{6,5},{7,4},{8,11},{9,10},{10,... | collective-permute-start | bytes 98312 | tf_op jit(solution)/shard_map/ppermute | solution.py:460
  11.5 0.0 collective-permute-done.6.refs_1_
  11.5 2.1 %collective-permute-start.8 = (f32[2,2,2,16,128]{4,3,2,1,0:T(8,128)S(1)}, f32[2,2,2,16,128]{4,3,2,1,0:T(8,128)S(1)}, u32[]{:S(2)}, u32[]{:S(2)}) collective-permute-start(f32[2,2,2,16,128]{4,3,2,1,0:T(8,128)S(1)} %stack.3.rest_3_), channel_id=1, source_target_pairs={{0,4},{1,5},{2,6},{3,7},{4,0},{5,1},{6,2},{7,3},{8,12},{9,13},{10,... | collective-permute-start | bytes 196616 | tf_op jit(solution)/shard_map/ppermute | solution.py:362
  13.6 0.1 collective-permute-start.7
  13.7 0.0 collective-permute-done.2.refs_0_
  13.7 0.9 %collective-permute-done.3.refs_1_ = f32[2,2,16,128]{3,2,1,0:T(8,128)S(1)} collective-permute-done((f32[2,2,16,128]{3,2,1,0:T(8,128)S(1)}, f32[2,2,16,128]{3,2,1,0:T(8,128)S(1)}, u32[]{:S(2)}, u32[]{:S(2)}) %collective-permute-start.3) | collective-permute-done | bytes 32800 | tf_op jit(solution)/shard_map/ppermute | solution.py:460
  14.6 2.0 %collective-permute-start.5 = (f32[2,2,2,16,128]{4,3,2,1,0:T(8,128)S(1)}, f32[2,2,2,16,128]{4,3,2,1,0:T(8,128)S(1)}, u32[]{:S(2)}, u32[]{:S(2)}) collective-permute-start(f32[2,2,2,16,128]{4,3,2,1,0:T(8,128)S(1)} %stack.2.rest_0_), channel_id=1, source_target_pairs={{0,4},{1,5},{2,6},{3,7},{4,0},{5,1},{6,2},{7,3},{8,12},{9,13},{10,... | collective-permute-start | bytes 196616 | tf_op jit(solution)/shard_map/ppermute | solution.py:362
  16.6 0.0 collective-permute-start.4
  16.6 0.7 %write_fields.1 = (f32[1,8,16,128]{3,2,1,0:T(8,128)}, f32[1,8,16,128]{3,2,1,0:T(8,128)}) custom-call(f32[2,8,16,128]{3,2,1,0:T(8,128)S(1)} %get-tuple-element.34.final_ref), custom_call_target="tpu_custom_call" | custom-call | tf_op jit(solution)/shard_map/write_fields/pallas_call | solution.py:469
  17.3 0.0 collective-permute-done.8.rest_5_
  17.3 0.0 collective-permute-done.7.rest_4_
  17.3 1.7 %collective-permute-done.5.rest_2_ = f32[2,2,2,16,128]{4,3,2,1,0:T(8,128)S(1)} collective-permute-done((f32[2,2,2,16,128]{4,3,2,1,0:T(8,128)S(1)}, f32[2,2,2,16,128]{4,3,2,1,0:T(8,128)S(1)}, u32[]{:S(2)}, u32[]{:S(2)}) %collective-permute-start.5) | collective-permute-done | bytes 65568 | tf_op jit(solution)/shard_map/ppermute | solution.py:362
  19.0 0.0 collective-permute-done.4.rest_1_
  19.0 0.9 %image_products.1 = f32[33,2,16,128]{3,2,1,0:T(8,128)} custom-call(s32[8,128]{1,0:T(8,128)S(1)} %get-tuple-element.24.up_first_ref, s32[8,128]{1,0:T(8,128)S(1)} %get-tuple-element.25.inside_ref, f32[2,2,2,16,128]{4,3,2,1,0:T(8,128)S(1)} %stack.2.rest_0_, f32[2,2,2,16,128]{4,3,2,1,0:T(8,128)S(1)} %collective-permute-done.4.rest_1_, ...), custom_call_target="tpu_custom_call" | custom-call | tf_op jit(solution)/shard_map/image_products/pallas_call | solution.py:491
  (2 shorter events, 0.0 us)
Async XLA Ops:
  2.1 5.4 %collective-permute-start = (f32[20,8,128]{2,1,0:T(8,128)S(1)}, f32[20,8,128]{2,1,0:T(8,128)S(1)}, u32[]{:S(2)}, u32[]{:S(2)}) collective-permute-start(f32[20,8,128]{2,1,0:T(8,128)S(1)} %get-tuple-element.32), channel_id=1, source_target_pairs={{0,1},{1,0},{2,3},{3,2},{4,8},{5,9},{6,10},{7,11},{8,4},{9,5},{10,... | collective-permute-start | bytes 245768 | tf_op jit(solution)/shard_map/ppermute | solution.py:362
  2.6 6.6 %collective-permute-start.1 = (f32[20,8,128]{2,1,0:T(8,128)S(1)}, f32[20,8,128]{2,1,0:T(8,128)S(1)}, u32[]{:S(2)}, u32[]{:S(2)}) collective-permute-start(f32[20,8,128]{2,1,0:T(8,128)S(1)} %get-tuple-element.33), channel_id=1, source_target_pairs={{0,4},{1,5},{2,6},{3,7},{4,0},{5,1},{6,2},{7,3},{8,12},{9,13},{10,... | collective-permute-start | bytes 245768 | tf_op jit(solution)/shard_map/ppermute | solution.py:362
  9.6 1.9 %collective-permute-start.6 = (f32[2,2,16,128]{3,2,1,0:T(8,128)S(1)}, f32[2,2,16,128]{3,2,1,0:T(8,128)S(1)}, u32[]{:S(2)}, u32[]{:S(2)}) collective-permute-start(f32[2,2,16,128]{3,2,1,0:T(8,128)S(1)} %get-tuple-element.40), channel_id=1, source_target_pairs={{0,1},{1,0},{2,3},{3,2},{4,5},{5,4},{6,7},{7,6},{8,9},{9,8},{10,11... | collective-permute-start | bytes 98312 | tf_op jit(solution)/shard_map/ppermute | solution.py:460
  9.7 4.0 %collective-permute-start.2 = (f32[2,2,16,128]{3,2,1,0:T(8,128)S(1)}, f32[2,2,16,128]{3,2,1,0:T(8,128)S(1)}, u32[]{:S(2)}, u32[]{:S(2)}) collective-permute-start(f32[2,2,16,128]{3,2,1,0:T(8,128)S(1)} %get-tuple-element.37), channel_id=1, source_target_pairs={{0,2},{1,3},{2,0},{3,1},{4,6},{5,7},{6,4},{7,5},{8,10},{9,11},{10,... | collective-permute-start | bytes 98312 | tf_op jit(solution)/shard_map/ppermute | solution.py:460
  11.2 3.3 %collective-permute-start.3 = (f32[2,2,16,128]{3,2,1,0:T(8,128)S(1)}, f32[2,2,16,128]{3,2,1,0:T(8,128)S(1)}, u32[]{:S(2)}, u32[]{:S(2)}) collective-permute-start(f32[2,2,16,128]{3,2,1,0:T(8,128)S(1)} %get-tuple-element.38), channel_id=1, source_target_pairs={{0,3},{1,2},{2,1},{3,0},{4,7},{5,6},{6,5},{7,4},{8,11},{9,10},{10,... | collective-permute-start | bytes 98312 | tf_op jit(solution)/shard_map/ppermute | solution.py:460
  11.5 5.7 %collective-permute-start.8 = (f32[2,2,2,16,128]{4,3,2,1,0:T(8,128)S(1)}, f32[2,2,2,16,128]{4,3,2,1,0:T(8,128)S(1)}, u32[]{:S(2)}, u32[]{:S(2)}) collective-permute-start(f32[2,2,2,16,128]{4,3,2,1,0:T(8,128)S(1)} %stack.3.rest_3_), channel_id=1, source_target_pairs={{0,4},{1,5},{2,6},{3,7},{4,0},{5,1},{6,2},{7,3},{8,12},{9,13},{10,... | collective-permute-start | bytes 196616 | tf_op jit(solution)/shard_map/ppermute | solution.py:362
  13.6 3.7 %collective-permute-start.7 = (f32[2,2,2,16,128]{4,3,2,1,0:T(8,128)S(1)}, f32[2,2,2,16,128]{4,3,2,1,0:T(8,128)S(1)}, u32[]{:S(2)}, u32[]{:S(2)}) collective-permute-start(f32[2,2,2,16,128]{4,3,2,1,0:T(8,128)S(1)} %stack.3.rest_3_), channel_id=1, source_target_pairs={{0,1},{1,0},{2,3},{3,2},{4,8},{5,9},{6,10},{7,11},{8,4},{9,5},{10,... | collective-permute-start | bytes 196616 | tf_op jit(solution)/shard_map/ppermute | solution.py:362
  14.6 4.4 %collective-permute-start.5 = (f32[2,2,2,16,128]{4,3,2,1,0:T(8,128)S(1)}, f32[2,2,2,16,128]{4,3,2,1,0:T(8,128)S(1)}, u32[]{:S(2)}, u32[]{:S(2)}) collective-permute-start(f32[2,2,2,16,128]{4,3,2,1,0:T(8,128)S(1)} %stack.2.rest_0_), channel_id=1, source_target_pairs={{0,4},{1,5},{2,6},{3,7},{4,0},{5,1},{6,2},{7,3},{8,12},{9,13},{10,... | collective-permute-start | bytes 196616 | tf_op jit(solution)/shard_map/ppermute | solution.py:362
  16.6 2.4 %collective-permute-start.4 = (f32[2,2,2,16,128]{4,3,2,1,0:T(8,128)S(1)}, f32[2,2,2,16,128]{4,3,2,1,0:T(8,128)S(1)}, u32[]{:S(2)}, u32[]{:S(2)}) collective-permute-start(f32[2,2,2,16,128]{4,3,2,1,0:T(8,128)S(1)} %stack.2.rest_0_), channel_id=1, source_target_pairs={{0,1},{1,0},{2,3},{3,2},{4,8},{5,9},{6,10},{7,11},{8,4},{9,5},{10,... | collective-permute-start | bytes 196616 | tf_op jit(solution)/shard_map/ppermute | solution.py:362

commit v12 on v11

--- a/solution.py
+++ b/solution.py
@@ -11,6 +11,7 @@
 REACH = OFFS // 2
 HALO = 4
 LEAD = 8
+ROUNDS = 3
 
 COEFS = (-205.0 / 72.0, 8.0 / 5.0, -1.0 / 5.0, 8.0 / 315.0, -1.0 / 560.0)
 
@@ -53,7 +54,7 @@
 
 
 def source_and_order(
-    width, cell_ref, amps_ref, later_ref, source_ref, source_later_ref, up_first_ref, inside_ref, bits_ref
+    width, cell_ref, amps_ref, later_ref, source_ref, source_later_ref, up_first_ref, inside_ref, sides_ref, bits_ref
 ):
     levels, extent, across = source_later_ref.shape
     cell = cell_ref[0]
@@ -72,9 +73,12 @@
     up_first_ref[...] = jnp.full(
         up_first_ref.shape, jnp.where(goes_up_first(), 1, 0), dtype=jnp.int32
     )
-    tile = lax.axis_index("tile")
-    inside = (tile > 0) & (tile < lax.axis_size("tile") - 1)
+    tile, tiles = lax.axis_index("tile"), lax.axis_size("tile")
+    inside = (tile > 0) & (tile < tiles - 1)
     inside_ref[...] = jnp.full(inside_ref.shape, jnp.where(inside, 1, 0), dtype=jnp.int32)
+    rounds = (tile % ROUNDS, jnp.where(tile > 0, 1, 0), jnp.where(tile < tiles - 1, 1, 0))
+    for place, value in enumerate(rounds):
+        sides_ref[place] = jnp.full(sides_ref.shape[1:], value, dtype=jnp.int32)
     shot = jnp.full(bits_ref.shape[1:], lax.axis_index("shot"), dtype=jnp.int32)
     for bit in range(bits_ref.shape[0]):
         bits_ref[bit] = shot & (1 << bit)
@@ -95,15 +99,11 @@
     part_ref,
     later_ref,
     coef_ref,
-    sent_first_ref,
-    sent_last_ref,
-    table,
-    spots_ref,
-    traces_ref,
-    ids_ref,
-    prev_ref,
-    sems,
+    *rest,
 ):
+    sent_refs, rest = rest[:ROUNDS], rest[ROUNDS:]
+    table, spots_ref, traces_ref, ids_ref, prev_ref, sems = rest
+
     levels, extent, across = ids_ref.shape
     shape = (extent, across)
     regions = table_hbm.shape[1]
@@ -131,15 +131,15 @@
             wide[field, level, 0:LEAD, :] = zeros
             wide[field, level, end : end + LEAD, :] = zeros
     weights = lane_weights(shape)
-    up_first = goes_up_first()
+    my_round = lax.rem(lax.axis_index("tile"), ROUNDS)
     for copy in copies:
         copy.wait()
 
     def send(place, rows, value):
         low = value[0:HALO, :]
         high = value[extent - HALO : extent, :]
-        sent_first_ref[place, rows, :] = jnp.where(up_first, high, low)
-        sent_last_ref[place, rows, :] = jnp.where(up_first, low, high)
+        for number, sent_ref in enumerate(sent_refs):
+            sent_ref[place, rows, :] = jnp.where(my_round == number, high, low)
 
     spots = spots_ref[...]
     column = lax.broadcasted_iota(jnp.int32, (extent, spots.shape[1]), 0) * across
@@ -186,8 +186,7 @@
 
 
 def both_steps(
-    up_first_ref,
-    inside_ref,
+    sides_ref,
     bits_ref,
     own,
     part_ref,
@@ -195,25 +194,24 @@
     source_ref,
     source_later_ref,
     coef_ref,
-    came_last_ref,
-    came_first_ref,
-    final_ref,
-    mine_ref,
     *rest,
 ):
-    *theirs, other, middle = rest
-    blocks = [mine_ref, *theirs]
+    came_refs, (final_ref, *blocks, other, middle) = rest[:ROUNDS], rest[ROUNDS:]
     levels, extent, across = coef_ref.shape
     shape = (extent, across)
-    share = mine_ref.shape[1]
+    share = blocks[0].shape[1]
     end = LEAD + extent
-    up_first = up_first_ref[0:HALO, :] != 0
-    inside = inside_ref[0:HALO, :] != 0
+    my_round = sides_ref[0, 0:HALO, :]
+    has_low = sides_ref[1, 0:HALO, :] != 0
+    has_high = sides_ref[2, 0:HALO, :] != 0
 
     def received(place, rows):
-        first = came_first_ref[place, rows, :]
-        last = jnp.where(inside, came_last_ref[place, rows, :], 0.0)
-        return jnp.where(up_first, last, first), jnp.where(up_first, first, last)
+        came = [ref[place, rows, :] for ref in came_refs]
+        low, high = came[-1], came[0]
+        for number in range(1, ROUNDS):
+            low = jnp.where(my_round == number, came[number - 1], low)
+            high = jnp.where(my_round == number, came[number], high)
+        return jnp.where(has_low, low, 0.0), jnp.where(has_high, high, 0.0)
 
     for field in range(2):
         for level in range(levels):
@@ -348,21 +346,24 @@
         copy.wait()
 
 
-def swap_sides(first, last):
+def swap_tiles(value, lower):
     tiles, shots = lax.axis_size("tile"), lax.axis_size("shot")
-
-    def swap(value, begin):
-        pairs = []
-        for tile in range(tiles):
-            partner = tile + 1 if (tile - begin) % 2 == 0 else tile - 1
-            inside = 0 <= partner < tiles
-            for shot in range(shots):
-                target = partner * shots + shot if inside else tile * shots + (shot ^ 1)
-                pairs.append((tile * shots + shot, target))
-        return lax.ppermute(value, ("tile", "shot"), pairs)
-
-    came_last = swap(last, 1)
-    return swap(first, 0), came_last
+    partner = {}
+    for tile in lower:
+        partner[tile], partner[tile + 1] = tile + 1, tile
+    pairs = []
+    for tile in range(tiles):
+        for shot in range(shots):
+            here = tile * shots + shot
+            there = partner[tile] * shots + shot if tile in partner else here ^ 1
+            pairs.append((here, there))
+    return lax.ppermute(value, ("tile", "shot"), pairs)
+
+
+def swap_sides(value):
+    tiles = lax.axis_size("tile")
+    came_last = swap_tiles(value, range(1, tiles - 1, 2))
+    return swap_tiles(value, range(0, tiles - 1, 2)), came_last
 
 
 def per_device(
@@ -392,7 +393,7 @@
 
     wide_shape = (2, levels, extent + 2 * LEAD, across)
     message = struct(2 * levels + levels // 2, 2 * HALO, across)
-    amps, own, part, later, coef, first, last = pl.pallas_call(
+    amps, own, part, later, coef, *sent = pl.pallas_call(
         own_part,
         out_shape=(
             struct(*wavelet.shape),
@@ -400,11 +401,10 @@
             struct(2, levels, extent, across),
             struct(2, levels, extent, across),
             struct(levels, extent, across),
-            message,
-            message,
+            *([message] * ROUNDS),
         ),
         in_specs=[HBM] * 9,
-        out_specs=[VMEM] * 7,
+        out_specs=[VMEM] * (5 + ROUNDS),
         scratch_shapes=[
             scratch(1, speed_table.shape[0]),
             scratch(*receiver_cell.shape, dtype=jnp.int32),
@@ -431,18 +431,21 @@
             )
         )
     )
-    came_first, came_last = swap_sides(first, last)
-    source, source_later, up_first, inside, bits = pl.pallas_call(
+    sides = [
+        swap_tiles(message, range(number, tiles - 1, ROUNDS)) for number, message in enumerate(sent)
+    ]
+    source, source_later, up_first, inside, edges, bits = pl.pallas_call(
         functools.partial(source_and_order, width),
         out_shape=(
             struct(levels, extent + 2 * LEAD, across),
             struct(levels, extent, across),
             jax.ShapeDtypeStruct((8, across), jnp.int32),
             jax.ShapeDtypeStruct((8, across), jnp.int32),
+            jax.ShapeDtypeStruct((3, 8, across), jnp.int32),
             jax.ShapeDtypeStruct((shots.bit_length() - 1, 8, across), jnp.int32),
         ),
         in_specs=[SMEM] + [VMEM] * 2,
-        out_specs=[VMEM] * 5,
+        out_specs=[VMEM] * 6,
         compiler_params=params,
         name="source_and_order",
     )(source_cell, amps, later)
@@ -450,12 +453,12 @@
     final, own_block, *blocks = pl.pallas_call(
         both_steps,
         out_shape=(struct(2, levels, extent, across), *([block] * shots)),
-        in_specs=[VMEM] * 11,
+        in_specs=[VMEM] * (8 + ROUNDS),
         out_specs=[VMEM] * (1 + shots),
         scratch_shapes=[scratch(*wide_shape), scratch(*wide_shape)],
         compiler_params=params,
         name="both_steps",
-    )(up_first, inside, bits, own, part, later, source, source_later, coef, came_last, came_first)
+    )(edges, bits, own, part, later, source, source_later, coef, *sides)
     came = [
         lax.ppermute(sent, "shot", [(shot, shot ^ (1 + i)) for shot in range(shots)])
         for i, sent in enumerate(blocks)
@@ -476,7 +479,7 @@
         name="write_fields",
     )(final)
     operands, wides = [], []
-    for blocks in ([own_block, came[0]], came[1:]):
+    for blocks in ([own_block, came[0]], came[:0:-1]):
         group = pl.pallas_call(
             stack,
             out_shape=struct(len(blocks), *own_block.shape),
@@ -485,7 +488,7 @@
             compiler_params=params,
             name="stack",
         )(*blocks)
-        fields_first, fields_last = swap_sides(group, group)
+        fields_first, fields_last = swap_sides(group)
         operands = [group, fields_last, fields_first, *operands]
         wides.insert(0, wide_scratch(group))
     image = pl.pallas_call(

time: 20.2 us -> 20.2 us (level)
  the two profiles are of different devices: /device:TPU:0 before, /device:TPU:16 now
where the time goes in v12:
time: 20.2 us; the launch traced here: 20 us
  waiting for transfers between devices  7.82 us (39%)
  starting transfers between devices  7.17 us (35%)
  Pallas kernels  3.61 us (18%)
  between operations  1.35 us (7%)
    ppermute x7, waiting for transfers between devices, swap_tiles(): return lax.ppermute(value, ('tile', 'shot'), pairs)  5.71 us
    ppermute x7, starting transfers between devices, swap_tiles(): return lax.ppermute(value, ('tile', 'shot'), pairs)  4.96 us
    ppermute x3, starting transfers between devices, per_device(): lax.ppermute(sent, 'shot', [(shot, shot ^ 1 + i) for shot in range(shots)])  2.21 us
    ppermute x3, waiting for transfers between devices, per_device(): lax.ppermute(sent, 'shot', [(shot, shot ^ 1 + i) for shot in range(shots)])  2.11 us
    pallas_call x1, Pallas kernels, per_device(): pl.pallas_call(own_part, out_shape=(struct(*wavelet.shape), struct(*wide_...  1.47 us
    pallas_call x1, Pallas kernels, per_device(): pl.pallas_call(functools.partial(image_products, weight), out_shape=struc...  0.94 us
    pallas_call x1, Pallas kernels, per_device(): pl.pallas_call(write_fields, out_shape=(struct(1, levels, extent, across)...  0.67 us
    pallas_call x1, Pallas kernels, per_device(): pl.pallas_call(both_steps, out_shape=(struct(2, levels, extent, across),...  0.43 us
  transfers between devices with their start and end apart: 10, of which 6 were waited for; matrix products, arithmetic and copies ran while one was open for 0% of the time, Pallas kernels for 4%

profile of v12, /device:TPU:16, one launch (start us, length us, event | category | flops | bytes accessed | tf_op | source)
XLA Modules:
  0.0 20.0 jit_solution(2467921126883067194)
XLA Ops:
  0.6 1.5 %own_part.1 = (f32[1,2]{1,0:T(1,128)S(1)}, f32[2,8,32,128]{3,2,1,0:T(8,128)S(1)}, f32[2,8,16,128]{3,2,1,0:T(8,128)S(1)}, f32[2,8,16,128]{3,2,1,0:T(8,128)S(1)}, ...) custom-call(f32[1,16]{1,0:T(1,128)} %bitcast.1, ...), custom_call_target="tpu_custom_call" | custom-call | tf_op jit(solution)/shard_map/own_part/pallas_call | solution.py:396
  2.1 0.1 collective-permute-start
  2.2 0.5 %collective-permute-start.1 = (f32[20,8,128]{2,1,0:T(8,128)S(1)}, f32[20,8,128]{2,1,0:T(8,128)S(1)}, u32[]{:S(2)}, u32[]{:S(2)}) collective-permute-start(f32[20,8,128]{2,1,0:T(8,128)S(1)} %get-tuple-element.34), channel_id=1, source_target_pairs={{0,1},{1,0},{2,3},{3,2},{4,8},{5,9},{6,10},{7,11},{8,4},{9,5},{10,... | collective-permute-start | bytes 245768 | tf_op jit(solution)/shard_map/ppermute | solution.py:360
  2.7 1.6 %collective-permute-start.2 = (f32[20,8,128]{2,1,0:T(8,128)S(1)}, f32[20,8,128]{2,1,0:T(8,128)S(1)}, u32[]{:S(2)}, u32[]{:S(2)}) collective-permute-start(f32[20,8,128]{2,1,0:T(8,128)S(1)} %get-tuple-element.35), channel_id=1, source_target_pairs={{0,1},{1,0},{2,3},{3,2},{4,5},{5,4},{6,7},{7,6},{8,12},{9,13},{10,... | collective-permute-start | bytes 245768 | tf_op jit(solution)/shard_map/ppermute | solution.py:360
  4.9 0.1 source_and_order.1
  5.0 0.0 collective-permute-done.rest_0_
  5.0 2.0 %collective-permute-done.1.rest_1_ = f32[20,8,128]{2,1,0:T(8,128)S(1)} collective-permute-done((f32[20,8,128]{2,1,0:T(8,128)S(1)}, f32[20,8,128]{2,1,0:T(8,128)S(1)}, u32[]{:S(2)}, u32[]{:S(2)}) %collective-permute-start.1) | collective-permute-done | bytes 81952 | tf_op jit(solution)/shard_map/ppermute | solution.py:360
  7.0 0.1 collective-permute-done.2.rest_2_
  7.1 0.4 %both_steps.1 = (f32[2,8,16,128]{3,2,1,0:T(8,128)S(1)}, f32[2,2,16,128]{3,2,1,0:T(8,128)S(1)}, f32[2,2,16,128]{3,2,1,0:T(8,128)S(1)}, f32[2,2,16,128]{3,2,1,0:T(8,128)S(1)}, f32[2,2,16,128]{3,2,1,0:T(8,128)S(1)}) custom-call(s32[3,8,128]{2,1,0:T(8,128)S(1)} %get-tuple-element.26.sides_ref, s32[2,8,128]{2,1,0:T(8,128)S(1)} %get-tuple-element.27.bits_ref, ...), custom_call_target="tpu_custom_call" | custom-call | tf_op jit(solution)/shard_map/both_steps/pallas_call | solution.py:453
  7.6 0.1 collective-permute-start.7
  7.7 2.0 %collective-permute-start.3 = (f32[2,2,16,128]{3,2,1,0:T(8,128)S(1)}, f32[2,2,16,128]{3,2,1,0:T(8,128)S(1)}, u32[]{:S(2)}, u32[]{:S(2)}) collective-permute-start(f32[2,2,16,128]{3,2,1,0:T(8,128)S(1)} %get-tuple-element.41), channel_id=1, source_target_pairs={{0,3},{1,2},{2,1},{3,0},{4,7},{5,6},{6,5},{7,4},{8,11},{9,10},{10,... | collective-permute-start | bytes 98312 | tf_op jit(solution)/shard_map/ppermute | solution.py:463
  9.6 0.2 collective-permute-start.4
  9.8 0.0 collective-permute-done.7.refs_1_
  9.8 1.6 %collective-permute-start.9 = (f32[2,2,2,16,128]{4,3,2,1,0:T(8,128)S(1)}, f32[2,2,2,16,128]{4,3,2,1,0:T(8,128)S(1)}, u32[]{:S(2)}, u32[]{:S(2)}) collective-permute-start(f32[2,2,2,16,128]{4,3,2,1,0:T(8,128)S(1)} %stack.3.rest_3_), channel_id=1, source_target_pairs={{0,4},{1,5},{2,6},{3,7},{4,0},{5,1},{6,2},{7,3},{8,12},{9,13},{10,... | collective-permute-start | bytes 196616 | tf_op jit(solution)/shard_map/ppermute | solution.py:360
  11.4 0.0 collective-permute-start.8
  11.4 0.0 collective-permute-done.3.refs_0_
  11.4 2.1 %collective-permute-done.4.refs_1_ = f32[2,2,16,128]{3,2,1,0:T(8,128)S(1)} collective-permute-done((f32[2,2,16,128]{3,2,1,0:T(8,128)S(1)}, f32[2,2,16,128]{3,2,1,0:T(8,128)S(1)}, u32[]{:S(2)}, u32[]{:S(2)}) %collective-permute-start.4) | collective-permute-done | bytes 32800 | tf_op jit(solution)/shard_map/ppermute | solution.py:463
  13.6 1.2 %collective-permute-start.6 = (f32[2,2,2,16,128]{4,3,2,1,0:T(8,128)S(1)}, f32[2,2,2,16,128]{4,3,2,1,0:T(8,128)S(1)}, u32[]{:S(2)}, u32[]{:S(2)}) collective-permute-start(f32[2,2,2,16,128]{4,3,2,1,0:T(8,128)S(1)} %stack.2.rest_0_), channel_id=1, source_target_pairs={{0,4},{1,5},{2,6},{3,7},{4,0},{5,1},{6,2},{7,3},{8,12},{9,13},{10,... | collective-permute-start | bytes 196616 | tf_op jit(solution)/shard_map/ppermute | solution.py:360
  14.8 0.0 collective-permute-start.5
  14.8 0.7 %write_fields.1 = (f32[1,8,16,128]{3,2,1,0:T(8,128)}, f32[1,8,16,128]{3,2,1,0:T(8,128)}) custom-call(f32[2,8,16,128]{3,2,1,0:T(8,128)S(1)} %get-tuple-element.36.final_ref), custom_call_target="tpu_custom_call" | custom-call | tf_op jit(solution)/shard_map/write_fields/pallas_call | solution.py:472
  15.4 0.0 collective-permute-done.9.rest_5_
  15.4 0.3 %collective-permute-done.8.rest_4_ = f32[2,2,2,16,128]{4,3,2,1,0:T(8,128)S(1)} collective-permute-done((f32[2,2,2,16,128]{4,3,2,1,0:T(8,128)S(1)}, f32[2,2,2,16,128]{4,3,2,1,0:T(8,128)S(1)}, u32[]{:S(2)}, u32[]{:S(2)}) %collective-permute-start.8) | collective-permute-done | bytes 65568 | tf_op jit(solution)/shard_map/ppermute | solution.py:360
  15.7 2.1 %collective-permute-done.6.rest_2_ = f32[2,2,2,16,128]{4,3,2,1,0:T(8,128)S(1)} collective-permute-done((f32[2,2,2,16,128]{4,3,2,1,0:T(8,128)S(1)}, f32[2,2,2,16,128]{4,3,2,1,0:T(8,128)S(1)}, u32[]{:S(2)}, u32[]{:S(2)}) %collective-permute-start.6) | collective-permute-done | bytes 65568 | tf_op jit(solution)/shard_map/ppermute | solution.py:360
  17.8 1.2 %collective-permute-done.5.rest_1_ = f32[2,2,2,16,128]{4,3,2,1,0:T(8,128)S(1)} collective-permute-done((f32[2,2,2,16,128]{4,3,2,1,0:T(8,128)S(1)}, f32[2,2,2,16,128]{4,3,2,1,0:T(8,128)S(1)}, u32[]{:S(2)}, u32[]{:S(2)}) %collective-permute-start.5) | collective-permute-done | bytes 65568 | tf_op jit(solution)/shard_map/ppermute | solution.py:360
  19.0 0.9 %image_products.1 = f32[33,2,16,128]{3,2,1,0:T(8,128)} custom-call(s32[8,128]{1,0:T(8,128)S(1)} %get-tuple-element.39.up_first_ref, s32[8,128]{1,0:T(8,128)S(1)} %get-tuple-element.40.inside_ref, f32[2,2,2,16,128]{4,3,2,1,0:T(8,128)S(1)} %stack.2.rest_0_, f32[2,2,2,16,128]{4,3,2,1,0:T(8,128)S(1)} %collective-permute-done.5.rest_1_, ...), custom_call_target="tpu_custom_call" | custom-call | tf_op jit(solution)/shard_map/image_products/pallas_call | solution.py:494
  (2 shorter events, 0.0 us)
Async XLA Ops:
  2.1 2.9 %collective-permute-start = (f32[20,8,128]{2,1,0:T(8,128)S(1)}, f32[20,8,128]{2,1,0:T(8,128)S(1)}, u32[]{:S(2)}, u32[]{:S(2)}) collective-permute-start(f32[20,8,128]{2,1,0:T(8,128)S(1)} %get-tuple-element.33), channel_id=1, source_target_pairs={{0,4},{1,5},{2,6},{3,7},{4,0},{5,1},{6,2},{7,3},{8,9},{9,8},{10,11... | collective-permute-start | bytes 245768 | tf_op jit(solution)/shard_map/ppermute | solution.py:360
  2.2 4.9 %collective-permute-start.1 = (f32[20,8,128]{2,1,0:T(8,128)S(1)}, f32[20,8,128]{2,1,0:T(8,128)S(1)}, u32[]{:S(2)}, u32[]{:S(2)}) collective-permute-start(f32[20,8,128]{2,1,0:T(8,128)S(1)} %get-tuple-element.34), channel_id=1, source_target_pairs={{0,1},{1,0},{2,3},{3,2},{4,8},{5,9},{6,10},{7,11},{8,4},{9,5},{10,... | collective-permute-start | bytes 245768 | tf_op jit(solution)/shard_map/ppermute | solution.py:360
  2.7 4.4 %collective-permute-start.2 = (f32[20,8,128]{2,1,0:T(8,128)S(1)}, f32[20,8,128]{2,1,0:T(8,128)S(1)}, u32[]{:S(2)}, u32[]{:S(2)}) collective-permute-start(f32[20,8,128]{2,1,0:T(8,128)S(1)} %get-tuple-element.35), channel_id=1, source_target_pairs={{0,1},{1,0},{2,3},{3,2},{4,5},{5,4},{6,7},{7,6},{8,12},{9,13},{10,... | collective-permute-start | bytes 245768 | tf_op jit(solution)/shard_map/ppermute | solution.py:360
  7.6 2.2 %collective-permute-start.7 = (f32[2,2,16,128]{3,2,1,0:T(8,128)S(1)}, f32[2,2,16,128]{3,2,1,0:T(8,128)S(1)}, u32[]{:S(2)}, u32[]{:S(2)}) collective-permute-start(f32[2,2,16,128]{3,2,1,0:T(8,128)S(1)} %get-tuple-element.44), channel_id=1, source_target_pairs={{0,1},{1,0},{2,3},{3,2},{4,5},{5,4},{6,7},{7,6},{8,9},{9,8},{10,11... | collective-permute-start | bytes 98312 | tf_op jit(solution)/shard_map/ppermute | solution.py:463
  7.7 3.8 %collective-permute-start.3 = (f32[2,2,16,128]{3,2,1,0:T(8,128)S(1)}, f32[2,2,16,128]{3,2,1,0:T(8,128)S(1)}, u32[]{:S(2)}, u32[]{:S(2)}) collective-permute-start(f32[2,2,16,128]{3,2,1,0:T(8,128)S(1)} %get-tuple-element.41), channel_id=1, source_target_pairs={{0,3},{1,2},{2,1},{3,0},{4,7},{5,6},{6,5},{7,4},{8,11},{9,10},{10,... | collective-permute-start | bytes 98312 | tf_op jit(solution)/shard_map/ppermute | solution.py:463
  9.6 3.9 %collective-permute-start.4 = (f32[2,2,16,128]{3,2,1,0:T(8,128)S(1)}, f32[2,2,16,128]{3,2,1,0:T(8,128)S(1)}, u32[]{:S(2)}, u32[]{:S(2)}) collective-permute-start(f32[2,2,16,128]{3,2,1,0:T(8,128)S(1)} %get-tuple-element.42), channel_id=1, source_target_pairs={{0,2},{1,3},{2,0},{3,1},{4,6},{5,7},{6,4},{7,5},{8,10},{9,11},{10,... | collective-permute-start | bytes 98312 | tf_op jit(solution)/shard_map/ppermute | solution.py:463
  9.8 5.6 %collective-permute-start.9 = (f32[2,2,2,16,128]{4,3,2,1,0:T(8,128)S(1)}, f32[2,2,2,16,128]{4,3,2,1,0:T(8,128)S(1)}, u32[]{:S(2)}, u32[]{:S(2)}) collective-permute-start(f32[2,2,2,16,128]{4,3,2,1,0:T(8,128)S(1)} %stack.3.rest_3_), channel_id=1, source_target_pairs={{0,4},{1,5},{2,6},{3,7},{4,0},{5,1},{6,2},{7,3},{8,12},{9,13},{10,... | collective-permute-start | bytes 196616 | tf_op jit(solution)/shard_map/ppermute | solution.py:360
  11.4 4.3 %collective-permute-start.8 = (f32[2,2,2,16,128]{4,3,2,1,0:T(8,128)S(1)}, f32[2,2,2,16,128]{4,3,2,1,0:T(8,128)S(1)}, u32[]{:S(2)}, u32[]{:S(2)}) collective-permute-start(f32[2,2,2,16,128]{4,3,2,1,0:T(8,128)S(1)} %stack.3.rest_3_), channel_id=1, source_target_pairs={{0,1},{1,0},{2,3},{3,2},{4,8},{5,9},{6,10},{7,11},{8,4},{9,5},{10,... | collective-permute-start | bytes 196616 | tf_op jit(solution)/shard_map/ppermute | solution.py:360
  13.6 4.3 %collective-permute-start.6 = (f32[2,2,2,16,128]{4,3,2,1,0:T(8,128)S(1)}, f32[2,2,2,16,128]{4,3,2,1,0:T(8,128)S(1)}, u32[]{:S(2)}, u32[]{:S(2)}) collective-permute-start(f32[2,2,2,16,128]{4,3,2,1,0:T(8,128)S(1)} %stack.2.rest_0_), channel_id=1, source_target_pairs={{0,4},{1,5},{2,6},{3,7},{4,0},{5,1},{6,2},{7,3},{8,12},{9,13},{10,... | collective-permute-start | bytes 196616 | tf_op jit(solution)/shard_map/ppermute | solution.py:360
  14.8 4.3 %collective-permute-start.5 = (f32[2,2,2,16,128]{4,3,2,1,0:T(8,128)S(1)}, f32[2,2,2,16,128]{4,3,2,1,0:T(8,128)S(1)}, u32[]{:S(2)}, u32[]{:S(2)}) collective-permute-start(f32[2,2,2,16,128]{4,3,2,1,0:T(8,128)S(1)} %stack.2.rest_0_), channel_id=1, source_target_pairs={{0,1},{1,0},{2,3},{3,2},{4,8},{5,9},{6,10},{7,11},{8,4},{9,5},{10,... | collective-permute-start | bytes 196616 | tf_op jit(solution)/shard_map/ppermute | solution.py:360

commit v13 on v12

--- a/solution.py
+++ b/solution.py
@@ -12,6 +12,7 @@
 HALO = 4
 LEAD = 8
 ROUNDS = 3
+SHIFTS = {2: 1, 3: 0}
 
 COEFS = (-205.0 / 72.0, 8.0 / 5.0, -1.0 / 5.0, 8.0 / 315.0, -1.0 / 560.0)
 
@@ -49,12 +50,8 @@
     return total
 
 
-def goes_up_first():
-    return lax.rem(lax.axis_index("tile"), 2) == 0
-
-
 def source_and_order(
-    width, cell_ref, amps_ref, later_ref, source_ref, source_later_ref, up_first_ref, inside_ref, sides_ref, bits_ref
+    width, cell_ref, amps_ref, later_ref, source_ref, source_later_ref, sides_ref, bits_ref
 ):
     levels, extent, across = source_later_ref.shape
     cell = cell_ref[0]
@@ -70,14 +67,10 @@
         source_later_ref[level] = (
             later_ref[0, level] + here[LEAD : LEAD + extent, :] * amps_ref[0:1, 1:2]
         )
-    up_first_ref[...] = jnp.full(
-        up_first_ref.shape, jnp.where(goes_up_first(), 1, 0), dtype=jnp.int32
-    )
     tile, tiles = lax.axis_index("tile"), lax.axis_size("tile")
-    inside = (tile > 0) & (tile < tiles - 1)
-    inside_ref[...] = jnp.full(inside_ref.shape, jnp.where(inside, 1, 0), dtype=jnp.int32)
-    rounds = (tile % ROUNDS, jnp.where(tile > 0, 1, 0), jnp.where(tile < tiles - 1, 1, 0))
-    for place, value in enumerate(rounds):
+    places = (jnp.where(tile > 0, 1, 0), jnp.where(tile < tiles - 1, 1, 0))
+    places += tuple((tile + SHIFTS[rounds]) % rounds for rounds in (2, 3))
+    for place, value in enumerate(places):
         sides_ref[place] = jnp.full(sides_ref.shape[1:], value, dtype=jnp.int32)
     shot = jnp.full(bits_ref.shape[1:], lax.axis_index("shot"), dtype=jnp.int32)
     for bit in range(bits_ref.shape[0]):
@@ -185,6 +178,15 @@
             send(place, pl.ds(HALO, HALO), value)
 
 
+def both_sides(sides, came):
+    has_low, has_high, my_round = sides[0], sides[1], sides[len(came)]
+    low, high = came[-1], came[0]
+    for number in range(1, len(came)):
+        low = jnp.where(my_round == number, came[number - 1], low)
+        high = jnp.where(my_round == number, came[number], high)
+    return jnp.where(has_low != 0, low, 0.0), jnp.where(has_high != 0, high, 0.0)
+
+
 def both_steps(
     sides_ref,
     bits_ref,
@@ -201,17 +203,10 @@
     shape = (extent, across)
     share = blocks[0].shape[1]
     end = LEAD + extent
-    my_round = sides_ref[0, 0:HALO, :]
-    has_low = sides_ref[1, 0:HALO, :] != 0
-    has_high = sides_ref[2, 0:HALO, :] != 0
+    sides = [sides_ref[place, 0:HALO, :] for place in range(4)]
 
     def received(place, rows):
-        came = [ref[place, rows, :] for ref in came_refs]
-        low, high = came[-1], came[0]
-        for number in range(1, ROUNDS):
-            low = jnp.where(my_round == number, came[number - 1], low)
-            high = jnp.where(my_round == number, came[number], high)
-        return jnp.where(has_low, low, 0.0), jnp.where(has_high, high, 0.0)
+        return both_sides(sides, [ref[place, rows, :] for ref in came_refs])
 
     for field in range(2):
         for level in range(levels):
@@ -274,25 +269,22 @@
                 block[field, level] = part
 
 
-def widen(weight, masks, blocks, wide):
-    mine_ref, came_last_ref, came_first_ref = blocks
+def widen(weight, sides_ref, blocks, wide):
+    mine_ref, *came_refs = blocks
     shots, _, share, extent, _ = mine_ref.shape
-    up_first, inside = (
-        jnp.concatenate([mask[...]] * (extent // 8), axis=0) != 0 for mask in masks
-    )
+    sides = [
+        jnp.concatenate([sides_ref[place]] * (extent // 8), axis=0) for place in range(4)
+    ]
     for shot in range(shots):
         for field in range(2):
             for level in range(share):
                 scale = weight if field == 0 else 1.0
-                first = scale * came_first_ref[shot, field, level]
-                last = jnp.where(inside, scale * came_last_ref[shot, field, level], 0.0)
-                wide[shot, field, level, 0:extent, :] = jnp.where(up_first, last, first)
+                low, high = both_sides(sides, [ref[shot, field, level] for ref in came_refs])
+                wide[shot, field, level, 0:extent, :] = scale * low
                 wide[shot, field, level, extent : 2 * extent, :] = (
                     scale * mine_ref[shot, field, level]
                 )
-                wide[shot, field, level, 2 * extent : 3 * extent, :] = jnp.where(
-                    up_first, first, last
-                )
+                wide[shot, field, level, 2 * extent : 3 * extent, :] = scale * high
 
 
 def offset_product(wide, offset, level, total):
@@ -324,10 +316,15 @@
         copy.wait()
 
 
-def image_products(weight, up_first_ref, inside_ref, *rest):
-    groups, (image_hbm, *wides, image_ref, sems) = (rest[0:3], rest[3:6]), rest[6:]
+def image_products(weight, rounds, sides_ref, *rest):
+    groups, begin = [], 0
+    for count in rounds:
+        mine_ref, *came_refs = rest[begin : begin + 1 + count]
+        groups.append((mine_ref, *came_refs[::-1]))
+        begin += 1 + count
+    image_hbm, *wides, image_ref, sems = rest[begin:]
     for blocks, wide in zip(groups, wides):
-        widen(weight, (up_first_ref, inside_ref), blocks, wide)
+        widen(weight, sides_ref, blocks, wide)
     parts = sems.shape[0]
     copies = []
     for piece in range(parts):
@@ -360,10 +357,12 @@
     return lax.ppermute(value, ("tile", "shot"), pairs)
 
 
-def swap_sides(value):
-    tiles = lax.axis_size("tile")
-    came_last = swap_tiles(value, range(1, tiles - 1, 2))
-    return swap_tiles(value, range(0, tiles - 1, 2)), came_last
+def swap_rounds(values):
+    tiles, rounds = lax.axis_size("tile"), len(values)
+    return [
+        swap_tiles(value, range((number - SHIFTS[rounds]) % rounds, tiles - 1, rounds))
+        for number, value in enumerate(values)
+    ]
 
 
 def per_device(
@@ -431,21 +430,17 @@
             )
         )
     )
-    sides = [
-        swap_tiles(message, range(number, tiles - 1, ROUNDS)) for number, message in enumerate(sent)
-    ]
-    source, source_later, up_first, inside, edges, bits = pl.pallas_call(
+    came_sides = swap_rounds(sent)
+    source, source_later, sides, bits = pl.pallas_call(
         functools.partial(source_and_order, width),
         out_shape=(
             struct(levels, extent + 2 * LEAD, across),
             struct(levels, extent, across),
-            jax.ShapeDtypeStruct((8, across), jnp.int32),
-            jax.ShapeDtypeStruct((8, across), jnp.int32),
-            jax.ShapeDtypeStruct((3, 8, across), jnp.int32),
+            jax.ShapeDtypeStruct((4, 8, across), jnp.int32),
             jax.ShapeDtypeStruct((shots.bit_length() - 1, 8, across), jnp.int32),
         ),
         in_specs=[SMEM] + [VMEM] * 2,
-        out_specs=[VMEM] * 6,
+        out_specs=[VMEM] * 4,
         compiler_params=params,
         name="source_and_order",
     )(source_cell, amps, later)
@@ -458,7 +453,7 @@
         scratch_shapes=[scratch(*wide_shape), scratch(*wide_shape)],
         compiler_params=params,
         name="both_steps",
-    )(edges, bits, own, part, later, source, source_later, coef, *sides)
+    )(sides, bits, own, part, later, source, source_later, coef, *came_sides)
     came = [
         lax.ppermute(sent, "shot", [(shot, shot ^ (1 + i)) for shot in range(shots)])
         for i, sent in enumerate(blocks)
@@ -478,8 +473,8 @@
         compiler_params=params,
         name="write_fields",
     )(final)
-    operands, wides = [], []
-    for blocks in ([own_block, came[0]], came[:0:-1]):
+    operands, wides, rounds = [], [], []
+    for blocks, count in (([own_block, came[0]], 2), (came[1:], 3)):
         group = pl.pallas_call(
             stack,
             out_shape=struct(len(blocks), *own_block.shape),
@@ -488,18 +483,18 @@
             compiler_params=params,
             name="stack",
         )(*blocks)
-        fields_first, fields_last = swap_sides(group)
-        operands = [group, fields_last, fields_first, *operands]
+        operands = [group, *swap_rounds([group] * count)[::-1], *operands]
         wides.insert(0, wide_scratch(group))
+        rounds.insert(0, count)
     image = pl.pallas_call(
-        functools.partial(image_products, weight),
+        functools.partial(image_products, weight, rounds),
         out_shape=struct(*image_shape),
-        in_specs=[VMEM] * (2 + len(operands)),
+        in_specs=[VMEM] * (1 + len(operands)),
         out_specs=HBM,
         scratch_shapes=[*wides, scratch(*image_shape), pltpu.SemaphoreType.DMA((11,))],
         compiler_params=params,
         name="image_products",
-    )(up_first, inside, *operands)
+    )(sides, *operands)
     return src_next, rec_next, image
 
 

time: 20.2 us -> 19.9 us (0.985)
  the two profiles are of different devices: /device:TPU:16 before, /device:TPU:0 now
where the time goes in v13:
time: 19.9 us; the launch traced here: 19.7 us
  starting transfers between devices  11.5 us (58%)
  Pallas kernels  3.63 us (18%)
  waiting for transfers between devices  3.17 us (16%)
  between operations  1.35 us (7%)
    ppermute x8, starting transfers between devices, swap_tiles(): return lax.ppermute(value, ('tile', 'shot'), pairs)  9.38 us
    ppermute x8, waiting for transfers between devices, swap_tiles(): return lax.ppermute(value, ('tile', 'shot'), pairs)  3.16 us
    ppermute x3, starting transfers between devices, per_device(): lax.ppermute(sent, 'shot', [(shot, shot ^ 1 + i) for shot in range(shots)])  2.12 us
    pallas_call x1, Pallas kernels, per_device(): pl.pallas_call(own_part, out_shape=(struct(*wavelet.shape), struct(*wide_...  1.47 us
    pallas_call x1, Pallas kernels, per_device(): pl.pallas_call(functools.partial(image_products, weight, rounds), out_sha...  0.94 us
    pallas_call x1, Pallas kernels, per_device(): pl.pallas_call(write_fields, out_shape=(struct(1, levels, extent, across)...  0.67 us
    pallas_call x1, Pallas kernels, per_device(): pl.pallas_call(both_steps, out_shape=(struct(2, levels, extent, across),...  0.45 us
  transfers between devices with their start and end apart: 11, of which 2 were waited for; matrix products, arithmetic and copies ran while one was open for 0% of the time, Pallas kernels for 4%

profile of v13, /device:TPU:0, one launch (start us, length us, event | category | flops | bytes accessed | tf_op | source)
XLA Modules:
  0.0 19.7 jit_solution(3623273182270855325)
XLA Ops:
  0.6 1.5 %own_part.1 = (f32[1,2]{1,0:T(1,128)S(1)}, f32[2,8,32,128]{3,2,1,0:T(8,128)S(1)}, f32[2,8,16,128]{3,2,1,0:T(8,128)S(1)}, f32[2,8,16,128]{3,2,1,0:T(8,128)S(1)}, ...) custom-call(f32[1,16]{1,0:T(1,128)} %bitcast.1, ...), custom_call_target="tpu_custom_call" | custom-call | tf_op jit(solution)/shard_map/own_part/pallas_call | solution.py:395
  2.1 3.1 %collective-permute-start = (f32[20,8,128]{2,1,0:T(8,128)S(1)}, f32[20,8,128]{2,1,0:T(8,128)S(1)}, u32[]{:S(2)}, u32[]{:S(2)}) collective-permute-start(f32[20,8,128]{2,1,0:T(8,128)S(1)} %get-tuple-element.31), channel_id=1, source_target_pairs={{0,4},{1,5},{2,6},{3,7},{4,0},{5,1},{6,2},{7,3},{8,9},{9,8},{10,11... | collective-permute-start | bytes 245768 | tf_op jit(solution)/shard_map/ppermute | solution.py:357
  5.2 0.0 collective-permute-start.1
  5.2 0.5 %collective-permute-start.2 = (f32[20,8,128]{2,1,0:T(8,128)S(1)}, f32[20,8,128]{2,1,0:T(8,128)S(1)}, u32[]{:S(2)}, u32[]{:S(2)}) collective-permute-start(f32[20,8,128]{2,1,0:T(8,128)S(1)} %get-tuple-element.33), channel_id=1, source_target_pairs={{0,1},{1,0},{2,3},{3,2},{4,5},{5,4},{6,7},{7,6},{8,12},{9,13},{10,... | collective-permute-start | bytes 245768 | tf_op jit(solution)/shard_map/ppermute | solution.py:357
  6.4 0.1 source_and_order.1
  6.5 1.2 %collective-permute-done.rest_0_ = f32[20,8,128]{2,1,0:T(8,128)S(1)} collective-permute-done((f32[20,8,128]{2,1,0:T(8,128)S(1)}, f32[20,8,128]{2,1,0:T(8,128)S(1)}, u32[]{:S(2)}, u32[]{:S(2)}) %collective-permute-start) | collective-permute-done | bytes 81952 | tf_op jit(solution)/shard_map/ppermute | solution.py:357
  7.6 0.0 collective-permute-done.1.rest_1_
  7.7 0.0 collective-permute-done.2.rest_2_
  7.7 0.4 %both_steps.1 = (f32[2,8,16,128]{3,2,1,0:T(8,128)S(1)}, f32[2,2,16,128]{3,2,1,0:T(8,128)S(1)}, f32[2,2,16,128]{3,2,1,0:T(8,128)S(1)}, f32[2,2,16,128]{3,2,1,0:T(8,128)S(1)}, f32[2,2,16,128]{3,2,1,0:T(8,128)S(1)}) custom-call(s32[4,8,128]{2,1,0:T(8,128)S(1)} %get-tuple-element.24.sides_ref, s32[2,8,128]{2,1,0:T(8,128)S(1)} %get-tuple-element.25.bits_ref, ...), custom_call_target="tpu_custom_call" | custom-call | tf_op jit(solution)/shard_map/both_steps/pallas_call | solution.py:448
  8.1 0.1 collective-permute-start.8
  8.2 2.0 %collective-permute-start.3 = (f32[2,2,16,128]{3,2,1,0:T(8,128)S(1)}, f32[2,2,16,128]{3,2,1,0:T(8,128)S(1)}, u32[]{:S(2)}, u32[]{:S(2)}) collective-permute-start(f32[2,2,16,128]{3,2,1,0:T(8,128)S(1)} %get-tuple-element.37), channel_id=1, source_target_pairs={{0,2},{1,3},{2,0},{3,1},{4,6},{5,7},{6,4},{7,5},{8,10},{9,11},{10,... | collective-permute-start | bytes 98312 | tf_op jit(solution)/shard_map/ppermute | solution.py:458
  10.2 0.1 collective-permute-start.4
  10.2 0.0 collective-permute-done.8.refs_1_
  10.2 0.2 %collective-permute-start.10 = (f32[2,2,2,16,128]{4,3,2,1,0:T(8,128)S(1)}, f32[2,2,2,16,128]{4,3,2,1,0:T(8,128)S(1)}, u32[]{:S(2)}, u32[]{:S(2)}) collective-permute-start(f32[2,2,2,16,128]{4,3,2,1,0:T(8,128)S(1)} %stack.3.rest_4_), channel_id=1, source_target_pairs={{0,1},{1,0},{2,3},{3,2},{4,8},{5,9},{6,10},{7,11},{8,4},{9,5},{10,... | collective-permute-start | bytes 196616 | tf_op jit(solution)/shard_map/ppermute | solution.py:357
  10.5 3.9 %collective-permute-start.9 = (f32[2,2,2,16,128]{4,3,2,1,0:T(8,128)S(1)}, f32[2,2,2,16,128]{4,3,2,1,0:T(8,128)S(1)}, u32[]{:S(2)}, u32[]{:S(2)}) collective-permute-start(f32[2,2,2,16,128]{4,3,2,1,0:T(8,128)S(1)} %stack.3.rest_4_), channel_id=1, source_target_pairs={{0,4},{1,5},{2,6},{3,7},{4,0},{5,1},{6,2},{7,3},{8,12},{9,13},{10,... | collective-permute-start | bytes 196616 | tf_op jit(solution)/shard_map/ppermute | solution.py:357
  14.4 0.0 collective-permute-done.3.refs_0_
  14.4 0.0 collective-permute-done.4.refs_1_
  14.4 1.2 %collective-permute-start.7 = (f32[2,2,2,16,128]{4,3,2,1,0:T(8,128)S(1)}, f32[2,2,2,16,128]{4,3,2,1,0:T(8,128)S(1)}, u32[]{:S(2)}, u32[]{:S(2)}) collective-permute-start(f32[2,2,2,16,128]{4,3,2,1,0:T(8,128)S(1)} %stack.2.rest_0_), channel_id=1, source_target_pairs={{0,4},{1,5},{2,6},{3,7},{4,0},{5,1},{6,2},{7,3},{8,9},{9,8},{10,11... | collective-permute-start | bytes 196616 | tf_op jit(solution)/shard_map/ppermute | solution.py:357
  15.5 0.0 collective-permute-start.6
  15.5 0.5 %collective-permute-start.5 = (f32[2,2,2,16,128]{4,3,2,1,0:T(8,128)S(1)}, f32[2,2,2,16,128]{4,3,2,1,0:T(8,128)S(1)}, u32[]{:S(2)}, u32[]{:S(2)}) collective-permute-start(f32[2,2,2,16,128]{4,3,2,1,0:T(8,128)S(1)} %stack.2.rest_0_), channel_id=1, source_target_pairs={{0,1},{1,0},{2,3},{3,2},{4,5},{5,4},{6,7},{7,6},{8,12},{9,13},{10,... | collective-permute-start | bytes 196616 | tf_op jit(solution)/shard_map/ppermute | solution.py:357
  16.0 0.7 %write_fields.1 = (f32[1,8,16,128]{3,2,1,0:T(8,128)}, f32[1,8,16,128]{3,2,1,0:T(8,128)}) custom-call(f32[2,8,16,128]{3,2,1,0:T(8,128)S(1)} %get-tuple-element.34.final_ref), custom_call_target="tpu_custom_call" | custom-call | tf_op jit(solution)/shard_map/write_fields/pallas_call | solution.py:467
  16.7 0.0 collective-permute-done.10.rest_6_
  16.7 0.0 collective-permute-done.9.rest_5_
  16.7 2.0 %collective-permute-done.7.rest_3_ = f32[2,2,2,16,128]{4,3,2,1,0:T(8,128)S(1)} collective-permute-done((f32[2,2,2,16,128]{4,3,2,1,0:T(8,128)S(1)}, f32[2,2,2,16,128]{4,3,2,1,0:T(8,128)S(1)}, u32[]{:S(2)}, u32[]{:S(2)}) %collective-permute-start.7) | collective-permute-done | bytes 65568 | tf_op jit(solution)/shard_map/ppermute | solution.py:357
  18.7 0.0 collective-permute-done.6.rest_2_
  18.7 0.0 collective-permute-done.5.rest_1_
  18.7 0.9 %image_products.1 = f32[33,2,16,128]{3,2,1,0:T(8,128)} custom-call(s32[4,8,128]{2,1,0:T(8,128)S(1)} %get-tuple-element.24.sides_ref, f32[2,2,2,16,128]{4,3,2,1,0:T(8,128)S(1)} %stack.2.rest_0_, f32[2,2,2,16,128]{4,3,2,1,0:T(8,128)S(1)} %collective-permute-done.5.rest_1_, f32[2,2,2,16,128]{4,3,2,1,0:T(8,128)S(1)} %collective-permute-done.6.rest_2_, ...), custom_call_target="tpu_custom_call" | custom-call | tf_op jit(solution)/shard_map/image_products/pallas_call | solution.py:489
  (2 shorter events, 0.0 us)
Async XLA Ops:
  2.1 5.5 %collective-permute-start = (f32[20,8,128]{2,1,0:T(8,128)S(1)}, f32[20,8,128]{2,1,0:T(8,128)S(1)}, u32[]{:S(2)}, u32[]{:S(2)}) collective-permute-start(f32[20,8,128]{2,1,0:T(8,128)S(1)} %get-tuple-element.31), channel_id=1, source_target_pairs={{0,4},{1,5},{2,6},{3,7},{4,0},{5,1},{6,2},{7,3},{8,9},{9,8},{10,11... | collective-permute-start | bytes 245768 | tf_op jit(solution)/shard_map/ppermute | solution.py:357
  5.2 2.4 %collective-permute-start.1 = (f32[20,8,128]{2,1,0:T(8,128)S(1)}, f32[20,8,128]{2,1,0:T(8,128)S(1)}, u32[]{:S(2)}, u32[]{:S(2)}) collective-permute-start(f32[20,8,128]{2,1,0:T(8,128)S(1)} %get-tuple-element.32), channel_id=1, source_target_pairs={{0,1},{1,0},{2,3},{3,2},{4,8},{5,9},{6,10},{7,11},{8,4},{9,5},{10,... | collective-permute-start | bytes 245768 | tf_op jit(solution)/shard_map/ppermute | solution.py:357
  5.2 2.4 %collective-permute-start.2 = (f32[20,8,128]{2,1,0:T(8,128)S(1)}, f32[20,8,128]{2,1,0:T(8,128)S(1)}, u32[]{:S(2)}, u32[]{:S(2)}) collective-permute-start(f32[20,8,128]{2,1,0:T(8,128)S(1)} %get-tuple-element.33), channel_id=1, source_target_pairs={{0,1},{1,0},{2,3},{3,2},{4,5},{5,4},{6,7},{7,6},{8,12},{9,13},{10,... | collective-permute-start | bytes 245768 | tf_op jit(solution)/shard_map/ppermute | solution.py:357
  8.1 2.1 %collective-permute-start.8 = (f32[2,2,16,128]{3,2,1,0:T(8,128)S(1)}, f32[2,2,16,128]{3,2,1,0:T(8,128)S(1)}, u32[]{:S(2)}, u32[]{:S(2)}) collective-permute-start(f32[2,2,16,128]{3,2,1,0:T(8,128)S(1)} %get-tuple-element.40), channel_id=1, source_target_pairs={{0,1},{1,0},{2,3},{3,2},{4,5},{5,4},{6,7},{7,6},{8,9},{9,8},{10,11... | collective-permute-start | bytes 98312 | tf_op jit(solution)/shard_map/ppermute | solution.py:458
  8.2 6.2 %collective-permute-start.3 = (f32[2,2,16,128]{3,2,1,0:T(8,128)S(1)}, f32[2,2,16,128]{3,2,1,0:T(8,128)S(1)}, u32[]{:S(2)}, u32[]{:S(2)}) collective-permute-start(f32[2,2,16,128]{3,2,1,0:T(8,128)S(1)} %get-tuple-element.37), channel_id=1, source_target_pairs={{0,2},{1,3},{2,0},{3,1},{4,6},{5,7},{6,4},{7,5},{8,10},{9,11},{10,... | collective-permute-start | bytes 98312 | tf_op jit(solution)/shard_map/ppermute | solution.py:458
  10.2 4.2 %collective-permute-start.4 = (f32[2,2,16,128]{3,2,1,0:T(8,128)S(1)}, f32[2,2,16,128]{3,2,1,0:T(8,128)S(1)}, u32[]{:S(2)}, u32[]{:S(2)}) collective-permute-start(f32[2,2,16,128]{3,2,1,0:T(8,128)S(1)} %get-tuple-element.38), channel_id=1, source_target_pairs={{0,3},{1,2},{2,1},{3,0},{4,7},{5,6},{6,5},{7,4},{8,11},{9,10},{10,... | collective-permute-start | bytes 98312 | tf_op jit(solution)/shard_map/ppermute | solution.py:458
  10.2 6.5 %collective-permute-start.10 = (f32[2,2,2,16,128]{4,3,2,1,0:T(8,128)S(1)}, f32[2,2,2,16,128]{4,3,2,1,0:T(8,128)S(1)}, u32[]{:S(2)}, u32[]{:S(2)}) collective-permute-start(f32[2,2,2,16,128]{4,3,2,1,0:T(8,128)S(1)} %stack.3.rest_4_), channel_id=1, source_target_pairs={{0,1},{1,0},{2,3},{3,2},{4,8},{5,9},{6,10},{7,11},{8,4},{9,5},{10,... | collective-permute-start | bytes 196616 | tf_op jit(solution)/shard_map/ppermute | solution.py:357
  10.5 6.3 %collective-permute-start.9 = (f32[2,2,2,16,128]{4,3,2,1,0:T(8,128)S(1)}, f32[2,2,2,16,128]{4,3,2,1,0:T(8,128)S(1)}, u32[]{:S(2)}, u32[]{:S(2)}) collective-permute-start(f32[2,2,2,16,128]{4,3,2,1,0:T(8,128)S(1)} %stack.3.rest_4_), channel_id=1, source_target_pairs={{0,4},{1,5},{2,6},{3,7},{4,0},{5,1},{6,2},{7,3},{8,12},{9,13},{10,... | collective-permute-start | bytes 196616 | tf_op jit(solution)/shard_map/ppermute | solution.py:357
  14.4 4.3 %collective-permute-start.7 = (f32[2,2,2,16,128]{4,3,2,1,0:T(8,128)S(1)}, f32[2,2,2,16,128]{4,3,2,1,0:T(8,128)S(1)}, u32[]{:S(2)}, u32[]{:S(2)}) collective-permute-start(f32[2,2,2,16,128]{4,3,2,1,0:T(8,128)S(1)} %stack.2.rest_0_), channel_id=1, source_target_pairs={{0,4},{1,5},{2,6},{3,7},{4,0},{5,1},{6,2},{7,3},{8,9},{9,8},{10,11... | collective-permute-start | bytes 196616 | tf_op jit(solution)/shard_map/ppermute | solution.py:357
  15.5 3.2 %collective-permute-start.6 = (f32[2,2,2,16,128]{4,3,2,1,0:T(8,128)S(1)}, f32[2,2,2,16,128]{4,3,2,1,0:T(8,128)S(1)}, u32[]{:S(2)}, u32[]{:S(2)}) collective-permute-start(f32[2,2,2,16,128]{4,3,2,1,0:T(8,128)S(1)} %stack.2.rest_0_), channel_id=1, source_target_pairs={{0,1},{1,0},{2,3},{3,2},{4,8},{5,9},{6,10},{7,11},{8,4},{9,5},{10,... | collective-permute-start | bytes 196616 | tf_op jit(solution)/shard_map/ppermute | solution.py:357
  15.5 3.2 %collective-permute-start.5 = (f32[2,2,2,16,128]{4,3,2,1,0:T(8,128)S(1)}, f32[2,2,2,16,128]{4,3,2,1,0:T(8,128)S(1)}, u32[]{:S(2)}, u32[]{:S(2)}) collective-permute-start(f32[2,2,2,16,128]{4,3,2,1,0:T(8,128)S(1)} %stack.2.rest_0_), channel_id=1, source_target_pairs={{0,1},{1,0},{2,3},{3,2},{4,5},{5,4},{6,7},{7,6},{8,12},{9,13},{10,... | collective-permute-start | bytes 196616 | tf_op jit(solution)/shard_map/ppermute | solution.py:357

commit v14 on v13

--- a/solution.py
+++ b/solution.py
@@ -12,7 +12,7 @@
 HALO = 4
 LEAD = 8
 ROUNDS = 3
-SHIFTS = {2: 1, 3: 0}
+SHIFTS = {2: 0, 3: 0}
 
 COEFS = (-205.0 / 72.0, 8.0 / 5.0, -1.0 / 5.0, 8.0 / 315.0, -1.0 / 560.0)
 

time: 19.9 us -> 19.3 us (0.970)
  starting transfers between devices: 11.5 us -> 10.8 us
    ppermute x3, waiting for transfers between devices: 0.01 us -> 1.08 us  [per_device(): lax.ppermute(sent, 'shot', [(shot, shot ^ 1 + i) for shot in range(shots)])]
    ppermute x8, waiting for transfers between devices: 3.16 us -> 2.24 us  [swap_tiles(): return lax.ppermute(value, ('tile', 'shot'), pairs)]
    ppermute x8, starting transfers between devices: 9.38 us -> 8.64 us  [swap_tiles(): return lax.ppermute(value, ('tile', 'shot'), pairs)]
  transfers between devices with their start and end apart: 11 -> 11, of which waited for: 2 -> 3; matrix products, arithmetic and copies ran while one was open for 0% -> 0% of each run, Pallas kernels for 4% -> 4%
where the time goes in v14:
time: 19.3 us; the launch traced here: 19.1 us
  starting transfers between devices  10.8 us (56%)
  Pallas kernels  3.63 us (19%)
  waiting for transfers between devices  3.32 us (17%)
  between operations  1.35 us (7%)
    ppermute x8, starting transfers between devices, swap_tiles(): return lax.ppermute(value, ('tile', 'shot'), pairs)  8.64 us
    ppermute x8, waiting for transfers between devices, swap_tiles(): return lax.ppermute(value, ('tile', 'shot'), pairs)  2.24 us
    ppermute x3, starting transfers between devices, per_device(): lax.ppermute(sent, 'shot', [(shot, shot ^ 1 + i) for shot in range(shots)])  2.12 us
    pallas_call x1, Pallas kernels, per_device(): pl.pallas_call(own_part, out_shape=(struct(*wavelet.shape), struct(*wide_...  1.47 us
    ppermute x3, waiting for transfers between devices, per_device(): lax.ppermute(sent, 'shot', [(shot, shot ^ 1 + i) for shot in range(shots)])  1.08 us
    pallas_call x1, Pallas kernels, per_device(): pl.pallas_call(functools.partial(image_products, weight, rounds), out_sha...  0.94 us
    pallas_call x1, Pallas kernels, per_device(): pl.pallas_call(write_fields, out_shape=(struct(1, levels, extent, across)...  0.67 us
    pallas_call x1, Pallas kernels, per_device(): pl.pallas_call(both_steps, out_shape=(struct(2, levels, extent, across),...  0.45 us
  transfers between devices with their start and end apart: 11, of which 3 were waited for; matrix products, arithmetic and copies ran while one was open for 0% of the time, Pallas kernels for 4%

profile of v14, /device:TPU:0, one launch (start us, length us, event | category | flops | bytes accessed | tf_op | source)
XLA Modules:
  0.0 19.1 jit_solution(17888885417080019122)
XLA Ops:
  0.6 1.5 %own_part.1 = (f32[1,2]{1,0:T(1,128)S(1)}, f32[2,8,32,128]{3,2,1,0:T(8,128)S(1)}, f32[2,8,16,128]{3,2,1,0:T(8,128)S(1)}, f32[2,8,16,128]{3,2,1,0:T(8,128)S(1)}, ...) custom-call(f32[1,16]{1,0:T(1,128)} %bitcast.1, ...), custom_call_target="tpu_custom_call" | custom-call | tf_op jit(solution)/shard_map/own_part/pallas_call | solution.py:395
  2.1 3.1 %collective-permute-start = (f32[20,8,128]{2,1,0:T(8,128)S(1)}, f32[20,8,128]{2,1,0:T(8,128)S(1)}, u32[]{:S(2)}, u32[]{:S(2)}) collective-permute-start(f32[20,8,128]{2,1,0:T(8,128)S(1)} %get-tuple-element.31), channel_id=1, source_target_pairs={{0,4},{1,5},{2,6},{3,7},{4,0},{5,1},{6,2},{7,3},{8,9},{9,8},{10,11... | collective-permute-start | bytes 245768 | tf_op jit(solution)/shard_map/ppermute | solution.py:357
  5.2 0.0 collective-permute-start.1
  5.2 0.5 %collective-permute-start.2 = (f32[20,8,128]{2,1,0:T(8,128)S(1)}, f32[20,8,128]{2,1,0:T(8,128)S(1)}, u32[]{:S(2)}, u32[]{:S(2)}) collective-permute-start(f32[20,8,128]{2,1,0:T(8,128)S(1)} %get-tuple-element.33), channel_id=1, source_target_pairs={{0,1},{1,0},{2,3},{3,2},{4,5},{5,4},{6,7},{7,6},{8,12},{9,13},{10,... | collective-permute-start | bytes 245768 | tf_op jit(solution)/shard_map/ppermute | solution.py:357
  6.4 0.1 source_and_order.1
  6.5 1.2 %collective-permute-done.rest_0_ = f32[20,8,128]{2,1,0:T(8,128)S(1)} collective-permute-done((f32[20,8,128]{2,1,0:T(8,128)S(1)}, f32[20,8,128]{2,1,0:T(8,128)S(1)}, u32[]{:S(2)}, u32[]{:S(2)}) %collective-permute-start) | collective-permute-done | bytes 81952 | tf_op jit(solution)/shard_map/ppermute | solution.py:357
  7.6 0.0 collective-permute-done.1.rest_1_
  7.7 0.0 collective-permute-done.2.rest_2_
  7.7 0.4 %both_steps.1 = (f32[2,8,16,128]{3,2,1,0:T(8,128)S(1)}, f32[2,2,16,128]{3,2,1,0:T(8,128)S(1)}, f32[2,2,16,128]{3,2,1,0:T(8,128)S(1)}, f32[2,2,16,128]{3,2,1,0:T(8,128)S(1)}, f32[2,2,16,128]{3,2,1,0:T(8,128)S(1)}) custom-call(s32[4,8,128]{2,1,0:T(8,128)S(1)} %get-tuple-element.24.sides_ref, s32[2,8,128]{2,1,0:T(8,128)S(1)} %get-tuple-element.25.bits_ref, ...), custom_call_target="tpu_custom_call" | custom-call | tf_op jit(solution)/shard_map/both_steps/pallas_call | solution.py:448
  8.1 0.1 collective-permute-start.8
  8.2 2.0 %collective-permute-start.3 = (f32[2,2,16,128]{3,2,1,0:T(8,128)S(1)}, f32[2,2,16,128]{3,2,1,0:T(8,128)S(1)}, u32[]{:S(2)}, u32[]{:S(2)}) collective-permute-start(f32[2,2,16,128]{3,2,1,0:T(8,128)S(1)} %get-tuple-element.37), channel_id=1, source_target_pairs={{0,2},{1,3},{2,0},{3,1},{4,6},{5,7},{6,4},{7,5},{8,10},{9,11},{10,... | collective-permute-start | bytes 98312 | tf_op jit(solution)/shard_map/ppermute | solution.py:458
  10.2 0.1 collective-permute-start.4
  10.2 0.0 collective-permute-done.8.refs_1_
  10.2 2.1 %collective-permute-start.10 = (f32[2,2,2,16,128]{4,3,2,1,0:T(8,128)S(1)}, f32[2,2,2,16,128]{4,3,2,1,0:T(8,128)S(1)}, u32[]{:S(2)}, u32[]{:S(2)}) collective-permute-start(f32[2,2,2,16,128]{4,3,2,1,0:T(8,128)S(1)} %stack.3.rest_4_), channel_id=1, source_target_pairs={{0,4},{1,5},{2,6},{3,7},{4,0},{5,1},{6,2},{7,3},{8,12},{9,13},{10,... | collective-permute-start | bytes 196616 | tf_op jit(solution)/shard_map/ppermute | solution.py:357
  12.4 0.1 collective-permute-start.9
  12.4 0.0 collective-permute-done.3.refs_0_
  12.4 1.1 %collective-permute-done.4.refs_1_ = f32[2,2,16,128]{3,2,1,0:T(8,128)S(1)} collective-permute-done((f32[2,2,16,128]{3,2,1,0:T(8,128)S(1)}, f32[2,2,16,128]{3,2,1,0:T(8,128)S(1)}, u32[]{:S(2)}, u32[]{:S(2)}) %collective-permute-start.4) | collective-permute-done | bytes 32800 | tf_op jit(solution)/shard_map/ppermute | solution.py:458
  13.5 2.3 %collective-permute-start.7 = (f32[2,2,2,16,128]{4,3,2,1,0:T(8,128)S(1)}, f32[2,2,2,16,128]{4,3,2,1,0:T(8,128)S(1)}, u32[]{:S(2)}, u32[]{:S(2)}) collective-permute-start(f32[2,2,2,16,128]{4,3,2,1,0:T(8,128)S(1)} %stack.2.rest_0_), channel_id=1, source_target_pairs={{0,4},{1,5},{2,6},{3,7},{4,0},{5,1},{6,2},{7,3},{8,9},{9,8},{10,11... | collective-permute-start | bytes 196616 | tf_op jit(solution)/shard_map/ppermute | solution.py:357
  15.9 0.0 collective-permute-start.6
  15.9 0.5 %collective-permute-start.5 = (f32[2,2,2,16,128]{4,3,2,1,0:T(8,128)S(1)}, f32[2,2,2,16,128]{4,3,2,1,0:T(8,128)S(1)}, u32[]{:S(2)}, u32[]{:S(2)}) collective-permute-start(f32[2,2,2,16,128]{4,3,2,1,0:T(8,128)S(1)} %stack.2.rest_0_), channel_id=1, source_target_pairs={{0,1},{1,0},{2,3},{3,2},{4,5},{5,4},{6,7},{7,6},{8,12},{9,13},{10,... | collective-permute-start | bytes 196616 | tf_op jit(solution)/shard_map/ppermute | solution.py:357
  16.4 0.7 %write_fields.1 = (f32[1,8,16,128]{3,2,1,0:T(8,128)}, f32[1,8,16,128]{3,2,1,0:T(8,128)}) custom-call(f32[2,8,16,128]{3,2,1,0:T(8,128)S(1)} %get-tuple-element.34.final_ref), custom_call_target="tpu_custom_call" | custom-call | tf_op jit(solution)/shard_map/write_fields/pallas_call | solution.py:467
  17.0 0.0 collective-permute-done.10.rest_6_
  17.1 0.0 collective-permute-done.9.rest_5_
  17.1 1.0 %collective-permute-done.7.rest_3_ = f32[2,2,2,16,128]{4,3,2,1,0:T(8,128)S(1)} collective-permute-done((f32[2,2,2,16,128]{4,3,2,1,0:T(8,128)S(1)}, f32[2,2,2,16,128]{4,3,2,1,0:T(8,128)S(1)}, u32[]{:S(2)}, u32[]{:S(2)}) %collective-permute-start.7) | collective-permute-done | bytes 65568 | tf_op jit(solution)/shard_map/ppermute | solution.py:357
  18.1 0.0 collective-permute-done.6.rest_2_
  18.1 0.0 collective-permute-done.5.rest_1_
  18.1 0.9 %image_products.1 = f32[33,2,16,128]{3,2,1,0:T(8,128)} custom-call(s32[4,8,128]{2,1,0:T(8,128)S(1)} %get-tuple-element.24.sides_ref, f32[2,2,2,16,128]{4,3,2,1,0:T(8,128)S(1)} %stack.2.rest_0_, f32[2,2,2,16,128]{4,3,2,1,0:T(8,128)S(1)} %collective-permute-done.5.rest_1_, f32[2,2,2,16,128]{4,3,2,1,0:T(8,128)S(1)} %collective-permute-done.6.rest_2_, ...), custom_call_target="tpu_custom_call" | custom-call | tf_op jit(solution)/shard_map/image_products/pallas_call | solution.py:489
  (2 shorter events, 0.0 us)
Async XLA Ops:
  2.1 5.5 %collective-permute-start = (f32[20,8,128]{2,1,0:T(8,128)S(1)}, f32[20,8,128]{2,1,0:T(8,128)S(1)}, u32[]{:S(2)}, u32[]{:S(2)}) collective-permute-start(f32[20,8,128]{2,1,0:T(8,128)S(1)} %get-tuple-element.31), channel_id=1, source_target_pairs={{0,4},{1,5},{2,6},{3,7},{4,0},{5,1},{6,2},{7,3},{8,9},{9,8},{10,11... | collective-permute-start | bytes 245768 | tf_op jit(solution)/shard_map/ppermute | solution.py:357
  5.2 2.4 %collective-permute-start.1 = (f32[20,8,128]{2,1,0:T(8,128)S(1)}, f32[20,8,128]{2,1,0:T(8,128)S(1)}, u32[]{:S(2)}, u32[]{:S(2)}) collective-permute-start(f32[20,8,128]{2,1,0:T(8,128)S(1)} %get-tuple-element.32), channel_id=1, source_target_pairs={{0,1},{1,0},{2,3},{3,2},{4,8},{5,9},{6,10},{7,11},{8,4},{9,5},{10,... | collective-permute-start | bytes 245768 | tf_op jit(solution)/shard_map/ppermute | solution.py:357
  5.2 2.4 %collective-permute-start.2 = (f32[20,8,128]{2,1,0:T(8,128)S(1)}, f32[20,8,128]{2,1,0:T(8,128)S(1)}, u32[]{:S(2)}, u32[]{:S(2)}) collective-permute-start(f32[20,8,128]{2,1,0:T(8,128)S(1)} %get-tuple-element.33), channel_id=1, source_target_pairs={{0,1},{1,0},{2,3},{3,2},{4,5},{5,4},{6,7},{7,6},{8,12},{9,13},{10,... | collective-permute-start | bytes 245768 | tf_op jit(solution)/shard_map/ppermute | solution.py:357
  8.1 2.1 %collective-permute-start.8 = (f32[2,2,16,128]{3,2,1,0:T(8,128)S(1)}, f32[2,2,16,128]{3,2,1,0:T(8,128)S(1)}, u32[]{:S(2)}, u32[]{:S(2)}) collective-permute-start(f32[2,2,16,128]{3,2,1,0:T(8,128)S(1)} %get-tuple-element.40), channel_id=1, source_target_pairs={{0,1},{1,0},{2,3},{3,2},{4,5},{5,4},{6,7},{7,6},{8,9},{9,8},{10,11... | collective-permute-start | bytes 98312 | tf_op jit(solution)/shard_map/ppermute | solution.py:458
  8.2 4.3 %collective-permute-start.3 = (f32[2,2,16,128]{3,2,1,0:T(8,128)S(1)}, f32[2,2,16,128]{3,2,1,0:T(8,128)S(1)}, u32[]{:S(2)}, u32[]{:S(2)}) collective-permute-start(f32[2,2,16,128]{3,2,1,0:T(8,128)S(1)} %get-tuple-element.37), channel_id=1, source_target_pairs={{0,2},{1,3},{2,0},{3,1},{4,6},{5,7},{6,4},{7,5},{8,10},{9,11},{10,... | collective-permute-start | bytes 98312 | tf_op jit(solution)/shard_map/ppermute | solution.py:458
  10.2 3.3 %collective-permute-start.4 = (f32[2,2,16,128]{3,2,1,0:T(8,128)S(1)}, f32[2,2,16,128]{3,2,1,0:T(8,128)S(1)}, u32[]{:S(2)}, u32[]{:S(2)}) collective-permute-start(f32[2,2,16,128]{3,2,1,0:T(8,128)S(1)} %get-tuple-element.38), channel_id=1, source_target_pairs={{0,3},{1,2},{2,1},{3,0},{4,7},{5,6},{6,5},{7,4},{8,11},{9,10},{10,... | collective-permute-start | bytes 98312 | tf_op jit(solution)/shard_map/ppermute | solution.py:458
  10.2 6.8 %collective-permute-start.10 = (f32[2,2,2,16,128]{4,3,2,1,0:T(8,128)S(1)}, f32[2,2,2,16,128]{4,3,2,1,0:T(8,128)S(1)}, u32[]{:S(2)}, u32[]{:S(2)}) collective-permute-start(f32[2,2,2,16,128]{4,3,2,1,0:T(8,128)S(1)} %stack.3.rest_4_), channel_id=1, source_target_pairs={{0,4},{1,5},{2,6},{3,7},{4,0},{5,1},{6,2},{7,3},{8,12},{9,13},{10,... | collective-permute-start | bytes 196616 | tf_op jit(solution)/shard_map/ppermute | solution.py:357
  12.4 4.7 %collective-permute-start.9 = (f32[2,2,2,16,128]{4,3,2,1,0:T(8,128)S(1)}, f32[2,2,2,16,128]{4,3,2,1,0:T(8,128)S(1)}, u32[]{:S(2)}, u32[]{:S(2)}) collective-permute-start(f32[2,2,2,16,128]{4,3,2,1,0:T(8,128)S(1)} %stack.3.rest_4_), channel_id=1, source_target_pairs={{0,1},{1,0},{2,3},{3,2},{4,8},{5,9},{6,10},{7,11},{8,4},{9,5},{10,... | collective-permute-start | bytes 196616 | tf_op jit(solution)/shard_map/ppermute | solution.py:357
  13.5 4.6 %collective-permute-start.7 = (f32[2,2,2,16,128]{4,3,2,1,0:T(8,128)S(1)}, f32[2,2,2,16,128]{4,3,2,1,0:T(8,128)S(1)}, u32[]{:S(2)}, u32[]{:S(2)}) collective-permute-start(f32[2,2,2,16,128]{4,3,2,1,0:T(8,128)S(1)} %stack.2.rest_0_), channel_id=1, source_target_pairs={{0,4},{1,5},{2,6},{3,7},{4,0},{5,1},{6,2},{7,3},{8,9},{9,8},{10,11... | collective-permute-start | bytes 196616 | tf_op jit(solution)/shard_map/ppermute | solution.py:357
  15.9 2.2 %collective-permute-start.6 = (f32[2,2,2,16,128]{4,3,2,1,0:T(8,128)S(1)}, f32[2,2,2,16,128]{4,3,2,1,0:T(8,128)S(1)}, u32[]{:S(2)}, u32[]{:S(2)}) collective-permute-start(f32[2,2,2,16,128]{4,3,2,1,0:T(8,128)S(1)} %stack.2.rest_0_), channel_id=1, source_target_pairs={{0,1},{1,0},{2,3},{3,2},{4,8},{5,9},{6,10},{7,11},{8,4},{9,5},{10,... | collective-permute-start | bytes 196616 | tf_op jit(solution)/shard_map/ppermute | solution.py:357
  15.9 2.2 %collective-permute-start.5 = (f32[2,2,2,16,128]{4,3,2,1,0:T(8,128)S(1)}, f32[2,2,2,16,128]{4,3,2,1,0:T(8,128)S(1)}, u32[]{:S(2)}, u32[]{:S(2)}) collective-permute-start(f32[2,2,2,16,128]{4,3,2,1,0:T(8,128)S(1)} %stack.2.rest_0_), channel_id=1, source_target_pairs={{0,1},{1,0},{2,3},{3,2},{4,5},{5,4},{6,7},{7,6},{8,12},{9,13},{10,... | collective-permute-start | bytes 196616 | tf_op jit(solution)/shard_map/ppermute | solution.py:357

commit v15 on v14

--- a/solution.py
+++ b/solution.py
@@ -30,54 +30,48 @@
     return after, before
 
 
-def laplace_level(wide, field, level, levels, extent, weights):
+def lane_sum(centre, weights):
     after, before = weights
-    centre = wide[field, level, LEAD : LEAD + extent, :]
     across = centre.shape[1]
     total = 3.0 * COEFS[0] * centre
     for k in range(1, HALO + 1):
-        beside = (
-            wide[field, level, LEAD + k : LEAD + k + extent, :]
-            + wide[field, level, LEAD - k : LEAD - k + extent, :]
-        )
-        if level + k < levels:
-            beside = beside + wide[field, level + k, LEAD : LEAD + extent, :]
-        if level - k >= 0:
-            beside = beside + wide[field, level - k, LEAD : LEAD + extent, :]
-        total = total + COEFS[k] * beside
         total = total + after[k - 1] * pltpu.roll(centre, across - k, 1)
         total = total + before[k - 1] * pltpu.roll(centre, k, 1)
     return total
 
 
-def source_and_order(
-    width, cell_ref, amps_ref, later_ref, source_ref, source_later_ref, sides_ref, bits_ref
-):
-    levels, extent, across = source_later_ref.shape
-    cell = cell_ref[0]
-    deep = lax.div(cell, width * across)
-    row = lax.rem(lax.div(cell, across), width) - lax.axis_index("tile") * extent + LEAD
-    shape = (extent + 2 * LEAD, across)
-    rows = lax.broadcasted_iota(jnp.int32, shape, 0)
-    lanes = lax.broadcasted_iota(jnp.int32, shape, 1)
-    hit = jnp.where((rows == row) & (lanes == lax.rem(cell, across)), 1.0, 0.0)
-    for level in range(levels):
-        here = hit * jnp.where(deep == level, 1.0, 0.0)
-        source_ref[level] = here * amps_ref[0:1, 0:1]
-        source_later_ref[level] = (
-            later_ref[0, level] + here[LEAD : LEAD + extent, :] * amps_ref[0:1, 1:2]
+def beside_sum(wide, field, level, begin, count):
+    total = None
+    for k in range(1, HALO + 1):
+        pair = (
+            wide[field, level, begin + k : begin + k + count, :]
+            + wide[field, level, begin - k : begin - k + count, :]
         )
-    tile, tiles = lax.axis_index("tile"), lax.axis_size("tile")
-    places = (jnp.where(tile > 0, 1, 0), jnp.where(tile < tiles - 1, 1, 0))
-    places += tuple((tile + SHIFTS[rounds]) % rounds for rounds in (2, 3))
-    for place, value in enumerate(places):
-        sides_ref[place] = jnp.full(sides_ref.shape[1:], value, dtype=jnp.int32)
-    shot = jnp.full(bits_ref.shape[1:], lax.axis_index("shot"), dtype=jnp.int32)
-    for bit in range(bits_ref.shape[0]):
-        bits_ref[bit] = shot & (1 << bit)
-
-
-def own_part(
+        total = COEFS[k] * pair if total is None else total + COEFS[k] * pair
+    return total
+
+
+def depth_sum(rows_of, level, levels, total):
+    for k in range(1, HALO + 1):
+        for near in (level - k, level + k):
+            if 0 <= near < levels:
+                total = total + COEFS[k] * rows_of(near)
+    return total
+
+
+def laplace_level(wide, field, level, levels, extent, weights):
+    def rows_of(near):
+        return wide[field, near, LEAD : LEAD + extent, :]
+
+    total = lane_sum(rows_of(level), weights) + beside_sum(wide, field, level, LEAD, extent)
+    return depth_sum(rows_of, level, levels, total)
+
+
+def is_low(across):
+    return lax.broadcasted_iota(jnp.int32, (8, across), 0) < HALO
+
+
+def own_edges(
     table_hbm,
     spots_hbm,
     traces_hbm,
@@ -89,16 +83,15 @@
     rec_prev,
     amps_ref,
     wide,
-    part_ref,
-    later_ref,
-    coef_ref,
+    prev_ref,
+    ids_ref,
+    speeds_ref,
+    planes_ref,
     *rest,
 ):
     sent_refs, rest = rest[:ROUNDS], rest[ROUNDS:]
-    table, spots_ref, traces_ref, ids_ref, prev_ref, sems = rest
-
+    table, spots_ref, traces_ref, edges, sems = rest
     levels, extent, across = ids_ref.shape
-    shape = (extent, across)
     regions = table_hbm.shape[1]
     end = LEAD + extent
     rows = pl.ds(LEAD, extent)
@@ -123,16 +116,11 @@
         for level in range(levels):
             wide[field, level, 0:LEAD, :] = zeros
             wide[field, level, end : end + LEAD, :] = zeros
-    weights = lane_weights(shape)
+    weights = lane_weights((8, across))
+    low_half = is_low(across)
     my_round = lax.rem(lax.axis_index("tile"), ROUNDS)
     for copy in copies:
         copy.wait()
-
-    def send(place, rows, value):
-        low = value[0:HALO, :]
-        high = value[extent - HALO : extent, :]
-        for number, sent_ref in enumerate(sent_refs):
-            sent_ref[place, rows, :] = jnp.where(my_round == number, high, low)
 
     spots = spots_ref[...]
     column = lax.broadcasted_iota(jnp.int32, (extent, spots.shape[1]), 0) * across
@@ -149,33 +137,130 @@
         precision=lax.Precision.HIGHEST,
         preferred_element_type=jnp.float32,
     )
+    planes_ref[...] = planes
+
+    def send(place, low, high):
+        for number, sent_ref in enumerate(sent_refs):
+            sent_ref[place] = jnp.where(my_round == number, high, low)
+
+    def halves(ref, *place):
+        return jnp.where(
+            low_half, ref[(*place, pl.ds(0, 8))], ref[(*place, pl.ds(extent - 8, 8))]
+        )
 
     speeds = jnp.concatenate(
         [table[...], jnp.zeros((1, across - regions), jnp.float32)], axis=1
     )
     speeds = jnp.broadcast_to(speeds, (8, across))
+    speeds_ref[...] = speeds
+    coefs = [
+        jnp.take_along_axis(speeds, halves(ids_ref, level), axis=1, mode="promise_in_bounds")
+        for level in range(levels)
+    ]
+    for level in range(0, levels, 2):
+        here, after = coefs[level], coefs[level + 1]
+        send(
+            2 * levels + level // 2,
+            jnp.where(low_half, here, pltpu.roll(after, HALO, 0)),
+            jnp.where(low_half, pltpu.roll(here, HALO, 0), after),
+        )
+
+    for field in range(2):
+        for level in range(levels):
+            edges[field, level] = jnp.where(
+                low_half, wide[field, level, LEAD : LEAD + 8, :], wide[field, level, end - 8 : end, :]
+            )
+    for field in range(2):
+        for level in range(levels):
+            now = edges[field, level]
+            total = lane_sum(now, weights) + jnp.where(
+                low_half,
+                beside_sum(wide, field, level, LEAD, 8),
+                beside_sum(wide, field, level, end - 8, 8),
+            )
+            total = depth_sum(lambda near: edges[field, near], level, levels, total)
+            value = 2.0 * now - halves(prev_ref, field, level) + coefs[level] * total
+            if field == 1 and level == 0:
+                value = value + jnp.where(low_half, planes[0:8, :], planes[extent - 8 : extent, :])
+            send(
+                field * levels + level,
+                jnp.where(low_half, now, pltpu.roll(value, HALO, 0)),
+                jnp.where(low_half, pltpu.roll(now, HALO, 0), value),
+            )
+
+
+def own_steps(
+    width,
+    cell_ref,
+    amps_ref,
+    own,
+    prev_ref,
+    ids_ref,
+    speeds_ref,
+    planes_ref,
+    coef_ref,
+    steps_ref,
+    outside_ref,
+    source_ref,
+    sides_ref,
+    bits_ref,
+    middle,
+):
+    levels, extent, across = ids_ref.shape
+    end = LEAD + extent
+    cell = cell_ref[0]
+    deep = lax.div(cell, width * across)
+    row = lax.rem(lax.div(cell, across), width) - lax.axis_index("tile") * extent + LEAD
+    shape = (extent + 2 * LEAD, across)
+    rows = lax.broadcasted_iota(jnp.int32, shape, 0)
+    lanes = lax.broadcasted_iota(jnp.int32, shape, 1)
+    hit = jnp.where((rows == row) & (lanes == lax.rem(cell, across)), 1.0, 0.0)
+    weights = lane_weights((extent, across))
+    speeds = speeds_ref[...]
+    zeros = jnp.zeros((LEAD, across), jnp.float32)
     for level in range(levels):
-        for row in range(0, extent, 8):
-            ids = ids_ref[level, row : row + 8, :]
-            coef_ref[level, row : row + 8, :] = jnp.take_along_axis(
-                speeds, ids, axis=1, mode="promise_in_bounds"
+        here = hit * jnp.where(deep == level, 1.0, 0.0)
+        source_ref[level] = here * amps_ref[0:1, 0:1]
+        steps_ref[0, level] = here[LEAD:end, :] * amps_ref[0:1, 1:2] - own[0, level, LEAD:end, :]
+        steps_ref[1, level] = -own[1, level, LEAD:end, :]
+        for begin in range(0, extent, 8):
+            coef_ref[level, begin : begin + 8, :] = jnp.take_along_axis(
+                speeds, ids_ref[level, begin : begin + 8, :], axis=1, mode="promise_in_bounds"
             )
-        send(2 * levels + level // 2, pl.ds(level % 2 * HALO, HALO), coef_ref[level])
-
-    for field in range(2):
-        for level in range(levels):
-            total = laplace_level(wide, field, level, levels, extent, weights)
-            now = wide[field, level, LEAD:end, :]
-            value = 2.0 * now - prev_ref[field, level] + coef_ref[level] * total
-            later = -now
-            if field == 1 and level == 0:
-                value = value + planes[:extent, :]
-                later = later + planes[extent:, :]
-            part_ref[field, level] = value
-            later_ref[field, level] = later
-            place = field * levels + level
-            send(place, pl.ds(0, HALO), now)
-            send(place, pl.ds(HALO, HALO), value)
+    steps_ref[1, 0] += planes_ref[extent:, :]
+    for field in range(2):
+        for level in range(levels):
+            total = laplace_level(own, field, level, levels, extent, weights)
+            value = 2.0 * own[field, level, LEAD:end, :] - prev_ref[field, level]
+            value = value + coef_ref[level] * total
+            if field == 0:
+                value = value + source_ref[level, LEAD:end, :]
+            elif level == 0:
+                value = value + planes_ref[:extent, :]
+            middle[field, level, 0:LEAD, :] = zeros
+            middle[field, level, LEAD:end, :] = value
+            middle[field, level, end : end + LEAD, :] = zeros
+            below = above = jnp.zeros((HALO, across), jnp.float32)
+            for k in range(1, HALO + 1):
+                begin = LEAD - HALO + k
+                below = below + COEFS[k] * own[field, level, begin : begin + HALO, :]
+                above = above + COEFS[k] * own[field, level, end - k : end - k + HALO, :]
+            outside_ref[field, level, 0:HALO, :] = below
+            outside_ref[field, level, HALO : 2 * HALO, :] = above
+    for field in range(2):
+        for level in range(levels):
+            total = laplace_level(middle, field, level, levels, extent, weights)
+            steps_ref[field, level] += (
+                2.0 * middle[field, level, LEAD:end, :] + coef_ref[level] * total
+            )
+    tile, tiles = lax.axis_index("tile"), lax.axis_size("tile")
+    places = (jnp.where(tile > 0, 1, 0), jnp.where(tile < tiles - 1, 1, 0))
+    places += tuple((tile + SHIFTS[rounds]) % rounds for rounds in (2, 3))
+    for place, value in enumerate(places):
+        sides_ref[place] = jnp.full(sides_ref.shape[1:], value, dtype=jnp.int32)
+    shot = jnp.full(bits_ref.shape[1:], lax.axis_index("shot"), dtype=jnp.int32)
+    for bit in range(bits_ref.shape[0]):
+        bits_ref[bit] = shot & (1 << bit)
 
 
 def both_sides(sides, came):
@@ -187,72 +272,65 @@
     return jnp.where(has_low != 0, low, 0.0), jnp.where(has_high != 0, high, 0.0)
 
 
-def both_steps(
-    sides_ref,
-    bits_ref,
-    own,
-    part_ref,
-    later_ref,
-    source_ref,
-    source_later_ref,
-    coef_ref,
-    *rest,
+def neighbours_part(
+    sides_ref, bits_ref, steps_ref, outside_ref, source_ref, coef_ref, *rest
 ):
-    came_refs, (final_ref, *blocks, other, middle) = rest[:ROUNDS], rest[ROUNDS:]
+    came_refs, (final_ref, *blocks, other, change, edges) = rest[:ROUNDS], rest[ROUNDS:]
     levels, extent, across = coef_ref.shape
-    shape = (extent, across)
     share = blocks[0].shape[1]
     end = LEAD + extent
-    sides = [sides_ref[place, 0:HALO, :] for place in range(4)]
-
-    def received(place, rows):
-        return both_sides(sides, [ref[place, rows, :] for ref in came_refs])
-
-    for field in range(2):
-        for level in range(levels):
-            low, high = received(field * levels + level, pl.ds(0, HALO))
-            other[field, level, LEAD:end, :] = jnp.zeros(shape, jnp.float32)
-            other[field, level, LEAD - HALO : LEAD, :] = low
-            other[field, level, end : end + HALO, :] = high
-    for field in range(2):
-        for level in range(levels):
-            below = jnp.zeros((HALO, across), jnp.float32)
-            above = jnp.zeros((HALO, across), jnp.float32)
-            left = jnp.zeros((8, across), jnp.float32)
-            right = jnp.zeros((8, across), jnp.float32)
+    low_half = is_low(across)
+    weights = lane_weights((8, across))
+    sides = [sides_ref[place] for place in range(4)]
+    zeros = jnp.zeros((8, across), jnp.float32)
+
+    def received(place):
+        return both_sides(sides, [ref[place] for ref in came_refs])
+
+    coefs = [received(2 * levels + pair) for pair in range(levels // 2)]
+    for field in range(2):
+        for level in range(levels):
+            low, high = received(field * levels + level)
+            other[field, level, LEAD : LEAD + 8, :] = zeros
+            other[field, level, end - 8 : end, :] = zeros
+            other[field, level, LEAD - HALO : LEAD, :] = low[0:HALO, :]
+            other[field, level, end : end + HALO, :] = high[0:HALO, :]
+            half = slice(level % 2 * HALO, level % 2 * HALO + HALO)
+            low_coef, high_coef = (coef[half, :] for coef in coefs[level // 2])
+            low = low[HALO:, :] + low_coef * outside_ref[field, level, 0:HALO, :]
+            high = high[HALO:, :] + high_coef * outside_ref[field, level, HALO : 2 * HALO, :]
+            if field == 0:
+                low = low + source_ref[level, LEAD - HALO : LEAD, :]
+                high = high + source_ref[level, end : end + HALO, :]
+            change[field, level, LEAD - HALO : LEAD, :] = low
+            change[field, level, end : end + HALO, :] = high
+    for field in range(2):
+        for level in range(levels):
+            left = right = zeros
             for k in range(1, HALO + 1):
-                begin = LEAD - HALO + k
-                below = below + COEFS[k] * own[field, level, begin : begin + HALO, :]
-                above = above + COEFS[k] * own[field, level, end - k : end - k + HALO, :]
                 left = left + COEFS[k] * other[field, level, LEAD - k : LEAD - k + 8, :]
                 right = right + COEFS[k] * other[field, level, end - 8 + k : end + k, :]
-            low, high = received(field * levels + level, pl.ds(HALO, HALO))
-            low_coef, high_coef = received(
-                2 * levels + level // 2, pl.ds(level % 2 * HALO, HALO)
+            left = coef_ref[level, 0:8, :] * left
+            right = coef_ref[level, extent - 8 : extent, :] * right
+            change[field, level, LEAD : LEAD + 8, :] = left
+            change[field, level, end - 8 : end, :] = right
+            edges[field, level] = left + right
+    for field in range(2):
+        for level in range(levels):
+            total = depth_sum(
+                lambda near: edges[field, near],
+                level,
+                levels,
+                lane_sum(edges[field, level], weights),
             )
-            low = low + low_coef * below
-            high = high + high_coef * above
-            left = part_ref[field, level, 0:8, :] + coef_ref[level, 0:8, :] * left
-            right = (
-                part_ref[field, level, extent - 8 : extent, :]
-                + coef_ref[level, extent - 8 : extent, :] * right
-            )
-            if field == 0:
-                low = low + source_ref[level, LEAD - HALO : LEAD, :]
-                left = left + source_ref[level, LEAD : LEAD + 8, :]
-                right = right + source_ref[level, end - 8 : end, :]
-                high = high + source_ref[level, end : end + HALO, :]
-            middle[field, level, LEAD - HALO : LEAD, :] = low
-            middle[field, level, LEAD : LEAD + 8, :] = left
-            middle[field, level, end - 8 : end, :] = right
-            middle[field, level, end : end + HALO, :] = high
-    weights = lane_weights(shape)
-    for field in range(2):
-        for level in range(levels):
-            total = laplace_level(middle, field, level, levels, extent, weights)
-            later = source_later_ref[level] if field == 0 else later_ref[field, level]
-            value = 2.0 * middle[field, level, LEAD:end, :] + later
-            final_ref[field, level] = value + coef_ref[level] * total
+            for begin, mine in ((0, low_half), (extent - 8, ~low_half)):
+                part = beside_sum(change, field, level, LEAD + begin, 8)
+                part = part + jnp.where(mine, total, 0.0)
+                final_ref[field, level, begin : begin + 8, :] = (
+                    steps_ref[field, level, begin : begin + 8, :]
+                    + 2.0 * change[field, level, LEAD + begin : LEAD + begin + 8, :]
+                    + coef_ref[level, begin : begin + 8, :] * part
+                )
     masks = [
         jnp.concatenate([bits_ref[bit]] * (extent // 8), axis=0) != 0
         for bit in range(bits_ref.shape[0])
@@ -392,28 +470,29 @@
 
     wide_shape = (2, levels, extent + 2 * LEAD, across)
     message = struct(2 * levels + levels // 2, 2 * HALO, across)
-    amps, own, part, later, coef, *sent = pl.pallas_call(
-        own_part,
+    fields_shape = (2, levels, extent, across)
+    amps, own, prev, ids, speeds, planes, *sent = pl.pallas_call(
+        own_edges,
         out_shape=(
             struct(*wavelet.shape),
             struct(*wide_shape),
-            struct(2, levels, extent, across),
-            struct(2, levels, extent, across),
-            struct(levels, extent, across),
+            struct(*fields_shape),
+            jax.ShapeDtypeStruct(region_ids.shape, jnp.int32),
+            struct(8, across),
+            struct(2 * extent, across),
             *([message] * ROUNDS),
         ),
         in_specs=[HBM] * 9,
-        out_specs=[VMEM] * (5 + ROUNDS),
+        out_specs=[VMEM] * (6 + ROUNDS),
         scratch_shapes=[
             scratch(1, speed_table.shape[0]),
             scratch(*receiver_cell.shape, dtype=jnp.int32),
             scratch(*receiver_data.shape),
-            scratch(levels, extent, across, dtype=jnp.int32),
-            scratch(2, levels, extent, across),
+            scratch(2, levels, 8, across),
             pltpu.SemaphoreType.DMA((14,)),
         ],
         compiler_params=params,
-        name="own_part",
+        name="own_edges",
     )(
         *(
             pltpu.with_memory_space_constraint(array, pltpu.HBM)
@@ -431,29 +510,36 @@
         )
     )
     came_sides = swap_rounds(sent)
-    source, source_later, sides, bits = pl.pallas_call(
-        functools.partial(source_and_order, width),
+    coef, steps, outside, source, sides, bits = pl.pallas_call(
+        functools.partial(own_steps, width),
         out_shape=(
+            struct(levels, extent, across),
+            struct(*fields_shape),
+            struct(2, levels, 2 * HALO, across),
             struct(levels, extent + 2 * LEAD, across),
-            struct(levels, extent, across),
             jax.ShapeDtypeStruct((4, 8, across), jnp.int32),
             jax.ShapeDtypeStruct((shots.bit_length() - 1, 8, across), jnp.int32),
         ),
-        in_specs=[SMEM] + [VMEM] * 2,
-        out_specs=[VMEM] * 4,
+        in_specs=[SMEM] + [VMEM] * 6,
+        out_specs=[VMEM] * 6,
+        scratch_shapes=[scratch(*wide_shape)],
         compiler_params=params,
-        name="source_and_order",
-    )(source_cell, amps, later)
+        name="own_steps",
+    )(source_cell, amps, own, prev, ids, speeds, planes)
     block = struct(2, share, extent, across)
     final, own_block, *blocks = pl.pallas_call(
-        both_steps,
-        out_shape=(struct(2, levels, extent, across), *([block] * shots)),
-        in_specs=[VMEM] * (8 + ROUNDS),
+        neighbours_part,
+        out_shape=(struct(*fields_shape), *([block] * shots)),
+        in_specs=[VMEM] * (6 + ROUNDS),
         out_specs=[VMEM] * (1 + shots),
-        scratch_shapes=[scratch(*wide_shape), scratch(*wide_shape)],
+        scratch_shapes=[
+            scratch(*wide_shape),
+            scratch(*wide_shape),
+            scratch(2, levels, 8, across),
+        ],
         compiler_params=params,
-        name="both_steps",
-    )(sides, bits, own, part, later, source, source_later, coef, *came_sides)
+        name="neighbours_part",
+    )(sides, bits, steps, outside, source, coef, *came_sides)
     came = [
         lax.ppermute(sent, "shot", [(shot, shot ^ (1 + i)) for shot in range(shots)])
         for i, sent in enumerate(blocks)

time: 19.3 us -> 19 us (0.984)
  waiting for transfers between devices: 3.32 us -> 2.69 us
  Pallas kernels: 3.63 us -> 3.95 us
    ppermute x8, waiting for transfers between devices: 2.24 us -> 1.61 us  [swap_tiles(): return lax.ppermute(value, ('tile', 'shot'), pairs)]
    pallas_call x3, Pallas kernels: 2.01 us -> 2.33 us  [the longest x1 1.33 us: per_device(): pl.pallas_call(own_edges, out_shape=(struct(*wavelet.shape), struct(*wide...]
  transfers between devices with their start and end apart: 11 -> 11, of which waited for: 3 -> 3; matrix products, arithmetic and copies ran while one was open for 0% -> 0% of each run, Pallas kernels for 4% -> 7%
where the time goes in v15:
time: 19 us; the launch traced here: 18.8 us
  starting transfers between devices  10.8 us (57%)
  Pallas kernels  3.95 us (21%)
  waiting for transfers between devices  2.69 us (14%)
  between operations  1.35 us (7%)
    ppermute x8, starting transfers between devices, swap_tiles(): return lax.ppermute(value, ('tile', 'shot'), pairs)  8.64 us
    ppermute x3, starting transfers between devices, per_device(): lax.ppermute(sent, 'shot', [(shot, shot ^ 1 + i) for shot in range(shots)])  2.12 us
    ppermute x8, waiting for transfers between devices, swap_tiles(): return lax.ppermute(value, ('tile', 'shot'), pairs)  1.61 us
    pallas_call x1, Pallas kernels, per_device(): pl.pallas_call(own_edges, out_shape=(struct(*wavelet.shape), struct(*wide...  1.33 us
    ppermute x3, waiting for transfers between devices, per_device(): lax.ppermute(sent, 'shot', [(shot, shot ^ 1 + i) for shot in range(shots)])  1.08 us
    pallas_call x1, Pallas kernels, per_device(): pl.pallas_call(functools.partial(image_products, weight, rounds), out_sha...  0.94 us
    pallas_call x1, Pallas kernels, per_device(): pl.pallas_call(functools.partial(own_steps, width), out_shape=(struct(lev...  0.72 us
    pallas_call x1, Pallas kernels, per_device(): pl.pallas_call(write_fields, out_shape=(struct(1, levels, extent, across)...  0.67 us
  transfers between devices with their start and end apart: 11, of which 3 were waited for; matrix products, arithmetic and copies ran while one was open for 0% of the time, Pallas kernels for 7%

profile of v15, /device:TPU:0, one launch (start us, length us, event | category | flops | bytes accessed | tf_op | source)
XLA Modules:
  0.0 18.8 jit_solution(7575722402343002504)
XLA Ops:
  0.6 1.3 %own_edges.1 = (f32[1,2]{1,0:T(1,128)S(1)}, f32[2,8,32,128]{3,2,1,0:T(8,128)S(1)}, f32[2,8,16,128]{3,2,1,0:T(8,128)S(1)}, s32[8,16,128]{2,1,0:T(8,128)S(1)}, f32...) custom-call(f32[1,16]{1,0:T(1,128)} %bitcast.1, ...), custom_call_target="tpu_custom_call" | custom-call | tf_op jit(solution)/shard_map/own_edges/pallas_call | solution.py:474
  2.0 3.1 %collective-permute-start = (f32[20,8,128]{2,1,0:T(8,128)S(1)}, f32[20,8,128]{2,1,0:T(8,128)S(1)}, u32[]{:S(2)}, u32[]{:S(2)}) collective-permute-start(f32[20,8,128]{2,1,0:T(8,128)S(1)} %get-tuple-element.37), channel_id=1, source_target_pairs={{0,4},{1,5},{2,6},{3,7},{4,0},{5,1},{6,2},{7,3},{8,9},{9,8},{10,11... | collective-permute-start | bytes 245768 | tf_op jit(solution)/shard_map/ppermute | solution.py:435
  5.1 0.0 collective-permute-start.1
  5.1 0.5 %collective-permute-start.2 = (f32[20,8,128]{2,1,0:T(8,128)S(1)}, f32[20,8,128]{2,1,0:T(8,128)S(1)}, u32[]{:S(2)}, u32[]{:S(2)}) collective-permute-start(f32[20,8,128]{2,1,0:T(8,128)S(1)} %get-tuple-element.39), channel_id=1, source_target_pairs={{0,1},{1,0},{2,3},{3,2},{4,5},{5,4},{6,7},{7,6},{8,12},{9,13},{10,... | collective-permute-start | bytes 245768 | tf_op jit(solution)/shard_map/ppermute | solution.py:435
  6.2 0.7 %own_steps.1 = (f32[8,16,128]{2,1,0:T(8,128)S(1)}, f32[2,8,16,128]{3,2,1,0:T(8,128)S(1)}, f32[2,8,8,128]{3,2,1,0:T(8,128)S(1)}, f32[8,32,128]{2,1,0:T(8,128)S(1)...) custom-call(s32[1]{0:T(128)S(6)} %copy.13.cell_ref, f32[1,2]{1,0:T(1,128)S(1)} %get-tuple-element.25.amps_ref, ...), custom_call_target="tpu_custom_call" | custom-call | tf_op jit(solution)/shard_map/own_steps/pallas_call | solution.py:513
  6.9 0.6 %collective-permute-done.rest_0_ = f32[20,8,128]{2,1,0:T(8,128)S(1)} collective-permute-done((f32[20,8,128]{2,1,0:T(8,128)S(1)}, f32[20,8,128]{2,1,0:T(8,128)S(1)}, u32[]{:S(2)}, u32[]{:S(2)}) %collective-permute-start) | collective-permute-done | bytes 81952 | tf_op jit(solution)/shard_map/ppermute | solution.py:435
  7.5 0.0 collective-permute-done.1.rest_1_
  7.5 0.0 collective-permute-done.2.rest_2_
  7.5 0.3 %neighbours_part.1 = (f32[2,8,16,128]{3,2,1,0:T(8,128)S(1)}, f32[2,2,16,128]{3,2,1,0:T(8,128)S(1)}, f32[2,2,16,128]{3,2,1,0:T(8,128)S(1)}, f32[2,2,16,128]{3,2,1,0:T(8,128)S(1)}, f32[2,2,16,128]{3,2,1,0:T(8,128)S(1)}) custom-call(s32[4,8,128]{2,1,0:T(8,128)S(1)} %get-tuple-element.31.sides_ref, s32[2,8,128]{2,1,0:T(8,128)S(1)} %get-tuple-element.32.bits_ref, ...), custom_call_target="tpu_custom_call" | custom-call | tf_op jit(solution)/shard_map/neighbours_part/pallas_call | solution.py:530
  7.8 0.1 collective-permute-start.8
  7.9 2.0 %collective-permute-start.3 = (f32[2,2,16,128]{3,2,1,0:T(8,128)S(1)}, f32[2,2,16,128]{3,2,1,0:T(8,128)S(1)}, u32[]{:S(2)}, u32[]{:S(2)}) collective-permute-start(f32[2,2,16,128]{3,2,1,0:T(8,128)S(1)} %get-tuple-element.43), channel_id=1, source_target_pairs={{0,2},{1,3},{2,0},{3,1},{4,6},{5,7},{6,4},{7,5},{8,10},{9,11},{10,... | collective-permute-start | bytes 98312 | tf_op jit(solution)/shard_map/ppermute | solution.py:544
  9.9 0.1 collective-permute-start.4
  9.9 0.0 collective-permute-done.8.refs_1_
  9.9 2.1 %collective-permute-start.10 = (f32[2,2,2,16,128]{4,3,2,1,0:T(8,128)S(1)}, f32[2,2,2,16,128]{4,3,2,1,0:T(8,128)S(1)}, u32[]{:S(2)}, u32[]{:S(2)}) collective-permute-start(f32[2,2,2,16,128]{4,3,2,1,0:T(8,128)S(1)} %stack.3.rest_4_), channel_id=1, source_target_pairs={{0,4},{1,5},{2,6},{3,7},{4,0},{5,1},{6,2},{7,3},{8,12},{9,13},{10,... | collective-permute-start | bytes 196616 | tf_op jit(solution)/shard_map/ppermute | solution.py:435
  12.1 0.1 collective-permute-start.9
  12.1 0.0 collective-permute-done.3.refs_0_
  12.1 1.1 %collective-permute-done.4.refs_1_ = f32[2,2,16,128]{3,2,1,0:T(8,128)S(1)} collective-permute-done((f32[2,2,16,128]{3,2,1,0:T(8,128)S(1)}, f32[2,2,16,128]{3,2,1,0:T(8,128)S(1)}, u32[]{:S(2)}, u32[]{:S(2)}) %collective-permute-start.4) | collective-permute-done | bytes 32800 | tf_op jit(solution)/shard_map/ppermute | solution.py:544
  13.2 2.3 %collective-permute-start.7 = (f32[2,2,2,16,128]{4,3,2,1,0:T(8,128)S(1)}, f32[2,2,2,16,128]{4,3,2,1,0:T(8,128)S(1)}, u32[]{:S(2)}, u32[]{:S(2)}) collective-permute-start(f32[2,2,2,16,128]{4,3,2,1,0:T(8,128)S(1)} %stack.2.rest_0_), channel_id=1, source_target_pairs={{0,4},{1,5},{2,6},{3,7},{4,0},{5,1},{6,2},{7,3},{8,9},{9,8},{10,11... | collective-permute-start | bytes 196616 | tf_op jit(solution)/shard_map/ppermute | solution.py:435
  15.6 0.0 collective-permute-start.6
  15.6 0.5 %collective-permute-start.5 = (f32[2,2,2,16,128]{4,3,2,1,0:T(8,128)S(1)}, f32[2,2,2,16,128]{4,3,2,1,0:T(8,128)S(1)}, u32[]{:S(2)}, u32[]{:S(2)}) collective-permute-start(f32[2,2,2,16,128]{4,3,2,1,0:T(8,128)S(1)} %stack.2.rest_0_), channel_id=1, source_target_pairs={{0,1},{1,0},{2,3},{3,2},{4,5},{5,4},{6,7},{7,6},{8,12},{9,13},{10,... | collective-permute-start | bytes 196616 | tf_op jit(solution)/shard_map/ppermute | solution.py:435
  16.1 0.7 %write_fields.1 = (f32[1,8,16,128]{3,2,1,0:T(8,128)}, f32[1,8,16,128]{3,2,1,0:T(8,128)}) custom-call(f32[2,8,16,128]{3,2,1,0:T(8,128)S(1)} %get-tuple-element.40.final_ref), custom_call_target="tpu_custom_call" | custom-call | tf_op jit(solution)/shard_map/write_fields/pallas_call | solution.py:553
  16.7 0.0 collective-permute-done.10.rest_6_
  16.8 0.0 collective-permute-done.9.rest_5_
  16.8 1.0 %collective-permute-done.7.rest_3_ = f32[2,2,2,16,128]{4,3,2,1,0:T(8,128)S(1)} collective-permute-done((f32[2,2,2,16,128]{4,3,2,1,0:T(8,128)S(1)}, f32[2,2,2,16,128]{4,3,2,1,0:T(8,128)S(1)}, u32[]{:S(2)}, u32[]{:S(2)}) %collective-permute-start.7) | collective-permute-done | bytes 65568 | tf_op jit(solution)/shard_map/ppermute | solution.py:435
  17.8 0.0 collective-permute-done.6.rest_2_
  17.8 0.0 collective-permute-done.5.rest_1_
  17.8 0.9 %image_products.1 = f32[33,2,16,128]{3,2,1,0:T(8,128)} custom-call(s32[4,8,128]{2,1,0:T(8,128)S(1)} %get-tuple-element.31.sides_ref, f32[2,2,2,16,128]{4,3,2,1,0:T(8,128)S(1)} %stack.2.rest_0_, f32[2,2,2,16,128]{4,3,2,1,0:T(8,128)S(1)} %collective-permute-done.5.rest_1_, f32[2,2,2,16,128]{4,3,2,1,0:T(8,128)S(1)} %collective-permute-done.6.rest_2_, ...), custom_call_target="tpu_custom_call" | custom-call | tf_op jit(solution)/shard_map/image_products/pallas_call | solution.py:575
  (2 shorter events, 0.0 us)
Async XLA Ops:
  2.0 5.5 %collective-permute-start = (f32[20,8,128]{2,1,0:T(8,128)S(1)}, f32[20,8,128]{2,1,0:T(8,128)S(1)}, u32[]{:S(2)}, u32[]{:S(2)}) collective-permute-start(f32[20,8,128]{2,1,0:T(8,128)S(1)} %get-tuple-element.37), channel_id=1, source_target_pairs={{0,4},{1,5},{2,6},{3,7},{4,0},{5,1},{6,2},{7,3},{8,9},{9,8},{10,11... | collective-permute-start | bytes 245768 | tf_op jit(solution)/shard_map/ppermute | solution.py:435
  5.1 2.4 %collective-permute-start.1 = (f32[20,8,128]{2,1,0:T(8,128)S(1)}, f32[20,8,128]{2,1,0:T(8,128)S(1)}, u32[]{:S(2)}, u32[]{:S(2)}) collective-permute-start(f32[20,8,128]{2,1,0:T(8,128)S(1)} %get-tuple-element.38), channel_id=1, source_target_pairs={{0,1},{1,0},{2,3},{3,2},{4,8},{5,9},{6,10},{7,11},{8,4},{9,5},{10,... | collective-permute-start | bytes 245768 | tf_op jit(solution)/shard_map/ppermute | solution.py:435
  5.1 2.4 %collective-permute-start.2 = (f32[20,8,128]{2,1,0:T(8,128)S(1)}, f32[20,8,128]{2,1,0:T(8,128)S(1)}, u32[]{:S(2)}, u32[]{:S(2)}) collective-permute-start(f32[20,8,128]{2,1,0:T(8,128)S(1)} %get-tuple-element.39), channel_id=1, source_target_pairs={{0,1},{1,0},{2,3},{3,2},{4,5},{5,4},{6,7},{7,6},{8,12},{9,13},{10,... | collective-permute-start | bytes 245768 | tf_op jit(solution)/shard_map/ppermute | solution.py:435
  7.8 2.1 %collective-permute-start.8 = (f32[2,2,16,128]{3,2,1,0:T(8,128)S(1)}, f32[2,2,16,128]{3,2,1,0:T(8,128)S(1)}, u32[]{:S(2)}, u32[]{:S(2)}) collective-permute-start(f32[2,2,16,128]{3,2,1,0:T(8,128)S(1)} %get-tuple-element.46), channel_id=1, source_target_pairs={{0,1},{1,0},{2,3},{3,2},{4,5},{5,4},{6,7},{7,6},{8,9},{9,8},{10,11... | collective-permute-start | bytes 98312 | tf_op jit(solution)/shard_map/ppermute | solution.py:544
  7.9 4.3 %collective-permute-start.3 = (f32[2,2,16,128]{3,2,1,0:T(8,128)S(1)}, f32[2,2,16,128]{3,2,1,0:T(8,128)S(1)}, u32[]{:S(2)}, u32[]{:S(2)}) collective-permute-start(f32[2,2,16,128]{3,2,1,0:T(8,128)S(1)} %get-tuple-element.43), channel_id=1, source_target_pairs={{0,2},{1,3},{2,0},{3,1},{4,6},{5,7},{6,4},{7,5},{8,10},{9,11},{10,... | collective-permute-start | bytes 98312 | tf_op jit(solution)/shard_map/ppermute | solution.py:544
  9.9 3.3 %collective-permute-start.4 = (f32[2,2,16,128]{3,2,1,0:T(8,128)S(1)}, f32[2,2,16,128]{3,2,1,0:T(8,128)S(1)}, u32[]{:S(2)}, u32[]{:S(2)}) collective-permute-start(f32[2,2,16,128]{3,2,1,0:T(8,128)S(1)} %get-tuple-element.44), channel_id=1, source_target_pairs={{0,3},{1,2},{2,1},{3,0},{4,7},{5,6},{6,5},{7,4},{8,11},{9,10},{10,... | collective-permute-start | bytes 98312 | tf_op jit(solution)/shard_map/ppermute | solution.py:544
  9.9 6.8 %collective-permute-start.10 = (f32[2,2,2,16,128]{4,3,2,1,0:T(8,128)S(1)}, f32[2,2,2,16,128]{4,3,2,1,0:T(8,128)S(1)}, u32[]{:S(2)}, u32[]{:S(2)}) collective-permute-start(f32[2,2,2,16,128]{4,3,2,1,0:T(8,128)S(1)} %stack.3.rest_4_), channel_id=1, source_target_pairs={{0,4},{1,5},{2,6},{3,7},{4,0},{5,1},{6,2},{7,3},{8,12},{9,13},{10,... | collective-permute-start | bytes 196616 | tf_op jit(solution)/shard_map/ppermute | solution.py:435
  12.1 4.7 %collective-permute-start.9 = (f32[2,2,2,16,128]{4,3,2,1,0:T(8,128)S(1)}, f32[2,2,2,16,128]{4,3,2,1,0:T(8,128)S(1)}, u32[]{:S(2)}, u32[]{:S(2)}) collective-permute-start(f32[2,2,2,16,128]{4,3,2,1,0:T(8,128)S(1)} %stack.3.rest_4_), channel_id=1, source_target_pairs={{0,1},{1,0},{2,3},{3,2},{4,8},{5,9},{6,10},{7,11},{8,4},{9,5},{10,... | collective-permute-start | bytes 196616 | tf_op jit(solution)/shard_map/ppermute | solution.py:435
  13.2 4.6 %collective-permute-start.7 = (f32[2,2,2,16,128]{4,3,2,1,0:T(8,128)S(1)}, f32[2,2,2,16,128]{4,3,2,1,0:T(8,128)S(1)}, u32[]{:S(2)}, u32[]{:S(2)}) collective-permute-start(f32[2,2,2,16,128]{4,3,2,1,0:T(8,128)S(1)} %stack.2.rest_0_), channel_id=1, source_target_pairs={{0,4},{1,5},{2,6},{3,7},{4,0},{5,1},{6,2},{7,3},{8,9},{9,8},{10,11... | collective-permute-start | bytes 196616 | tf_op jit(solution)/shard_map/ppermute | solution.py:435
  15.6 2.2 %collective-permute-start.6 = (f32[2,2,2,16,128]{4,3,2,1,0:T(8,128)S(1)}, f32[2,2,2,16,128]{4,3,2,1,0:T(8,128)S(1)}, u32[]{:S(2)}, u32[]{:S(2)}) collective-permute-start(f32[2,2,2,16,128]{4,3,2,1,0:T(8,128)S(1)} %stack.2.rest_0_), channel_id=1, source_target_pairs={{0,1},{1,0},{2,3},{3,2},{4,8},{5,9},{6,10},{7,11},{8,4},{9,5},{10,... | collective-permute-start | bytes 196616 | tf_op jit(solution)/shard_map/ppermute | solution.py:435
  15.6 2.2 %collective-permute-start.5 = (f32[2,2,2,16,128]{4,3,2,1,0:T(8,128)S(1)}, f32[2,2,2,16,128]{4,3,2,1,0:T(8,128)S(1)}, u32[]{:S(2)}, u32[]{:S(2)}) collective-permute-start(f32[2,2,2,16,128]{4,3,2,1,0:T(8,128)S(1)} %stack.2.rest_0_), channel_id=1, source_target_pairs={{0,1},{1,0},{2,3},{3,2},{4,5},{5,4},{6,7},{7,6},{8,12},{9,13},{10,... | collective-permute-start | bytes 196616 | tf_op jit(solution)/shard_map/ppermute | solution.py:435

commit v16 on v15

--- a/solution.py
+++ b/solution.py
@@ -275,9 +275,10 @@
 def neighbours_part(
     sides_ref, bits_ref, steps_ref, outside_ref, source_ref, coef_ref, *rest
 ):
-    came_refs, (final_ref, *blocks, other, change, edges) = rest[:ROUNDS], rest[ROUNDS:]
+    came_refs, (final_ref, mine_ref, *blocks, other, change, edges) = rest[:ROUNDS], rest[ROUNDS:]
+    blocks = [mine_ref.at[0], mine_ref.at[1], *blocks]
     levels, extent, across = coef_ref.shape
-    share = blocks[0].shape[1]
+    share = mine_ref.shape[2]
     end = LEAD + extent
     low_half = is_low(across)
     weights = lane_weights((8, across))
@@ -347,28 +348,25 @@
                 block[field, level] = part
 
 
-def widen(weight, sides_ref, blocks, wide):
-    mine_ref, *came_refs = blocks
-    shots, _, share, extent, _ = mine_ref.shape
+def widen(weight, sides_ref, shot, mine_ref, came_refs, wide):
+    _, share, extent, _ = mine_ref.shape
     sides = [
         jnp.concatenate([sides_ref[place]] * (extent // 8), axis=0) for place in range(4)
     ]
-    for shot in range(shots):
-        for field in range(2):
-            for level in range(share):
-                scale = weight if field == 0 else 1.0
-                low, high = both_sides(sides, [ref[shot, field, level] for ref in came_refs])
-                wide[shot, field, level, 0:extent, :] = scale * low
-                wide[shot, field, level, extent : 2 * extent, :] = (
-                    scale * mine_ref[shot, field, level]
-                )
-                wide[shot, field, level, 2 * extent : 3 * extent, :] = scale * high
-
-
-def offset_product(wide, offset, level, total):
+    for field in range(2):
+        for level in range(share):
+            scale = weight if field == 0 else 1.0
+            low, high = both_sides(sides, [ref[field, level] for ref in came_refs])
+            wide[shot, field, level, 0:extent, :] = scale * low
+            wide[shot, field, level, extent : 2 * extent, :] = scale * mine_ref[field, level]
+            wide[shot, field, level, 2 * extent : 3 * extent, :] = scale * high
+
+
+def offset_product(wide, offset, level):
     extent = wide.shape[3] // 3
     lower = extent + REACH - offset
     upper = extent - REACH + offset
+    total = None
     for shot in range(wide.shape[0]):
         product = (
             wide[shot, 0, level, lower : lower + extent, :]
@@ -394,25 +392,24 @@
         copy.wait()
 
 
-def image_products(weight, rounds, sides_ref, *rest):
-    groups, begin = [], 0
-    for count in rounds:
-        mine_ref, *came_refs = rest[begin : begin + 1 + count]
-        groups.append((mine_ref, *came_refs[::-1]))
-        begin += 1 + count
-    image_hbm, *wides, image_ref, sems = rest[begin:]
-    for blocks, wide in zip(groups, wides):
-        widen(weight, sides_ref, blocks, wide)
+def image_products(weight, sides_ref, others_ref, *rest):
+    others_sides, rest = rest[ROUNDS - 1 :: -1], rest[ROUNDS:]
+    mine_ref, last_ref, first_ref, *partner_refs, image_hbm, wide, image_ref, sems = rest
+    places = [
+        (mine_ref.at[0], (first_ref.at[0], last_ref.at[0])),
+        (partner_refs[0], partner_refs[1:]),
+    ]
+    for place in range(others_ref.shape[0]):
+        places.append((others_ref.at[place], [ref.at[place] for ref in others_sides]))
+    for shot, (own_ref, came_refs) in enumerate(places):
+        widen(weight, sides_ref, shot, own_ref, came_refs, wide)
     parts = sems.shape[0]
     copies = []
     for piece in range(parts):
         offsets = range(piece * OFFS // parts, (piece + 1) * OFFS // parts)
         for offset in offsets:
             for level in range(image_ref.shape[1]):
-                total = None
-                for wide in wides:
-                    total = offset_product(wide, offset, level, total)
-                image_ref[offset, level] = total
+                image_ref[offset, level] = offset_product(wide, offset, level)
         rows = pl.ds(offsets[0], len(offsets))
         copy = pltpu.make_async_copy(image_ref.at[rows], image_hbm.at[rows], sems.at[piece])
         copy.start()
@@ -527,11 +524,11 @@
         name="own_steps",
     )(source_cell, amps, own, prev, ids, speeds, planes)
     block = struct(2, share, extent, across)
-    final, own_block, *blocks = pl.pallas_call(
+    final, mine, *blocks = pl.pallas_call(
         neighbours_part,
-        out_shape=(struct(*fields_shape), *([block] * shots)),
+        out_shape=(struct(*fields_shape), struct(2, *block.shape), *([block] * (shots - 2))),
         in_specs=[VMEM] * (6 + ROUNDS),
-        out_specs=[VMEM] * (1 + shots),
+        out_specs=[VMEM] * shots,
         scratch_shapes=[
             scratch(*wide_shape),
             scratch(*wide_shape),
@@ -540,15 +537,12 @@
         compiler_params=params,
         name="neighbours_part",
     )(sides, bits, steps, outside, source, coef, *came_sides)
-    came = [
-        lax.ppermute(sent, "shot", [(shot, shot ^ (1 + i)) for shot in range(shots)])
-        for i, sent in enumerate(blocks)
-    ]
+    def swap_shots(value, number):
+        return lax.ppermute(value, "shot", [(shot, shot ^ number) for shot in range(shots)])
+
+    came = [swap_shots(sent, 2 + i) for i, sent in enumerate(blocks)]
     weight = 1.0 / shots
     image_shape = (OFFS, share, extent, across)
-
-    def wide_scratch(blocks):
-        return scratch(blocks.shape[0], 2, share, 3 * extent, across)
 
     src_next, rec_next = pl.pallas_call(
         write_fields,
@@ -559,25 +553,28 @@
         compiler_params=params,
         name="write_fields",
     )(final)
-    operands, wides, rounds = [], [], []
-    for blocks, count in (([own_block, came[0]], 2), (came[1:], 3)):
-        group = pl.pallas_call(
-            stack,
-            out_shape=struct(len(blocks), *own_block.shape),
-            in_specs=[VMEM] * len(blocks),
-            out_specs=VMEM,
-            compiler_params=params,
-            name="stack",
-        )(*blocks)
-        operands = [group, *swap_rounds([group] * count)[::-1], *operands]
-        wides.insert(0, wide_scratch(group))
-        rounds.insert(0, count)
+    others = pl.pallas_call(
+        stack,
+        out_shape=struct(len(came), *block.shape),
+        in_specs=[VMEM] * len(came),
+        out_specs=VMEM,
+        compiler_params=params,
+        name="stack",
+    )(*came[::-1])
+    mine_sides = swap_rounds([mine] * 2)
+    others_sides = swap_rounds([others] * ROUNDS)
+    partner = [swap_shots(value[1], 1) for value in (mine, *mine_sides)]
+    operands = [others, *others_sides[::-1], mine, *mine_sides[::-1], *partner]
     image = pl.pallas_call(
-        functools.partial(image_products, weight, rounds),
+        functools.partial(image_products, weight),
         out_shape=struct(*image_shape),
         in_specs=[VMEM] * (1 + len(operands)),
         out_specs=HBM,
-        scratch_shapes=[*wides, scratch(*image_shape), pltpu.SemaphoreType.DMA((11,))],
+        scratch_shapes=[
+            scratch(shots, 2, share, 3 * extent, across),
+            scratch(*image_shape),
+            pltpu.SemaphoreType.DMA((11,)),
+        ],
         compiler_params=params,
         name="image_products",
     )(sides, *operands)

time: 19 us -> 19.1 us (level)
  starting transfers between devices: 10.8 us -> 12 us
  waiting for transfers between devices: 2.69 us -> 1.62 us
    ppermute x3 -> x5, starting transfers between devices: 2.12 us -> 3.07 us  [swap_shots(): lax.ppermute(value, 'shot', [(shot, shot ^ number) for shot in range(shot...]
    ppermute x3 -> x5, waiting for transfers between devices: 1.08 us -> 0.25 us  [swap_shots(): lax.ppermute(value, 'shot', [(shot, shot ^ number) for shot in range(shot...]
    ppermute x8, starting transfers between devices: 8.64 us -> 8.91 us  [swap_tiles(): return lax.ppermute(value, ('tile', 'shot'), pairs)]
    ppermute x8, waiting for transfers between devices: 1.61 us -> 1.37 us  [swap_tiles(): return lax.ppermute(value, ('tile', 'shot'), pairs)]
    pallas_call x4 -> x3, Pallas kernels: 1.24 us -> 1.23 us  [the longest x1 0.94 us: per_device(): pl.pallas_call(functools.partial(image_products, weight), out_shape=struc...]
  transfers between devices with their start and end apart: 11 -> 13, of which waited for: 3 -> 3; matrix products, arithmetic and copies ran while one was open for 0% -> 0% of each run, Pallas kernels for 7% -> 7%
where the time goes in v16:
time: 19.1 us; the launch traced here: 18.9 us
  starting transfers between devices  12 us (63%)
  Pallas kernels  3.95 us (21%)
  waiting for transfers between devices  1.62 us (8%)
  between operations  1.33 us (7%)
    ppermute x8, starting transfers between devices, swap_tiles(): return lax.ppermute(value, ('tile', 'shot'), pairs)  8.91 us
    ppermute x5, starting transfers between devices, swap_shots(): lax.ppermute(value, 'shot', [(shot, shot ^ number) for shot in range(shot...  3.07 us
    ppermute x8, waiting for transfers between devices, swap_tiles(): return lax.ppermute(value, ('tile', 'shot'), pairs)  1.37 us
    pallas_call x1, Pallas kernels, per_device(): pl.pallas_call(own_edges, out_shape=(struct(*wavelet.shape), struct(*wide...  1.33 us
    pallas_call x1, Pallas kernels, per_device(): pl.pallas_call(functools.partial(image_products, weight), out_shape=struc...  0.94 us
    pallas_call x1, Pallas kernels, per_device(): pl.pallas_call(functools.partial(own_steps, width), out_shape=(struct(lev...  0.72 us
    pallas_call x1, Pallas kernels, per_device(): pl.pallas_call(write_fields, out_shape=(struct(1, levels, extent, across)...  0.67 us
  transfers between devices with their start and end apart: 13, of which 3 were waited for; matrix products, arithmetic and copies ran while one was open for 0% of the time, Pallas kernels for 7%

profile of v16, /device:TPU:0, one launch (start us, length us, event | category | flops | bytes accessed | tf_op | source)
XLA Modules:
  0.0 18.9 jit_solution(15503065120542227986)
XLA Ops:
  0.6 1.3 %own_edges.1 = (f32[1,2]{1,0:T(1,128)S(1)}, f32[2,8,32,128]{3,2,1,0:T(8,128)S(1)}, f32[2,8,16,128]{3,2,1,0:T(8,128)S(1)}, s32[8,16,128]{2,1,0:T(8,128)S(1)}, f32...) custom-call(f32[1,16]{1,0:T(1,128)} %bitcast.7, ...), custom_call_target="tpu_custom_call" | custom-call | tf_op jit(solution)/shard_map/own_edges/pallas_call | solution.py:471
  2.0 3.1 %collective-permute-start = (f32[20,8,128]{2,1,0:T(8,128)S(1)}, f32[20,8,128]{2,1,0:T(8,128)S(1)}, u32[]{:S(2)}, u32[]{:S(2)}) collective-permute-start(f32[20,8,128]{2,1,0:T(8,128)S(1)} %get-tuple-element.36), channel_id=1, source_target_pairs={{0,4},{1,5},{2,6},{3,7},{4,0},{5,1},{6,2},{7,3},{8,9},{9,8},{10,11... | collective-permute-start | bytes 245768 | tf_op jit(solution)/shard_map/ppermute | solution.py:432
  5.1 0.0 collective-permute-start.1
  5.1 0.5 %collective-permute-start.2 = (f32[20,8,128]{2,1,0:T(8,128)S(1)}, f32[20,8,128]{2,1,0:T(8,128)S(1)}, u32[]{:S(2)}, u32[]{:S(2)}) collective-permute-start(f32[20,8,128]{2,1,0:T(8,128)S(1)} %get-tuple-element.38), channel_id=1, source_target_pairs={{0,1},{1,0},{2,3},{3,2},{4,5},{5,4},{6,7},{7,6},{8,12},{9,13},{10,... | collective-permute-start | bytes 245768 | tf_op jit(solution)/shard_map/ppermute | solution.py:432
  6.2 0.7 %own_steps.1 = (f32[8,16,128]{2,1,0:T(8,128)S(1)}, f32[2,8,16,128]{3,2,1,0:T(8,128)S(1)}, f32[2,8,8,128]{3,2,1,0:T(8,128)S(1)}, f32[8,32,128]{2,1,0:T(8,128)S(1)...) custom-call(s32[1]{0:T(128)S(6)} %copy.13.cell_ref, f32[1,2]{1,0:T(1,128)S(1)} %get-tuple-element.24.amps_ref, ...), custom_call_target="tpu_custom_call" | custom-call | tf_op jit(solution)/shard_map/own_steps/pallas_call | solution.py:510
  6.9 0.6 %collective-permute-done.rest_0_ = f32[20,8,128]{2,1,0:T(8,128)S(1)} collective-permute-done((f32[20,8,128]{2,1,0:T(8,128)S(1)}, f32[20,8,128]{2,1,0:T(8,128)S(1)}, u32[]{:S(2)}, u32[]{:S(2)}) %collective-permute-start) | collective-permute-done | bytes 81952 | tf_op jit(solution)/shard_map/ppermute | solution.py:432
  7.5 0.0 collective-permute-done.1.rest_1_
  7.5 0.0 collective-permute-done.2.rest_2_
  7.5 0.3 %neighbours_part.1 = (f32[2,8,16,128]{3,2,1,0:T(8,128)S(1)}, f32[2,2,2,16,128]{4,3,2,1,0:T(8,128)S(1)}, f32[2,2,16,128]{3,2,1,0:T(8,128)S(1)}, f32[2,2,16,128]{3,2,1,0:T(8,128)S(1)}) custom-call(s32[4,8,128]{2,1,0:T(8,128)S(1)} %get-tuple-element.30.sides_ref, s32[2,8,128]{2,1,0:T(8,128)S(1)} %get-tuple-element.31.bits_ref, ...), custom_call_target="tpu_custom_call" | custom-call | tf_op jit(solution)/shard_map/neighbours_part/pallas_call | solution.py:527
  7.8 0.6 %collective-permute-start.3 = (f32[2,2,16,128]{3,2,1,0:T(8,128)S(1)}, f32[2,2,16,128]{3,2,1,0:T(8,128)S(1)}, u32[]{:S(2)}, u32[]{:S(2)}) collective-permute-start(f32[2,2,16,128]{3,2,1,0:T(8,128)S(1)} %get-tuple-element.42), channel_id=1, source_target_pairs={{0,3},{1,2},{2,1},{3,0},{4,7},{5,6},{6,5},{7,4},{8,11},{9,10},{10,... | collective-permute-start | bytes 98312 | tf_op jit(solution)/shard_map/ppermute | solution.py:541
  8.4 1.4 %collective-permute-start.4 = (f32[2,2,16,128]{3,2,1,0:T(8,128)S(1)}, f32[2,2,16,128]{3,2,1,0:T(8,128)S(1)}, u32[]{:S(2)}, u32[]{:S(2)}) collective-permute-start(f32[2,2,16,128]{3,2,1,0:T(8,128)S(1)} %get-tuple-element.43), channel_id=1, source_target_pairs={{0,2},{1,3},{2,0},{3,1},{4,6},{5,7},{6,4},{7,5},{8,10},{9,11},{10,... | collective-permute-start | bytes 98312 | tf_op jit(solution)/shard_map/ppermute | solution.py:541
  9.9 2.0 %collective-permute-start.9 = (f32[2,2,2,16,128]{4,3,2,1,0:T(8,128)S(1)}, f32[2,2,2,16,128]{4,3,2,1,0:T(8,128)S(1)}, u32[]{:S(2)}, u32[]{:S(2)}) collective-permute-start(f32[2,2,2,16,128]{4,3,2,1,0:T(8,128)S(1)} %get-tuple-element.44.rest_3_), channel_id=1, source_target_pairs={{0,4},{1,5},{2,6},{3,7},{4,0},{5,1},{6,2},{7,3},{8,12},{9,13},{10,... | collective-permute-start | bytes 196616 | tf_op jit(solution)/shard_map/ppermute | solution.py:432
  11.9 0.0 collective-permute-start.8
  11.9 0.5 %collective-permute-start.10 = (f32[2,2,16,128]{3,2,1,0:T(8,128)S(1)}, f32[2,2,16,128]{3,2,1,0:T(8,128)S(1)}, u32[]{:S(2)}, u32[]{:S(2)}) collective-permute-start(f32[2,2,16,128]{3,2,1,0:T(8,128)S(1)} %slice_bitcast_fusion.2), channel_id=1, source_target_pairs={{0,1},{1,0},{2,3},{3,2},{4,5},{5,4},{6,7},{7,6},{8,9},{9,8},{10,11... | collective-permute-start | bytes 98312 | tf_op jit(solution)/shard_map/ppermute | solution.py:541
  12.4 0.0 collective-permute-done.3.refs_0_
  12.4 0.0 collective-permute-done.4.refs_1_
  12.4 2.8 %collective-permute-start.7 = (f32[2,2,2,16,128]{4,3,2,1,0:T(8,128)S(1)}, f32[2,2,2,16,128]{4,3,2,1,0:T(8,128)S(1)}, u32[]{:S(2)}, u32[]{:S(2)}) collective-permute-start(f32[2,2,2,16,128]{4,3,2,1,0:T(8,128)S(1)} %stack.1.others_ref), channel_id=1, source_target_pairs={{0,4},{1,5},{2,6},{3,7},{4,0},{5,1},{6,2},{7,3},{8,9},{9,8},{10,11... | collective-permute-start | bytes 196616 | tf_op jit(solution)/shard_map/ppermute | solution.py:432
  15.2 0.2 %collective-permute-start.6 = (f32[2,2,2,16,128]{4,3,2,1,0:T(8,128)S(1)}, f32[2,2,2,16,128]{4,3,2,1,0:T(8,128)S(1)}, u32[]{:S(2)}, u32[]{:S(2)}) collective-permute-start(f32[2,2,2,16,128]{4,3,2,1,0:T(8,128)S(1)} %stack.1.others_ref), channel_id=1, source_target_pairs={{0,1},{1,0},{2,3},{3,2},{4,8},{5,9},{6,10},{7,11},{8,4},{9,5},{10,... | collective-permute-start | bytes 196616 | tf_op jit(solution)/shard_map/ppermute | solution.py:432
  15.4 0.0 collective-permute-done.9.rest_5_
  15.4 0.3 %collective-permute-start.5 = (f32[2,2,2,16,128]{4,3,2,1,0:T(8,128)S(1)}, f32[2,2,2,16,128]{4,3,2,1,0:T(8,128)S(1)}, u32[]{:S(2)}, u32[]{:S(2)}) collective-permute-start(f32[2,2,2,16,128]{4,3,2,1,0:T(8,128)S(1)} %stack.1.others_ref), channel_id=1, source_target_pairs={{0,1},{1,0},{2,3},{3,2},{4,5},{5,4},{6,7},{7,6},{8,12},{9,13},{10,... | collective-permute-start | bytes 196616 | tf_op jit(solution)/shard_map/ppermute | solution.py:432
  15.7 0.0 collective-permute-done.8.rest_4_
  15.7 0.2 %collective-permute-start.11 = (f32[2,2,16,128]{3,2,1,0:T(8,128)S(1)}, f32[2,2,16,128]{3,2,1,0:T(8,128)S(1)}, u32[]{:S(2)}, u32[]{:S(2)}) collective-permute-start(f32[2,2,16,128]{3,2,1,0:T(8,128)S(1)} %slice_bitcast_fusion.1), channel_id=1, source_target_pairs={{0,1},{1,0},{2,3},{3,2},{4,5},{5,4},{6,7},{7,6},{8,9},{9,8},{10,11... | collective-permute-start | bytes 98312 | tf_op jit(solution)/shard_map/ppermute | solution.py:541
  15.9 0.0 collective-permute-done.10.rest_6_
  15.9 0.3 %collective-permute-start.12 = (f32[2,2,16,128]{3,2,1,0:T(8,128)S(1)}, f32[2,2,16,128]{3,2,1,0:T(8,128)S(1)}, u32[]{:S(2)}, u32[]{:S(2)}) collective-permute-start(f32[2,2,16,128]{3,2,1,0:T(8,128)S(1)} %slice_bitcast_fusion), channel_id=1, source_target_pairs={{0,1},{1,0},{2,3},{3,2},{4,5},{5,4},{6,7},{7,6},{8,9},{9,8},{10,11... | collective-permute-start | bytes 98312 | tf_op jit(solution)/shard_map/ppermute | solution.py:541
  16.2 0.7 %write_fields.1 = (f32[1,8,16,128]{3,2,1,0:T(8,128)}, f32[1,8,16,128]{3,2,1,0:T(8,128)}) custom-call(f32[2,8,16,128]{3,2,1,0:T(8,128)S(1)} %get-tuple-element.39.final_ref), custom_call_target="tpu_custom_call" | custom-call | tf_op jit(solution)/shard_map/write_fields/pallas_call | solution.py:547
  16.9 0.0 collective-permute-done.11.rest_7_
  16.9 0.2 %collective-permute-done.12.rest_8_ = f32[2,2,16,128]{3,2,1,0:T(8,128)S(1)} collective-permute-done((f32[2,2,16,128]{3,2,1,0:T(8,128)S(1)}, f32[2,2,16,128]{3,2,1,0:T(8,128)S(1)}, u32[]{:S(2)}, u32[]{:S(2)}) %collective-permute-start.12) | collective-permute-done | bytes 32800 | tf_op jit(solution)/shard_map/ppermute | solution.py:541
  17.1 0.8 %collective-permute-done.7.rest_2_ = f32[2,2,2,16,128]{4,3,2,1,0:T(8,128)S(1)} collective-permute-done((f32[2,2,2,16,128]{4,3,2,1,0:T(8,128)S(1)}, f32[2,2,2,16,128]{4,3,2,1,0:T(8,128)S(1)}, u32[]{:S(2)}, u32[]{:S(2)}) %collective-permute-start.7) | collective-permute-done | bytes 65568 | tf_op jit(solution)/shard_map/ppermute | solution.py:432
  17.9 0.0 collective-permute-done.6.rest_1_
  17.9 0.0 collective-permute-done.5.rest_0_
  18.0 0.9 %image_products.1 = f32[33,2,16,128]{3,2,1,0:T(8,128)} custom-call(s32[4,8,128]{2,1,0:T(8,128)S(1)} %get-tuple-element.30.sides_ref, f32[2,2,2,16,128]{4,3,2,1,0:T(8,128)S(1)} %stack.1.others_ref, f32[2,2,2,16,128]{4,3,2,1,0:T(8,128)S(1)} %collective-permute-done.5.rest_0_, f32[2,2,2,16,128]{4,3,2,1,0:T(8,128)S(1)} %collective-permute-done.6.rest_1_, ...), custom_call_target="tpu_custom_call" | custom-call | tf_op jit(solution)/shard_map/image_products/pallas_call | solution.py:568
  (4 shorter events, 0.0 us)
Async XLA Ops:
  2.0 5.5 %collective-permute-start = (f32[20,8,128]{2,1,0:T(8,128)S(1)}, f32[20,8,128]{2,1,0:T(8,128)S(1)}, u32[]{:S(2)}, u32[]{:S(2)}) collective-permute-start(f32[20,8,128]{2,1,0:T(8,128)S(1)} %get-tuple-element.36), channel_id=1, source_target_pairs={{0,4},{1,5},{2,6},{3,7},{4,0},{5,1},{6,2},{7,3},{8,9},{9,8},{10,11... | collective-permute-start | bytes 245768 | tf_op jit(solution)/shard_map/ppermute | solution.py:432
  5.1 2.4 %collective-permute-start.1 = (f32[20,8,128]{2,1,0:T(8,128)S(1)}, f32[20,8,128]{2,1,0:T(8,128)S(1)}, u32[]{:S(2)}, u32[]{:S(2)}) collective-permute-start(f32[20,8,128]{2,1,0:T(8,128)S(1)} %get-tuple-element.37), channel_id=1, source_target_pairs={{0,1},{1,0},{2,3},{3,2},{4,8},{5,9},{6,10},{7,11},{8,4},{9,5},{10,... | collective-permute-start | bytes 245768 | tf_op jit(solution)/shard_map/ppermute | solution.py:432
  5.1 2.4 %collective-permute-start.2 = (f32[20,8,128]{2,1,0:T(8,128)S(1)}, f32[20,8,128]{2,1,0:T(8,128)S(1)}, u32[]{:S(2)}, u32[]{:S(2)}) collective-permute-start(f32[20,8,128]{2,1,0:T(8,128)S(1)} %get-tuple-element.38), channel_id=1, source_target_pairs={{0,1},{1,0},{2,3},{3,2},{4,5},{5,4},{6,7},{7,6},{8,12},{9,13},{10,... | collective-permute-start | bytes 245768 | tf_op jit(solution)/shard_map/ppermute | solution.py:432
  7.8 4.6 %collective-permute-start.3 = (f32[2,2,16,128]{3,2,1,0:T(8,128)S(1)}, f32[2,2,16,128]{3,2,1,0:T(8,128)S(1)}, u32[]{:S(2)}, u32[]{:S(2)}) collective-permute-start(f32[2,2,16,128]{3,2,1,0:T(8,128)S(1)} %get-tuple-element.42), channel_id=1, source_target_pairs={{0,3},{1,2},{2,1},{3,0},{4,7},{5,6},{6,5},{7,4},{8,11},{9,10},{10,... | collective-permute-start | bytes 98312 | tf_op jit(solution)/shard_map/ppermute | solution.py:541
  8.4 4.0 %collective-permute-start.4 = (f32[2,2,16,128]{3,2,1,0:T(8,128)S(1)}, f32[2,2,16,128]{3,2,1,0:T(8,128)S(1)}, u32[]{:S(2)}, u32[]{:S(2)}) collective-permute-start(f32[2,2,16,128]{3,2,1,0:T(8,128)S(1)} %get-tuple-element.43), channel_id=1, source_target_pairs={{0,2},{1,3},{2,0},{3,1},{4,6},{5,7},{6,4},{7,5},{8,10},{9,11},{10,... | collective-permute-start | bytes 98312 | tf_op jit(solution)/shard_map/ppermute | solution.py:541
  9.9 5.6 %collective-permute-start.9 = (f32[2,2,2,16,128]{4,3,2,1,0:T(8,128)S(1)}, f32[2,2,2,16,128]{4,3,2,1,0:T(8,128)S(1)}, u32[]{:S(2)}, u32[]{:S(2)}) collective-permute-start(f32[2,2,2,16,128]{4,3,2,1,0:T(8,128)S(1)} %get-tuple-element.44.rest_3_), channel_id=1, source_target_pairs={{0,4},{1,5},{2,6},{3,7},{4,0},{5,1},{6,2},{7,3},{8,12},{9,13},{10,... | collective-permute-start | bytes 196616 | tf_op jit(solution)/shard_map/ppermute | solution.py:432
  11.9 3.8 %collective-permute-start.8 = (f32[2,2,2,16,128]{4,3,2,1,0:T(8,128)S(1)}, f32[2,2,2,16,128]{4,3,2,1,0:T(8,128)S(1)}, u32[]{:S(2)}, u32[]{:S(2)}) collective-permute-start(f32[2,2,2,16,128]{4,3,2,1,0:T(8,128)S(1)} %get-tuple-element.44.rest_3_), channel_id=1, source_target_pairs={{0,1},{1,0},{2,3},{3,2},{4,8},{5,9},{6,10},{7,11},{8,4},{9,5},{10,... | collective-permute-start | bytes 196616 | tf_op jit(solution)/shard_map/ppermute | solution.py:432
  11.9 4.0 %collective-permute-start.10 = (f32[2,2,16,128]{3,2,1,0:T(8,128)S(1)}, f32[2,2,16,128]{3,2,1,0:T(8,128)S(1)}, u32[]{:S(2)}, u32[]{:S(2)}) collective-permute-start(f32[2,2,16,128]{3,2,1,0:T(8,128)S(1)} %slice_bitcast_fusion.2), channel_id=1, source_target_pairs={{0,1},{1,0},{2,3},{3,2},{4,5},{5,4},{6,7},{7,6},{8,9},{9,8},{10,11... | collective-permute-start | bytes 98312 | tf_op jit(solution)/shard_map/ppermute | solution.py:541
  12.4 5.5 %collective-permute-start.7 = (f32[2,2,2,16,128]{4,3,2,1,0:T(8,128)S(1)}, f32[2,2,2,16,128]{4,3,2,1,0:T(8,128)S(1)}, u32[]{:S(2)}, u32[]{:S(2)}) collective-permute-start(f32[2,2,2,16,128]{4,3,2,1,0:T(8,128)S(1)} %stack.1.others_ref), channel_id=1, source_target_pairs={{0,4},{1,5},{2,6},{3,7},{4,0},{5,1},{6,2},{7,3},{8,9},{9,8},{10,11... | collective-permute-start | bytes 196616 | tf_op jit(solution)/shard_map/ppermute | solution.py:432
  15.2 2.8 %collective-permute-start.6 = (f32[2,2,2,16,128]{4,3,2,1,0:T(8,128)S(1)}, f32[2,2,2,16,128]{4,3,2,1,0:T(8,128)S(1)}, u32[]{:S(2)}, u32[]{:S(2)}) collective-permute-start(f32[2,2,2,16,128]{4,3,2,1,0:T(8,128)S(1)} %stack.1.others_ref), channel_id=1, source_target_pairs={{0,1},{1,0},{2,3},{3,2},{4,8},{5,9},{6,10},{7,11},{8,4},{9,5},{10,... | collective-permute-start | bytes 196616 | tf_op jit(solution)/shard_map/ppermute | solution.py:432
  15.4 2.5 %collective-permute-start.5 = (f32[2,2,2,16,128]{4,3,2,1,0:T(8,128)S(1)}, f32[2,2,2,16,128]{4,3,2,1,0:T(8,128)S(1)}, u32[]{:S(2)}, u32[]{:S(2)}) collective-permute-start(f32[2,2,2,16,128]{4,3,2,1,0:T(8,128)S(1)} %stack.1.others_ref), channel_id=1, source_target_pairs={{0,1},{1,0},{2,3},{3,2},{4,5},{5,4},{6,7},{7,6},{8,12},{9,13},{10,... | collective-permute-start | bytes 196616 | tf_op jit(solution)/shard_map/ppermute | solution.py:432
  15.7 1.2 %collective-permute-start.11 = (f32[2,2,16,128]{3,2,1,0:T(8,128)S(1)}, f32[2,2,16,128]{3,2,1,0:T(8,128)S(1)}, u32[]{:S(2)}, u32[]{:S(2)}) collective-permute-start(f32[2,2,16,128]{3,2,1,0:T(8,128)S(1)} %slice_bitcast_fusion.1), channel_id=1, source_target_pairs={{0,1},{1,0},{2,3},{3,2},{4,5},{5,4},{6,7},{7,6},{8,9},{9,8},{10,11... | collective-permute-start | bytes 98312 | tf_op jit(solution)/shard_map/ppermute | solution.py:541
  15.9 1.2 %collective-permute-start.12 = (f32[2,2,16,128]{3,2,1,0:T(8,128)S(1)}, f32[2,2,16,128]{3,2,1,0:T(8,128)S(1)}, u32[]{:S(2)}, u32[]{:S(2)}) collective-permute-start(f32[2,2,16,128]{3,2,1,0:T(8,128)S(1)} %slice_bitcast_fusion), channel_id=1, source_target_pairs={{0,1},{1,0},{2,3},{3,2},{4,5},{5,4},{6,7},{7,6},{8,9},{9,8},{10,11... | collective-permute-start | bytes 98312 | tf_op jit(solution)/shard_map/ppermute | solution.py:541

commit v17 on v15

--- a/solution.py
+++ b/solution.py
@@ -96,15 +96,13 @@
     end = LEAD + extent
     rows = pl.ds(LEAD, extent)
     moves = [(table_hbm, table), (spots_hbm, spots_ref), (traces_hbm, traces_ref)]
-    for begin in range(0, levels, levels // 2):
-        part = pl.ds(begin, levels // 2)
-        moves += [
-            (src_now.at[0, part], wide.at[0, part, rows, :]),
-            (rec_now.at[0, part], wide.at[1, part, rows, :]),
-            (ids_hbm.at[part], ids_ref.at[part]),
-            (src_prev.at[0, part], prev_ref.at[0, part]),
-            (rec_prev.at[0, part], prev_ref.at[1, part]),
-        ]
+    moves += [
+        (src_now.at[0], wide.at[0, :, rows, :]),
+        (rec_now.at[0], wide.at[1, :, rows, :]),
+        (ids_hbm, ids_ref),
+        (src_prev.at[0], prev_ref.at[0]),
+        (rec_prev.at[0], prev_ref.at[1]),
+    ]
     moves.append((amps_hbm, amps_ref))
     copies = [
         pltpu.make_async_copy(here, there, sems.at[i]) for i, (here, there) in enumerate(moves)
@@ -394,25 +392,25 @@
         copy.wait()
 
 
-def image_products(weight, rounds, sides_ref, *rest):
-    groups, begin = [], 0
-    for count in rounds:
-        mine_ref, *came_refs = rest[begin : begin + 1 + count]
-        groups.append((mine_ref, *came_refs[::-1]))
-        begin += 1 + count
-    image_hbm, *wides, image_ref, sems = rest[begin:]
-    for blocks, wide in zip(groups, wides):
-        widen(weight, sides_ref, blocks, wide)
+def early_products(weight, sides_ref, mine_ref, last_ref, first_ref, image_ref, wide):
+    widen(weight, sides_ref, (mine_ref, first_ref, last_ref), wide)
+    for offset in range(OFFS):
+        for level in range(wide.shape[2]):
+            image_ref[offset, level] = offset_product(wide, offset, level, None)
+
+
+def image_products(weight, sides_ref, mine_ref, *rest):
+    came_refs, (early_ref, image_hbm, wide, image_ref, sems) = rest[ROUNDS - 1 :: -1], rest[ROUNDS:]
+    widen(weight, sides_ref, (mine_ref, *came_refs), wide)
     parts = sems.shape[0]
     copies = []
     for piece in range(parts):
         offsets = range(piece * OFFS // parts, (piece + 1) * OFFS // parts)
         for offset in offsets:
             for level in range(image_ref.shape[1]):
-                total = None
-                for wide in wides:
-                    total = offset_product(wide, offset, level, total)
-                image_ref[offset, level] = total
+                image_ref[offset, level] = offset_product(
+                    wide, offset, level, early_ref[offset, level]
+                )
         rows = pl.ds(offsets[0], len(offsets))
         copy = pltpu.make_async_copy(image_ref.at[rows], image_hbm.at[rows], sems.at[piece])
         copy.start()
@@ -489,7 +487,7 @@
             scratch(*receiver_cell.shape, dtype=jnp.int32),
             scratch(*receiver_data.shape),
             scratch(2, levels, 8, across),
-            pltpu.SemaphoreType.DMA((14,)),
+            pltpu.SemaphoreType.DMA((9,)),
         ],
         compiler_params=params,
         name="own_edges",
@@ -559,8 +557,8 @@
         compiler_params=params,
         name="write_fields",
     )(final)
-    operands, wides, rounds = [], [], []
-    for blocks, count in (([own_block, came[0]], 2), (came[1:], 3)):
+    groups = []
+    for blocks in ([own_block, came[0]], came[1:]):
         group = pl.pallas_call(
             stack,
             out_shape=struct(len(blocks), *own_block.shape),
@@ -569,18 +567,29 @@
             compiler_params=params,
             name="stack",
         )(*blocks)
-        operands = [group, *swap_rounds([group] * count)[::-1], *operands]
-        wides.insert(0, wide_scratch(group))
-        rounds.insert(0, count)
+        groups.append(group)
+    early = pl.pallas_call(
+        functools.partial(early_products, weight),
+        out_shape=struct(*image_shape),
+        in_specs=[VMEM] * 4,
+        out_specs=VMEM,
+        scratch_shapes=[wide_scratch(groups[0])],
+        compiler_params=params,
+        name="early_products",
+    )(sides, groups[0], *swap_rounds([groups[0]] * 2)[::-1])
     image = pl.pallas_call(
-        functools.partial(image_products, weight, rounds),
+        functools.partial(image_products, weight),
         out_shape=struct(*image_shape),
-        in_specs=[VMEM] * (1 + len(operands)),
+        in_specs=[VMEM] * (3 + ROUNDS),
         out_specs=HBM,
-        scratch_shapes=[*wides, scratch(*image_shape), pltpu.SemaphoreType.DMA((11,))],
+        scratch_shapes=[
+            wide_scratch(groups[1]),
+            scratch(*image_shape),
+            pltpu.SemaphoreType.DMA((11,)),
+        ],
         compiler_params=params,
         name="image_products",
-    )(sides, *operands)
+    )(sides, groups[1], *swap_rounds([groups[1]] * ROUNDS)[::-1], early)
     return src_next, rec_next, image
 
 

time: 19 us -> 18.9 us (level)
    pallas_call x1 -> x2, Pallas kernels: 0.94 us -> 1.01 us  [the longest x1 0.91 us: per_device(): pl.pallas_call(functools.partial(image_products, weight), out_shape=struc...]
  transfers between devices with their start and end apart: 11 -> 11, of which waited for: 3 -> 3; matrix products, arithmetic and copies ran while one was open for 0% -> 0% of each run, Pallas kernels for 7% -> 8%
where the time goes in v17:
time: 18.9 us; the launch traced here: 18.7 us
  starting transfers between devices  10.8 us (57%)
  Pallas kernels  4.04 us (21%)
  waiting for transfers between devices  2.58 us (14%)
  between operations  1.36 us (7%)
    ppermute x8, starting transfers between devices, swap_tiles(): return lax.ppermute(value, ('tile', 'shot'), pairs)  8.64 us
    ppermute x3, starting transfers between devices, per_device(): lax.ppermute(sent, 'shot', [(shot, shot ^ 1 + i) for shot in range(shots)])  2.12 us
    ppermute x8, waiting for transfers between devices, swap_tiles(): return lax.ppermute(value, ('tile', 'shot'), pairs)  1.5 us
    pallas_call x1, Pallas kernels, per_device(): pl.pallas_call(own_edges, out_shape=(struct(*wavelet.shape), struct(*wide...  1.35 us
    ppermute x3, waiting for transfers between devices, per_device(): lax.ppermute(sent, 'shot', [(shot, shot ^ 1 + i) for shot in range(shots)])  1.08 us
    pallas_call x1, Pallas kernels, per_device(): pl.pallas_call(functools.partial(image_products, weight), out_shape=struc...  0.91 us
    pallas_call x1, Pallas kernels, per_device(): pl.pallas_call(functools.partial(own_steps, width), out_shape=(struct(lev...  0.72 us
    pallas_call x1, Pallas kernels, per_device(): pl.pallas_call(write_fields, out_shape=(struct(1, levels, extent, across)...  0.67 us
  transfers between devices with their start and end apart: 11, of which 3 were waited for; matrix products, arithmetic and copies ran while one was open for 0% of the time, Pallas kernels for 8%

profile of v17, /device:TPU:0, one launch (start us, length us, event | category | flops | bytes accessed | tf_op | source)
XLA Modules:
  0.0 18.7 jit_solution(4601788380378530852)
XLA Ops:
  0.6 1.4 %own_edges.1 = (f32[1,2]{1,0:T(1,128)S(1)}, f32[2,8,32,128]{3,2,1,0:T(8,128)S(1)}, f32[2,8,16,128]{3,2,1,0:T(8,128)S(1)}, s32[8,16,128]{2,1,0:T(8,128)S(1)}, f32...) custom-call(f32[1,16]{1,0:T(1,128)} %bitcast.1, ...), custom_call_target="tpu_custom_call" | custom-call | tf_op jit(solution)/shard_map/own_edges/pallas_call | solution.py:472
  2.0 3.1 %collective-permute-start = (f32[20,8,128]{2,1,0:T(8,128)S(1)}, f32[20,8,128]{2,1,0:T(8,128)S(1)}, u32[]{:S(2)}, u32[]{:S(2)}) collective-permute-start(f32[20,8,128]{2,1,0:T(8,128)S(1)} %get-tuple-element.37), channel_id=1, source_target_pairs={{0,4},{1,5},{2,6},{3,7},{4,0},{5,1},{6,2},{7,3},{8,9},{9,8},{10,11... | collective-permute-start | bytes 245768 | tf_op jit(solution)/shard_map/ppermute | solution.py:433
  5.1 0.0 collective-permute-start.1
  5.1 0.5 %collective-permute-start.2 = (f32[20,8,128]{2,1,0:T(8,128)S(1)}, f32[20,8,128]{2,1,0:T(8,128)S(1)}, u32[]{:S(2)}, u32[]{:S(2)}) collective-permute-start(f32[20,8,128]{2,1,0:T(8,128)S(1)} %get-tuple-element.39), channel_id=1, source_target_pairs={{0,1},{1,0},{2,3},{3,2},{4,5},{5,4},{6,7},{7,6},{8,12},{9,13},{10,... | collective-permute-start | bytes 245768 | tf_op jit(solution)/shard_map/ppermute | solution.py:433
  6.2 0.7 %own_steps.1 = (f32[8,16,128]{2,1,0:T(8,128)S(1)}, f32[2,8,16,128]{3,2,1,0:T(8,128)S(1)}, f32[2,8,8,128]{3,2,1,0:T(8,128)S(1)}, f32[8,32,128]{2,1,0:T(8,128)S(1)...) custom-call(s32[1]{0:T(128)S(6)} %copy.13.cell_ref, f32[1,2]{1,0:T(1,128)S(1)} %get-tuple-element.25.amps_ref, ...), custom_call_target="tpu_custom_call" | custom-call | tf_op jit(solution)/shard_map/own_steps/pallas_call | solution.py:511
  7.0 0.6 %collective-permute-done.rest_0_ = f32[20,8,128]{2,1,0:T(8,128)S(1)} collective-permute-done((f32[20,8,128]{2,1,0:T(8,128)S(1)}, f32[20,8,128]{2,1,0:T(8,128)S(1)}, u32[]{:S(2)}, u32[]{:S(2)}) %collective-permute-start) | collective-permute-done | bytes 81952 | tf_op jit(solution)/shard_map/ppermute | solution.py:433
  7.5 0.0 collective-permute-done.1.rest_1_
  7.5 0.0 collective-permute-done.2.rest_2_
  7.5 0.3 %neighbours_part.1 = (f32[2,8,16,128]{3,2,1,0:T(8,128)S(1)}, f32[2,2,16,128]{3,2,1,0:T(8,128)S(1)}, f32[2,2,16,128]{3,2,1,0:T(8,128)S(1)}, f32[2,2,16,128]{3,2,1,0:T(8,128)S(1)}, f32[2,2,16,128]{3,2,1,0:T(8,128)S(1)}) custom-call(s32[4,8,128]{2,1,0:T(8,128)S(1)} %get-tuple-element.31.sides_ref, s32[2,8,128]{2,1,0:T(8,128)S(1)} %get-tuple-element.32.bits_ref, ...), custom_call_target="tpu_custom_call" | custom-call | tf_op jit(solution)/shard_map/neighbours_part/pallas_call | solution.py:528
  7.8 0.1 collective-permute-start.8
  7.9 2.0 %collective-permute-start.3 = (f32[2,2,16,128]{3,2,1,0:T(8,128)S(1)}, f32[2,2,16,128]{3,2,1,0:T(8,128)S(1)}, u32[]{:S(2)}, u32[]{:S(2)}) collective-permute-start(f32[2,2,16,128]{3,2,1,0:T(8,128)S(1)} %get-tuple-element.43), channel_id=1, source_target_pairs={{0,2},{1,3},{2,0},{3,1},{4,6},{5,7},{6,4},{7,5},{8,10},{9,11},{10,... | collective-permute-start | bytes 98312 | tf_op jit(solution)/shard_map/ppermute | solution.py:542
  9.9 0.1 collective-permute-start.4
  9.9 0.0 collective-permute-done.8.refs_1_
  10.0 2.1 %collective-permute-start.10 = (f32[2,2,2,16,128]{4,3,2,1,0:T(8,128)S(1)}, f32[2,2,2,16,128]{4,3,2,1,0:T(8,128)S(1)}, u32[]{:S(2)}, u32[]{:S(2)}) collective-permute-start(f32[2,2,2,16,128]{4,3,2,1,0:T(8,128)S(1)} %stack.3.mine_ref), channel_id=1, source_target_pairs={{0,4},{1,5},{2,6},{3,7},{4,0},{5,1},{6,2},{7,3},{8,12},{9,13},{10,... | collective-permute-start | bytes 196616 | tf_op jit(solution)/shard_map/ppermute | solution.py:433
  12.1 0.1 collective-permute-start.9
  12.2 0.0 collective-permute-done.3.refs_0_
  12.2 1.1 %collective-permute-done.4.refs_1_ = f32[2,2,16,128]{3,2,1,0:T(8,128)S(1)} collective-permute-done((f32[2,2,16,128]{3,2,1,0:T(8,128)S(1)}, f32[2,2,16,128]{3,2,1,0:T(8,128)S(1)}, u32[]{:S(2)}, u32[]{:S(2)}) %collective-permute-start.4) | collective-permute-done | bytes 32800 | tf_op jit(solution)/shard_map/ppermute | solution.py:542
  13.2 2.3 %collective-permute-start.7 = (f32[2,2,2,16,128]{4,3,2,1,0:T(8,128)S(1)}, f32[2,2,2,16,128]{4,3,2,1,0:T(8,128)S(1)}, u32[]{:S(2)}, u32[]{:S(2)}) collective-permute-start(f32[2,2,2,16,128]{4,3,2,1,0:T(8,128)S(1)} %stack.2.mine_ref), channel_id=1, source_target_pairs={{0,4},{1,5},{2,6},{3,7},{4,0},{5,1},{6,2},{7,3},{8,9},{9,8},{10,11... | collective-permute-start | bytes 196616 | tf_op jit(solution)/shard_map/ppermute | solution.py:433
  15.6 0.0 collective-permute-start.6
  15.6 0.5 %collective-permute-start.5 = (f32[2,2,2,16,128]{4,3,2,1,0:T(8,128)S(1)}, f32[2,2,2,16,128]{4,3,2,1,0:T(8,128)S(1)}, u32[]{:S(2)}, u32[]{:S(2)}) collective-permute-start(f32[2,2,2,16,128]{4,3,2,1,0:T(8,128)S(1)} %stack.2.mine_ref), channel_id=1, source_target_pairs={{0,1},{1,0},{2,3},{3,2},{4,5},{5,4},{6,7},{7,6},{8,12},{9,13},{10,... | collective-permute-start | bytes 196616 | tf_op jit(solution)/shard_map/ppermute | solution.py:433
  16.1 0.7 %write_fields.1 = (f32[1,8,16,128]{3,2,1,0:T(8,128)}, f32[1,8,16,128]{3,2,1,0:T(8,128)}) custom-call(f32[2,8,16,128]{3,2,1,0:T(8,128)S(1)} %get-tuple-element.40.final_ref), custom_call_target="tpu_custom_call" | custom-call | tf_op jit(solution)/shard_map/write_fields/pallas_call | solution.py:551
  16.8 0.0 collective-permute-done.10.first_ref
  16.8 0.0 collective-permute-done.9.last_ref
  16.8 0.1 early_products.1.rest_3_
  16.9 0.9 %collective-permute-done.7.rest_2_ = f32[2,2,2,16,128]{4,3,2,1,0:T(8,128)S(1)} collective-permute-done((f32[2,2,2,16,128]{4,3,2,1,0:T(8,128)S(1)}, f32[2,2,2,16,128]{4,3,2,1,0:T(8,128)S(1)}, u32[]{:S(2)}, u32[]{:S(2)}) %collective-permute-start.7) | collective-permute-done | bytes 65568 | tf_op jit(solution)/shard_map/ppermute | solution.py:433
  17.8 0.0 collective-permute-done.6.rest_1_
  17.8 0.0 collective-permute-done.5.rest_0_
  17.8 0.9 %image_products.1 = f32[33,2,16,128]{3,2,1,0:T(8,128)} custom-call(s32[4,8,128]{2,1,0:T(8,128)S(1)} %get-tuple-element.31.sides_ref, f32[2,2,2,16,128]{4,3,2,1,0:T(8,128)S(1)} %stack.2.mine_ref, f32[2,2,2,16,128]{4,3,2,1,0:T(8,128)S(1)} %collective-permute-done.5.rest_0_, f32[2,2,2,16,128]{4,3,2,1,0:T(8,128)S(1)} %collective-permute-done.6.rest_1_, ...), custom_call_target="tpu_custom_call" | custom-call | tf_op jit(solution)/shard_map/image_products/pallas_call | solution.py:580
  (2 shorter events, 0.0 us)
Async XLA Ops:
  2.0 5.5 %collective-permute-start = (f32[20,8,128]{2,1,0:T(8,128)S(1)}, f32[20,8,128]{2,1,0:T(8,128)S(1)}, u32[]{:S(2)}, u32[]{:S(2)}) collective-permute-start(f32[20,8,128]{2,1,0:T(8,128)S(1)} %get-tuple-element.37), channel_id=1, source_target_pairs={{0,4},{1,5},{2,6},{3,7},{4,0},{5,1},{6,2},{7,3},{8,9},{9,8},{10,11... | collective-permute-start | bytes 245768 | tf_op jit(solution)/shard_map/ppermute | solution.py:433
  5.1 2.4 %collective-permute-start.1 = (f32[20,8,128]{2,1,0:T(8,128)S(1)}, f32[20,8,128]{2,1,0:T(8,128)S(1)}, u32[]{:S(2)}, u32[]{:S(2)}) collective-permute-start(f32[20,8,128]{2,1,0:T(8,128)S(1)} %get-tuple-element.38), channel_id=1, source_target_pairs={{0,1},{1,0},{2,3},{3,2},{4,8},{5,9},{6,10},{7,11},{8,4},{9,5},{10,... | collective-permute-start | bytes 245768 | tf_op jit(solution)/shard_map/ppermute | solution.py:433
  5.1 2.4 %collective-permute-start.2 = (f32[20,8,128]{2,1,0:T(8,128)S(1)}, f32[20,8,128]{2,1,0:T(8,128)S(1)}, u32[]{:S(2)}, u32[]{:S(2)}) collective-permute-start(f32[20,8,128]{2,1,0:T(8,128)S(1)} %get-tuple-element.39), channel_id=1, source_target_pairs={{0,1},{1,0},{2,3},{3,2},{4,5},{5,4},{6,7},{7,6},{8,12},{9,13},{10,... | collective-permute-start | bytes 245768 | tf_op jit(solution)/shard_map/ppermute | solution.py:433
  7.8 2.1 %collective-permute-start.8 = (f32[2,2,16,128]{3,2,1,0:T(8,128)S(1)}, f32[2,2,16,128]{3,2,1,0:T(8,128)S(1)}, u32[]{:S(2)}, u32[]{:S(2)}) collective-permute-start(f32[2,2,16,128]{3,2,1,0:T(8,128)S(1)} %get-tuple-element.46), channel_id=1, source_target_pairs={{0,1},{1,0},{2,3},{3,2},{4,5},{5,4},{6,7},{7,6},{8,9},{9,8},{10,11... | collective-permute-start | bytes 98312 | tf_op jit(solution)/shard_map/ppermute | solution.py:542
  7.9 4.3 %collective-permute-start.3 = (f32[2,2,16,128]{3,2,1,0:T(8,128)S(1)}, f32[2,2,16,128]{3,2,1,0:T(8,128)S(1)}, u32[]{:S(2)}, u32[]{:S(2)}) collective-permute-start(f32[2,2,16,128]{3,2,1,0:T(8,128)S(1)} %get-tuple-element.43), channel_id=1, source_target_pairs={{0,2},{1,3},{2,0},{3,1},{4,6},{5,7},{6,4},{7,5},{8,10},{9,11},{10,... | collective-permute-start | bytes 98312 | tf_op jit(solution)/shard_map/ppermute | solution.py:542
  9.9 3.3 %collective-permute-start.4 = (f32[2,2,16,128]{3,2,1,0:T(8,128)S(1)}, f32[2,2,16,128]{3,2,1,0:T(8,128)S(1)}, u32[]{:S(2)}, u32[]{:S(2)}) collective-permute-start(f32[2,2,16,128]{3,2,1,0:T(8,128)S(1)} %get-tuple-element.44), channel_id=1, source_target_pairs={{0,3},{1,2},{2,1},{3,0},{4,7},{5,6},{6,5},{7,4},{8,11},{9,10},{10,... | collective-permute-start | bytes 98312 | tf_op jit(solution)/shard_map/ppermute | solution.py:542
  10.0 6.8 %collective-permute-start.10 = (f32[2,2,2,16,128]{4,3,2,1,0:T(8,128)S(1)}, f32[2,2,2,16,128]{4,3,2,1,0:T(8,128)S(1)}, u32[]{:S(2)}, u32[]{:S(2)}) collective-permute-start(f32[2,2,2,16,128]{4,3,2,1,0:T(8,128)S(1)} %stack.3.mine_ref), channel_id=1, source_target_pairs={{0,4},{1,5},{2,6},{3,7},{4,0},{5,1},{6,2},{7,3},{8,12},{9,13},{10,... | collective-permute-start | bytes 196616 | tf_op jit(solution)/shard_map/ppermute | solution.py:433
  12.1 4.7 %collective-permute-start.9 = (f32[2,2,2,16,128]{4,3,2,1,0:T(8,128)S(1)}, f32[2,2,2,16,128]{4,3,2,1,0:T(8,128)S(1)}, u32[]{:S(2)}, u32[]{:S(2)}) collective-permute-start(f32[2,2,2,16,128]{4,3,2,1,0:T(8,128)S(1)} %stack.3.mine_ref), channel_id=1, source_target_pairs={{0,1},{1,0},{2,3},{3,2},{4,8},{5,9},{6,10},{7,11},{8,4},{9,5},{10,... | collective-permute-start | bytes 196616 | tf_op jit(solution)/shard_map/ppermute | solution.py:433
  13.2 4.6 %collective-permute-start.7 = (f32[2,2,2,16,128]{4,3,2,1,0:T(8,128)S(1)}, f32[2,2,2,16,128]{4,3,2,1,0:T(8,128)S(1)}, u32[]{:S(2)}, u32[]{:S(2)}) collective-permute-start(f32[2,2,2,16,128]{4,3,2,1,0:T(8,128)S(1)} %stack.2.mine_ref), channel_id=1, source_target_pairs={{0,4},{1,5},{2,6},{3,7},{4,0},{5,1},{6,2},{7,3},{8,9},{9,8},{10,11... | collective-permute-start | bytes 196616 | tf_op jit(solution)/shard_map/ppermute | solution.py:433
  15.6 2.2 %collective-permute-start.6 = (f32[2,2,2,16,128]{4,3,2,1,0:T(8,128)S(1)}, f32[2,2,2,16,128]{4,3,2,1,0:T(8,128)S(1)}, u32[]{:S(2)}, u32[]{:S(2)}) collective-permute-start(f32[2,2,2,16,128]{4,3,2,1,0:T(8,128)S(1)} %stack.2.mine_ref), channel_id=1, source_target_pairs={{0,1},{1,0},{2,3},{3,2},{4,8},{5,9},{6,10},{7,11},{8,4},{9,5},{10,... | collective-permute-start | bytes 196616 | tf_op jit(solution)/shard_map/ppermute | solution.py:433
  15.6 2.2 %collective-permute-start.5 = (f32[2,2,2,16,128]{4,3,2,1,0:T(8,128)S(1)}, f32[2,2,2,16,128]{4,3,2,1,0:T(8,128)S(1)}, u32[]{:S(2)}, u32[]{:S(2)}) collective-permute-start(f32[2,2,2,16,128]{4,3,2,1,0:T(8,128)S(1)} %stack.2.mine_ref), channel_id=1, source_target_pairs={{0,1},{1,0},{2,3},{3,2},{4,5},{5,4},{6,7},{7,6},{8,12},{9,13},{10,... | collective-permute-start | bytes 196616 | tf_op jit(solution)/shard_map/ppermute | solution.py:433

commit v18 on v17

--- a/solution.py
+++ b/solution.py
@@ -65,6 +65,26 @@
 
     total = lane_sum(rows_of(level), weights) + beside_sum(wide, field, level, LEAD, extent)
     return depth_sum(rows_of, level, levels, total)
+
+
+def receiver_rows(spots, across):
+    lane = lax.broadcasted_iota(jnp.int32, (across, spots.shape[1]), 0)
+    return jnp.where(lax.rem(spots, across) == lane, 1.0, 0.0)
+
+
+def receiver_values(spots, trace, columns, across):
+    begin = columns * across
+    return jnp.where((spots >= begin) & (spots < begin + across), trace, 0.0)
+
+
+def receiver_product(values, rows, precision=None):
+    return lax.dot_general(
+        values,
+        rows,
+        (((1,), (1,)), ((), ())),
+        precision=precision,
+        preferred_element_type=jnp.float32,
+    )
 
 
 def is_low(across):
@@ -86,11 +106,12 @@
     prev_ref,
     ids_ref,
     speeds_ref,
-    planes_ref,
+    spots_ref,
+    traces_ref,
     *rest,
 ):
     sent_refs, rest = rest[:ROUNDS], rest[ROUNDS:]
-    table, spots_ref, traces_ref, edges, sems = rest
+    table, edges, sems = rest
     levels, extent, across = ids_ref.shape
     regions = table_hbm.shape[1]
     end = LEAD + extent
@@ -121,21 +142,16 @@
         copy.wait()
 
     spots = spots_ref[...]
-    column = lax.broadcasted_iota(jnp.int32, (extent, spots.shape[1]), 0) * across
-    in_column = (spots >= column) & (spots < column + across)
-    lane = lax.broadcasted_iota(jnp.int32, (across, spots.shape[1]), 0)
-    in_row = jnp.where(lax.rem(spots, across) == lane, 1.0, 0.0)
-    traces = jnp.concatenate(
-        [jnp.where(in_column, traces_ref[0, t : t + 1, :], 0.0) for t in range(2)], axis=0
-    )
-    planes = lax.dot_general(
-        traces,
-        in_row,
-        (((1,), (1,)), ((), ())),
-        precision=lax.Precision.HIGHEST,
-        preferred_element_type=jnp.float32,
-    )
-    planes_ref[...] = planes
+    row = lax.broadcasted_iota(jnp.int32, (8, spots.shape[1]), 0)
+    columns = jnp.where(row < HALO, row, row + extent - 8)
+    values = receiver_values(spots, traces_ref[0, 0:1, :], columns, across)
+    parts = []
+    for _ in range(3):
+        parts.append(values.astype(jnp.bfloat16).astype(jnp.float32))
+        values = values - parts[-1]
+    parts = jnp.concatenate([*parts, jnp.zeros_like(values)], axis=0).astype(jnp.bfloat16)
+    planes = receiver_product(parts, receiver_rows(spots, across).astype(jnp.bfloat16))
+    injected = planes[0:8, :] + planes[8:16, :] + planes[16:24, :]
 
     def send(place, low, high):
         for number, sent_ref in enumerate(sent_refs):
@@ -179,7 +195,7 @@
             total = depth_sum(lambda near: edges[field, near], level, levels, total)
             value = 2.0 * now - halves(prev_ref, field, level) + coefs[level] * total
             if field == 1 and level == 0:
-                value = value + jnp.where(low_half, planes[0:8, :], planes[extent - 8 : extent, :])
+                value = value + injected
             send(
                 field * levels + level,
                 jnp.where(low_half, now, pltpu.roll(value, HALO, 0)),
@@ -195,7 +211,8 @@
     prev_ref,
     ids_ref,
     speeds_ref,
-    planes_ref,
+    spots_ref,
+    traces_ref,
     coef_ref,
     steps_ref,
     outside_ref,
@@ -225,7 +242,20 @@
             coef_ref[level, begin : begin + 8, :] = jnp.take_along_axis(
                 speeds, ids_ref[level, begin : begin + 8, :], axis=1, mode="promise_in_bounds"
             )
-    steps_ref[1, 0] += planes_ref[extent:, :]
+    spots = spots_ref[...]
+    columns = lax.broadcasted_iota(jnp.int32, (extent, spots.shape[1]), 0)
+    planes = receiver_product(
+        jnp.concatenate(
+            [
+                receiver_values(spots, traces_ref[0, t : t + 1, :], columns, across)
+                for t in range(2)
+            ],
+            axis=0,
+        ),
+        receiver_rows(spots, across),
+        lax.Precision.HIGHEST,
+    )
+    steps_ref[1, 0] += planes[extent:, :]
     for field in range(2):
         for level in range(levels):
             total = laplace_level(own, field, level, levels, extent, weights)
@@ -234,7 +264,7 @@
             if field == 0:
                 value = value + source_ref[level, LEAD:end, :]
             elif level == 0:
-                value = value + planes_ref[:extent, :]
+                value = value + planes[:extent, :]
             middle[field, level, 0:LEAD, :] = zeros
             middle[field, level, LEAD:end, :] = value
             middle[field, level, end : end + LEAD, :] = zeros
@@ -469,7 +499,7 @@
     wide_shape = (2, levels, extent + 2 * LEAD, across)
     message = struct(2 * levels + levels // 2, 2 * HALO, across)
     fields_shape = (2, levels, extent, across)
-    amps, own, prev, ids, speeds, planes, *sent = pl.pallas_call(
+    amps, own, prev, ids, speeds, spots, traces, *sent = pl.pallas_call(
         own_edges,
         out_shape=(
             struct(*wavelet.shape),
@@ -477,15 +507,14 @@
             struct(*fields_shape),
             jax.ShapeDtypeStruct(region_ids.shape, jnp.int32),
             struct(8, across),
-            struct(2 * extent, across),
+            jax.ShapeDtypeStruct(receiver_cell.shape, jnp.int32),
+            struct(*receiver_data.shape),
             *([message] * ROUNDS),
         ),
         in_specs=[HBM] * 9,
-        out_specs=[VMEM] * (6 + ROUNDS),
+        out_specs=[VMEM] * (7 + ROUNDS),
         scratch_shapes=[
             scratch(1, speed_table.shape[0]),
-            scratch(*receiver_cell.shape, dtype=jnp.int32),
-            scratch(*receiver_data.shape),
             scratch(2, levels, 8, across),
             pltpu.SemaphoreType.DMA((9,)),
         ],
@@ -518,12 +547,12 @@
             jax.ShapeDtypeStruct((4, 8, across), jnp.int32),
             jax.ShapeDtypeStruct((shots.bit_length() - 1, 8, across), jnp.int32),
         ),
-        in_specs=[SMEM] + [VMEM] * 6,
+        in_specs=[SMEM] + [VMEM] * 7,
         out_specs=[VMEM] * 6,
         scratch_shapes=[scratch(*wide_shape)],
         compiler_params=params,
         name="own_steps",
-    )(source_cell, amps, own, prev, ids, speeds, planes)
+    )(source_cell, amps, own, prev, ids, speeds, spots, traces)
     block = struct(2, share, extent, across)
     final, own_block, *blocks = pl.pallas_call(
         neighbours_part,

time: 18.9 us -> 18.9 us (level)
  no operation moved by 1% of the time
where the time goes in v18:
time: 18.9 us; the launch traced here: 18.7 us
  starting transfers between devices  10.8 us (57%)
  Pallas kernels  4.03 us (21%)
  waiting for transfers between devices  2.58 us (14%)
  between operations  1.36 us (7%)
    ppermute x8, starting transfers between devices, swap_tiles(): return lax.ppermute(value, ('tile', 'shot'), pairs)  8.64 us
    ppermute x3, starting transfers between devices, per_device(): lax.ppermute(sent, 'shot', [(shot, shot ^ 1 + i) for shot in range(shots)])  2.12 us
    ppermute x8, waiting for transfers between devices, swap_tiles(): return lax.ppermute(value, ('tile', 'shot'), pairs)  1.5 us
    pallas_call x1, Pallas kernels, per_device(): pl.pallas_call(own_edges, out_shape=(struct(*wavelet.shape), struct(*wide...  1.35 us
    ppermute x3, waiting for transfers between devices, per_device(): lax.ppermute(sent, 'shot', [(shot, shot ^ 1 + i) for shot in range(shots)])  1.08 us
    pallas_call x1, Pallas kernels, per_device(): pl.pallas_call(functools.partial(image_products, weight), out_shape=struc...  0.91 us
    pallas_call x1, Pallas kernels, per_device(): pl.pallas_call(functools.partial(own_steps, width), out_shape=(struct(lev...  0.71 us
    pallas_call x1, Pallas kernels, per_device(): pl.pallas_call(write_fields, out_shape=(struct(1, levels, extent, across)...  0.67 us
  transfers between devices with their start and end apart: 11, of which 3 were waited for; matrix products, arithmetic and copies ran while one was open for 0% of the time, Pallas kernels for 8%

profile of v18, /device:TPU:0, one launch (start us, length us, event | category | flops | bytes accessed | tf_op | source)
XLA Modules:
  0.0 18.7 jit_solution(10418627321209545059)
XLA Ops:
  0.6 1.3 %own_edges.1 = (f32[1,2]{1,0:T(1,128)S(1)}, f32[2,8,32,128]{3,2,1,0:T(8,128)S(1)}, f32[2,8,16,128]{3,2,1,0:T(8,128)S(1)}, s32[8,16,128]{2,1,0:T(8,128)S(1)}, f32...) custom-call(f32[1,16]{1,0:T(1,128)} %bitcast.1, ...), custom_call_target="tpu_custom_call" | custom-call | tf_op jit(solution)/shard_map/own_edges/pallas_call | solution.py:502
  2.0 3.1 %collective-permute-start = (f32[20,8,128]{2,1,0:T(8,128)S(1)}, f32[20,8,128]{2,1,0:T(8,128)S(1)}, u32[]{:S(2)}, u32[]{:S(2)}) collective-permute-start(f32[20,8,128]{2,1,0:T(8,128)S(1)} %get-tuple-element.39), channel_id=1, source_target_pairs={{0,4},{1,5},{2,6},{3,7},{4,0},{5,1},{6,2},{7,3},{8,9},{9,8},{10,11... | collective-permute-start | bytes 245768 | tf_op jit(solution)/shard_map/ppermute | solution.py:463
  5.1 0.0 collective-permute-start.1
  5.1 0.5 %collective-permute-start.2 = (f32[20,8,128]{2,1,0:T(8,128)S(1)}, f32[20,8,128]{2,1,0:T(8,128)S(1)}, u32[]{:S(2)}, u32[]{:S(2)}) collective-permute-start(f32[20,8,128]{2,1,0:T(8,128)S(1)} %get-tuple-element.41), channel_id=1, source_target_pairs={{0,1},{1,0},{2,3},{3,2},{4,5},{5,4},{6,7},{7,6},{8,12},{9,13},{10,... | collective-permute-start | bytes 245768 | tf_op jit(solution)/shard_map/ppermute | solution.py:463
  6.2 0.7 %own_steps.1 = (f32[8,16,128]{2,1,0:T(8,128)S(1)}, f32[2,8,16,128]{3,2,1,0:T(8,128)S(1)}, f32[2,8,8,128]{3,2,1,0:T(8,128)S(1)}, f32[8,32,128]{2,1,0:T(8,128)S(1)...) custom-call(s32[1]{0:T(128)S(6)} %copy.13.cell_ref, f32[1,2]{1,0:T(1,128)S(1)} %get-tuple-element.26.amps_ref, ...), custom_call_target="tpu_custom_call" | custom-call | tf_op jit(solution)/shard_map/own_steps/pallas_call | solution.py:540
  7.0 0.6 %collective-permute-done.rest_0_ = f32[20,8,128]{2,1,0:T(8,128)S(1)} collective-permute-done((f32[20,8,128]{2,1,0:T(8,128)S(1)}, f32[20,8,128]{2,1,0:T(8,128)S(1)}, u32[]{:S(2)}, u32[]{:S(2)}) %collective-permute-start) | collective-permute-done | bytes 81952 | tf_op jit(solution)/shard_map/ppermute | solution.py:463
  7.5 0.0 collective-permute-done.1.rest_1_
  7.5 0.0 collective-permute-done.2.rest_2_
  7.5 0.3 %neighbours_part.1 = (f32[2,8,16,128]{3,2,1,0:T(8,128)S(1)}, f32[2,2,16,128]{3,2,1,0:T(8,128)S(1)}, f32[2,2,16,128]{3,2,1,0:T(8,128)S(1)}, f32[2,2,16,128]{3,2,1,0:T(8,128)S(1)}, f32[2,2,16,128]{3,2,1,0:T(8,128)S(1)}) custom-call(s32[4,8,128]{2,1,0:T(8,128)S(1)} %get-tuple-element.33.sides_ref, s32[2,8,128]{2,1,0:T(8,128)S(1)} %get-tuple-element.34.bits_ref, ...), custom_call_target="tpu_custom_call" | custom-call | tf_op jit(solution)/shard_map/neighbours_part/pallas_call | solution.py:557
  7.8 0.1 collective-permute-start.8
  7.9 2.0 %collective-permute-start.3 = (f32[2,2,16,128]{3,2,1,0:T(8,128)S(1)}, f32[2,2,16,128]{3,2,1,0:T(8,128)S(1)}, u32[]{:S(2)}, u32[]{:S(2)}) collective-permute-start(f32[2,2,16,128]{3,2,1,0:T(8,128)S(1)} %get-tuple-element.45), channel_id=1, source_target_pairs={{0,2},{1,3},{2,0},{3,1},{4,6},{5,7},{6,4},{7,5},{8,10},{9,11},{10,... | collective-permute-start | bytes 98312 | tf_op jit(solution)/shard_map/ppermute | solution.py:571
  9.9 0.1 collective-permute-start.4
  9.9 0.0 collective-permute-done.8.refs_1_
  9.9 2.1 %collective-permute-start.10 = (f32[2,2,2,16,128]{4,3,2,1,0:T(8,128)S(1)}, f32[2,2,2,16,128]{4,3,2,1,0:T(8,128)S(1)}, u32[]{:S(2)}, u32[]{:S(2)}) collective-permute-start(f32[2,2,2,16,128]{4,3,2,1,0:T(8,128)S(1)} %stack.3.mine_ref), channel_id=1, source_target_pairs={{0,4},{1,5},{2,6},{3,7},{4,0},{5,1},{6,2},{7,3},{8,12},{9,13},{10,... | collective-permute-start | bytes 196616 | tf_op jit(solution)/shard_map/ppermute | solution.py:463
  12.1 0.1 collective-permute-start.9
  12.1 0.0 collective-permute-done.3.refs_0_
  12.1 1.1 %collective-permute-done.4.refs_1_ = f32[2,2,16,128]{3,2,1,0:T(8,128)S(1)} collective-permute-done((f32[2,2,16,128]{3,2,1,0:T(8,128)S(1)}, f32[2,2,16,128]{3,2,1,0:T(8,128)S(1)}, u32[]{:S(2)}, u32[]{:S(2)}) %collective-permute-start.4) | collective-permute-done | bytes 32800 | tf_op jit(solution)/shard_map/ppermute | solution.py:571
  13.2 2.3 %collective-permute-start.7 = (f32[2,2,2,16,128]{4,3,2,1,0:T(8,128)S(1)}, f32[2,2,2,16,128]{4,3,2,1,0:T(8,128)S(1)}, u32[]{:S(2)}, u32[]{:S(2)}) collective-permute-start(f32[2,2,2,16,128]{4,3,2,1,0:T(8,128)S(1)} %stack.2.mine_ref), channel_id=1, source_target_pairs={{0,4},{1,5},{2,6},{3,7},{4,0},{5,1},{6,2},{7,3},{8,9},{9,8},{10,11... | collective-permute-start | bytes 196616 | tf_op jit(solution)/shard_map/ppermute | solution.py:463
  15.6 0.0 collective-permute-start.6
  15.6 0.5 %collective-permute-start.5 = (f32[2,2,2,16,128]{4,3,2,1,0:T(8,128)S(1)}, f32[2,2,2,16,128]{4,3,2,1,0:T(8,128)S(1)}, u32[]{:S(2)}, u32[]{:S(2)}) collective-permute-start(f32[2,2,2,16,128]{4,3,2,1,0:T(8,128)S(1)} %stack.2.mine_ref), channel_id=1, source_target_pairs={{0,1},{1,0},{2,3},{3,2},{4,5},{5,4},{6,7},{7,6},{8,12},{9,13},{10,... | collective-permute-start | bytes 196616 | tf_op jit(solution)/shard_map/ppermute | solution.py:463
  16.1 0.7 %write_fields.1 = (f32[1,8,16,128]{3,2,1,0:T(8,128)}, f32[1,8,16,128]{3,2,1,0:T(8,128)}) custom-call(f32[2,8,16,128]{3,2,1,0:T(8,128)S(1)} %get-tuple-element.42.final_ref), custom_call_target="tpu_custom_call" | custom-call | tf_op jit(solution)/shard_map/write_fields/pallas_call | solution.py:580
  16.7 0.0 collective-permute-done.10.first_ref
  16.8 0.0 collective-permute-done.9.last_ref
  16.8 0.1 early_products.1.rest_3_
  16.9 0.9 %collective-permute-done.7.rest_2_ = f32[2,2,2,16,128]{4,3,2,1,0:T(8,128)S(1)} collective-permute-done((f32[2,2,2,16,128]{4,3,2,1,0:T(8,128)S(1)}, f32[2,2,2,16,128]{4,3,2,1,0:T(8,128)S(1)}, u32[]{:S(2)}, u32[]{:S(2)}) %collective-permute-start.7) | collective-permute-done | bytes 65568 | tf_op jit(solution)/shard_map/ppermute | solution.py:463
  17.8 0.0 collective-permute-done.6.rest_1_
  17.8 0.0 collective-permute-done.5.rest_0_
  17.8 0.9 %image_products.1 = f32[33,2,16,128]{3,2,1,0:T(8,128)} custom-call(s32[4,8,128]{2,1,0:T(8,128)S(1)} %get-tuple-element.33.sides_ref, f32[2,2,2,16,128]{4,3,2,1,0:T(8,128)S(1)} %stack.2.mine_ref, f32[2,2,2,16,128]{4,3,2,1,0:T(8,128)S(1)} %collective-permute-done.5.rest_0_, f32[2,2,2,16,128]{4,3,2,1,0:T(8,128)S(1)} %collective-permute-done.6.rest_1_, ...), custom_call_target="tpu_custom_call" | custom-call | tf_op jit(solution)/shard_map/image_products/pallas_call | solution.py:609
  (2 shorter events, 0.0 us)
Async XLA Ops:
  2.0 5.5 %collective-permute-start = (f32[20,8,128]{2,1,0:T(8,128)S(1)}, f32[20,8,128]{2,1,0:T(8,128)S(1)}, u32[]{:S(2)}, u32[]{:S(2)}) collective-permute-start(f32[20,8,128]{2,1,0:T(8,128)S(1)} %get-tuple-element.39), channel_id=1, source_target_pairs={{0,4},{1,5},{2,6},{3,7},{4,0},{5,1},{6,2},{7,3},{8,9},{9,8},{10,11... | collective-permute-start | bytes 245768 | tf_op jit(solution)/shard_map/ppermute | solution.py:463
  5.1 2.4 %collective-permute-start.1 = (f32[20,8,128]{2,1,0:T(8,128)S(1)}, f32[20,8,128]{2,1,0:T(8,128)S(1)}, u32[]{:S(2)}, u32[]{:S(2)}) collective-permute-start(f32[20,8,128]{2,1,0:T(8,128)S(1)} %get-tuple-element.40), channel_id=1, source_target_pairs={{0,1},{1,0},{2,3},{3,2},{4,8},{5,9},{6,10},{7,11},{8,4},{9,5},{10,... | collective-permute-start | bytes 245768 | tf_op jit(solution)/shard_map/ppermute | solution.py:463
  5.1 2.4 %collective-permute-start.2 = (f32[20,8,128]{2,1,0:T(8,128)S(1)}, f32[20,8,128]{2,1,0:T(8,128)S(1)}, u32[]{:S(2)}, u32[]{:S(2)}) collective-permute-start(f32[20,8,128]{2,1,0:T(8,128)S(1)} %get-tuple-element.41), channel_id=1, source_target_pairs={{0,1},{1,0},{2,3},{3,2},{4,5},{5,4},{6,7},{7,6},{8,12},{9,13},{10,... | collective-permute-start | bytes 245768 | tf_op jit(solution)/shard_map/ppermute | solution.py:463
  7.8 2.1 %collective-permute-start.8 = (f32[2,2,16,128]{3,2,1,0:T(8,128)S(1)}, f32[2,2,16,128]{3,2,1,0:T(8,128)S(1)}, u32[]{:S(2)}, u32[]{:S(2)}) collective-permute-start(f32[2,2,16,128]{3,2,1,0:T(8,128)S(1)} %get-tuple-element.48), channel_id=1, source_target_pairs={{0,1},{1,0},{2,3},{3,2},{4,5},{5,4},{6,7},{7,6},{8,9},{9,8},{10,11... | collective-permute-start | bytes 98312 | tf_op jit(solution)/shard_map/ppermute | solution.py:571
  7.9 4.3 %collective-permute-start.3 = (f32[2,2,16,128]{3,2,1,0:T(8,128)S(1)}, f32[2,2,16,128]{3,2,1,0:T(8,128)S(1)}, u32[]{:S(2)}, u32[]{:S(2)}) collective-permute-start(f32[2,2,16,128]{3,2,1,0:T(8,128)S(1)} %get-tuple-element.45), channel_id=1, source_target_pairs={{0,2},{1,3},{2,0},{3,1},{4,6},{5,7},{6,4},{7,5},{8,10},{9,11},{10,... | collective-permute-start | bytes 98312 | tf_op jit(solution)/shard_map/ppermute | solution.py:571
  9.9 3.3 %collective-permute-start.4 = (f32[2,2,16,128]{3,2,1,0:T(8,128)S(1)}, f32[2,2,16,128]{3,2,1,0:T(8,128)S(1)}, u32[]{:S(2)}, u32[]{:S(2)}) collective-permute-start(f32[2,2,16,128]{3,2,1,0:T(8,128)S(1)} %get-tuple-element.46), channel_id=1, source_target_pairs={{0,3},{1,2},{2,1},{3,0},{4,7},{5,6},{6,5},{7,4},{8,11},{9,10},{10,... | collective-permute-start | bytes 98312 | tf_op jit(solution)/shard_map/ppermute | solution.py:571
  9.9 6.8 %collective-permute-start.10 = (f32[2,2,2,16,128]{4,3,2,1,0:T(8,128)S(1)}, f32[2,2,2,16,128]{4,3,2,1,0:T(8,128)S(1)}, u32[]{:S(2)}, u32[]{:S(2)}) collective-permute-start(f32[2,2,2,16,128]{4,3,2,1,0:T(8,128)S(1)} %stack.3.mine_ref), channel_id=1, source_target_pairs={{0,4},{1,5},{2,6},{3,7},{4,0},{5,1},{6,2},{7,3},{8,12},{9,13},{10,... | collective-permute-start | bytes 196616 | tf_op jit(solution)/shard_map/ppermute | solution.py:463
  12.1 4.7 %collective-permute-start.9 = (f32[2,2,2,16,128]{4,3,2,1,0:T(8,128)S(1)}, f32[2,2,2,16,128]{4,3,2,1,0:T(8,128)S(1)}, u32[]{:S(2)}, u32[]{:S(2)}) collective-permute-start(f32[2,2,2,16,128]{4,3,2,1,0:T(8,128)S(1)} %stack.3.mine_ref), channel_id=1, source_target_pairs={{0,1},{1,0},{2,3},{3,2},{4,8},{5,9},{6,10},{7,11},{8,4},{9,5},{10,... | collective-permute-start | bytes 196616 | tf_op jit(solution)/shard_map/ppermute | solution.py:463
  13.2 4.6 %collective-permute-start.7 = (f32[2,2,2,16,128]{4,3,2,1,0:T(8,128)S(1)}, f32[2,2,2,16,128]{4,3,2,1,0:T(8,128)S(1)}, u32[]{:S(2)}, u32[]{:S(2)}) collective-permute-start(f32[2,2,2,16,128]{4,3,2,1,0:T(8,128)S(1)} %stack.2.mine_ref), channel_id=1, source_target_pairs={{0,4},{1,5},{2,6},{3,7},{4,0},{5,1},{6,2},{7,3},{8,9},{9,8},{10,11... | collective-permute-start | bytes 196616 | tf_op jit(solution)/shard_map/ppermute | solution.py:463
  15.6 2.2 %collective-permute-start.6 = (f32[2,2,2,16,128]{4,3,2,1,0:T(8,128)S(1)}, f32[2,2,2,16,128]{4,3,2,1,0:T(8,128)S(1)}, u32[]{:S(2)}, u32[]{:S(2)}) collective-permute-start(f32[2,2,2,16,128]{4,3,2,1,0:T(8,128)S(1)} %stack.2.mine_ref), channel_id=1, source_target_pairs={{0,1},{1,0},{2,3},{3,2},{4,8},{5,9},{6,10},{7,11},{8,4},{9,5},{10,... | collective-permute-start | bytes 196616 | tf_op jit(solution)/shard_map/ppermute | solution.py:463
  15.6 2.2 %collective-permute-start.5 = (f32[2,2,2,16,128]{4,3,2,1,0:T(8,128)S(1)}, f32[2,2,2,16,128]{4,3,2,1,0:T(8,128)S(1)}, u32[]{:S(2)}, u32[]{:S(2)}) collective-permute-start(f32[2,2,2,16,128]{4,3,2,1,0:T(8,128)S(1)} %stack.2.mine_ref), channel_id=1, source_target_pairs={{0,1},{1,0},{2,3},{3,2},{4,5},{5,4},{6,7},{7,6},{8,12},{9,13},{10,... | collective-permute-start | bytes 196616 | tf_op jit(solution)/shard_map/ppermute | solution.py:463

commit v19 on v16

--- a/solution.py
+++ b/solution.py
@@ -393,7 +393,7 @@
 
 
 def image_products(weight, sides_ref, others_ref, *rest):
-    others_sides, rest = rest[ROUNDS - 1 :: -1], rest[ROUNDS:]
+    others_sides, rest = rest[1::-1], rest[2:]
     mine_ref, last_ref, first_ref, *partner_refs, image_hbm, wide, image_ref, sems = rest
     places = [
         (mine_ref.at[0], (first_ref.at[0], last_ref.at[0])),
@@ -562,7 +562,7 @@
         name="stack",
     )(*came[::-1])
     mine_sides = swap_rounds([mine] * 2)
-    others_sides = swap_rounds([others] * ROUNDS)
+    others_sides = swap_rounds([others] * 2)
     partner = [swap_shots(value[1], 1) for value in (mine, *mine_sides)]
     operands = [others, *others_sides[::-1], mine, *mine_sides[::-1], *partner]
     image = pl.pallas_call(

time: 19.1 us -> 19.1 us (level)
  starting transfers between devices: 12 us -> 11.7 us
  waiting for transfers between devices: 1.62 us -> 1.9 us
    ppermute x8 -> x7, starting transfers between devices: 8.91 us -> 8.62 us  [swap_tiles(): return lax.ppermute(value, ('tile', 'shot'), pairs)]
    ppermute x8 -> x7, waiting for transfers between devices: 1.37 us -> 1.59 us  [swap_tiles(): return lax.ppermute(value, ('tile', 'shot'), pairs)]
  transfers between devices with their start and end apart: 13 -> 12, of which waited for: 3 -> 3; matrix products, arithmetic and copies ran while one was open for 0% -> 0% of each run, Pallas kernels for 7% -> 7%
where the time goes in v19:
time: 19.1 us; the launch traced here: 18.9 us
  starting transfers between devices  11.7 us (61%)
  Pallas kernels  3.94 us (21%)
  waiting for transfers between devices  1.9 us (10%)
  between operations  1.35 us (7%)
    ppermute x7, starting transfers between devices, swap_tiles(): return lax.ppermute(value, ('tile', 'shot'), pairs)  8.62 us
    ppermute x5, starting transfers between devices, swap_shots(): lax.ppermute(value, 'shot', [(shot, shot ^ number) for shot in range(shot...  3.07 us
    ppermute x7, waiting for transfers between devices, swap_tiles(): return lax.ppermute(value, ('tile', 'shot'), pairs)  1.59 us
    pallas_call x1, Pallas kernels, per_device(): pl.pallas_call(own_edges, out_shape=(struct(*wavelet.shape), struct(*wide...  1.33 us
    pallas_call x1, Pallas kernels, per_device(): pl.pallas_call(functools.partial(image_products, weight), out_shape=struc...  0.94 us
    pallas_call x1, Pallas kernels, per_device(): pl.pallas_call(functools.partial(own_steps, width), out_shape=(struct(lev...  0.72 us
    pallas_call x1, Pallas kernels, per_device(): pl.pallas_call(write_fields, out_shape=(struct(1, levels, extent, across)...  0.67 us
  transfers between devices with their start and end apart: 12, of which 3 were waited for; matrix products, arithmetic and copies ran while one was open for 0% of the time, Pallas kernels for 7%

profile of v19, /device:TPU:0, one launch (start us, length us, event | category | flops | bytes accessed | tf_op | source)
XLA Modules:
  0.0 18.9 jit_solution(1818148423700988808)
XLA Ops:
  0.6 1.3 %own_edges.1 = (f32[1,2]{1,0:T(1,128)S(1)}, f32[2,8,32,128]{3,2,1,0:T(8,128)S(1)}, f32[2,8,16,128]{3,2,1,0:T(8,128)S(1)}, s32[8,16,128]{2,1,0:T(8,128)S(1)}, f32...) custom-call(f32[1,16]{1,0:T(1,128)} %bitcast.7, ...), custom_call_target="tpu_custom_call" | custom-call | tf_op jit(solution)/shard_map/own_edges/pallas_call | solution.py:471
  2.0 3.1 %collective-permute-start = (f32[20,8,128]{2,1,0:T(8,128)S(1)}, f32[20,8,128]{2,1,0:T(8,128)S(1)}, u32[]{:S(2)}, u32[]{:S(2)}) collective-permute-start(f32[20,8,128]{2,1,0:T(8,128)S(1)} %get-tuple-element.36), channel_id=1, source_target_pairs={{0,4},{1,5},{2,6},{3,7},{4,0},{5,1},{6,2},{7,3},{8,9},{9,8},{10,11... | collective-permute-start | bytes 245768 | tf_op jit(solution)/shard_map/ppermute | solution.py:432
  5.1 0.0 collective-permute-start.1
  5.1 0.5 %collective-permute-start.2 = (f32[20,8,128]{2,1,0:T(8,128)S(1)}, f32[20,8,128]{2,1,0:T(8,128)S(1)}, u32[]{:S(2)}, u32[]{:S(2)}) collective-permute-start(f32[20,8,128]{2,1,0:T(8,128)S(1)} %get-tuple-element.38), channel_id=1, source_target_pairs={{0,1},{1,0},{2,3},{3,2},{4,5},{5,4},{6,7},{7,6},{8,12},{9,13},{10,... | collective-permute-start | bytes 245768 | tf_op jit(solution)/shard_map/ppermute | solution.py:432
  6.2 0.7 %own_steps.1 = (f32[8,16,128]{2,1,0:T(8,128)S(1)}, f32[2,8,16,128]{3,2,1,0:T(8,128)S(1)}, f32[2,8,8,128]{3,2,1,0:T(8,128)S(1)}, f32[8,32,128]{2,1,0:T(8,128)S(1)...) custom-call(s32[1]{0:T(128)S(6)} %copy.13.cell_ref, f32[1,2]{1,0:T(1,128)S(1)} %get-tuple-element.24.amps_ref, ...), custom_call_target="tpu_custom_call" | custom-call | tf_op jit(solution)/shard_map/own_steps/pallas_call | solution.py:510
  6.9 0.6 %collective-permute-done.rest_0_ = f32[20,8,128]{2,1,0:T(8,128)S(1)} collective-permute-done((f32[20,8,128]{2,1,0:T(8,128)S(1)}, f32[20,8,128]{2,1,0:T(8,128)S(1)}, u32[]{:S(2)}, u32[]{:S(2)}) %collective-permute-start) | collective-permute-done | bytes 81952 | tf_op jit(solution)/shard_map/ppermute | solution.py:432
  7.5 0.0 collective-permute-done.1.rest_1_
  7.5 0.0 collective-permute-done.2.rest_2_
  7.5 0.3 %neighbours_part.1 = (f32[2,8,16,128]{3,2,1,0:T(8,128)S(1)}, f32[2,2,2,16,128]{4,3,2,1,0:T(8,128)S(1)}, f32[2,2,16,128]{3,2,1,0:T(8,128)S(1)}, f32[2,2,16,128]{3,2,1,0:T(8,128)S(1)}) custom-call(s32[4,8,128]{2,1,0:T(8,128)S(1)} %get-tuple-element.30.sides_ref, s32[2,8,128]{2,1,0:T(8,128)S(1)} %get-tuple-element.31.bits_ref, ...), custom_call_target="tpu_custom_call" | custom-call | tf_op jit(solution)/shard_map/neighbours_part/pallas_call | solution.py:527
  7.8 0.6 %collective-permute-start.3 = (f32[2,2,16,128]{3,2,1,0:T(8,128)S(1)}, f32[2,2,16,128]{3,2,1,0:T(8,128)S(1)}, u32[]{:S(2)}, u32[]{:S(2)}) collective-permute-start(f32[2,2,16,128]{3,2,1,0:T(8,128)S(1)} %get-tuple-element.42), channel_id=1, source_target_pairs={{0,3},{1,2},{2,1},{3,0},{4,7},{5,6},{6,5},{7,4},{8,11},{9,10},{10,... | collective-permute-start | bytes 98312 | tf_op jit(solution)/shard_map/ppermute | solution.py:541
  8.4 1.4 %collective-permute-start.4 = (f32[2,2,16,128]{3,2,1,0:T(8,128)S(1)}, f32[2,2,16,128]{3,2,1,0:T(8,128)S(1)}, u32[]{:S(2)}, u32[]{:S(2)}) collective-permute-start(f32[2,2,16,128]{3,2,1,0:T(8,128)S(1)} %get-tuple-element.43), channel_id=1, source_target_pairs={{0,2},{1,3},{2,0},{3,1},{4,6},{5,7},{6,4},{7,5},{8,10},{9,11},{10,... | collective-permute-start | bytes 98312 | tf_op jit(solution)/shard_map/ppermute | solution.py:541
  9.9 2.0 %collective-permute-start.8 = (f32[2,2,2,16,128]{4,3,2,1,0:T(8,128)S(1)}, f32[2,2,2,16,128]{4,3,2,1,0:T(8,128)S(1)}, u32[]{:S(2)}, u32[]{:S(2)}) collective-permute-start(f32[2,2,2,16,128]{4,3,2,1,0:T(8,128)S(1)} %get-tuple-element.44.rest_2_), channel_id=1, source_target_pairs={{0,4},{1,5},{2,6},{3,7},{4,0},{5,1},{6,2},{7,3},{8,12},{9,13},{10,... | collective-permute-start | bytes 196616 | tf_op jit(solution)/shard_map/ppermute | solution.py:432
  11.9 0.0 collective-permute-start.7
  11.9 0.5 %collective-permute-start.9 = (f32[2,2,16,128]{3,2,1,0:T(8,128)S(1)}, f32[2,2,16,128]{3,2,1,0:T(8,128)S(1)}, u32[]{:S(2)}, u32[]{:S(2)}) collective-permute-start(f32[2,2,16,128]{3,2,1,0:T(8,128)S(1)} %slice_bitcast_fusion.2), channel_id=1, source_target_pairs={{0,1},{1,0},{2,3},{3,2},{4,5},{5,4},{6,7},{7,6},{8,9},{9,8},{10,11... | collective-permute-start | bytes 98312 | tf_op jit(solution)/shard_map/ppermute | solution.py:541
  12.4 0.0 collective-permute-done.3.refs_0_
  12.4 0.0 collective-permute-done.4.refs_1_
  12.4 2.8 %collective-permute-start.6 = (f32[2,2,2,16,128]{4,3,2,1,0:T(8,128)S(1)}, f32[2,2,2,16,128]{4,3,2,1,0:T(8,128)S(1)}, u32[]{:S(2)}, u32[]{:S(2)}) collective-permute-start(f32[2,2,2,16,128]{4,3,2,1,0:T(8,128)S(1)} %stack.1.others_ref), channel_id=1, source_target_pairs={{0,4},{1,5},{2,6},{3,7},{4,0},{5,1},{6,2},{7,3},{8,12},{9,13},{10,... | collective-permute-start | bytes 196616 | tf_op jit(solution)/shard_map/ppermute | solution.py:432
  15.2 0.2 %collective-permute-start.5 = (f32[2,2,2,16,128]{4,3,2,1,0:T(8,128)S(1)}, f32[2,2,2,16,128]{4,3,2,1,0:T(8,128)S(1)}, u32[]{:S(2)}, u32[]{:S(2)}) collective-permute-start(f32[2,2,2,16,128]{4,3,2,1,0:T(8,128)S(1)} %stack.1.others_ref), channel_id=1, source_target_pairs={{0,1},{1,0},{2,3},{3,2},{4,8},{5,9},{6,10},{7,11},{8,4},{9,5},{10,... | collective-permute-start | bytes 196616 | tf_op jit(solution)/shard_map/ppermute | solution.py:432
  15.4 0.0 collective-permute-done.8.rest_4_
  15.4 0.3 %collective-permute-start.10 = (f32[2,2,16,128]{3,2,1,0:T(8,128)S(1)}, f32[2,2,16,128]{3,2,1,0:T(8,128)S(1)}, u32[]{:S(2)}, u32[]{:S(2)}) collective-permute-start(f32[2,2,16,128]{3,2,1,0:T(8,128)S(1)} %slice_bitcast_fusion.1), channel_id=1, source_target_pairs={{0,1},{1,0},{2,3},{3,2},{4,5},{5,4},{6,7},{7,6},{8,9},{9,8},{10,11... | collective-permute-start | bytes 98312 | tf_op jit(solution)/shard_map/ppermute | solution.py:541
  15.7 0.0 collective-permute-done.7.rest_3_
  15.7 0.2 %collective-permute-start.11 = (f32[2,2,16,128]{3,2,1,0:T(8,128)S(1)}, f32[2,2,16,128]{3,2,1,0:T(8,128)S(1)}, u32[]{:S(2)}, u32[]{:S(2)}) collective-permute-start(f32[2,2,16,128]{3,2,1,0:T(8,128)S(1)} %slice_bitcast_fusion), channel_id=1, source_target_pairs={{0,1},{1,0},{2,3},{3,2},{4,5},{5,4},{6,7},{7,6},{8,9},{9,8},{10,11... | collective-permute-start | bytes 98312 | tf_op jit(solution)/shard_map/ppermute | solution.py:541
  15.9 0.7 %write_fields.1 = (f32[1,8,16,128]{3,2,1,0:T(8,128)}, f32[1,8,16,128]{3,2,1,0:T(8,128)}) custom-call(f32[2,8,16,128]{3,2,1,0:T(8,128)S(1)} %get-tuple-element.39.final_ref), custom_call_target="tpu_custom_call" | custom-call | tf_op jit(solution)/shard_map/write_fields/pallas_call | solution.py:547
  16.6 0.0 collective-permute-done.9.rest_5_
  16.6 0.0 collective-permute-done.10.rest_6_
  16.6 0.3 %collective-permute-done.11.rest_7_ = f32[2,2,16,128]{3,2,1,0:T(8,128)S(1)} collective-permute-done((f32[2,2,16,128]{3,2,1,0:T(8,128)S(1)}, f32[2,2,16,128]{3,2,1,0:T(8,128)S(1)}, u32[]{:S(2)}, u32[]{:S(2)}) %collective-permute-start.11) | collective-permute-done | bytes 32800 | tf_op jit(solution)/shard_map/ppermute | solution.py:541
  16.9 1.0 %collective-permute-done.6.rest_1_ = f32[2,2,2,16,128]{4,3,2,1,0:T(8,128)S(1)} collective-permute-done((f32[2,2,2,16,128]{4,3,2,1,0:T(8,128)S(1)}, f32[2,2,2,16,128]{4,3,2,1,0:T(8,128)S(1)}, u32[]{:S(2)}, u32[]{:S(2)}) %collective-permute-start.6) | collective-permute-done | bytes 65568 | tf_op jit(solution)/shard_map/ppermute | solution.py:432
  17.9 0.0 collective-permute-done.5.rest_0_
  17.9 0.9 %image_products.1 = f32[33,2,16,128]{3,2,1,0:T(8,128)} custom-call(s32[4,8,128]{2,1,0:T(8,128)S(1)} %get-tuple-element.30.sides_ref, f32[2,2,2,16,128]{4,3,2,1,0:T(8,128)S(1)} %stack.1.others_ref, f32[2,2,2,16,128]{4,3,2,1,0:T(8,128)S(1)} %collective-permute-done.5.rest_0_, f32[2,2,2,16,128]{4,3,2,1,0:T(8,128)S(1)} %collective-permute-done.6.rest_1_, ...), custom_call_target="tpu_custom_call" | custom-call | tf_op jit(solution)/shard_map/image_products/pallas_call | solution.py:568
  (4 shorter events, 0.0 us)
Async XLA Ops:
  2.0 5.5 %collective-permute-start = (f32[20,8,128]{2,1,0:T(8,128)S(1)}, f32[20,8,128]{2,1,0:T(8,128)S(1)}, u32[]{:S(2)}, u32[]{:S(2)}) collective-permute-start(f32[20,8,128]{2,1,0:T(8,128)S(1)} %get-tuple-element.36), channel_id=1, source_target_pairs={{0,4},{1,5},{2,6},{3,7},{4,0},{5,1},{6,2},{7,3},{8,9},{9,8},{10,11... | collective-permute-start | bytes 245768 | tf_op jit(solution)/shard_map/ppermute | solution.py:432
  5.1 2.4 %collective-permute-start.1 = (f32[20,8,128]{2,1,0:T(8,128)S(1)}, f32[20,8,128]{2,1,0:T(8,128)S(1)}, u32[]{:S(2)}, u32[]{:S(2)}) collective-permute-start(f32[20,8,128]{2,1,0:T(8,128)S(1)} %get-tuple-element.37), channel_id=1, source_target_pairs={{0,1},{1,0},{2,3},{3,2},{4,8},{5,9},{6,10},{7,11},{8,4},{9,5},{10,... | collective-permute-start | bytes 245768 | tf_op jit(solution)/shard_map/ppermute | solution.py:432
  5.1 2.4 %collective-permute-start.2 = (f32[20,8,128]{2,1,0:T(8,128)S(1)}, f32[20,8,128]{2,1,0:T(8,128)S(1)}, u32[]{:S(2)}, u32[]{:S(2)}) collective-permute-start(f32[20,8,128]{2,1,0:T(8,128)S(1)} %get-tuple-element.38), channel_id=1, source_target_pairs={{0,1},{1,0},{2,3},{3,2},{4,5},{5,4},{6,7},{7,6},{8,12},{9,13},{10,... | collective-permute-start | bytes 245768 | tf_op jit(solution)/shard_map/ppermute | solution.py:432
  7.8 4.6 %collective-permute-start.3 = (f32[2,2,16,128]{3,2,1,0:T(8,128)S(1)}, f32[2,2,16,128]{3,2,1,0:T(8,128)S(1)}, u32[]{:S(2)}, u32[]{:S(2)}) collective-permute-start(f32[2,2,16,128]{3,2,1,0:T(8,128)S(1)} %get-tuple-element.42), channel_id=1, source_target_pairs={{0,3},{1,2},{2,1},{3,0},{4,7},{5,6},{6,5},{7,4},{8,11},{9,10},{10,... | collective-permute-start | bytes 98312 | tf_op jit(solution)/shard_map/ppermute | solution.py:541
  8.4 4.0 %collective-permute-start.4 = (f32[2,2,16,128]{3,2,1,0:T(8,128)S(1)}, f32[2,2,16,128]{3,2,1,0:T(8,128)S(1)}, u32[]{:S(2)}, u32[]{:S(2)}) collective-permute-start(f32[2,2,16,128]{3,2,1,0:T(8,128)S(1)} %get-tuple-element.43), channel_id=1, source_target_pairs={{0,2},{1,3},{2,0},{3,1},{4,6},{5,7},{6,4},{7,5},{8,10},{9,11},{10,... | collective-permute-start | bytes 98312 | tf_op jit(solution)/shard_map/ppermute | solution.py:541
  9.9 5.6 %collective-permute-start.8 = (f32[2,2,2,16,128]{4,3,2,1,0:T(8,128)S(1)}, f32[2,2,2,16,128]{4,3,2,1,0:T(8,128)S(1)}, u32[]{:S(2)}, u32[]{:S(2)}) collective-permute-start(f32[2,2,2,16,128]{4,3,2,1,0:T(8,128)S(1)} %get-tuple-element.44.rest_2_), channel_id=1, source_target_pairs={{0,4},{1,5},{2,6},{3,7},{4,0},{5,1},{6,2},{7,3},{8,12},{9,13},{10,... | collective-permute-start | bytes 196616 | tf_op jit(solution)/shard_map/ppermute | solution.py:432
  11.9 3.8 %collective-permute-start.7 = (f32[2,2,2,16,128]{4,3,2,1,0:T(8,128)S(1)}, f32[2,2,2,16,128]{4,3,2,1,0:T(8,128)S(1)}, u32[]{:S(2)}, u32[]{:S(2)}) collective-permute-start(f32[2,2,2,16,128]{4,3,2,1,0:T(8,128)S(1)} %get-tuple-element.44.rest_2_), channel_id=1, source_target_pairs={{0,1},{1,0},{2,3},{3,2},{4,8},{5,9},{6,10},{7,11},{8,4},{9,5},{10,... | collective-permute-start | bytes 196616 | tf_op jit(solution)/shard_map/ppermute | solution.py:432
  11.9 4.7 %collective-permute-start.9 = (f32[2,2,16,128]{3,2,1,0:T(8,128)S(1)}, f32[2,2,16,128]{3,2,1,0:T(8,128)S(1)}, u32[]{:S(2)}, u32[]{:S(2)}) collective-permute-start(f32[2,2,16,128]{3,2,1,0:T(8,128)S(1)} %slice_bitcast_fusion.2), channel_id=1, source_target_pairs={{0,1},{1,0},{2,3},{3,2},{4,5},{5,4},{6,7},{7,6},{8,9},{9,8},{10,11... | collective-permute-start | bytes 98312 | tf_op jit(solution)/shard_map/ppermute | solution.py:541
  12.4 5.5 %collective-permute-start.6 = (f32[2,2,2,16,128]{4,3,2,1,0:T(8,128)S(1)}, f32[2,2,2,16,128]{4,3,2,1,0:T(8,128)S(1)}, u32[]{:S(2)}, u32[]{:S(2)}) collective-permute-start(f32[2,2,2,16,128]{4,3,2,1,0:T(8,128)S(1)} %stack.1.others_ref), channel_id=1, source_target_pairs={{0,4},{1,5},{2,6},{3,7},{4,0},{5,1},{6,2},{7,3},{8,12},{9,13},{10,... | collective-permute-start | bytes 196616 | tf_op jit(solution)/shard_map/ppermute | solution.py:432
  15.2 2.8 %collective-permute-start.5 = (f32[2,2,2,16,128]{4,3,2,1,0:T(8,128)S(1)}, f32[2,2,2,16,128]{4,3,2,1,0:T(8,128)S(1)}, u32[]{:S(2)}, u32[]{:S(2)}) collective-permute-start(f32[2,2,2,16,128]{4,3,2,1,0:T(8,128)S(1)} %stack.1.others_ref), channel_id=1, source_target_pairs={{0,1},{1,0},{2,3},{3,2},{4,8},{5,9},{6,10},{7,11},{8,4},{9,5},{10,... | collective-permute-start | bytes 196616 | tf_op jit(solution)/shard_map/ppermute | solution.py:432
  15.4 1.2 %collective-permute-start.10 = (f32[2,2,16,128]{3,2,1,0:T(8,128)S(1)}, f32[2,2,16,128]{3,2,1,0:T(8,128)S(1)}, u32[]{:S(2)}, u32[]{:S(2)}) collective-permute-start(f32[2,2,16,128]{3,2,1,0:T(8,128)S(1)} %slice_bitcast_fusion.1), channel_id=1, source_target_pairs={{0,1},{1,0},{2,3},{3,2},{4,5},{5,4},{6,7},{7,6},{8,9},{9,8},{10,11... | collective-permute-start | bytes 98312 | tf_op jit(solution)/shard_map/ppermute | solution.py:541
  15.7 1.2 %collective-permute-start.11 = (f32[2,2,16,128]{3,2,1,0:T(8,128)S(1)}, f32[2,2,16,128]{3,2,1,0:T(8,128)S(1)}, u32[]{:S(2)}, u32[]{:S(2)}) collective-permute-start(f32[2,2,16,128]{3,2,1,0:T(8,128)S(1)} %slice_bitcast_fusion), channel_id=1, source_target_pairs={{0,1},{1,0},{2,3},{3,2},{4,5},{5,4},{6,7},{7,6},{8,9},{9,8},{10,11... | collective-permute-start | bytes 98312 | tf_op jit(solution)/shard_map/ppermute | solution.py:541

commit v20 on v19

--- a/solution.py
+++ b/solution.py
@@ -394,7 +394,7 @@
 
 def image_products(weight, sides_ref, others_ref, *rest):
     others_sides, rest = rest[1::-1], rest[2:]
-    mine_ref, last_ref, first_ref, *partner_refs, image_hbm, wide, image_ref, sems = rest
+    mine_ref, first_ref, last_ref, *partner_refs, image_hbm, wide, image_ref, sems = rest
     places = [
         (mine_ref.at[0], (first_ref.at[0], last_ref.at[0])),
         (partner_refs[0], partner_refs[1:]),
@@ -564,7 +564,7 @@
     mine_sides = swap_rounds([mine] * 2)
     others_sides = swap_rounds([others] * 2)
     partner = [swap_shots(value[1], 1) for value in (mine, *mine_sides)]
-    operands = [others, *others_sides[::-1], mine, *mine_sides[::-1], *partner]
+    operands = [others, *others_sides[::-1], mine, *mine_sides, *partner]
     image = pl.pallas_call(
         functools.partial(image_products, weight),
         out_shape=struct(*image_shape),

time: 19.1 us -> 19.6 us (1.026)
  waiting for transfers between devices: 1.9 us -> 3.48 us
  starting transfers between devices: 11.7 us -> 10.6 us
    ppermute x7, waiting for transfers between devices: 1.59 us -> 2.97 us  [swap_tiles(): return lax.ppermute(value, ('tile', 'shot'), pairs)]
    ppermute x5, starting transfers between devices: 3.07 us -> 2.36 us  [swap_shots(): lax.ppermute(value, 'shot', [(shot, shot ^ number) for shot in range(shot...]
    ppermute x7, starting transfers between devices: 8.62 us -> 8.29 us  [swap_tiles(): return lax.ppermute(value, ('tile', 'shot'), pairs)]
    ppermute x5, waiting for transfers between devices: 0.31 us -> 0.52 us  [swap_shots(): lax.ppermute(value, 'shot', [(shot, shot ^ number) for shot in range(shot...]
  transfers between devices with their start and end apart: 12 -> 12, of which waited for: 3 -> 4; matrix products, arithmetic and copies ran while one was open for 0% -> 0% of each run, Pallas kernels for 7% -> 7%
where the time goes in v20:
time: 19.6 us; the launch traced here: 19.4 us
  starting transfers between devices  10.6 us (54%)
  Pallas kernels  3.94 us (20%)
  waiting for transfers between devices  3.48 us (18%)
  between operations  1.35 us (7%)
    ppermute x7, starting transfers between devices, swap_tiles(): return lax.ppermute(value, ('tile', 'shot'), pairs)  8.29 us
    ppermute x7, waiting for transfers between devices, swap_tiles(): return lax.ppermute(value, ('tile', 'shot'), pairs)  2.97 us
    ppermute x5, starting transfers between devices, swap_shots(): lax.ppermute(value, 'shot', [(shot, shot ^ number) for shot in range(shot...  2.36 us
    pallas_call x1, Pallas kernels, per_device(): pl.pallas_call(own_edges, out_shape=(struct(*wavelet.shape), struct(*wide...  1.33 us
    pallas_call x1, Pallas kernels, per_device(): pl.pallas_call(functools.partial(image_products, weight), out_shape=struc...  0.94 us
    pallas_call x1, Pallas kernels, per_device(): pl.pallas_call(functools.partial(own_steps, width), out_shape=(struct(lev...  0.72 us
    pallas_call x1, Pallas kernels, per_device(): pl.pallas_call(write_fields, out_shape=(struct(1, levels, extent, across)...  0.67 us
    ppermute x5, waiting for transfers between devices, swap_shots(): lax.ppermute(value, 'shot', [(shot, shot ^ number) for shot in range(shot...  0.52 us
  transfers between devices with their start and end apart: 12, of which 4 were waited for; matrix products, arithmetic and copies ran while one was open for 0% of the time, Pallas kernels for 7%

profile of v20, /device:TPU:0, one launch (start us, length us, event | category | flops | bytes accessed | tf_op | source)
XLA Modules:
  0.0 19.4 jit_solution(17693289930008373236)
XLA Ops:
  0.6 1.3 %own_edges.1 = (f32[1,2]{1,0:T(1,128)S(1)}, f32[2,8,32,128]{3,2,1,0:T(8,128)S(1)}, f32[2,8,16,128]{3,2,1,0:T(8,128)S(1)}, s32[8,16,128]{2,1,0:T(8,128)S(1)}, f32...) custom-call(f32[1,16]{1,0:T(1,128)} %bitcast.7, ...), custom_call_target="tpu_custom_call" | custom-call | tf_op jit(solution)/shard_map/own_edges/pallas_call | solution.py:471
  2.0 3.1 %collective-permute-start = (f32[20,8,128]{2,1,0:T(8,128)S(1)}, f32[20,8,128]{2,1,0:T(8,128)S(1)}, u32[]{:S(2)}, u32[]{:S(2)}) collective-permute-start(f32[20,8,128]{2,1,0:T(8,128)S(1)} %get-tuple-element.36), channel_id=1, source_target_pairs={{0,4},{1,5},{2,6},{3,7},{4,0},{5,1},{6,2},{7,3},{8,9},{9,8},{10,11... | collective-permute-start | bytes 245768 | tf_op jit(solution)/shard_map/ppermute | solution.py:432
  5.1 0.0 collective-permute-start.1
  5.1 0.5 %collective-permute-start.2 = (f32[20,8,128]{2,1,0:T(8,128)S(1)}, f32[20,8,128]{2,1,0:T(8,128)S(1)}, u32[]{:S(2)}, u32[]{:S(2)}) collective-permute-start(f32[20,8,128]{2,1,0:T(8,128)S(1)} %get-tuple-element.38), channel_id=1, source_target_pairs={{0,1},{1,0},{2,3},{3,2},{4,5},{5,4},{6,7},{7,6},{8,12},{9,13},{10,... | collective-permute-start | bytes 245768 | tf_op jit(solution)/shard_map/ppermute | solution.py:432
  6.2 0.7 %own_steps.1 = (f32[8,16,128]{2,1,0:T(8,128)S(1)}, f32[2,8,16,128]{3,2,1,0:T(8,128)S(1)}, f32[2,8,8,128]{3,2,1,0:T(8,128)S(1)}, f32[8,32,128]{2,1,0:T(8,128)S(1)...) custom-call(s32[1]{0:T(128)S(6)} %copy.13.cell_ref, f32[1,2]{1,0:T(1,128)S(1)} %get-tuple-element.24.amps_ref, ...), custom_call_target="tpu_custom_call" | custom-call | tf_op jit(solution)/shard_map/own_steps/pallas_call | solution.py:510
  6.9 0.6 %collective-permute-done.rest_0_ = f32[20,8,128]{2,1,0:T(8,128)S(1)} collective-permute-done((f32[20,8,128]{2,1,0:T(8,128)S(1)}, f32[20,8,128]{2,1,0:T(8,128)S(1)}, u32[]{:S(2)}, u32[]{:S(2)}) %collective-permute-start) | collective-permute-done | bytes 81952 | tf_op jit(solution)/shard_map/ppermute | solution.py:432
  7.5 0.0 collective-permute-done.1.rest_1_
  7.5 0.0 collective-permute-done.2.rest_2_
  7.5 0.3 %neighbours_part.1 = (f32[2,8,16,128]{3,2,1,0:T(8,128)S(1)}, f32[2,2,2,16,128]{4,3,2,1,0:T(8,128)S(1)}, f32[2,2,16,128]{3,2,1,0:T(8,128)S(1)}, f32[2,2,16,128]{3,2,1,0:T(8,128)S(1)}) custom-call(s32[4,8,128]{2,1,0:T(8,128)S(1)} %get-tuple-element.30.sides_ref, s32[2,8,128]{2,1,0:T(8,128)S(1)} %get-tuple-element.31.bits_ref, ...), custom_call_target="tpu_custom_call" | custom-call | tf_op jit(solution)/shard_map/neighbours_part/pallas_call | solution.py:527
  7.8 0.6 %collective-permute-start.3 = (f32[2,2,16,128]{3,2,1,0:T(8,128)S(1)}, f32[2,2,16,128]{3,2,1,0:T(8,128)S(1)}, u32[]{:S(2)}, u32[]{:S(2)}) collective-permute-start(f32[2,2,16,128]{3,2,1,0:T(8,128)S(1)} %get-tuple-element.42), channel_id=1, source_target_pairs={{0,3},{1,2},{2,1},{3,0},{4,7},{5,6},{6,5},{7,4},{8,11},{9,10},{10,... | collective-permute-start | bytes 98312 | tf_op jit(solution)/shard_map/ppermute | solution.py:541
  8.4 1.4 %collective-permute-start.4 = (f32[2,2,16,128]{3,2,1,0:T(8,128)S(1)}, f32[2,2,16,128]{3,2,1,0:T(8,128)S(1)}, u32[]{:S(2)}, u32[]{:S(2)}) collective-permute-start(f32[2,2,16,128]{3,2,1,0:T(8,128)S(1)} %get-tuple-element.43), channel_id=1, source_target_pairs={{0,2},{1,3},{2,0},{3,1},{4,6},{5,7},{6,4},{7,5},{8,10},{9,11},{10,... | collective-permute-start | bytes 98312 | tf_op jit(solution)/shard_map/ppermute | solution.py:541
  9.9 0.0 collective-permute-start.8
  9.9 4.0 %collective-permute-start.7 = (f32[2,2,2,16,128]{4,3,2,1,0:T(8,128)S(1)}, f32[2,2,2,16,128]{4,3,2,1,0:T(8,128)S(1)}, u32[]{:S(2)}, u32[]{:S(2)}) collective-permute-start(f32[2,2,2,16,128]{4,3,2,1,0:T(8,128)S(1)} %get-tuple-element.44.rest_2_), channel_id=1, source_target_pairs={{0,4},{1,5},{2,6},{3,7},{4,0},{5,1},{6,2},{7,3},{8,12},{9,13},{10,... | collective-permute-start | bytes 196616 | tf_op jit(solution)/shard_map/ppermute | solution.py:432
  13.9 0.0 collective-permute-start.9
  13.9 0.0 collective-permute-done.3.refs_0_
  13.9 0.0 collective-permute-done.4.refs_1_
  13.9 0.4 %collective-permute-start.6 = (f32[2,2,2,16,128]{4,3,2,1,0:T(8,128)S(1)}, f32[2,2,2,16,128]{4,3,2,1,0:T(8,128)S(1)}, u32[]{:S(2)}, u32[]{:S(2)}) collective-permute-start(f32[2,2,2,16,128]{4,3,2,1,0:T(8,128)S(1)} %stack.1.others_ref), channel_id=1, source_target_pairs={{0,4},{1,5},{2,6},{3,7},{4,0},{5,1},{6,2},{7,3},{8,12},{9,13},{10,... | collective-permute-start | bytes 196616 | tf_op jit(solution)/shard_map/ppermute | solution.py:432
  14.4 0.2 %collective-permute-start.5 = (f32[2,2,2,16,128]{4,3,2,1,0:T(8,128)S(1)}, f32[2,2,2,16,128]{4,3,2,1,0:T(8,128)S(1)}, u32[]{:S(2)}, u32[]{:S(2)}) collective-permute-start(f32[2,2,2,16,128]{4,3,2,1,0:T(8,128)S(1)} %stack.1.others_ref), channel_id=1, source_target_pairs={{0,1},{1,0},{2,3},{3,2},{4,8},{5,9},{6,10},{7,11},{8,4},{9,5},{10,... | collective-permute-start | bytes 196616 | tf_op jit(solution)/shard_map/ppermute | solution.py:432
  14.6 0.0 collective-permute-done.8.rest_4_
  14.6 0.3 %collective-permute-start.11 = (f32[2,2,16,128]{3,2,1,0:T(8,128)S(1)}, f32[2,2,16,128]{3,2,1,0:T(8,128)S(1)}, u32[]{:S(2)}, u32[]{:S(2)}) collective-permute-start(f32[2,2,16,128]{3,2,1,0:T(8,128)S(1)} %slice_bitcast_fusion), channel_id=1, source_target_pairs={{0,1},{1,0},{2,3},{3,2},{4,5},{5,4},{6,7},{7,6},{8,9},{9,8},{10,11... | collective-permute-start | bytes 98312 | tf_op jit(solution)/shard_map/ppermute | solution.py:541
  14.9 1.4 %collective-permute-done.7.rest_3_ = f32[2,2,2,16,128]{4,3,2,1,0:T(8,128)S(1)} collective-permute-done((f32[2,2,2,16,128]{4,3,2,1,0:T(8,128)S(1)}, f32[2,2,2,16,128]{4,3,2,1,0:T(8,128)S(1)}, u32[]{:S(2)}, u32[]{:S(2)}) %collective-permute-start.7) | collective-permute-done | bytes 65568 | tf_op jit(solution)/shard_map/ppermute | solution.py:432
  16.3 0.0 collective-permute-start.10
  16.3 0.7 %write_fields.1 = (f32[1,8,16,128]{3,2,1,0:T(8,128)}, f32[1,8,16,128]{3,2,1,0:T(8,128)}) custom-call(f32[2,8,16,128]{3,2,1,0:T(8,128)S(1)} %get-tuple-element.39.final_ref), custom_call_target="tpu_custom_call" | custom-call | tf_op jit(solution)/shard_map/write_fields/pallas_call | solution.py:547
  17.0 0.0 collective-permute-done.9.rest_5_
  17.0 0.0 collective-permute-done.11.rest_7_
  17.0 0.5 %collective-permute-done.10.rest_6_ = f32[2,2,16,128]{3,2,1,0:T(8,128)S(1)} collective-permute-done((f32[2,2,16,128]{3,2,1,0:T(8,128)S(1)}, f32[2,2,16,128]{3,2,1,0:T(8,128)S(1)}, u32[]{:S(2)}, u32[]{:S(2)}) %collective-permute-start.10) | collective-permute-done | bytes 32800 | tf_op jit(solution)/shard_map/ppermute | solution.py:541
  17.5 1.0 %collective-permute-done.6.rest_1_ = f32[2,2,2,16,128]{4,3,2,1,0:T(8,128)S(1)} collective-permute-done((f32[2,2,2,16,128]{4,3,2,1,0:T(8,128)S(1)}, f32[2,2,2,16,128]{4,3,2,1,0:T(8,128)S(1)}, u32[]{:S(2)}, u32[]{:S(2)}) %collective-permute-start.6) | collective-permute-done | bytes 65568 | tf_op jit(solution)/shard_map/ppermute | solution.py:432
  18.5 0.0 collective-permute-done.5.rest_0_
  18.5 0.9 %image_products.1 = f32[33,2,16,128]{3,2,1,0:T(8,128)} custom-call(s32[4,8,128]{2,1,0:T(8,128)S(1)} %get-tuple-element.30.sides_ref, f32[2,2,2,16,128]{4,3,2,1,0:T(8,128)S(1)} %stack.1.others_ref, f32[2,2,2,16,128]{4,3,2,1,0:T(8,128)S(1)} %collective-permute-done.5.rest_0_, f32[2,2,2,16,128]{4,3,2,1,0:T(8,128)S(1)} %collective-permute-done.6.rest_1_, ...), custom_call_target="tpu_custom_call" | custom-call | tf_op jit(solution)/shard_map/image_products/pallas_call | solution.py:568
  (4 shorter events, 0.0 us)
Async XLA Ops:
  2.0 5.5 %collective-permute-start = (f32[20,8,128]{2,1,0:T(8,128)S(1)}, f32[20,8,128]{2,1,0:T(8,128)S(1)}, u32[]{:S(2)}, u32[]{:S(2)}) collective-permute-start(f32[20,8,128]{2,1,0:T(8,128)S(1)} %get-tuple-element.36), channel_id=1, source_target_pairs={{0,4},{1,5},{2,6},{3,7},{4,0},{5,1},{6,2},{7,3},{8,9},{9,8},{10,11... | collective-permute-start | bytes 245768 | tf_op jit(solution)/shard_map/ppermute | solution.py:432
  5.1 2.4 %collective-permute-start.1 = (f32[20,8,128]{2,1,0:T(8,128)S(1)}, f32[20,8,128]{2,1,0:T(8,128)S(1)}, u32[]{:S(2)}, u32[]{:S(2)}) collective-permute-start(f32[20,8,128]{2,1,0:T(8,128)S(1)} %get-tuple-element.37), channel_id=1, source_target_pairs={{0,1},{1,0},{2,3},{3,2},{4,8},{5,9},{6,10},{7,11},{8,4},{9,5},{10,... | collective-permute-start | bytes 245768 | tf_op jit(solution)/shard_map/ppermute | solution.py:432
  5.1 2.4 %collective-permute-start.2 = (f32[20,8,128]{2,1,0:T(8,128)S(1)}, f32[20,8,128]{2,1,0:T(8,128)S(1)}, u32[]{:S(2)}, u32[]{:S(2)}) collective-permute-start(f32[20,8,128]{2,1,0:T(8,128)S(1)} %get-tuple-element.38), channel_id=1, source_target_pairs={{0,1},{1,0},{2,3},{3,2},{4,5},{5,4},{6,7},{7,6},{8,12},{9,13},{10,... | collective-permute-start | bytes 245768 | tf_op jit(solution)/shard_map/ppermute | solution.py:432
  7.8 6.1 %collective-permute-start.3 = (f32[2,2,16,128]{3,2,1,0:T(8,128)S(1)}, f32[2,2,16,128]{3,2,1,0:T(8,128)S(1)}, u32[]{:S(2)}, u32[]{:S(2)}) collective-permute-start(f32[2,2,16,128]{3,2,1,0:T(8,128)S(1)} %get-tuple-element.42), channel_id=1, source_target_pairs={{0,3},{1,2},{2,1},{3,0},{4,7},{5,6},{6,5},{7,4},{8,11},{9,10},{10,... | collective-permute-start | bytes 98312 | tf_op jit(solution)/shard_map/ppermute | solution.py:541
  8.4 5.5 %collective-permute-start.4 = (f32[2,2,16,128]{3,2,1,0:T(8,128)S(1)}, f32[2,2,16,128]{3,2,1,0:T(8,128)S(1)}, u32[]{:S(2)}, u32[]{:S(2)}) collective-permute-start(f32[2,2,16,128]{3,2,1,0:T(8,128)S(1)} %get-tuple-element.43), channel_id=1, source_target_pairs={{0,2},{1,3},{2,0},{3,1},{4,6},{5,7},{6,4},{7,5},{8,10},{9,11},{10,... | collective-permute-start | bytes 98312 | tf_op jit(solution)/shard_map/ppermute | solution.py:541
  9.9 4.7 %collective-permute-start.8 = (f32[2,2,2,16,128]{4,3,2,1,0:T(8,128)S(1)}, f32[2,2,2,16,128]{4,3,2,1,0:T(8,128)S(1)}, u32[]{:S(2)}, u32[]{:S(2)}) collective-permute-start(f32[2,2,2,16,128]{4,3,2,1,0:T(8,128)S(1)} %get-tuple-element.44.rest_2_), channel_id=1, source_target_pairs={{0,1},{1,0},{2,3},{3,2},{4,8},{5,9},{6,10},{7,11},{8,4},{9,5},{10,... | collective-permute-start | bytes 196616 | tf_op jit(solution)/shard_map/ppermute | solution.py:432
  9.9 6.4 %collective-permute-start.7 = (f32[2,2,2,16,128]{4,3,2,1,0:T(8,128)S(1)}, f32[2,2,2,16,128]{4,3,2,1,0:T(8,128)S(1)}, u32[]{:S(2)}, u32[]{:S(2)}) collective-permute-start(f32[2,2,2,16,128]{4,3,2,1,0:T(8,128)S(1)} %get-tuple-element.44.rest_2_), channel_id=1, source_target_pairs={{0,4},{1,5},{2,6},{3,7},{4,0},{5,1},{6,2},{7,3},{8,12},{9,13},{10,... | collective-permute-start | bytes 196616 | tf_op jit(solution)/shard_map/ppermute | solution.py:432
  13.9 3.1 %collective-permute-start.9 = (f32[2,2,16,128]{3,2,1,0:T(8,128)S(1)}, f32[2,2,16,128]{3,2,1,0:T(8,128)S(1)}, u32[]{:S(2)}, u32[]{:S(2)}) collective-permute-start(f32[2,2,16,128]{3,2,1,0:T(8,128)S(1)} %slice_bitcast_fusion.2), channel_id=1, source_target_pairs={{0,1},{1,0},{2,3},{3,2},{4,5},{5,4},{6,7},{7,6},{8,9},{9,8},{10,11... | collective-permute-start | bytes 98312 | tf_op jit(solution)/shard_map/ppermute | solution.py:541
  13.9 4.6 %collective-permute-start.6 = (f32[2,2,2,16,128]{4,3,2,1,0:T(8,128)S(1)}, f32[2,2,2,16,128]{4,3,2,1,0:T(8,128)S(1)}, u32[]{:S(2)}, u32[]{:S(2)}) collective-permute-start(f32[2,2,2,16,128]{4,3,2,1,0:T(8,128)S(1)} %stack.1.others_ref), channel_id=1, source_target_pairs={{0,4},{1,5},{2,6},{3,7},{4,0},{5,1},{6,2},{7,3},{8,12},{9,13},{10,... | collective-permute-start | bytes 196616 | tf_op jit(solution)/shard_map/ppermute | solution.py:432
  14.4 4.1 %collective-permute-start.5 = (f32[2,2,2,16,128]{4,3,2,1,0:T(8,128)S(1)}, f32[2,2,2,16,128]{4,3,2,1,0:T(8,128)S(1)}, u32[]{:S(2)}, u32[]{:S(2)}) collective-permute-start(f32[2,2,2,16,128]{4,3,2,1,0:T(8,128)S(1)} %stack.1.others_ref), channel_id=1, source_target_pairs={{0,1},{1,0},{2,3},{3,2},{4,8},{5,9},{6,10},{7,11},{8,4},{9,5},{10,... | collective-permute-start | bytes 196616 | tf_op jit(solution)/shard_map/ppermute | solution.py:432
  14.6 2.4 %collective-permute-start.11 = (f32[2,2,16,128]{3,2,1,0:T(8,128)S(1)}, f32[2,2,16,128]{3,2,1,0:T(8,128)S(1)}, u32[]{:S(2)}, u32[]{:S(2)}) collective-permute-start(f32[2,2,16,128]{3,2,1,0:T(8,128)S(1)} %slice_bitcast_fusion), channel_id=1, source_target_pairs={{0,1},{1,0},{2,3},{3,2},{4,5},{5,4},{6,7},{7,6},{8,9},{9,8},{10,11... | collective-permute-start | bytes 98312 | tf_op jit(solution)/shard_map/ppermute | solution.py:541
  16.3 1.2 %collective-permute-start.10 = (f32[2,2,16,128]{3,2,1,0:T(8,128)S(1)}, f32[2,2,16,128]{3,2,1,0:T(8,128)S(1)}, u32[]{:S(2)}, u32[]{:S(2)}) collective-permute-start(f32[2,2,16,128]{3,2,1,0:T(8,128)S(1)} %slice_bitcast_fusion.1), channel_id=1, source_target_pairs={{0,1},{1,0},{2,3},{3,2},{4,5},{5,4},{6,7},{7,6},{8,9},{9,8},{10,11... | collective-permute-start | bytes 98312 | tf_op jit(solution)/shard_map/ppermute | solution.py:541

commit v21 on v19

--- a/solution.py
+++ b/solution.py
@@ -394,9 +394,12 @@
 
 def image_products(weight, sides_ref, others_ref, *rest):
     others_sides, rest = rest[1::-1], rest[2:]
-    mine_ref, last_ref, first_ref, *partner_refs, image_hbm, wide, image_ref, sems = rest
+    mine_ref, rest = rest[0], rest[1:]
+    mine_sides, rest = rest[ROUNDS - 1 :: -1], rest[ROUNDS:]
+    partner_refs, rest = rest[: 1 + ROUNDS], rest[1 + ROUNDS :]
+    image_hbm, wide, image_ref, sems = rest
     places = [
-        (mine_ref.at[0], (first_ref.at[0], last_ref.at[0])),
+        (mine_ref.at[0], [ref.at[0] for ref in mine_sides]),
         (partner_refs[0], partner_refs[1:]),
     ]
     for place in range(others_ref.shape[0]):
@@ -561,7 +564,7 @@
         compiler_params=params,
         name="stack",
     )(*came[::-1])
-    mine_sides = swap_rounds([mine] * 2)
+    mine_sides = swap_rounds([mine] * ROUNDS)
     others_sides = swap_rounds([others] * 2)
     partner = [swap_shots(value[1], 1) for value in (mine, *mine_sides)]
     operands = [others, *others_sides[::-1], mine, *mine_sides[::-1], *partner]

time: 19.1 us -> 18.6 us (0.974)
  the two profiles are of different devices: /device:TPU:0 before, /device:TPU:12 now
where the time goes in v21:
time: 18.6 us; the launch traced here: 18.4 us
  starting transfers between devices  8.42 us (45%)
  waiting for transfers between devices  4.6 us (25%)
  Pallas kernels  3.95 us (21%)
  between operations  1.37 us (7%)
    ppermute x8, starting transfers between devices, swap_tiles(): return lax.ppermute(value, ('tile', 'shot'), pairs)  5.67 us
    ppermute x8, waiting for transfers between devices, swap_tiles(): return lax.ppermute(value, ('tile', 'shot'), pairs)  4.19 us
    ppermute x6, starting transfers between devices, swap_shots(): lax.ppermute(value, 'shot', [(shot, shot ^ number) for shot in range(shot...  2.75 us
    pallas_call x1, Pallas kernels, per_device(): pl.pallas_call(own_edges, out_shape=(struct(*wavelet.shape), struct(*wide...  1.33 us
    pallas_call x1, Pallas kernels, per_device(): pl.pallas_call(functools.partial(image_products, weight), out_shape=struc...  0.94 us
    pallas_call x1, Pallas kernels, per_device(): pl.pallas_call(functools.partial(own_steps, width), out_shape=(struct(lev...  0.72 us
    pallas_call x1, Pallas kernels, per_device(): pl.pallas_call(write_fields, out_shape=(struct(1, levels, extent, across)...  0.67 us
    ppermute x6, waiting for transfers between devices, swap_shots(): lax.ppermute(value, 'shot', [(shot, shot ^ number) for shot in range(shot...  0.42 us
  transfers between devices with their start and end apart: 14, of which 5 were waited for; matrix products, arithmetic and copies ran while one was open for 0% of the time, Pallas kernels for 8%

profile of v21, /device:TPU:12, one launch (start us, length us, event | category | flops | bytes accessed | tf_op | source)
XLA Modules:
  0.0 18.4 jit_solution(18368001560540282661)
XLA Ops:
  0.6 1.3 %own_edges.1 = (f32[1,2]{1,0:T(1,128)S(1)}, f32[2,8,32,128]{3,2,1,0:T(8,128)S(1)}, f32[2,8,16,128]{3,2,1,0:T(8,128)S(1)}, s32[8,16,128]{2,1,0:T(8,128)S(1)}, f32...) custom-call(f32[1,16]{1,0:T(1,128)} %bitcast.9, ...), custom_call_target="tpu_custom_call" | custom-call | tf_op jit(solution)/shard_map/own_edges/pallas_call | solution.py:474
  2.0 0.5 %collective-permute-start = (f32[20,8,128]{2,1,0:T(8,128)S(1)}, f32[20,8,128]{2,1,0:T(8,128)S(1)}, u32[]{:S(2)}, u32[]{:S(2)}) collective-permute-start(f32[20,8,128]{2,1,0:T(8,128)S(1)} %get-tuple-element.36), channel_id=1, source_target_pairs={{0,4},{1,5},{2,6},{3,7},{4,0},{5,1},{6,2},{7,3},{8,9},{9,8},{10,11... | collective-permute-start | bytes 245768 | tf_op jit(solution)/shard_map/ppermute | solution.py:435
  2.5 1.2 %collective-permute-start.1 = (f32[20,8,128]{2,1,0:T(8,128)S(1)}, f32[20,8,128]{2,1,0:T(8,128)S(1)}, u32[]{:S(2)}, u32[]{:S(2)}) collective-permute-start(f32[20,8,128]{2,1,0:T(8,128)S(1)} %get-tuple-element.37), channel_id=1, source_target_pairs={{0,1},{1,0},{2,3},{3,2},{4,8},{5,9},{6,10},{7,11},{8,4},{9,5},{10,... | collective-permute-start | bytes 245768 | tf_op jit(solution)/shard_map/ppermute | solution.py:435
  3.7 0.2 collective-permute-start.2
  4.5 0.7 %own_steps.1 = (f32[8,16,128]{2,1,0:T(8,128)S(1)}, f32[2,8,16,128]{3,2,1,0:T(8,128)S(1)}, f32[2,8,8,128]{3,2,1,0:T(8,128)S(1)}, f32[8,32,128]{2,1,0:T(8,128)S(1)...) custom-call(s32[1]{0:T(128)S(6)} %copy.13.cell_ref, f32[1,2]{1,0:T(1,128)S(1)} %get-tuple-element.24.amps_ref, ...), custom_call_target="tpu_custom_call" | custom-call | tf_op jit(solution)/shard_map/own_steps/pallas_call | solution.py:513
  5.2 1.2 %collective-permute-done.rest_0_ = f32[20,8,128]{2,1,0:T(8,128)S(1)} collective-permute-done((f32[20,8,128]{2,1,0:T(8,128)S(1)}, f32[20,8,128]{2,1,0:T(8,128)S(1)}, u32[]{:S(2)}, u32[]{:S(2)}) %collective-permute-start) | collective-permute-done | bytes 81952 | tf_op jit(solution)/shard_map/ppermute | solution.py:435
  6.5 0.4 %collective-permute-done.1.rest_1_ = f32[20,8,128]{2,1,0:T(8,128)S(1)} collective-permute-done((f32[20,8,128]{2,1,0:T(8,128)S(1)}, f32[20,8,128]{2,1,0:T(8,128)S(1)}, u32[]{:S(2)}, u32[]{:S(2)}) %collective-permute-start.1) | collective-permute-done | bytes 81952 | tf_op jit(solution)/shard_map/ppermute | solution.py:435
  6.9 0.0 collective-permute-done.2.rest_2_
  6.9 0.3 %neighbours_part.1 = (f32[2,8,16,128]{3,2,1,0:T(8,128)S(1)}, f32[2,2,2,16,128]{4,3,2,1,0:T(8,128)S(1)}, f32[2,2,16,128]{3,2,1,0:T(8,128)S(1)}, f32[2,2,16,128]{3,2,1,0:T(8,128)S(1)}) custom-call(s32[4,8,128]{2,1,0:T(8,128)S(1)} %get-tuple-element.30.sides_ref, s32[2,8,128]{2,1,0:T(8,128)S(1)} %get-tuple-element.31.bits_ref, ...), custom_call_target="tpu_custom_call" | custom-call | tf_op jit(solution)/shard_map/neighbours_part/pallas_call | solution.py:530
  7.2 0.2 %collective-permute-start.3 = (f32[2,2,16,128]{3,2,1,0:T(8,128)S(1)}, f32[2,2,16,128]{3,2,1,0:T(8,128)S(1)}, u32[]{:S(2)}, u32[]{:S(2)}) collective-permute-start(f32[2,2,16,128]{3,2,1,0:T(8,128)S(1)} %get-tuple-element.42), channel_id=1, source_target_pairs={{0,3},{1,2},{2,1},{3,0},{4,7},{5,6},{6,5},{7,4},{8,11},{9,10},{10,... | collective-permute-start | bytes 98312 | tf_op jit(solution)/shard_map/ppermute | solution.py:544
  7.4 1.4 %collective-permute-start.4 = (f32[2,2,16,128]{3,2,1,0:T(8,128)S(1)}, f32[2,2,16,128]{3,2,1,0:T(8,128)S(1)}, u32[]{:S(2)}, u32[]{:S(2)}) collective-permute-start(f32[2,2,16,128]{3,2,1,0:T(8,128)S(1)} %get-tuple-element.43), channel_id=1, source_target_pairs={{0,2},{1,3},{2,0},{3,1},{4,6},{5,7},{6,4},{7,5},{8,10},{9,11},{10,... | collective-permute-start | bytes 98312 | tf_op jit(solution)/shard_map/ppermute | solution.py:544
  8.9 0.0 collective-permute-start.9
  8.9 2.3 %collective-permute-start.8 = (f32[2,2,2,16,128]{4,3,2,1,0:T(8,128)S(1)}, f32[2,2,2,16,128]{4,3,2,1,0:T(8,128)S(1)}, u32[]{:S(2)}, u32[]{:S(2)}) collective-permute-start(f32[2,2,2,16,128]{4,3,2,1,0:T(8,128)S(1)} %get-tuple-element.44.rest_2_), channel_id=1, source_target_pairs={{0,1},{1,0},{2,3},{3,2},{4,8},{5,9},{6,10},{7,11},{8,4},{9,5},{10,... | collective-permute-start | bytes 196616 | tf_op jit(solution)/shard_map/ppermute | solution.py:435
  11.2 0.0 collective-permute-start.7
  11.2 0.0 collective-permute-done.3.refs_0_
  11.2 0.5 %collective-permute-start.10 = (f32[2,2,16,128]{3,2,1,0:T(8,128)S(1)}, f32[2,2,16,128]{3,2,1,0:T(8,128)S(1)}, u32[]{:S(2)}, u32[]{:S(2)}) collective-permute-start(f32[2,2,16,128]{3,2,1,0:T(8,128)S(1)} %slice_bitcast_fusion.3), channel_id=1, source_target_pairs={{0,1},{1,0},{2,3},{3,2},{4,5},{5,4},{6,7},{7,6},{8,9},{9,8},{10,11... | collective-permute-start | bytes 98312 | tf_op jit(solution)/shard_map/ppermute | solution.py:544
  11.7 0.0 collective-permute-done.4.refs_1_
  11.7 0.1 collective-permute-start.6
  11.8 1.4 %collective-permute-done.9.rest_5_ = f32[2,2,2,16,128]{4,3,2,1,0:T(8,128)S(1)} collective-permute-done((f32[2,2,2,16,128]{4,3,2,1,0:T(8,128)S(1)}, f32[2,2,2,16,128]{4,3,2,1,0:T(8,128)S(1)}, u32[]{:S(2)}, u32[]{:S(2)}) %collective-permute-start.9) | collective-permute-done | bytes 65568 | tf_op jit(solution)/shard_map/ppermute | solution.py:435
  13.1 1.4 %collective-permute-start.5 = (f32[2,2,2,16,128]{4,3,2,1,0:T(8,128)S(1)}, f32[2,2,2,16,128]{4,3,2,1,0:T(8,128)S(1)}, u32[]{:S(2)}, u32[]{:S(2)}) collective-permute-start(f32[2,2,2,16,128]{4,3,2,1,0:T(8,128)S(1)} %stack.1.others_ref), channel_id=1, source_target_pairs={{0,1},{1,0},{2,3},{3,2},{4,8},{5,9},{6,10},{7,11},{8,4},{9,5},{10,... | collective-permute-start | bytes 196616 | tf_op jit(solution)/shard_map/ppermute | solution.py:435
  14.6 0.0 collective-permute-done.8.rest_4_
  14.6 0.0 collective-permute-start.11
  14.6 0.0 collective-permute-done.7.rest_3_
  14.6 0.5 %collective-permute-start.12 = (f32[2,2,16,128]{3,2,1,0:T(8,128)S(1)}, f32[2,2,16,128]{3,2,1,0:T(8,128)S(1)}, u32[]{:S(2)}, u32[]{:S(2)}) collective-permute-start(f32[2,2,16,128]{3,2,1,0:T(8,128)S(1)} %slice_bitcast_fusion.1), channel_id=1, source_target_pairs={{0,1},{1,0},{2,3},{3,2},{4,5},{5,4},{6,7},{7,6},{8,9},{9,8},{10,11... | collective-permute-start | bytes 98312 | tf_op jit(solution)/shard_map/ppermute | solution.py:544
  15.1 0.0 collective-permute-done.10.rest_6_
  15.1 0.1 collective-permute-start.13
  15.2 0.7 %write_fields.1 = (f32[1,8,16,128]{3,2,1,0:T(8,128)}, f32[1,8,16,128]{3,2,1,0:T(8,128)}) custom-call(f32[2,8,16,128]{3,2,1,0:T(8,128)S(1)} %get-tuple-element.39.final_ref), custom_call_target="tpu_custom_call" | custom-call | tf_op jit(solution)/shard_map/write_fields/pallas_call | solution.py:550
  15.9 0.0 collective-permute-done.11.rest_7_
  15.9 0.1 collective-permute-done.12.rest_8_
  15.9 0.4 %collective-permute-done.13.rest_9_ = f32[2,2,16,128]{3,2,1,0:T(8,128)S(1)} collective-permute-done((f32[2,2,16,128]{3,2,1,0:T(8,128)S(1)}, f32[2,2,16,128]{3,2,1,0:T(8,128)S(1)}, u32[]{:S(2)}, u32[]{:S(2)}) %collective-permute-start.13) | collective-permute-done | bytes 32800 | tf_op jit(solution)/shard_map/ppermute | solution.py:544
  16.3 0.0 collective-permute-done.6.rest_1_
  16.3 1.1 %collective-permute-done.5.rest_0_ = f32[2,2,2,16,128]{4,3,2,1,0:T(8,128)S(1)} collective-permute-done((f32[2,2,2,16,128]{4,3,2,1,0:T(8,128)S(1)}, f32[2,2,2,16,128]{4,3,2,1,0:T(8,128)S(1)}, u32[]{:S(2)}, u32[]{:S(2)}) %collective-permute-start.5) | collective-permute-done | bytes 65568 | tf_op jit(solution)/shard_map/ppermute | solution.py:435
  17.4 0.9 %image_products.1 = f32[33,2,16,128]{3,2,1,0:T(8,128)} custom-call(s32[4,8,128]{2,1,0:T(8,128)S(1)} %get-tuple-element.30.sides_ref, f32[2,2,2,16,128]{4,3,2,1,0:T(8,128)S(1)} %stack.1.others_ref, f32[2,2,2,16,128]{4,3,2,1,0:T(8,128)S(1)} %collective-permute-done.5.rest_0_, f32[2,2,2,16,128]{4,3,2,1,0:T(8,128)S(1)} %collective-permute-done.6.rest_1_, ...), custom_call_target="tpu_custom_call" | custom-call | tf_op jit(solution)/shard_map/image_products/pallas_call | solution.py:571
  (5 shorter events, 0.0 us)
Async XLA Ops:
  2.0 4.5 %collective-permute-start = (f32[20,8,128]{2,1,0:T(8,128)S(1)}, f32[20,8,128]{2,1,0:T(8,128)S(1)}, u32[]{:S(2)}, u32[]{:S(2)}) collective-permute-start(f32[20,8,128]{2,1,0:T(8,128)S(1)} %get-tuple-element.36), channel_id=1, source_target_pairs={{0,4},{1,5},{2,6},{3,7},{4,0},{5,1},{6,2},{7,3},{8,9},{9,8},{10,11... | collective-permute-start | bytes 245768 | tf_op jit(solution)/shard_map/ppermute | solution.py:435
  2.5 4.4 %collective-permute-start.1 = (f32[20,8,128]{2,1,0:T(8,128)S(1)}, f32[20,8,128]{2,1,0:T(8,128)S(1)}, u32[]{:S(2)}, u32[]{:S(2)}) collective-permute-start(f32[20,8,128]{2,1,0:T(8,128)S(1)} %get-tuple-element.37), channel_id=1, source_target_pairs={{0,1},{1,0},{2,3},{3,2},{4,8},{5,9},{6,10},{7,11},{8,4},{9,5},{10,... | collective-permute-start | bytes 245768 | tf_op jit(solution)/shard_map/ppermute | solution.py:435
  3.7 3.2 %collective-permute-start.2 = (f32[20,8,128]{2,1,0:T(8,128)S(1)}, f32[20,8,128]{2,1,0:T(8,128)S(1)}, u32[]{:S(2)}, u32[]{:S(2)}) collective-permute-start(f32[20,8,128]{2,1,0:T(8,128)S(1)} %get-tuple-element.38), channel_id=1, source_target_pairs={{0,1},{1,0},{2,3},{3,2},{4,5},{5,4},{6,7},{7,6},{8,12},{9,13},{10,... | collective-permute-start | bytes 245768 | tf_op jit(solution)/shard_map/ppermute | solution.py:435
  7.2 4.0 %collective-permute-start.3 = (f32[2,2,16,128]{3,2,1,0:T(8,128)S(1)}, f32[2,2,16,128]{3,2,1,0:T(8,128)S(1)}, u32[]{:S(2)}, u32[]{:S(2)}) collective-permute-start(f32[2,2,16,128]{3,2,1,0:T(8,128)S(1)} %get-tuple-element.42), channel_id=1, source_target_pairs={{0,3},{1,2},{2,1},{3,0},{4,7},{5,6},{6,5},{7,4},{8,11},{9,10},{10,... | collective-permute-start | bytes 98312 | tf_op jit(solution)/shard_map/ppermute | solution.py:544
  7.4 4.3 %collective-permute-start.4 = (f32[2,2,16,128]{3,2,1,0:T(8,128)S(1)}, f32[2,2,16,128]{3,2,1,0:T(8,128)S(1)}, u32[]{:S(2)}, u32[]{:S(2)}) collective-permute-start(f32[2,2,16,128]{3,2,1,0:T(8,128)S(1)} %get-tuple-element.43), channel_id=1, source_target_pairs={{0,2},{1,3},{2,0},{3,1},{4,6},{5,7},{6,4},{7,5},{8,10},{9,11},{10,... | collective-permute-start | bytes 98312 | tf_op jit(solution)/shard_map/ppermute | solution.py:544
  8.9 4.3 %collective-permute-start.9 = (f32[2,2,2,16,128]{4,3,2,1,0:T(8,128)S(1)}, f32[2,2,2,16,128]{4,3,2,1,0:T(8,128)S(1)}, u32[]{:S(2)}, u32[]{:S(2)}) collective-permute-start(f32[2,2,2,16,128]{4,3,2,1,0:T(8,128)S(1)} %get-tuple-element.44.rest_2_), channel_id=1, source_target_pairs={{0,4},{1,5},{2,6},{3,7},{4,0},{5,1},{6,2},{7,3},{8,9},{9,8},{10,11... | collective-permute-start | bytes 196616 | tf_op jit(solution)/shard_map/ppermute | solution.py:435
  8.9 5.7 %collective-permute-start.8 = (f32[2,2,2,16,128]{4,3,2,1,0:T(8,128)S(1)}, f32[2,2,2,16,128]{4,3,2,1,0:T(8,128)S(1)}, u32[]{:S(2)}, u32[]{:S(2)}) collective-permute-start(f32[2,2,2,16,128]{4,3,2,1,0:T(8,128)S(1)} %get-tuple-element.44.rest_2_), channel_id=1, source_target_pairs={{0,1},{1,0},{2,3},{3,2},{4,8},{5,9},{6,10},{7,11},{8,4},{9,5},{10,... | collective-permute-start | bytes 196616 | tf_op jit(solution)/shard_map/ppermute | solution.py:435
  11.2 3.4 %collective-permute-start.7 = (f32[2,2,2,16,128]{4,3,2,1,0:T(8,128)S(1)}, f32[2,2,2,16,128]{4,3,2,1,0:T(8,128)S(1)}, u32[]{:S(2)}, u32[]{:S(2)}) collective-permute-start(f32[2,2,2,16,128]{4,3,2,1,0:T(8,128)S(1)} %get-tuple-element.44.rest_2_), channel_id=1, source_target_pairs={{0,1},{1,0},{2,3},{3,2},{4,5},{5,4},{6,7},{7,6},{8,12},{9,13},{10,... | collective-permute-start | bytes 196616 | tf_op jit(solution)/shard_map/ppermute | solution.py:435
  11.2 3.9 %collective-permute-start.10 = (f32[2,2,16,128]{3,2,1,0:T(8,128)S(1)}, f32[2,2,16,128]{3,2,1,0:T(8,128)S(1)}, u32[]{:S(2)}, u32[]{:S(2)}) collective-permute-start(f32[2,2,16,128]{3,2,1,0:T(8,128)S(1)} %slice_bitcast_fusion.3), channel_id=1, source_target_pairs={{0,1},{1,0},{2,3},{3,2},{4,5},{5,4},{6,7},{7,6},{8,9},{9,8},{10,11... | collective-permute-start | bytes 98312 | tf_op jit(solution)/shard_map/ppermute | solution.py:544
  11.7 4.6 %collective-permute-start.6 = (f32[2,2,2,16,128]{4,3,2,1,0:T(8,128)S(1)}, f32[2,2,2,16,128]{4,3,2,1,0:T(8,128)S(1)}, u32[]{:S(2)}, u32[]{:S(2)}) collective-permute-start(f32[2,2,2,16,128]{4,3,2,1,0:T(8,128)S(1)} %stack.1.others_ref), channel_id=1, source_target_pairs={{0,4},{1,5},{2,6},{3,7},{4,0},{5,1},{6,2},{7,3},{8,12},{9,13},{10,... | collective-permute-start | bytes 196616 | tf_op jit(solution)/shard_map/ppermute | solution.py:435
  13.1 4.3 %collective-permute-start.5 = (f32[2,2,2,16,128]{4,3,2,1,0:T(8,128)S(1)}, f32[2,2,2,16,128]{4,3,2,1,0:T(8,128)S(1)}, u32[]{:S(2)}, u32[]{:S(2)}) collective-permute-start(f32[2,2,2,16,128]{4,3,2,1,0:T(8,128)S(1)} %stack.1.others_ref), channel_id=1, source_target_pairs={{0,1},{1,0},{2,3},{3,2},{4,8},{5,9},{6,10},{7,11},{8,4},{9,5},{10,... | collective-permute-start | bytes 196616 | tf_op jit(solution)/shard_map/ppermute | solution.py:435
  14.6 1.3 %collective-permute-start.11 = (f32[2,2,16,128]{3,2,1,0:T(8,128)S(1)}, f32[2,2,16,128]{3,2,1,0:T(8,128)S(1)}, u32[]{:S(2)}, u32[]{:S(2)}) collective-permute-start(f32[2,2,16,128]{3,2,1,0:T(8,128)S(1)} %slice_bitcast_fusion.2), channel_id=1, source_target_pairs={{0,1},{1,0},{2,3},{3,2},{4,5},{5,4},{6,7},{7,6},{8,9},{9,8},{10,11... | collective-permute-start | bytes 98312 | tf_op jit(solution)/shard_map/ppermute | solution.py:544
  14.6 1.3 %collective-permute-start.12 = (f32[2,2,16,128]{3,2,1,0:T(8,128)S(1)}, f32[2,2,16,128]{3,2,1,0:T(8,128)S(1)}, u32[]{:S(2)}, u32[]{:S(2)}) collective-permute-start(f32[2,2,16,128]{3,2,1,0:T(8,128)S(1)} %slice_bitcast_fusion.1), channel_id=1, source_target_pairs={{0,1},{1,0},{2,3},{3,2},{4,5},{5,4},{6,7},{7,6},{8,9},{9,8},{10,11... | collective-permute-start | bytes 98312 | tf_op jit(solution)/shard_map/ppermute | solution.py:544
  15.1 1.2 %collective-permute-start.13 = (f32[2,2,16,128]{3,2,1,0:T(8,128)S(1)}, f32[2,2,16,128]{3,2,1,0:T(8,128)S(1)}, u32[]{:S(2)}, u32[]{:S(2)}) collective-permute-start(f32[2,2,16,128]{3,2,1,0:T(8,128)S(1)} %slice_bitcast_fusion), channel_id=1, source_target_pairs={{0,1},{1,0},{2,3},{3,2},{4,5},{5,4},{6,7},{7,6},{8,9},{9,8},{10,11... | collective-permute-start | bytes 98312 | tf_op jit(solution)/shard_map/ppermute | solution.py:544

commit v22 on v21

--- a/solution.py
+++ b/solution.py
@@ -381,6 +381,10 @@
         refs[-1][place] = refs[place][...]
 
 
+def hold(mine_ref, _others_ref, held_ref):
+    held_ref[...] = mine_ref[...]
+
+
 def write_fields(final_ref, src_hbm, rec_hbm, sems):
     copies = [
         pltpu.make_async_copy(final_ref.at[field], out.at[0], sems.at[field])
@@ -393,7 +397,7 @@
 
 
 def image_products(weight, sides_ref, others_ref, *rest):
-    others_sides, rest = rest[1::-1], rest[2:]
+    others_sides, rest = rest[ROUNDS - 1 :: -1], rest[ROUNDS:]
     mine_ref, rest = rest[0], rest[1:]
     mine_sides, rest = rest[ROUNDS - 1 :: -1], rest[ROUNDS:]
     partner_refs, rest = rest[: 1 + ROUNDS], rest[1 + ROUNDS :]
@@ -565,8 +569,16 @@
         name="stack",
     )(*came[::-1])
     mine_sides = swap_rounds([mine] * ROUNDS)
-    others_sides = swap_rounds([others] * 2)
-    partner = [swap_shots(value[1], 1) for value in (mine, *mine_sides)]
+    others_sides = swap_rounds([others] * ROUNDS)
+    held = pl.pallas_call(
+        hold,
+        out_shape=block,
+        in_specs=[VMEM] * 2,
+        out_specs=VMEM,
+        compiler_params=params,
+        name="hold",
+    )(mine[1], others)
+    partner = [swap_shots(value, 1) for value in (held, *(side[1] for side in mine_sides))]
     operands = [others, *others_sides[::-1], mine, *mine_sides[::-1], *partner]
     image = pl.pallas_call(
         functools.partial(image_products, weight),

time: 18.6 us -> 18.7 us (level)
  the two profiles are of different devices: /device:TPU:12 before, /device:TPU:0 now
where the time goes in v22:
time: 18.7 us; the launch traced here: 18.4 us
  starting transfers between devices  11.7 us (63%)
  Pallas kernels  3.96 us (21%)
  waiting for transfers between devices  1.46 us (8%)
  between operations  1.34 us (7%)
    ppermute x9, starting transfers between devices, swap_tiles(): return lax.ppermute(value, ('tile', 'shot'), pairs)  8.6 us
    ppermute x6, starting transfers between devices, swap_shots(): lax.ppermute(value, 'shot', [(shot, shot ^ number) for shot in range(shot...  3.08 us
    pallas_call x1, Pallas kernels, per_device(): pl.pallas_call(own_edges, out_shape=(struct(*wavelet.shape), struct(*wide...  1.33 us
    pallas_call x1, Pallas kernels, per_device(): pl.pallas_call(functools.partial(image_products, weight), out_shape=struc...  0.95 us
    ppermute x6, waiting for transfers between devices, swap_shots(): lax.ppermute(value, 'shot', [(shot, shot ^ number) for shot in range(shot...  0.88 us
    pallas_call x1, Pallas kernels, per_device(): pl.pallas_call(functools.partial(own_steps, width), out_shape=(struct(lev...  0.72 us
    pallas_call x1, Pallas kernels, per_device(): pl.pallas_call(write_fields, out_shape=(struct(1, levels, extent, across)...  0.67 us
    ppermute x9, waiting for transfers between devices, swap_tiles(): return lax.ppermute(value, ('tile', 'shot'), pairs)  0.58 us
  transfers between devices with their start and end apart: 15, of which 3 were waited for; matrix products, arithmetic and copies ran while one was open for 0% of the time, Pallas kernels for 8%

profile of v22, /device:TPU:0, one launch (start us, length us, event | category | flops | bytes accessed | tf_op | source)
XLA Modules:
  0.0 18.4 jit_solution(14788408253621515510)
XLA Ops:
  0.6 1.3 %own_edges.1 = (f32[1,2]{1,0:T(1,128)S(1)}, f32[2,8,32,128]{3,2,1,0:T(8,128)S(1)}, f32[2,8,16,128]{3,2,1,0:T(8,128)S(1)}, s32[8,16,128]{2,1,0:T(8,128)S(1)}, f32...) custom-call(f32[1,16]{1,0:T(1,128)} %bitcast.9, ...), custom_call_target="tpu_custom_call" | custom-call | tf_op jit(solution)/shard_map/own_edges/pallas_call | solution.py:478
  2.0 3.1 %collective-permute-start = (f32[20,8,128]{2,1,0:T(8,128)S(1)}, f32[20,8,128]{2,1,0:T(8,128)S(1)}, u32[]{:S(2)}, u32[]{:S(2)}) collective-permute-start(f32[20,8,128]{2,1,0:T(8,128)S(1)} %get-tuple-element.36), channel_id=1, source_target_pairs={{0,4},{1,5},{2,6},{3,7},{4,0},{5,1},{6,2},{7,3},{8,9},{9,8},{10,11... | collective-permute-start | bytes 245768 | tf_op jit(solution)/shard_map/ppermute | solution.py:439
  5.1 0.0 collective-permute-start.1
  5.1 0.5 %collective-permute-start.2 = (f32[20,8,128]{2,1,0:T(8,128)S(1)}, f32[20,8,128]{2,1,0:T(8,128)S(1)}, u32[]{:S(2)}, u32[]{:S(2)}) collective-permute-start(f32[20,8,128]{2,1,0:T(8,128)S(1)} %get-tuple-element.38), channel_id=1, source_target_pairs={{0,1},{1,0},{2,3},{3,2},{4,5},{5,4},{6,7},{7,6},{8,12},{9,13},{10,... | collective-permute-start | bytes 245768 | tf_op jit(solution)/shard_map/ppermute | solution.py:439
  6.2 0.7 %own_steps.1 = (f32[8,16,128]{2,1,0:T(8,128)S(1)}, f32[2,8,16,128]{3,2,1,0:T(8,128)S(1)}, f32[2,8,8,128]{3,2,1,0:T(8,128)S(1)}, f32[8,32,128]{2,1,0:T(8,128)S(1)...) custom-call(s32[1]{0:T(128)S(6)} %copy.13.cell_ref, f32[1,2]{1,0:T(1,128)S(1)} %get-tuple-element.24.amps_ref, ...), custom_call_target="tpu_custom_call" | custom-call | tf_op jit(solution)/shard_map/own_steps/pallas_call | solution.py:517
  6.9 0.6 %collective-permute-done.rest_0_ = f32[20,8,128]{2,1,0:T(8,128)S(1)} collective-permute-done((f32[20,8,128]{2,1,0:T(8,128)S(1)}, f32[20,8,128]{2,1,0:T(8,128)S(1)}, u32[]{:S(2)}, u32[]{:S(2)}) %collective-permute-start) | collective-permute-done | bytes 81952 | tf_op jit(solution)/shard_map/ppermute | solution.py:439
  7.5 0.0 collective-permute-done.1.rest_1_
  7.5 0.0 collective-permute-done.2.rest_2_
  7.5 0.3 %neighbours_part.1 = (f32[2,8,16,128]{3,2,1,0:T(8,128)S(1)}, f32[2,2,2,16,128]{4,3,2,1,0:T(8,128)S(1)}, f32[2,2,16,128]{3,2,1,0:T(8,128)S(1)}, f32[2,2,16,128]{3,2,1,0:T(8,128)S(1)}) custom-call(s32[4,8,128]{2,1,0:T(8,128)S(1)} %get-tuple-element.30.sides_ref, s32[2,8,128]{2,1,0:T(8,128)S(1)} %get-tuple-element.31.bits_ref, ...), custom_call_target="tpu_custom_call" | custom-call | tf_op jit(solution)/shard_map/neighbours_part/pallas_call | solution.py:534
  7.8 0.6 %collective-permute-start.3 = (f32[2,2,16,128]{3,2,1,0:T(8,128)S(1)}, f32[2,2,16,128]{3,2,1,0:T(8,128)S(1)}, u32[]{:S(2)}, u32[]{:S(2)}) collective-permute-start(f32[2,2,16,128]{3,2,1,0:T(8,128)S(1)} %get-tuple-element.42), channel_id=1, source_target_pairs={{0,3},{1,2},{2,1},{3,0},{4,7},{5,6},{6,5},{7,4},{8,11},{9,10},{10,... | collective-permute-start | bytes 98312 | tf_op jit(solution)/shard_map/ppermute | solution.py:548
  8.4 1.4 %collective-permute-start.4 = (f32[2,2,16,128]{3,2,1,0:T(8,128)S(1)}, f32[2,2,16,128]{3,2,1,0:T(8,128)S(1)}, u32[]{:S(2)}, u32[]{:S(2)}) collective-permute-start(f32[2,2,16,128]{3,2,1,0:T(8,128)S(1)} %get-tuple-element.43), channel_id=1, source_target_pairs={{0,2},{1,3},{2,0},{3,1},{4,6},{5,7},{6,4},{7,5},{8,10},{9,11},{10,... | collective-permute-start | bytes 98312 | tf_op jit(solution)/shard_map/ppermute | solution.py:548
  9.9 2.0 %collective-permute-start.10 = (f32[2,2,2,16,128]{4,3,2,1,0:T(8,128)S(1)}, f32[2,2,2,16,128]{4,3,2,1,0:T(8,128)S(1)}, u32[]{:S(2)}, u32[]{:S(2)}) collective-permute-start(f32[2,2,2,16,128]{4,3,2,1,0:T(8,128)S(1)} %get-tuple-element.44.rest_3_), channel_id=1, source_target_pairs={{0,4},{1,5},{2,6},{3,7},{4,0},{5,1},{6,2},{7,3},{8,9},{9,8},{10,11... | collective-permute-start | bytes 196616 | tf_op jit(solution)/shard_map/ppermute | solution.py:439
  11.9 0.0 collective-permute-start.9
  11.9 0.5 %collective-permute-start.8 = (f32[2,2,2,16,128]{4,3,2,1,0:T(8,128)S(1)}, f32[2,2,2,16,128]{4,3,2,1,0:T(8,128)S(1)}, u32[]{:S(2)}, u32[]{:S(2)}) collective-permute-start(f32[2,2,2,16,128]{4,3,2,1,0:T(8,128)S(1)} %get-tuple-element.44.rest_3_), channel_id=1, source_target_pairs={{0,1},{1,0},{2,3},{3,2},{4,5},{5,4},{6,7},{7,6},{8,12},{9,13},{10,... | collective-permute-start | bytes 196616 | tf_op jit(solution)/shard_map/ppermute | solution.py:439
  12.4 0.0 collective-permute-done.3.refs_0_
  12.4 0.0 collective-permute-done.4.refs_1_
  12.4 1.9 %collective-permute-start.7 = (f32[2,2,2,16,128]{4,3,2,1,0:T(8,128)S(1)}, f32[2,2,2,16,128]{4,3,2,1,0:T(8,128)S(1)}, u32[]{:S(2)}, u32[]{:S(2)}) collective-permute-start(f32[2,2,2,16,128]{4,3,2,1,0:T(8,128)S(1)} %stack.1._others_ref.others_ref), channel_id=1, source_target_pairs={{0,4},{1,5},{2,6},{3,7},{4,0},{5,1},{6,2},{7,3},{8,9},{9,8},{10,11... | collective-permute-start | bytes 196616 | tf_op jit(solution)/shard_map/ppermute | solution.py:439
  14.4 0.0 collective-permute-start.6
  14.4 0.0 collective-permute-done.10.rest_6_
  14.4 0.5 %collective-permute-start.5 = (f32[2,2,2,16,128]{4,3,2,1,0:T(8,128)S(1)}, f32[2,2,2,16,128]{4,3,2,1,0:T(8,128)S(1)}, u32[]{:S(2)}, u32[]{:S(2)}) collective-permute-start(f32[2,2,2,16,128]{4,3,2,1,0:T(8,128)S(1)} %stack.1._others_ref.others_ref), channel_id=1, source_target_pairs={{0,1},{1,0},{2,3},{3,2},{4,5},{5,4},{6,7},{7,6},{8,12},{9,13},{10,... | collective-permute-start | bytes 196616 | tf_op jit(solution)/shard_map/ppermute | solution.py:439
  14.9 0.0 collective-permute-done.9.rest_5_
  14.9 0.1 collective-permute-start.11
  15.0 0.0 collective-permute-done.8.rest_4_
  15.0 0.4 %collective-permute-start.12 = (f32[2,2,16,128]{3,2,1,0:T(8,128)S(1)}, f32[2,2,16,128]{3,2,1,0:T(8,128)S(1)}, u32[]{:S(2)}, u32[]{:S(2)}) collective-permute-start(f32[2,2,16,128]{3,2,1,0:T(8,128)S(1)} %slice_bitcast_fusion.2), channel_id=1, source_target_pairs={{0,1},{1,0},{2,3},{3,2},{4,5},{5,4},{6,7},{7,6},{8,9},{9,8},{10,11... | collective-permute-start | bytes 98312 | tf_op jit(solution)/shard_map/ppermute | solution.py:548
  15.4 0.7 %collective-permute-done.11.rest_7_ = f32[2,2,16,128]{3,2,1,0:T(8,128)S(1)} collective-permute-done((f32[2,2,16,128]{3,2,1,0:T(8,128)S(1)}, f32[2,2,16,128]{3,2,1,0:T(8,128)S(1)}, u32[]{:S(2)}, u32[]{:S(2)}) %collective-permute-start.11) | collective-permute-done | bytes 32800 | tf_op jit(solution)/shard_map/ppermute | solution.py:548
  16.1 0.2 collective-permute-start.13
  16.3 0.0 collective-permute-done.12.rest_8_
  16.3 0.3 %collective-permute-start.14 = (f32[2,2,16,128]{3,2,1,0:T(8,128)S(1)}, f32[2,2,16,128]{3,2,1,0:T(8,128)S(1)}, u32[]{:S(2)}, u32[]{:S(2)}) collective-permute-start(f32[2,2,16,128]{3,2,1,0:T(8,128)S(1)} %slice_bitcast_fusion), channel_id=1, source_target_pairs={{0,1},{1,0},{2,3},{3,2},{4,5},{5,4},{6,7},{7,6},{8,9},{9,8},{10,11... | collective-permute-start | bytes 98312 | tf_op jit(solution)/shard_map/ppermute | solution.py:548
  16.6 0.7 %write_fields.1 = (f32[1,8,16,128]{3,2,1,0:T(8,128)}, f32[1,8,16,128]{3,2,1,0:T(8,128)}) custom-call(f32[2,8,16,128]{3,2,1,0:T(8,128)S(1)} %get-tuple-element.39.final_ref), custom_call_target="tpu_custom_call" | custom-call | tf_op jit(solution)/shard_map/write_fields/pallas_call | solution.py:554
  17.3 0.0 collective-permute-done.13.rest_9_
  17.3 0.2 collective-permute-done.14.rest_10_
  17.5 0.0 collective-permute-done.7.rest_2_
  17.5 0.0 collective-permute-done.6.rest_1_
  17.5 0.0 collective-permute-done.5.rest_0_
  17.5 1.0 %image_products.1 = f32[33,2,16,128]{3,2,1,0:T(8,128)} custom-call(s32[4,8,128]{2,1,0:T(8,128)S(1)} %get-tuple-element.30.sides_ref, f32[2,2,2,16,128]{4,3,2,1,0:T(8,128)S(1)} %stack.1._others_ref.others_ref, f32[2,2,2,16,128]{4,3,2,1,0:T(8,128)S(1)} %collective-permute-done.5.rest_0_, f32[2,2,2,16,128]{4,3,2,1,0:T(8,128)S(1)} %collective-permute-done.6.rest_1_, ...), custom_call_target="tpu_custom_call" | custom-call | tf_op jit(solution)/shard_map/image_products/pallas_call | solution.py:583
  (6 shorter events, 0.0 us)
Async XLA Ops:
  2.0 5.5 %collective-permute-start = (f32[20,8,128]{2,1,0:T(8,128)S(1)}, f32[20,8,128]{2,1,0:T(8,128)S(1)}, u32[]{:S(2)}, u32[]{:S(2)}) collective-permute-start(f32[20,8,128]{2,1,0:T(8,128)S(1)} %get-tuple-element.36), channel_id=1, source_target_pairs={{0,4},{1,5},{2,6},{3,7},{4,0},{5,1},{6,2},{7,3},{8,9},{9,8},{10,11... | collective-permute-start | bytes 245768 | tf_op jit(solution)/shard_map/ppermute | solution.py:439
  5.1 2.4 %collective-permute-start.1 = (f32[20,8,128]{2,1,0:T(8,128)S(1)}, f32[20,8,128]{2,1,0:T(8,128)S(1)}, u32[]{:S(2)}, u32[]{:S(2)}) collective-permute-start(f32[20,8,128]{2,1,0:T(8,128)S(1)} %get-tuple-element.37), channel_id=1, source_target_pairs={{0,1},{1,0},{2,3},{3,2},{4,8},{5,9},{6,10},{7,11},{8,4},{9,5},{10,... | collective-permute-start | bytes 245768 | tf_op jit(solution)/shard_map/ppermute | solution.py:439
  5.1 2.4 %collective-permute-start.2 = (f32[20,8,128]{2,1,0:T(8,128)S(1)}, f32[20,8,128]{2,1,0:T(8,128)S(1)}, u32[]{:S(2)}, u32[]{:S(2)}) collective-permute-start(f32[20,8,128]{2,1,0:T(8,128)S(1)} %get-tuple-element.38), channel_id=1, source_target_pairs={{0,1},{1,0},{2,3},{3,2},{4,5},{5,4},{6,7},{7,6},{8,12},{9,13},{10,... | collective-permute-start | bytes 245768 | tf_op jit(solution)/shard_map/ppermute | solution.py:439
  7.8 4.6 %collective-permute-start.3 = (f32[2,2,16,128]{3,2,1,0:T(8,128)S(1)}, f32[2,2,16,128]{3,2,1,0:T(8,128)S(1)}, u32[]{:S(2)}, u32[]{:S(2)}) collective-permute-start(f32[2,2,16,128]{3,2,1,0:T(8,128)S(1)} %get-tuple-element.42), channel_id=1, source_target_pairs={{0,3},{1,2},{2,1},{3,0},{4,7},{5,6},{6,5},{7,4},{8,11},{9,10},{10,... | collective-permute-start | bytes 98312 | tf_op jit(solution)/shard_map/ppermute | solution.py:548
  8.4 4.0 %collective-permute-start.4 = (f32[2,2,16,128]{3,2,1,0:T(8,128)S(1)}, f32[2,2,16,128]{3,2,1,0:T(8,128)S(1)}, u32[]{:S(2)}, u32[]{:S(2)}) collective-permute-start(f32[2,2,16,128]{3,2,1,0:T(8,128)S(1)} %get-tuple-element.43), channel_id=1, source_target_pairs={{0,2},{1,3},{2,0},{3,1},{4,6},{5,7},{6,4},{7,5},{8,10},{9,11},{10,... | collective-permute-start | bytes 98312 | tf_op jit(solution)/shard_map/ppermute | solution.py:548
  9.9 4.6 %collective-permute-start.10 = (f32[2,2,2,16,128]{4,3,2,1,0:T(8,128)S(1)}, f32[2,2,2,16,128]{4,3,2,1,0:T(8,128)S(1)}, u32[]{:S(2)}, u32[]{:S(2)}) collective-permute-start(f32[2,2,2,16,128]{4,3,2,1,0:T(8,128)S(1)} %get-tuple-element.44.rest_3_), channel_id=1, source_target_pairs={{0,4},{1,5},{2,6},{3,7},{4,0},{5,1},{6,2},{7,3},{8,9},{9,8},{10,11... | collective-permute-start | bytes 196616 | tf_op jit(solution)/shard_map/ppermute | solution.py:439
  11.9 3.0 %collective-permute-start.9 = (f32[2,2,2,16,128]{4,3,2,1,0:T(8,128)S(1)}, f32[2,2,2,16,128]{4,3,2,1,0:T(8,128)S(1)}, u32[]{:S(2)}, u32[]{:S(2)}) collective-permute-start(f32[2,2,2,16,128]{4,3,2,1,0:T(8,128)S(1)} %get-tuple-element.44.rest_3_), channel_id=1, source_target_pairs={{0,1},{1,0},{2,3},{3,2},{4,8},{5,9},{6,10},{7,11},{8,4},{9,5},{10,... | collective-permute-start | bytes 196616 | tf_op jit(solution)/shard_map/ppermute | solution.py:439
  11.9 3.1 %collective-permute-start.8 = (f32[2,2,2,16,128]{4,3,2,1,0:T(8,128)S(1)}, f32[2,2,2,16,128]{4,3,2,1,0:T(8,128)S(1)}, u32[]{:S(2)}, u32[]{:S(2)}) collective-permute-start(f32[2,2,2,16,128]{4,3,2,1,0:T(8,128)S(1)} %get-tuple-element.44.rest_3_), channel_id=1, source_target_pairs={{0,1},{1,0},{2,3},{3,2},{4,5},{5,4},{6,7},{7,6},{8,12},{9,13},{10,... | collective-permute-start | bytes 196616 | tf_op jit(solution)/shard_map/ppermute | solution.py:439
  12.4 5.1 %collective-permute-start.7 = (f32[2,2,2,16,128]{4,3,2,1,0:T(8,128)S(1)}, f32[2,2,2,16,128]{4,3,2,1,0:T(8,128)S(1)}, u32[]{:S(2)}, u32[]{:S(2)}) collective-permute-start(f32[2,2,2,16,128]{4,3,2,1,0:T(8,128)S(1)} %stack.1._others_ref.others_ref), channel_id=1, source_target_pairs={{0,4},{1,5},{2,6},{3,7},{4,0},{5,1},{6,2},{7,3},{8,9},{9,8},{10,11... | collective-permute-start | bytes 196616 | tf_op jit(solution)/shard_map/ppermute | solution.py:439
  14.4 3.1 %collective-permute-start.6 = (f32[2,2,2,16,128]{4,3,2,1,0:T(8,128)S(1)}, f32[2,2,2,16,128]{4,3,2,1,0:T(8,128)S(1)}, u32[]{:S(2)}, u32[]{:S(2)}) collective-permute-start(f32[2,2,2,16,128]{4,3,2,1,0:T(8,128)S(1)} %stack.1._others_ref.others_ref), channel_id=1, source_target_pairs={{0,1},{1,0},{2,3},{3,2},{4,8},{5,9},{6,10},{7,11},{8,4},{9,5},{10,... | collective-permute-start | bytes 196616 | tf_op jit(solution)/shard_map/ppermute | solution.py:439
  14.4 3.1 %collective-permute-start.5 = (f32[2,2,2,16,128]{4,3,2,1,0:T(8,128)S(1)}, f32[2,2,2,16,128]{4,3,2,1,0:T(8,128)S(1)}, u32[]{:S(2)}, u32[]{:S(2)}) collective-permute-start(f32[2,2,2,16,128]{4,3,2,1,0:T(8,128)S(1)} %stack.1._others_ref.others_ref), channel_id=1, source_target_pairs={{0,1},{1,0},{2,3},{3,2},{4,5},{5,4},{6,7},{7,6},{8,12},{9,13},{10,... | collective-permute-start | bytes 196616 | tf_op jit(solution)/shard_map/ppermute | solution.py:439
  14.9 1.2 %collective-permute-start.11 = (f32[2,2,16,128]{3,2,1,0:T(8,128)S(1)}, f32[2,2,16,128]{3,2,1,0:T(8,128)S(1)}, u32[]{:S(2)}, u32[]{:S(2)}) collective-permute-start(f32[2,2,16,128]{3,2,1,0:T(8,128)S(1)} %hold.1), channel_id=1, source_target_pairs={{0,1},{1,0},{2,3},{3,2},{4,5},{5,4},{6,7},{7,6},{8,9},{9,8},{10,11... | collective-permute-start | bytes 98312 | tf_op jit(solution)/shard_map/ppermute | solution.py:548
  15.0 1.3 %collective-permute-start.12 = (f32[2,2,16,128]{3,2,1,0:T(8,128)S(1)}, f32[2,2,16,128]{3,2,1,0:T(8,128)S(1)}, u32[]{:S(2)}, u32[]{:S(2)}) collective-permute-start(f32[2,2,16,128]{3,2,1,0:T(8,128)S(1)} %slice_bitcast_fusion.2), channel_id=1, source_target_pairs={{0,1},{1,0},{2,3},{3,2},{4,5},{5,4},{6,7},{7,6},{8,9},{9,8},{10,11... | collective-permute-start | bytes 98312 | tf_op jit(solution)/shard_map/ppermute | solution.py:548
  16.1 1.2 %collective-permute-start.13 = (f32[2,2,16,128]{3,2,1,0:T(8,128)S(1)}, f32[2,2,16,128]{3,2,1,0:T(8,128)S(1)}, u32[]{:S(2)}, u32[]{:S(2)}) collective-permute-start(f32[2,2,16,128]{3,2,1,0:T(8,128)S(1)} %slice_bitcast_fusion.1), channel_id=1, source_target_pairs={{0,1},{1,0},{2,3},{3,2},{4,5},{5,4},{6,7},{7,6},{8,9},{9,8},{10,11... | collective-permute-start | bytes 98312 | tf_op jit(solution)/shard_map/ppermute | solution.py:548
  16.3 1.2 %collective-permute-start.14 = (f32[2,2,16,128]{3,2,1,0:T(8,128)S(1)}, f32[2,2,16,128]{3,2,1,0:T(8,128)S(1)}, u32[]{:S(2)}, u32[]{:S(2)}) collective-permute-start(f32[2,2,16,128]{3,2,1,0:T(8,128)S(1)} %slice_bitcast_fusion), channel_id=1, source_target_pairs={{0,1},{1,0},{2,3},{3,2},{4,5},{5,4},{6,7},{7,6},{8,9},{9,8},{10,11... | collective-permute-start | bytes 98312 | tf_op jit(solution)/shard_map/ppermute | solution.py:548

commit v23 on v22

--- a/solution.py
+++ b/solution.py
@@ -385,23 +385,18 @@
     held_ref[...] = mine_ref[...]
 
 
-def write_fields(final_ref, src_hbm, rec_hbm, sems):
-    copies = [
-        pltpu.make_async_copy(final_ref.at[field], out.at[0], sems.at[field])
-        for field, out in enumerate((src_hbm, rec_hbm))
-    ]
-    for copy in copies:
-        copy.start()
-    for copy in copies:
-        copy.wait()
-
-
 def image_products(weight, sides_ref, others_ref, *rest):
     others_sides, rest = rest[ROUNDS - 1 :: -1], rest[ROUNDS:]
     mine_ref, rest = rest[0], rest[1:]
     mine_sides, rest = rest[ROUNDS - 1 :: -1], rest[ROUNDS:]
     partner_refs, rest = rest[: 1 + ROUNDS], rest[1 + ROUNDS :]
-    image_hbm, wide, image_ref, sems = rest
+    final_ref, src_hbm, rec_hbm, image_hbm, wide, image_ref, field_sems, sems = rest
+    copies = [
+        pltpu.make_async_copy(final_ref.at[field], out.at[0], field_sems.at[field])
+        for field, out in enumerate((src_hbm, rec_hbm))
+    ]
+    for copy in copies:
+        copy.start()
     places = [
         (mine_ref.at[0], [ref.at[0] for ref in mine_sides]),
         (partner_refs[0], partner_refs[1:]),
@@ -411,7 +406,6 @@
     for shot, (own_ref, came_refs) in enumerate(places):
         widen(weight, sides_ref, shot, own_ref, came_refs, wide)
     parts = sems.shape[0]
-    copies = []
     for piece in range(parts):
         offsets = range(piece * OFFS // parts, (piece + 1) * OFFS // parts)
         for offset in offsets:
@@ -551,15 +545,6 @@
     weight = 1.0 / shots
     image_shape = (OFFS, share, extent, across)
 
-    src_next, rec_next = pl.pallas_call(
-        write_fields,
-        out_shape=(struct(1, levels, extent, across), struct(1, levels, extent, across)),
-        in_specs=[VMEM],
-        out_specs=[HBM, HBM],
-        scratch_shapes=[pltpu.SemaphoreType.DMA((2,))],
-        compiler_params=params,
-        name="write_fields",
-    )(final)
     others = pl.pallas_call(
         stack,
         out_shape=struct(len(came), *block.shape),
@@ -580,20 +565,24 @@
     )(mine[1], others)
     partner = [swap_shots(value, 1) for value in (held, *(side[1] for side in mine_sides))]
     operands = [others, *others_sides[::-1], mine, *mine_sides[::-1], *partner]
-    image = pl.pallas_call(
+    return pl.pallas_call(
         functools.partial(image_products, weight),
-        out_shape=struct(*image_shape),
-        in_specs=[VMEM] * (1 + len(operands)),
-        out_specs=HBM,
+        out_shape=(
+            struct(1, levels, extent, across),
+            struct(1, levels, extent, across),
+            struct(*image_shape),
+        ),
+        in_specs=[VMEM] * (2 + len(operands)),
+        out_specs=[HBM] * 3,
         scratch_shapes=[
             scratch(shots, 2, share, 3 * extent, across),
             scratch(*image_shape),
+            pltpu.SemaphoreType.DMA((2,)),
             pltpu.SemaphoreType.DMA((11,)),
         ],
         compiler_params=params,
         name="image_products",
-    )(sides, *operands)
-    return src_next, rec_next, image
+    )(sides, *operands, final)
 
 
 def solution(mesh):

time: 18.7 us -> 18.7 us (level)
  waiting for transfers between devices: 1.46 us -> 2.13 us
  Pallas kernels: 3.96 us -> 3.32 us
    ppermute x6, waiting for transfers between devices: 0.88 us -> 1.56 us  [swap_shots(): lax.ppermute(value, 'shot', [(shot, shot ^ number) for shot in range(shot...]
    pallas_call x2 -> x1, Pallas kernels: 1.62 us -> 0.98 us  [per_device(): pl.pallas_call(functools.partial(image_products, weight), out_shape=(stru...]
  transfers between devices with their start and end apart: 15 -> 15, of which waited for: 3 -> 4; matrix products, arithmetic and copies ran while one was open for 0% -> 0% of each run, Pallas kernels for 8% -> 4%
where the time goes in v23:
time: 18.7 us; the launch traced here: 18.5 us
  starting transfers between devices  11.7 us (63%)
  Pallas kernels  3.32 us (18%)
  waiting for transfers between devices  2.13 us (11%)
  between operations  1.33 us (7%)
    ppermute x9, starting transfers between devices, swap_tiles(): return lax.ppermute(value, ('tile', 'shot'), pairs)  8.6 us
    ppermute x6, starting transfers between devices, swap_shots(): lax.ppermute(value, 'shot', [(shot, shot ^ number) for shot in range(shot...  3.08 us
    ppermute x6, waiting for transfers between devices, swap_shots(): lax.ppermute(value, 'shot', [(shot, shot ^ number) for shot in range(shot...  1.56 us
    pallas_call x1, Pallas kernels, per_device(): pl.pallas_call(own_edges, out_shape=(struct(*wavelet.shape), struct(*wide...  1.33 us
    pallas_call x1, Pallas kernels, per_device(): pl.pallas_call(functools.partial(image_products, weight), out_shape=(stru...  0.98 us
    pallas_call x1, Pallas kernels, per_device(): pl.pallas_call(functools.partial(own_steps, width), out_shape=(struct(lev...  0.72 us
    ppermute x9, waiting for transfers between devices, swap_tiles(): return lax.ppermute(value, ('tile', 'shot'), pairs)  0.58 us
  transfers between devices with their start and end apart: 15, of which 4 were waited for; matrix products, arithmetic and copies ran while one was open for 0% of the time, Pallas kernels for 4%

profile of v23, /device:TPU:0, one launch (start us, length us, event | category | flops | bytes accessed | tf_op | source)
XLA Modules:
  0.0 18.5 jit_solution(13969765079191984275)
XLA Ops:
  0.6 1.3 %own_edges.1 = (f32[1,2]{1,0:T(1,128)S(1)}, f32[2,8,32,128]{3,2,1,0:T(8,128)S(1)}, f32[2,8,16,128]{3,2,1,0:T(8,128)S(1)}, s32[8,16,128]{2,1,0:T(8,128)S(1)}, f32...) custom-call(f32[1,16]{1,0:T(1,128)} %bitcast.9, ...), custom_call_target="tpu_custom_call" | custom-call | tf_op jit(solution)/shard_map/own_edges/pallas_call | solution.py:472
  2.0 3.1 %collective-permute-start = (f32[20,8,128]{2,1,0:T(8,128)S(1)}, f32[20,8,128]{2,1,0:T(8,128)S(1)}, u32[]{:S(2)}, u32[]{:S(2)}) collective-permute-start(f32[20,8,128]{2,1,0:T(8,128)S(1)} %get-tuple-element.34), channel_id=1, source_target_pairs={{0,4},{1,5},{2,6},{3,7},{4,0},{5,1},{6,2},{7,3},{8,9},{9,8},{10,11... | collective-permute-start | bytes 245768 | tf_op jit(solution)/shard_map/ppermute | solution.py:433
  5.1 0.0 collective-permute-start.1
  5.1 0.5 %collective-permute-start.2 = (f32[20,8,128]{2,1,0:T(8,128)S(1)}, f32[20,8,128]{2,1,0:T(8,128)S(1)}, u32[]{:S(2)}, u32[]{:S(2)}) collective-permute-start(f32[20,8,128]{2,1,0:T(8,128)S(1)} %get-tuple-element.36), channel_id=1, source_target_pairs={{0,1},{1,0},{2,3},{3,2},{4,5},{5,4},{6,7},{7,6},{8,12},{9,13},{10,... | collective-permute-start | bytes 245768 | tf_op jit(solution)/shard_map/ppermute | solution.py:433
  6.2 0.7 %own_steps.1 = (f32[8,16,128]{2,1,0:T(8,128)S(1)}, f32[2,8,16,128]{3,2,1,0:T(8,128)S(1)}, f32[2,8,8,128]{3,2,1,0:T(8,128)S(1)}, f32[8,32,128]{2,1,0:T(8,128)S(1)...) custom-call(s32[1]{0:T(128)S(6)} %copy.13.cell_ref, f32[1,2]{1,0:T(1,128)S(1)} %get-tuple-element.22.amps_ref, ...), custom_call_target="tpu_custom_call" | custom-call | tf_op jit(solution)/shard_map/own_steps/pallas_call | solution.py:511
  6.9 0.6 %collective-permute-done.rest_0_ = f32[20,8,128]{2,1,0:T(8,128)S(1)} collective-permute-done((f32[20,8,128]{2,1,0:T(8,128)S(1)}, f32[20,8,128]{2,1,0:T(8,128)S(1)}, u32[]{:S(2)}, u32[]{:S(2)}) %collective-permute-start) | collective-permute-done | bytes 81952 | tf_op jit(solution)/shard_map/ppermute | solution.py:433
  7.5 0.0 collective-permute-done.1.rest_1_
  7.5 0.0 collective-permute-done.2.rest_2_
  7.5 0.3 %neighbours_part.1 = (f32[2,8,16,128]{3,2,1,0:T(8,128)S(1)}, f32[2,2,2,16,128]{4,3,2,1,0:T(8,128)S(1)}, f32[2,2,16,128]{3,2,1,0:T(8,128)S(1)}, f32[2,2,16,128]{3,2,1,0:T(8,128)S(1)}) custom-call(s32[4,8,128]{2,1,0:T(8,128)S(1)} %get-tuple-element.28.sides_ref, s32[2,8,128]{2,1,0:T(8,128)S(1)} %get-tuple-element.29.bits_ref, ...), custom_call_target="tpu_custom_call" | custom-call | tf_op jit(solution)/shard_map/neighbours_part/pallas_call | solution.py:528
  7.8 0.6 %collective-permute-start.3 = (f32[2,2,16,128]{3,2,1,0:T(8,128)S(1)}, f32[2,2,16,128]{3,2,1,0:T(8,128)S(1)}, u32[]{:S(2)}, u32[]{:S(2)}) collective-permute-start(f32[2,2,16,128]{3,2,1,0:T(8,128)S(1)} %get-tuple-element.37), channel_id=1, source_target_pairs={{0,3},{1,2},{2,1},{3,0},{4,7},{5,6},{6,5},{7,4},{8,11},{9,10},{10,... | collective-permute-start | bytes 98312 | tf_op jit(solution)/shard_map/ppermute | solution.py:542
  8.4 1.4 %collective-permute-start.4 = (f32[2,2,16,128]{3,2,1,0:T(8,128)S(1)}, f32[2,2,16,128]{3,2,1,0:T(8,128)S(1)}, u32[]{:S(2)}, u32[]{:S(2)}) collective-permute-start(f32[2,2,16,128]{3,2,1,0:T(8,128)S(1)} %get-tuple-element.38), channel_id=1, source_target_pairs={{0,2},{1,3},{2,0},{3,1},{4,6},{5,7},{6,4},{7,5},{8,10},{9,11},{10,... | collective-permute-start | bytes 98312 | tf_op jit(solution)/shard_map/ppermute | solution.py:542
  9.9 2.0 %collective-permute-start.10 = (f32[2,2,2,16,128]{4,3,2,1,0:T(8,128)S(1)}, f32[2,2,2,16,128]{4,3,2,1,0:T(8,128)S(1)}, u32[]{:S(2)}, u32[]{:S(2)}) collective-permute-start(f32[2,2,2,16,128]{4,3,2,1,0:T(8,128)S(1)} %get-tuple-element.39.rest_3_), channel_id=1, source_target_pairs={{0,4},{1,5},{2,6},{3,7},{4,0},{5,1},{6,2},{7,3},{8,9},{9,8},{10,11... | collective-permute-start | bytes 196616 | tf_op jit(solution)/shard_map/ppermute | solution.py:433
  11.9 0.0 collective-permute-start.9
  11.9 0.5 %collective-permute-start.8 = (f32[2,2,2,16,128]{4,3,2,1,0:T(8,128)S(1)}, f32[2,2,2,16,128]{4,3,2,1,0:T(8,128)S(1)}, u32[]{:S(2)}, u32[]{:S(2)}) collective-permute-start(f32[2,2,2,16,128]{4,3,2,1,0:T(8,128)S(1)} %get-tuple-element.39.rest_3_), channel_id=1, source_target_pairs={{0,1},{1,0},{2,3},{3,2},{4,5},{5,4},{6,7},{7,6},{8,12},{9,13},{10,... | collective-permute-start | bytes 196616 | tf_op jit(solution)/shard_map/ppermute | solution.py:433
  12.4 0.0 collective-permute-done.3.refs_0_
  12.4 0.0 collective-permute-done.4.refs_1_
  12.4 1.9 %collective-permute-start.7 = (f32[2,2,2,16,128]{4,3,2,1,0:T(8,128)S(1)}, f32[2,2,2,16,128]{4,3,2,1,0:T(8,128)S(1)}, u32[]{:S(2)}, u32[]{:S(2)}) collective-permute-start(f32[2,2,2,16,128]{4,3,2,1,0:T(8,128)S(1)} %stack.1._others_ref.others_ref), channel_id=1, source_target_pairs={{0,4},{1,5},{2,6},{3,7},{4,0},{5,1},{6,2},{7,3},{8,9},{9,8},{10,11... | collective-permute-start | bytes 196616 | tf_op jit(solution)/shard_map/ppermute | solution.py:433
  14.4 0.0 collective-permute-start.6
  14.4 0.0 collective-permute-done.10.rest_6_
  14.4 0.5 %collective-permute-start.5 = (f32[2,2,2,16,128]{4,3,2,1,0:T(8,128)S(1)}, f32[2,2,2,16,128]{4,3,2,1,0:T(8,128)S(1)}, u32[]{:S(2)}, u32[]{:S(2)}) collective-permute-start(f32[2,2,2,16,128]{4,3,2,1,0:T(8,128)S(1)} %stack.1._others_ref.others_ref), channel_id=1, source_target_pairs={{0,1},{1,0},{2,3},{3,2},{4,5},{5,4},{6,7},{7,6},{8,12},{9,13},{10,... | collective-permute-start | bytes 196616 | tf_op jit(solution)/shard_map/ppermute | solution.py:433
  14.9 0.0 collective-permute-done.9.rest_5_
  14.9 0.1 collective-permute-start.11
  15.0 0.0 collective-permute-done.8.rest_4_
  15.0 0.4 %collective-permute-start.12 = (f32[2,2,16,128]{3,2,1,0:T(8,128)S(1)}, f32[2,2,16,128]{3,2,1,0:T(8,128)S(1)}, u32[]{:S(2)}, u32[]{:S(2)}) collective-permute-start(f32[2,2,16,128]{3,2,1,0:T(8,128)S(1)} %slice_bitcast_fusion.2), channel_id=1, source_target_pairs={{0,1},{1,0},{2,3},{3,2},{4,5},{5,4},{6,7},{7,6},{8,9},{9,8},{10,11... | collective-permute-start | bytes 98312 | tf_op jit(solution)/shard_map/ppermute | solution.py:542
  15.4 0.7 %collective-permute-done.11.rest_7_ = f32[2,2,16,128]{3,2,1,0:T(8,128)S(1)} collective-permute-done((f32[2,2,16,128]{3,2,1,0:T(8,128)S(1)}, f32[2,2,16,128]{3,2,1,0:T(8,128)S(1)}, u32[]{:S(2)}, u32[]{:S(2)}) %collective-permute-start.11) | collective-permute-done | bytes 32800 | tf_op jit(solution)/shard_map/ppermute | solution.py:542
  16.1 0.2 collective-permute-start.13
  16.3 0.0 collective-permute-done.12.rest_8_
  16.3 0.3 %collective-permute-start.14 = (f32[2,2,16,128]{3,2,1,0:T(8,128)S(1)}, f32[2,2,16,128]{3,2,1,0:T(8,128)S(1)}, u32[]{:S(2)}, u32[]{:S(2)}) collective-permute-start(f32[2,2,16,128]{3,2,1,0:T(8,128)S(1)} %slice_bitcast_fusion), channel_id=1, source_target_pairs={{0,1},{1,0},{2,3},{3,2},{4,5},{5,4},{6,7},{7,6},{8,9},{9,8},{10,11... | collective-permute-start | bytes 98312 | tf_op jit(solution)/shard_map/ppermute | solution.py:542
  16.6 0.7 %collective-permute-done.13.rest_9_ = f32[2,2,16,128]{3,2,1,0:T(8,128)S(1)} collective-permute-done((f32[2,2,16,128]{3,2,1,0:T(8,128)S(1)}, f32[2,2,16,128]{3,2,1,0:T(8,128)S(1)}, u32[]{:S(2)}, u32[]{:S(2)}) %collective-permute-start.13) | collective-permute-done | bytes 32800 | tf_op jit(solution)/shard_map/ppermute | solution.py:542
  17.3 0.2 collective-permute-done.14.rest_10_
  17.5 0.0 collective-permute-done.7.rest_2_
  17.5 0.0 collective-permute-done.6.rest_1_
  17.5 0.0 collective-permute-done.5.rest_0_
  17.5 1.0 %image_products.1 = (f32[1,8,16,128]{3,2,1,0:T(8,128)}, f32[1,8,16,128]{3,2,1,0:T(8,128)}, f32[33,2,16,128]{3,2,1,0:T(8,128)}) custom-call(s32[4,8,128]{2,1,0:T(8,128)S(1)} %get-tuple-element.28.sides_ref, f32[2,2,2,16,128]{4,3,2,1,0:T(8,128)S(1)} %stack.1._others_ref.others_ref, f32[2,2,2,16,128]{4,3,2,1,0:T(8,128)S(1)} %collective-permute-done.5.rest_0_, ...), custom_call_target="tpu_custom_call" | custom-call | tf_op jit(solution)/shard_map/image_products/pallas_call | solution.py:568
  (6 shorter events, 0.0 us)
Async XLA Ops:
  2.0 5.5 %collective-permute-start = (f32[20,8,128]{2,1,0:T(8,128)S(1)}, f32[20,8,128]{2,1,0:T(8,128)S(1)}, u32[]{:S(2)}, u32[]{:S(2)}) collective-permute-start(f32[20,8,128]{2,1,0:T(8,128)S(1)} %get-tuple-element.34), channel_id=1, source_target_pairs={{0,4},{1,5},{2,6},{3,7},{4,0},{5,1},{6,2},{7,3},{8,9},{9,8},{10,11... | collective-permute-start | bytes 245768 | tf_op jit(solution)/shard_map/ppermute | solution.py:433
  5.1 2.4 %collective-permute-start.1 = (f32[20,8,128]{2,1,0:T(8,128)S(1)}, f32[20,8,128]{2,1,0:T(8,128)S(1)}, u32[]{:S(2)}, u32[]{:S(2)}) collective-permute-start(f32[20,8,128]{2,1,0:T(8,128)S(1)} %get-tuple-element.35), channel_id=1, source_target_pairs={{0,1},{1,0},{2,3},{3,2},{4,8},{5,9},{6,10},{7,11},{8,4},{9,5},{10,... | collective-permute-start | bytes 245768 | tf_op jit(solution)/shard_map/ppermute | solution.py:433
  5.1 2.4 %collective-permute-start.2 = (f32[20,8,128]{2,1,0:T(8,128)S(1)}, f32[20,8,128]{2,1,0:T(8,128)S(1)}, u32[]{:S(2)}, u32[]{:S(2)}) collective-permute-start(f32[20,8,128]{2,1,0:T(8,128)S(1)} %get-tuple-element.36), channel_id=1, source_target_pairs={{0,1},{1,0},{2,3},{3,2},{4,5},{5,4},{6,7},{7,6},{8,12},{9,13},{10,... | collective-permute-start | bytes 245768 | tf_op jit(solution)/shard_map/ppermute | solution.py:433
  7.8 4.6 %collective-permute-start.3 = (f32[2,2,16,128]{3,2,1,0:T(8,128)S(1)}, f32[2,2,16,128]{3,2,1,0:T(8,128)S(1)}, u32[]{:S(2)}, u32[]{:S(2)}) collective-permute-start(f32[2,2,16,128]{3,2,1,0:T(8,128)S(1)} %get-tuple-element.37), channel_id=1, source_target_pairs={{0,3},{1,2},{2,1},{3,0},{4,7},{5,6},{6,5},{7,4},{8,11},{9,10},{10,... | collective-permute-start | bytes 98312 | tf_op jit(solution)/shard_map/ppermute | solution.py:542
  8.4 4.0 %collective-permute-start.4 = (f32[2,2,16,128]{3,2,1,0:T(8,128)S(1)}, f32[2,2,16,128]{3,2,1,0:T(8,128)S(1)}, u32[]{:S(2)}, u32[]{:S(2)}) collective-permute-start(f32[2,2,16,128]{3,2,1,0:T(8,128)S(1)} %get-tuple-element.38), channel_id=1, source_target_pairs={{0,2},{1,3},{2,0},{3,1},{4,6},{5,7},{6,4},{7,5},{8,10},{9,11},{10,... | collective-permute-start | bytes 98312 | tf_op jit(solution)/shard_map/ppermute | solution.py:542
  9.9 4.6 %collective-permute-start.10 = (f32[2,2,2,16,128]{4,3,2,1,0:T(8,128)S(1)}, f32[2,2,2,16,128]{4,3,2,1,0:T(8,128)S(1)}, u32[]{:S(2)}, u32[]{:S(2)}) collective-permute-start(f32[2,2,2,16,128]{4,3,2,1,0:T(8,128)S(1)} %get-tuple-element.39.rest_3_), channel_id=1, source_target_pairs={{0,4},{1,5},{2,6},{3,7},{4,0},{5,1},{6,2},{7,3},{8,9},{9,8},{10,11... | collective-permute-start | bytes 196616 | tf_op jit(solution)/shard_map/ppermute | solution.py:433
  11.9 3.0 %collective-permute-start.9 = (f32[2,2,2,16,128]{4,3,2,1,0:T(8,128)S(1)}, f32[2,2,2,16,128]{4,3,2,1,0:T(8,128)S(1)}, u32[]{:S(2)}, u32[]{:S(2)}) collective-permute-start(f32[2,2,2,16,128]{4,3,2,1,0:T(8,128)S(1)} %get-tuple-element.39.rest_3_), channel_id=1, source_target_pairs={{0,1},{1,0},{2,3},{3,2},{4,8},{5,9},{6,10},{7,11},{8,4},{9,5},{10,... | collective-permute-start | bytes 196616 | tf_op jit(solution)/shard_map/ppermute | solution.py:433
  11.9 3.1 %collective-permute-start.8 = (f32[2,2,2,16,128]{4,3,2,1,0:T(8,128)S(1)}, f32[2,2,2,16,128]{4,3,2,1,0:T(8,128)S(1)}, u32[]{:S(2)}, u32[]{:S(2)}) collective-permute-start(f32[2,2,2,16,128]{4,3,2,1,0:T(8,128)S(1)} %get-tuple-element.39.rest_3_), channel_id=1, source_target_pairs={{0,1},{1,0},{2,3},{3,2},{4,5},{5,4},{6,7},{7,6},{8,12},{9,13},{10,... | collective-permute-start | bytes 196616 | tf_op jit(solution)/shard_map/ppermute | solution.py:433
  12.4 5.1 %collective-permute-start.7 = (f32[2,2,2,16,128]{4,3,2,1,0:T(8,128)S(1)}, f32[2,2,2,16,128]{4,3,2,1,0:T(8,128)S(1)}, u32[]{:S(2)}, u32[]{:S(2)}) collective-permute-start(f32[2,2,2,16,128]{4,3,2,1,0:T(8,128)S(1)} %stack.1._others_ref.others_ref), channel_id=1, source_target_pairs={{0,4},{1,5},{2,6},{3,7},{4,0},{5,1},{6,2},{7,3},{8,9},{9,8},{10,11... | collective-permute-start | bytes 196616 | tf_op jit(solution)/shard_map/ppermute | solution.py:433
  14.4 3.1 %collective-permute-start.6 = (f32[2,2,2,16,128]{4,3,2,1,0:T(8,128)S(1)}, f32[2,2,2,16,128]{4,3,2,1,0:T(8,128)S(1)}, u32[]{:S(2)}, u32[]{:S(2)}) collective-permute-start(f32[2,2,2,16,128]{4,3,2,1,0:T(8,128)S(1)} %stack.1._others_ref.others_ref), channel_id=1, source_target_pairs={{0,1},{1,0},{2,3},{3,2},{4,8},{5,9},{6,10},{7,11},{8,4},{9,5},{10,... | collective-permute-start | bytes 196616 | tf_op jit(solution)/shard_map/ppermute | solution.py:433
  14.4 3.1 %collective-permute-start.5 = (f32[2,2,2,16,128]{4,3,2,1,0:T(8,128)S(1)}, f32[2,2,2,16,128]{4,3,2,1,0:T(8,128)S(1)}, u32[]{:S(2)}, u32[]{:S(2)}) collective-permute-start(f32[2,2,2,16,128]{4,3,2,1,0:T(8,128)S(1)} %stack.1._others_ref.others_ref), channel_id=1, source_target_pairs={{0,1},{1,0},{2,3},{3,2},{4,5},{5,4},{6,7},{7,6},{8,12},{9,13},{10,... | collective-permute-start | bytes 196616 | tf_op jit(solution)/shard_map/ppermute | solution.py:433
  14.9 1.2 %collective-permute-start.11 = (f32[2,2,16,128]{3,2,1,0:T(8,128)S(1)}, f32[2,2,16,128]{3,2,1,0:T(8,128)S(1)}, u32[]{:S(2)}, u32[]{:S(2)}) collective-permute-start(f32[2,2,16,128]{3,2,1,0:T(8,128)S(1)} %hold.1), channel_id=1, source_target_pairs={{0,1},{1,0},{2,3},{3,2},{4,5},{5,4},{6,7},{7,6},{8,9},{9,8},{10,11... | collective-permute-start | bytes 98312 | tf_op jit(solution)/shard_map/ppermute | solution.py:542
  15.0 1.3 %collective-permute-start.12 = (f32[2,2,16,128]{3,2,1,0:T(8,128)S(1)}, f32[2,2,16,128]{3,2,1,0:T(8,128)S(1)}, u32[]{:S(2)}, u32[]{:S(2)}) collective-permute-start(f32[2,2,16,128]{3,2,1,0:T(8,128)S(1)} %slice_bitcast_fusion.2), channel_id=1, source_target_pairs={{0,1},{1,0},{2,3},{3,2},{4,5},{5,4},{6,7},{7,6},{8,9},{9,8},{10,11... | collective-permute-start | bytes 98312 | tf_op jit(solution)/shard_map/ppermute | solution.py:542
  16.1 1.2 %collective-permute-start.13 = (f32[2,2,16,128]{3,2,1,0:T(8,128)S(1)}, f32[2,2,16,128]{3,2,1,0:T(8,128)S(1)}, u32[]{:S(2)}, u32[]{:S(2)}) collective-permute-start(f32[2,2,16,128]{3,2,1,0:T(8,128)S(1)} %slice_bitcast_fusion.1), channel_id=1, source_target_pairs={{0,1},{1,0},{2,3},{3,2},{4,5},{5,4},{6,7},{7,6},{8,9},{9,8},{10,11... | collective-permute-start | bytes 98312 | tf_op jit(solution)/shard_map/ppermute | solution.py:542
  16.3 1.2 %collective-permute-start.14 = (f32[2,2,16,128]{3,2,1,0:T(8,128)S(1)}, f32[2,2,16,128]{3,2,1,0:T(8,128)S(1)}, u32[]{:S(2)}, u32[]{:S(2)}) collective-permute-start(f32[2,2,16,128]{3,2,1,0:T(8,128)S(1)} %slice_bitcast_fusion), channel_id=1, source_target_pairs={{0,1},{1,0},{2,3},{3,2},{4,5},{5,4},{6,7},{7,6},{8,9},{9,8},{10,11... | collective-permute-start | bytes 98312 | tf_op jit(solution)/shard_map/ppermute | solution.py:542

commit v24 on v23

--- a/solution.py
+++ b/solution.py
@@ -389,7 +389,8 @@
     others_sides, rest = rest[ROUNDS - 1 :: -1], rest[ROUNDS:]
     mine_ref, rest = rest[0], rest[1:]
     mine_sides, rest = rest[ROUNDS - 1 :: -1], rest[ROUNDS:]
-    partner_refs, rest = rest[: 1 + ROUNDS], rest[1 + ROUNDS :]
+    (own_first_ref, second_third_ref), rest = rest[:2], rest[2:]
+    partner_refs = [ref.at[place] for ref in (own_first_ref, second_third_ref) for place in range(2)]
     final_ref, src_hbm, rec_hbm, image_hbm, wide, image_ref, field_sems, sems = rest
     copies = [
         pltpu.make_async_copy(final_ref.at[field], out.at[0], field_sems.at[field])
@@ -545,14 +546,17 @@
     weight = 1.0 / shots
     image_shape = (OFFS, share, extent, across)
 
-    others = pl.pallas_call(
-        stack,
-        out_shape=struct(len(came), *block.shape),
-        in_specs=[VMEM] * len(came),
-        out_specs=VMEM,
-        compiler_params=params,
-        name="stack",
-    )(*came[::-1])
+    def stacked(blocks):
+        return pl.pallas_call(
+            stack,
+            out_shape=struct(len(blocks), *block.shape),
+            in_specs=[VMEM] * len(blocks),
+            out_specs=VMEM,
+            compiler_params=params,
+            name="stack",
+        )(*blocks)
+
+    others = stacked(came[::-1])
     mine_sides = swap_rounds([mine] * ROUNDS)
     others_sides = swap_rounds([others] * ROUNDS)
     held = pl.pallas_call(
@@ -563,7 +567,10 @@
         compiler_params=params,
         name="hold",
     )(mine[1], others)
-    partner = [swap_shots(value, 1) for value in (held, *(side[1] for side in mine_sides))]
+    pieces = [held, *(side[1] for side in mine_sides)]
+    partner = [
+        swap_shots(stacked(pieces[begin : begin + 2]), 1) for begin in range(0, len(pieces), 2)
+    ]
     operands = [others, *others_sides[::-1], mine, *mine_sides[::-1], *partner]
     return pl.pallas_call(
         functools.partial(image_products, weight),

time: 18.7 us -> 18.2 us (0.973)
  starting transfers between devices: 11.7 us -> 11.3 us
    ppermute x6 -> x4, waiting for transfers between devices: 1.56 us -> 0.01 us  [swap_shots(): lax.ppermute(value, 'shot', [(shot, shot ^ number) for shot in range(shot...]
    ppermute x9, waiting for transfers between devices: 0.58 us -> 1.94 us  [swap_tiles(): return lax.ppermute(value, ('tile', 'shot'), pairs)]
    ppermute x6 -> x4, starting transfers between devices: 3.08 us -> 2.7 us  [swap_shots(): lax.ppermute(value, 'shot', [(shot, shot ^ number) for shot in range(shot...]
  transfers between devices with their start and end apart: 15 -> 13, of which waited for: 4 -> 2; matrix products, arithmetic and copies ran while one was open for 0% -> 0% of each run, Pallas kernels for 4% -> 4%
where the time goes in v24:
time: 18.2 us; the launch traced here: 17.9 us
  starting transfers between devices  11.3 us (62%)
  Pallas kernels  3.33 us (18%)
  waiting for transfers between devices  1.95 us (11%)
  between operations  1.36 us (7%)
    ppermute x9, starting transfers between devices, swap_tiles(): return lax.ppermute(value, ('tile', 'shot'), pairs)  8.6 us
    ppermute x4, starting transfers between devices, swap_shots(): lax.ppermute(value, 'shot', [(shot, shot ^ number) for shot in range(shot...  2.7 us
    ppermute x9, waiting for transfers between devices, swap_tiles(): return lax.ppermute(value, ('tile', 'shot'), pairs)  1.94 us
    pallas_call x1, Pallas kernels, per_device(): pl.pallas_call(own_edges, out_shape=(struct(*wavelet.shape), struct(*wide...  1.33 us
    pallas_call x1, Pallas kernels, per_device(): pl.pallas_call(functools.partial(image_products, weight), out_shape=(stru...  0.97 us
    pallas_call x1, Pallas kernels, per_device(): pl.pallas_call(functools.partial(own_steps, width), out_shape=(struct(lev...  0.72 us
  transfers between devices with their start and end apart: 13, of which 2 were waited for; matrix products, arithmetic and copies ran while one was open for 0% of the time, Pallas kernels for 4%

profile of v24, /device:TPU:0, one launch (start us, length us, event | category | flops | bytes accessed | tf_op | source)
XLA Modules:
  0.0 17.9 jit_solution(12033043334645240786)
XLA Ops:
  0.6 1.3 %own_edges.1 = (f32[1,2]{1,0:T(1,128)S(1)}, f32[2,8,32,128]{3,2,1,0:T(8,128)S(1)}, f32[2,8,16,128]{3,2,1,0:T(8,128)S(1)}, s32[8,16,128]{2,1,0:T(8,128)S(1)}, f32...) custom-call(f32[1,16]{1,0:T(1,128)} %bitcast.9, ...), custom_call_target="tpu_custom_call" | custom-call | tf_op jit(solution)/shard_map/own_edges/pallas_call | solution.py:473
  2.0 3.1 %collective-permute-start = (f32[20,8,128]{2,1,0:T(8,128)S(1)}, f32[20,8,128]{2,1,0:T(8,128)S(1)}, u32[]{:S(2)}, u32[]{:S(2)}) collective-permute-start(f32[20,8,128]{2,1,0:T(8,128)S(1)} %get-tuple-element.34), channel_id=1, source_target_pairs={{0,4},{1,5},{2,6},{3,7},{4,0},{5,1},{6,2},{7,3},{8,9},{9,8},{10,11... | collective-permute-start | bytes 245768 | tf_op jit(solution)/shard_map/ppermute | solution.py:434
  5.1 0.0 collective-permute-start.1
  5.1 0.5 %collective-permute-start.2 = (f32[20,8,128]{2,1,0:T(8,128)S(1)}, f32[20,8,128]{2,1,0:T(8,128)S(1)}, u32[]{:S(2)}, u32[]{:S(2)}) collective-permute-start(f32[20,8,128]{2,1,0:T(8,128)S(1)} %get-tuple-element.36), channel_id=1, source_target_pairs={{0,1},{1,0},{2,3},{3,2},{4,5},{5,4},{6,7},{7,6},{8,12},{9,13},{10,... | collective-permute-start | bytes 245768 | tf_op jit(solution)/shard_map/ppermute | solution.py:434
  6.2 0.7 %own_steps.1 = (f32[8,16,128]{2,1,0:T(8,128)S(1)}, f32[2,8,16,128]{3,2,1,0:T(8,128)S(1)}, f32[2,8,8,128]{3,2,1,0:T(8,128)S(1)}, f32[8,32,128]{2,1,0:T(8,128)S(1)...) custom-call(s32[1]{0:T(128)S(6)} %copy.13.cell_ref, f32[1,2]{1,0:T(1,128)S(1)} %get-tuple-element.22.amps_ref, ...), custom_call_target="tpu_custom_call" | custom-call | tf_op jit(solution)/shard_map/own_steps/pallas_call | solution.py:512
  6.9 0.6 %collective-permute-done.rest_0_ = f32[20,8,128]{2,1,0:T(8,128)S(1)} collective-permute-done((f32[20,8,128]{2,1,0:T(8,128)S(1)}, f32[20,8,128]{2,1,0:T(8,128)S(1)}, u32[]{:S(2)}, u32[]{:S(2)}) %collective-permute-start) | collective-permute-done | bytes 81952 | tf_op jit(solution)/shard_map/ppermute | solution.py:434
  7.5 0.0 collective-permute-done.1.rest_1_
  7.5 0.0 collective-permute-done.2.rest_2_
  7.5 0.3 %neighbours_part.1 = (f32[2,8,16,128]{3,2,1,0:T(8,128)S(1)}, f32[2,2,2,16,128]{4,3,2,1,0:T(8,128)S(1)}, f32[2,2,16,128]{3,2,1,0:T(8,128)S(1)}, f32[2,2,16,128]{3,2,1,0:T(8,128)S(1)}) custom-call(s32[4,8,128]{2,1,0:T(8,128)S(1)} %get-tuple-element.28.sides_ref, s32[2,8,128]{2,1,0:T(8,128)S(1)} %get-tuple-element.29.bits_ref, ...), custom_call_target="tpu_custom_call" | custom-call | tf_op jit(solution)/shard_map/neighbours_part/pallas_call | solution.py:529
  7.8 0.6 %collective-permute-start.3 = (f32[2,2,16,128]{3,2,1,0:T(8,128)S(1)}, f32[2,2,16,128]{3,2,1,0:T(8,128)S(1)}, u32[]{:S(2)}, u32[]{:S(2)}) collective-permute-start(f32[2,2,16,128]{3,2,1,0:T(8,128)S(1)} %get-tuple-element.37), channel_id=1, source_target_pairs={{0,3},{1,2},{2,1},{3,0},{4,7},{5,6},{6,5},{7,4},{8,11},{9,10},{10,... | collective-permute-start | bytes 98312 | tf_op jit(solution)/shard_map/ppermute | solution.py:543
  8.4 1.4 %collective-permute-start.4 = (f32[2,2,16,128]{3,2,1,0:T(8,128)S(1)}, f32[2,2,16,128]{3,2,1,0:T(8,128)S(1)}, u32[]{:S(2)}, u32[]{:S(2)}) collective-permute-start(f32[2,2,16,128]{3,2,1,0:T(8,128)S(1)} %get-tuple-element.38), channel_id=1, source_target_pairs={{0,2},{1,3},{2,0},{3,1},{4,6},{5,7},{6,4},{7,5},{8,10},{9,11},{10,... | collective-permute-start | bytes 98312 | tf_op jit(solution)/shard_map/ppermute | solution.py:543
  9.9 2.0 %collective-permute-start.10 = (f32[2,2,2,16,128]{4,3,2,1,0:T(8,128)S(1)}, f32[2,2,2,16,128]{4,3,2,1,0:T(8,128)S(1)}, u32[]{:S(2)}, u32[]{:S(2)}) collective-permute-start(f32[2,2,2,16,128]{4,3,2,1,0:T(8,128)S(1)} %get-tuple-element.39.rest_3_), channel_id=1, source_target_pairs={{0,4},{1,5},{2,6},{3,7},{4,0},{5,1},{6,2},{7,3},{8,9},{9,8},{10,11... | collective-permute-start | bytes 196616 | tf_op jit(solution)/shard_map/ppermute | solution.py:434
  11.9 0.0 collective-permute-start.9
  11.9 0.5 %collective-permute-start.8 = (f32[2,2,2,16,128]{4,3,2,1,0:T(8,128)S(1)}, f32[2,2,2,16,128]{4,3,2,1,0:T(8,128)S(1)}, u32[]{:S(2)}, u32[]{:S(2)}) collective-permute-start(f32[2,2,2,16,128]{4,3,2,1,0:T(8,128)S(1)} %get-tuple-element.39.rest_3_), channel_id=1, source_target_pairs={{0,1},{1,0},{2,3},{3,2},{4,5},{5,4},{6,7},{7,6},{8,12},{9,13},{10,... | collective-permute-start | bytes 196616 | tf_op jit(solution)/shard_map/ppermute | solution.py:434
  12.4 0.0 collective-permute-done.3.refs_0_
  12.4 0.0 collective-permute-done.4.refs_1_
  12.4 1.9 %collective-permute-start.7 = (f32[2,2,2,16,128]{4,3,2,1,0:T(8,128)S(1)}, f32[2,2,2,16,128]{4,3,2,1,0:T(8,128)S(1)}, u32[]{:S(2)}, u32[]{:S(2)}) collective-permute-start(f32[2,2,2,16,128]{4,3,2,1,0:T(8,128)S(1)} %stack.3._others_ref.others_ref), channel_id=1, source_target_pairs={{0,4},{1,5},{2,6},{3,7},{4,0},{5,1},{6,2},{7,3},{8,9},{9,8},{10,11... | collective-permute-start | bytes 196616 | tf_op jit(solution)/shard_map/ppermute | solution.py:434
  14.4 0.0 collective-permute-start.6
  14.4 0.0 collective-permute-done.10.rest_6_
  14.4 0.5 %collective-permute-start.5 = (f32[2,2,2,16,128]{4,3,2,1,0:T(8,128)S(1)}, f32[2,2,2,16,128]{4,3,2,1,0:T(8,128)S(1)}, u32[]{:S(2)}, u32[]{:S(2)}) collective-permute-start(f32[2,2,2,16,128]{4,3,2,1,0:T(8,128)S(1)} %stack.3._others_ref.others_ref), channel_id=1, source_target_pairs={{0,1},{1,0},{2,3},{3,2},{4,5},{5,4},{6,7},{7,6},{8,12},{9,13},{10,... | collective-permute-start | bytes 196616 | tf_op jit(solution)/shard_map/ppermute | solution.py:434
  14.9 0.0 collective-permute-done.9.rest_5_
  14.9 0.2 collective-permute-start.11
  15.1 0.0 collective-permute-done.8.rest_4_
  15.1 0.5 %collective-permute-start.12 = (f32[2,2,2,16,128]{4,3,2,1,0:T(8,128)S(1)}, f32[2,2,2,16,128]{4,3,2,1,0:T(8,128)S(1)}, u32[]{:S(2)}, u32[]{:S(2)}) collective-permute-start(f32[2,2,2,16,128]{4,3,2,1,0:T(8,128)S(1)} %stack.5), channel_id=1, source_target_pairs={{0,1},{1,0},{2,3},{3,2},{4,5},{5,4},{6,7},{7,6},{8,9},{9,8},{10,11... | collective-permute-start | bytes 196616 | tf_op jit(solution)/shard_map/ppermute | solution.py:543
  15.6 1.4 %collective-permute-done.7.rest_2_ = f32[2,2,2,16,128]{4,3,2,1,0:T(8,128)S(1)} collective-permute-done((f32[2,2,2,16,128]{4,3,2,1,0:T(8,128)S(1)}, f32[2,2,2,16,128]{4,3,2,1,0:T(8,128)S(1)}, u32[]{:S(2)}, u32[]{:S(2)}) %collective-permute-start.7) | collective-permute-done | bytes 65568 | tf_op jit(solution)/shard_map/ppermute | solution.py:434
  16.9 0.0 collective-permute-done.6.rest_1_
  16.9 0.0 collective-permute-done.5.rest_0_
  17.0 0.0 collective-permute-done.11.rest_7_
  17.0 0.0 collective-permute-done.12.rest_8_
  17.0 1.0 %image_products.1 = (f32[1,8,16,128]{3,2,1,0:T(8,128)}, f32[1,8,16,128]{3,2,1,0:T(8,128)}, f32[33,2,16,128]{3,2,1,0:T(8,128)}) custom-call(s32[4,8,128]{2,1,0:T(8,128)S(1)} %get-tuple-element.28.sides_ref, f32[2,2,2,16,128]{4,3,2,1,0:T(8,128)S(1)} %stack.3._others_ref.others_ref, f32[2,2,2,16,128]{4,3,2,1,0:T(8,128)S(1)} %collective-permute-done.5.rest_0_, ...), custom_call_target="tpu_custom_call" | custom-call | tf_op jit(solution)/shard_map/image_products/pallas_call | solution.py:575
  (8 shorter events, 0.0 us)
Async XLA Ops:
  2.0 5.5 %collective-permute-start = (f32[20,8,128]{2,1,0:T(8,128)S(1)}, f32[20,8,128]{2,1,0:T(8,128)S(1)}, u32[]{:S(2)}, u32[]{:S(2)}) collective-permute-start(f32[20,8,128]{2,1,0:T(8,128)S(1)} %get-tuple-element.34), channel_id=1, source_target_pairs={{0,4},{1,5},{2,6},{3,7},{4,0},{5,1},{6,2},{7,3},{8,9},{9,8},{10,11... | collective-permute-start | bytes 245768 | tf_op jit(solution)/shard_map/ppermute | solution.py:434
  5.1 2.4 %collective-permute-start.1 = (f32[20,8,128]{2,1,0:T(8,128)S(1)}, f32[20,8,128]{2,1,0:T(8,128)S(1)}, u32[]{:S(2)}, u32[]{:S(2)}) collective-permute-start(f32[20,8,128]{2,1,0:T(8,128)S(1)} %get-tuple-element.35), channel_id=1, source_target_pairs={{0,1},{1,0},{2,3},{3,2},{4,8},{5,9},{6,10},{7,11},{8,4},{9,5},{10,... | collective-permute-start | bytes 245768 | tf_op jit(solution)/shard_map/ppermute | solution.py:434
  5.1 2.4 %collective-permute-start.2 = (f32[20,8,128]{2,1,0:T(8,128)S(1)}, f32[20,8,128]{2,1,0:T(8,128)S(1)}, u32[]{:S(2)}, u32[]{:S(2)}) collective-permute-start(f32[20,8,128]{2,1,0:T(8,128)S(1)} %get-tuple-element.36), channel_id=1, source_target_pairs={{0,1},{1,0},{2,3},{3,2},{4,5},{5,4},{6,7},{7,6},{8,12},{9,13},{10,... | collective-permute-start | bytes 245768 | tf_op jit(solution)/shard_map/ppermute | solution.py:434
  7.8 4.6 %collective-permute-start.3 = (f32[2,2,16,128]{3,2,1,0:T(8,128)S(1)}, f32[2,2,16,128]{3,2,1,0:T(8,128)S(1)}, u32[]{:S(2)}, u32[]{:S(2)}) collective-permute-start(f32[2,2,16,128]{3,2,1,0:T(8,128)S(1)} %get-tuple-element.37), channel_id=1, source_target_pairs={{0,3},{1,2},{2,1},{3,0},{4,7},{5,6},{6,5},{7,4},{8,11},{9,10},{10,... | collective-permute-start | bytes 98312 | tf_op jit(solution)/shard_map/ppermute | solution.py:543
  8.4 4.0 %collective-permute-start.4 = (f32[2,2,16,128]{3,2,1,0:T(8,128)S(1)}, f32[2,2,16,128]{3,2,1,0:T(8,128)S(1)}, u32[]{:S(2)}, u32[]{:S(2)}) collective-permute-start(f32[2,2,16,128]{3,2,1,0:T(8,128)S(1)} %get-tuple-element.38), channel_id=1, source_target_pairs={{0,2},{1,3},{2,0},{3,1},{4,6},{5,7},{6,4},{7,5},{8,10},{9,11},{10,... | collective-permute-start | bytes 98312 | tf_op jit(solution)/shard_map/ppermute | solution.py:543
  9.9 4.6 %collective-permute-start.10 = (f32[2,2,2,16,128]{4,3,2,1,0:T(8,128)S(1)}, f32[2,2,2,16,128]{4,3,2,1,0:T(8,128)S(1)}, u32[]{:S(2)}, u32[]{:S(2)}) collective-permute-start(f32[2,2,2,16,128]{4,3,2,1,0:T(8,128)S(1)} %get-tuple-element.39.rest_3_), channel_id=1, source_target_pairs={{0,4},{1,5},{2,6},{3,7},{4,0},{5,1},{6,2},{7,3},{8,9},{9,8},{10,11... | collective-permute-start | bytes 196616 | tf_op jit(solution)/shard_map/ppermute | solution.py:434
  11.9 3.0 %collective-permute-start.9 = (f32[2,2,2,16,128]{4,3,2,1,0:T(8,128)S(1)}, f32[2,2,2,16,128]{4,3,2,1,0:T(8,128)S(1)}, u32[]{:S(2)}, u32[]{:S(2)}) collective-permute-start(f32[2,2,2,16,128]{4,3,2,1,0:T(8,128)S(1)} %get-tuple-element.39.rest_3_), channel_id=1, source_target_pairs={{0,1},{1,0},{2,3},{3,2},{4,8},{5,9},{6,10},{7,11},{8,4},{9,5},{10,... | collective-permute-start | bytes 196616 | tf_op jit(solution)/shard_map/ppermute | solution.py:434
  11.9 3.2 %collective-permute-start.8 = (f32[2,2,2,16,128]{4,3,2,1,0:T(8,128)S(1)}, f32[2,2,2,16,128]{4,3,2,1,0:T(8,128)S(1)}, u32[]{:S(2)}, u32[]{:S(2)}) collective-permute-start(f32[2,2,2,16,128]{4,3,2,1,0:T(8,128)S(1)} %get-tuple-element.39.rest_3_), channel_id=1, source_target_pairs={{0,1},{1,0},{2,3},{3,2},{4,5},{5,4},{6,7},{7,6},{8,12},{9,13},{10,... | collective-permute-start | bytes 196616 | tf_op jit(solution)/shard_map/ppermute | solution.py:434
  12.4 4.5 %collective-permute-start.7 = (f32[2,2,2,16,128]{4,3,2,1,0:T(8,128)S(1)}, f32[2,2,2,16,128]{4,3,2,1,0:T(8,128)S(1)}, u32[]{:S(2)}, u32[]{:S(2)}) collective-permute-start(f32[2,2,2,16,128]{4,3,2,1,0:T(8,128)S(1)} %stack.3._others_ref.others_ref), channel_id=1, source_target_pairs={{0,4},{1,5},{2,6},{3,7},{4,0},{5,1},{6,2},{7,3},{8,9},{9,8},{10,11... | collective-permute-start | bytes 196616 | tf_op jit(solution)/shard_map/ppermute | solution.py:434
  14.4 2.6 %collective-permute-start.6 = (f32[2,2,2,16,128]{4,3,2,1,0:T(8,128)S(1)}, f32[2,2,2,16,128]{4,3,2,1,0:T(8,128)S(1)}, u32[]{:S(2)}, u32[]{:S(2)}) collective-permute-start(f32[2,2,2,16,128]{4,3,2,1,0:T(8,128)S(1)} %stack.3._others_ref.others_ref), channel_id=1, source_target_pairs={{0,1},{1,0},{2,3},{3,2},{4,8},{5,9},{6,10},{7,11},{8,4},{9,5},{10,... | collective-permute-start | bytes 196616 | tf_op jit(solution)/shard_map/ppermute | solution.py:434
  14.4 2.5 %collective-permute-start.5 = (f32[2,2,2,16,128]{4,3,2,1,0:T(8,128)S(1)}, f32[2,2,2,16,128]{4,3,2,1,0:T(8,128)S(1)}, u32[]{:S(2)}, u32[]{:S(2)}) collective-permute-start(f32[2,2,2,16,128]{4,3,2,1,0:T(8,128)S(1)} %stack.3._others_ref.others_ref), channel_id=1, source_target_pairs={{0,1},{1,0},{2,3},{3,2},{4,5},{5,4},{6,7},{7,6},{8,12},{9,13},{10,... | collective-permute-start | bytes 196616 | tf_op jit(solution)/shard_map/ppermute | solution.py:434
  14.9 2.0 %collective-permute-start.11 = (f32[2,2,2,16,128]{4,3,2,1,0:T(8,128)S(1)}, f32[2,2,2,16,128]{4,3,2,1,0:T(8,128)S(1)}, u32[]{:S(2)}, u32[]{:S(2)}) collective-permute-start(f32[2,2,2,16,128]{4,3,2,1,0:T(8,128)S(1)} %stack.4), channel_id=1, source_target_pairs={{0,1},{1,0},{2,3},{3,2},{4,5},{5,4},{6,7},{7,6},{8,9},{9,8},{10,11... | collective-permute-start | bytes 196616 | tf_op jit(solution)/shard_map/ppermute | solution.py:543
  15.1 1.9 %collective-permute-start.12 = (f32[2,2,2,16,128]{4,3,2,1,0:T(8,128)S(1)}, f32[2,2,2,16,128]{4,3,2,1,0:T(8,128)S(1)}, u32[]{:S(2)}, u32[]{:S(2)}) collective-permute-start(f32[2,2,2,16,128]{4,3,2,1,0:T(8,128)S(1)} %stack.5), channel_id=1, source_target_pairs={{0,1},{1,0},{2,3},{3,2},{4,5},{5,4},{6,7},{7,6},{8,9},{9,8},{10,11... | collective-permute-start | bytes 196616 | tf_op jit(solution)/shard_map/ppermute | solution.py:543

commit v25 on v24

--- a/solution.py
+++ b/solution.py
@@ -362,11 +362,10 @@
             wide[shot, field, level, 2 * extent : 3 * extent, :] = scale * high
 
 
-def offset_product(wide, offset, level):
+def offset_product(wide, offset, level, total):
     extent = wide.shape[3] // 3
     lower = extent + REACH - offset
     upper = extent - REACH + offset
-    total = None
     for shot in range(wide.shape[0]):
         product = (
             wide[shot, 0, level, lower : lower + extent, :]
@@ -385,23 +384,30 @@
     held_ref[...] = mine_ref[...]
 
 
-def image_products(weight, sides_ref, others_ref, *rest):
-    others_sides, rest = rest[ROUNDS - 1 :: -1], rest[ROUNDS:]
-    mine_ref, rest = rest[0], rest[1:]
-    mine_sides, rest = rest[ROUNDS - 1 :: -1], rest[ROUNDS:]
-    (own_first_ref, second_third_ref), rest = rest[:2], rest[2:]
-    partner_refs = [ref.at[place] for ref in (own_first_ref, second_third_ref) for place in range(2)]
-    final_ref, src_hbm, rec_hbm, image_hbm, wide, image_ref, field_sems, sems = rest
+def early_products(weight, sides_ref, mine_ref, third_ref, second_ref, first_ref, final_ref, *rest):
+    src_hbm, rec_hbm, image_ref, wide, sems = rest
     copies = [
-        pltpu.make_async_copy(final_ref.at[field], out.at[0], field_sems.at[field])
+        pltpu.make_async_copy(final_ref.at[field], out.at[0], sems.at[field])
         for field, out in enumerate((src_hbm, rec_hbm))
     ]
     for copy in copies:
         copy.start()
-    places = [
-        (mine_ref.at[0], [ref.at[0] for ref in mine_sides]),
-        (partner_refs[0], partner_refs[1:]),
-    ]
+    came_refs = [ref.at[0] for ref in (first_ref, second_ref, third_ref)]
+    widen(weight, sides_ref, 0, mine_ref.at[0], came_refs, wide)
+    for offset in range(OFFS):
+        for level in range(wide.shape[2]):
+            image_ref[offset, level] = offset_product(wide, offset, level, None)
+    for copy in copies:
+        copy.wait()
+
+
+def image_products(weight, sides_ref, others_ref, *rest):
+    others_sides, rest = rest[ROUNDS - 1 :: -1], rest[ROUNDS:]
+    (own_first_ref, second_third_ref, early_ref), rest = rest[:3], rest[3:]
+    partner_refs = [ref.at[place] for ref in (own_first_ref, second_third_ref) for place in range(2)]
+    image_hbm, wide, image_ref, sems = rest
+    copies = []
+    places = [(partner_refs[0], partner_refs[1:])]
     for place in range(others_ref.shape[0]):
         places.append((others_ref.at[place], [ref.at[place] for ref in others_sides]))
     for shot, (own_ref, came_refs) in enumerate(places):
@@ -411,7 +417,9 @@
         offsets = range(piece * OFFS // parts, (piece + 1) * OFFS // parts)
         for offset in offsets:
             for level in range(image_ref.shape[1]):
-                image_ref[offset, level] = offset_product(wide, offset, level)
+                image_ref[offset, level] = offset_product(
+                    wide, offset, level, early_ref[offset, level]
+                )
         rows = pl.ds(offsets[0], len(offsets))
         copy = pltpu.make_async_copy(image_ref.at[rows], image_hbm.at[rows], sems.at[piece])
         copy.start()
@@ -571,25 +579,37 @@
     partner = [
         swap_shots(stacked(pieces[begin : begin + 2]), 1) for begin in range(0, len(pieces), 2)
     ]
-    operands = [others, *others_sides[::-1], mine, *mine_sides[::-1], *partner]
-    return pl.pallas_call(
-        functools.partial(image_products, weight),
+    src_next, rec_next, early = pl.pallas_call(
+        functools.partial(early_products, weight),
         out_shape=(
             struct(1, levels, extent, across),
             struct(1, levels, extent, across),
             struct(*image_shape),
         ),
-        in_specs=[VMEM] * (2 + len(operands)),
-        out_specs=[HBM] * 3,
+        in_specs=[VMEM] * (3 + ROUNDS),
+        out_specs=[HBM, HBM, VMEM],
         scratch_shapes=[
-            scratch(shots, 2, share, 3 * extent, across),
+            scratch(1, 2, share, 3 * extent, across),
+            pltpu.SemaphoreType.DMA((2,)),
+        ],
+        compiler_params=params,
+        name="early_products",
+    )(sides, mine, *mine_sides[::-1], final)
+    operands = [others, *others_sides[::-1], *partner, early]
+    image = pl.pallas_call(
+        functools.partial(image_products, weight),
+        out_shape=struct(*image_shape),
+        in_specs=[VMEM] * (1 + len(operands)),
+        out_specs=HBM,
+        scratch_shapes=[
+            scratch(shots - 1, 2, share, 3 * extent, across),
             scratch(*image_shape),
-            pltpu.SemaphoreType.DMA((2,)),
             pltpu.SemaphoreType.DMA((11,)),
         ],
         compiler_params=params,
         name="image_products",
-    )(sides, *operands, final)
+    )(sides, *operands)
+    return src_next, rec_next, image
 
 
 def solution(mesh):

time: 18.2 us -> 18.1 us (level)
  waiting for transfers between devices: 1.95 us -> 1.28 us
  Pallas kernels: 3.33 us -> 3.94 us
    ppermute x9, waiting for transfers between devices: 1.94 us -> 1.27 us  [swap_tiles(): return lax.ppermute(value, ('tile', 'shot'), pairs)]
    pallas_call x1 -> x2, Pallas kernels: 0.97 us -> 1.59 us  [the longest x1 0.92 us: per_device(): pl.pallas_call(functools.partial(image_products, weight), out_shape=struc...]
  transfers between devices with their start and end apart: 13 -> 13, of which waited for: 2 -> 2; matrix products, arithmetic and copies ran while one was open for 0% -> 0% of each run, Pallas kernels for 4% -> 8%
where the time goes in v25:
time: 18.1 us; the launch traced here: 17.9 us
  starting transfers between devices  11.3 us (62%)
  Pallas kernels  3.94 us (22%)
  between operations  1.37 us (8%)
  waiting for transfers between devices  1.28 us (7%)
    ppermute x9, starting transfers between devices, swap_tiles(): return lax.ppermute(value, ('tile', 'shot'), pairs)  8.6 us
    ppermute x4, starting transfers between devices, swap_shots(): lax.ppermute(value, 'shot', [(shot, shot ^ number) for shot in range(shot...  2.7 us
    pallas_call x1, Pallas kernels, per_device(): pl.pallas_call(own_edges, out_shape=(struct(*wavelet.shape), struct(*wide...  1.33 us
    ppermute x9, waiting for transfers between devices, swap_tiles(): return lax.ppermute(value, ('tile', 'shot'), pairs)  1.27 us
    pallas_call x1, Pallas kernels, per_device(): pl.pallas_call(functools.partial(image_products, weight), out_shape=struc...  0.92 us
    pallas_call x1, Pallas kernels, per_device(): pl.pallas_call(functools.partial(own_steps, width), out_shape=(struct(lev...  0.72 us
    pallas_call x1, Pallas kernels, per_device(): pl.pallas_call(functools.partial(early_products, weight), out_shape=(stru...  0.67 us
  transfers between devices with their start and end apart: 13, of which 2 were waited for; matrix products, arithmetic and copies ran while one was open for 0% of the time, Pallas kernels for 8%

profile of v25, /device:TPU:0, one launch (start us, length us, event | category | flops | bytes accessed | tf_op | source)
XLA Modules:
  0.0 17.9 jit_solution(7169439872403352805)
XLA Ops:
  0.6 1.3 %own_edges.1 = (f32[1,2]{1,0:T(1,128)S(1)}, f32[2,8,32,128]{3,2,1,0:T(8,128)S(1)}, f32[2,8,16,128]{3,2,1,0:T(8,128)S(1)}, s32[8,16,128]{2,1,0:T(8,128)S(1)}, f32...) custom-call(f32[1,16]{1,0:T(1,128)} %bitcast.9, ...), custom_call_target="tpu_custom_call" | custom-call | tf_op jit(solution)/shard_map/own_edges/pallas_call | solution.py:481
  2.0 3.1 %collective-permute-start = (f32[20,8,128]{2,1,0:T(8,128)S(1)}, f32[20,8,128]{2,1,0:T(8,128)S(1)}, u32[]{:S(2)}, u32[]{:S(2)}) collective-permute-start(f32[20,8,128]{2,1,0:T(8,128)S(1)} %get-tuple-element.37), channel_id=1, source_target_pairs={{0,4},{1,5},{2,6},{3,7},{4,0},{5,1},{6,2},{7,3},{8,9},{9,8},{10,11... | collective-permute-start | bytes 245768 | tf_op jit(solution)/shard_map/ppermute | solution.py:442
  5.1 0.0 collective-permute-start.1
  5.1 0.5 %collective-permute-start.2 = (f32[20,8,128]{2,1,0:T(8,128)S(1)}, f32[20,8,128]{2,1,0:T(8,128)S(1)}, u32[]{:S(2)}, u32[]{:S(2)}) collective-permute-start(f32[20,8,128]{2,1,0:T(8,128)S(1)} %get-tuple-element.39), channel_id=1, source_target_pairs={{0,1},{1,0},{2,3},{3,2},{4,5},{5,4},{6,7},{7,6},{8,12},{9,13},{10,... | collective-permute-start | bytes 245768 | tf_op jit(solution)/shard_map/ppermute | solution.py:442
  6.2 0.7 %own_steps.1 = (f32[8,16,128]{2,1,0:T(8,128)S(1)}, f32[2,8,16,128]{3,2,1,0:T(8,128)S(1)}, f32[2,8,8,128]{3,2,1,0:T(8,128)S(1)}, f32[8,32,128]{2,1,0:T(8,128)S(1)...) custom-call(s32[1]{0:T(128)S(6)} %copy.13.cell_ref, f32[1,2]{1,0:T(1,128)S(1)} %get-tuple-element.25.amps_ref, ...), custom_call_target="tpu_custom_call" | custom-call | tf_op jit(solution)/shard_map/own_steps/pallas_call | solution.py:520
  6.9 0.6 %collective-permute-done.rest_0_ = f32[20,8,128]{2,1,0:T(8,128)S(1)} collective-permute-done((f32[20,8,128]{2,1,0:T(8,128)S(1)}, f32[20,8,128]{2,1,0:T(8,128)S(1)}, u32[]{:S(2)}, u32[]{:S(2)}) %collective-permute-start) | collective-permute-done | bytes 81952 | tf_op jit(solution)/shard_map/ppermute | solution.py:442
  7.5 0.0 collective-permute-done.1.rest_1_
  7.5 0.0 collective-permute-done.2.rest_2_
  7.5 0.3 %neighbours_part.1 = (f32[2,8,16,128]{3,2,1,0:T(8,128)S(1)}, f32[2,2,2,16,128]{4,3,2,1,0:T(8,128)S(1)}, f32[2,2,16,128]{3,2,1,0:T(8,128)S(1)}, f32[2,2,16,128]{3,2,1,0:T(8,128)S(1)}) custom-call(s32[4,8,128]{2,1,0:T(8,128)S(1)} %get-tuple-element.31.sides_ref, s32[2,8,128]{2,1,0:T(8,128)S(1)} %get-tuple-element.32.bits_ref, ...), custom_call_target="tpu_custom_call" | custom-call | tf_op jit(solution)/shard_map/neighbours_part/pallas_call | solution.py:537
  7.8 0.6 %collective-permute-start.6 = (f32[2,2,16,128]{3,2,1,0:T(8,128)S(1)}, f32[2,2,16,128]{3,2,1,0:T(8,128)S(1)}, u32[]{:S(2)}, u32[]{:S(2)}) collective-permute-start(f32[2,2,16,128]{3,2,1,0:T(8,128)S(1)} %get-tuple-element.44), channel_id=1, source_target_pairs={{0,3},{1,2},{2,1},{3,0},{4,7},{5,6},{6,5},{7,4},{8,11},{9,10},{10,... | collective-permute-start | bytes 98312 | tf_op jit(solution)/shard_map/ppermute | solution.py:551
  8.4 1.4 %collective-permute-start.7 = (f32[2,2,16,128]{3,2,1,0:T(8,128)S(1)}, f32[2,2,16,128]{3,2,1,0:T(8,128)S(1)}, u32[]{:S(2)}, u32[]{:S(2)}) collective-permute-start(f32[2,2,16,128]{3,2,1,0:T(8,128)S(1)} %get-tuple-element.45), channel_id=1, source_target_pairs={{0,2},{1,3},{2,0},{3,1},{4,6},{5,7},{6,4},{7,5},{8,10},{9,11},{10,... | collective-permute-start | bytes 98312 | tf_op jit(solution)/shard_map/ppermute | solution.py:551
  9.9 2.0 %collective-permute-start.5 = (f32[2,2,2,16,128]{4,3,2,1,0:T(8,128)S(1)}, f32[2,2,2,16,128]{4,3,2,1,0:T(8,128)S(1)}, u32[]{:S(2)}, u32[]{:S(2)}) collective-permute-start(f32[2,2,2,16,128]{4,3,2,1,0:T(8,128)S(1)} %get-tuple-element.40.mine_ref), channel_id=1, source_target_pairs={{0,4},{1,5},{2,6},{3,7},{4,0},{5,1},{6,2},{7,3},{8,9},{9,8},{10,11... | collective-permute-start | bytes 196616 | tf_op jit(solution)/shard_map/ppermute | solution.py:442
  11.9 0.0 collective-permute-start.4
  11.9 0.5 %collective-permute-start.3 = (f32[2,2,2,16,128]{4,3,2,1,0:T(8,128)S(1)}, f32[2,2,2,16,128]{4,3,2,1,0:T(8,128)S(1)}, u32[]{:S(2)}, u32[]{:S(2)}) collective-permute-start(f32[2,2,2,16,128]{4,3,2,1,0:T(8,128)S(1)} %get-tuple-element.40.mine_ref), channel_id=1, source_target_pairs={{0,1},{1,0},{2,3},{3,2},{4,5},{5,4},{6,7},{7,6},{8,12},{9,13},{10,... | collective-permute-start | bytes 196616 | tf_op jit(solution)/shard_map/ppermute | solution.py:442
  12.4 0.0 collective-permute-done.6.refs_0_
  12.4 0.0 collective-permute-done.7.refs_1_
  12.4 1.9 %collective-permute-start.10 = (f32[2,2,2,16,128]{4,3,2,1,0:T(8,128)S(1)}, f32[2,2,2,16,128]{4,3,2,1,0:T(8,128)S(1)}, u32[]{:S(2)}, u32[]{:S(2)}) collective-permute-start(f32[2,2,2,16,128]{4,3,2,1,0:T(8,128)S(1)} %stack.3._others_ref.others_ref), channel_id=1, source_target_pairs={{0,4},{1,5},{2,6},{3,7},{4,0},{5,1},{6,2},{7,3},{8,9},{9,8},{10,11... | collective-permute-start | bytes 196616 | tf_op jit(solution)/shard_map/ppermute | solution.py:442
  14.4 0.0 collective-permute-start.9
  14.4 0.0 collective-permute-done.5.first_ref
  14.4 0.5 %collective-permute-start.8 = (f32[2,2,2,16,128]{4,3,2,1,0:T(8,128)S(1)}, f32[2,2,2,16,128]{4,3,2,1,0:T(8,128)S(1)}, u32[]{:S(2)}, u32[]{:S(2)}) collective-permute-start(f32[2,2,2,16,128]{4,3,2,1,0:T(8,128)S(1)} %stack.3._others_ref.others_ref), channel_id=1, source_target_pairs={{0,1},{1,0},{2,3},{3,2},{4,5},{5,4},{6,7},{7,6},{8,12},{9,13},{10,... | collective-permute-start | bytes 196616 | tf_op jit(solution)/shard_map/ppermute | solution.py:442
  14.9 0.0 collective-permute-done.4.second_ref
  14.9 0.2 collective-permute-start.11
  15.1 0.0 collective-permute-done.3.third_ref
  15.1 0.5 %collective-permute-start.12 = (f32[2,2,2,16,128]{4,3,2,1,0:T(8,128)S(1)}, f32[2,2,2,16,128]{4,3,2,1,0:T(8,128)S(1)}, u32[]{:S(2)}, u32[]{:S(2)}) collective-permute-start(f32[2,2,2,16,128]{4,3,2,1,0:T(8,128)S(1)} %stack.5), channel_id=1, source_target_pairs={{0,1},{1,0},{2,3},{3,2},{4,5},{5,4},{6,7},{7,6},{8,9},{9,8},{10,11... | collective-permute-start | bytes 196616 | tf_op jit(solution)/shard_map/ppermute | solution.py:551
  15.6 0.7 %early_products.1 = (f32[1,8,16,128]{3,2,1,0:T(8,128)}, f32[1,8,16,128]{3,2,1,0:T(8,128)}, f32[33,2,16,128]{3,2,1,0:T(8,128)S(1)}) custom-call(s32[4,8,128]{2,1,0:T(8,128)S(1)} %get-tuple-element.31.sides_ref, f32[2,2,2,16,128]{4,3,2,1,0:T(8,128)S(1)} %get-tuple-element.40.mine_ref, f32[2,2,2,16,128]{4,3,2,1,0:T(8,128)S(1)} %collective-permute-done.3.third_ref, ...), custom_call_target="tpu_custom_call" | custom-call | tf_op jit(solution)/shard_map/early_products/pallas_call | solution.py:582
  16.3 0.7 %collective-permute-done.10.rest_2_ = f32[2,2,2,16,128]{4,3,2,1,0:T(8,128)S(1)} collective-permute-done((f32[2,2,2,16,128]{4,3,2,1,0:T(8,128)S(1)}, f32[2,2,2,16,128]{4,3,2,1,0:T(8,128)S(1)}, u32[]{:S(2)}, u32[]{:S(2)}) %collective-permute-start.10) | collective-permute-done | bytes 65568 | tf_op jit(solution)/shard_map/ppermute | solution.py:442
  16.9 0.0 collective-permute-done.9.rest_1_
  16.9 0.0 collective-permute-done.8.rest_0_
  17.0 0.0 collective-permute-done.11.rest_3_
  17.0 0.0 collective-permute-done.12.rest_4_
  17.0 0.9 %image_products.1 = f32[33,2,16,128]{3,2,1,0:T(8,128)} custom-call(s32[4,8,128]{2,1,0:T(8,128)S(1)} %get-tuple-element.31.sides_ref, f32[2,2,2,16,128]{4,3,2,1,0:T(8,128)S(1)} %stack.3._others_ref.others_ref, f32[2,2,2,16,128]{4,3,2,1,0:T(8,128)S(1)} %collective-permute-done.8.rest_0_, f32[2,2,2,16,128]{4,3,2,1,0:T(8,128)S(1)} %collective-permute-done.9.rest_1_, ...), custom_call_target="tpu_custom_call" | custom-call | tf_op jit(solution)/shard_map/image_products/pallas_call | solution.py:599
  (8 shorter events, 0.0 us)
Async XLA Ops:
  2.0 5.5 %collective-permute-start = (f32[20,8,128]{2,1,0:T(8,128)S(1)}, f32[20,8,128]{2,1,0:T(8,128)S(1)}, u32[]{:S(2)}, u32[]{:S(2)}) collective-permute-start(f32[20,8,128]{2,1,0:T(8,128)S(1)} %get-tuple-element.37), channel_id=1, source_target_pairs={{0,4},{1,5},{2,6},{3,7},{4,0},{5,1},{6,2},{7,3},{8,9},{9,8},{10,11... | collective-permute-start | bytes 245768 | tf_op jit(solution)/shard_map/ppermute | solution.py:442
  5.1 2.4 %collective-permute-start.1 = (f32[20,8,128]{2,1,0:T(8,128)S(1)}, f32[20,8,128]{2,1,0:T(8,128)S(1)}, u32[]{:S(2)}, u32[]{:S(2)}) collective-permute-start(f32[20,8,128]{2,1,0:T(8,128)S(1)} %get-tuple-element.38), channel_id=1, source_target_pairs={{0,1},{1,0},{2,3},{3,2},{4,8},{5,9},{6,10},{7,11},{8,4},{9,5},{10,... | collective-permute-start | bytes 245768 | tf_op jit(solution)/shard_map/ppermute | solution.py:442
  5.1 2.4 %collective-permute-start.2 = (f32[20,8,128]{2,1,0:T(8,128)S(1)}, f32[20,8,128]{2,1,0:T(8,128)S(1)}, u32[]{:S(2)}, u32[]{:S(2)}) collective-permute-start(f32[20,8,128]{2,1,0:T(8,128)S(1)} %get-tuple-element.39), channel_id=1, source_target_pairs={{0,1},{1,0},{2,3},{3,2},{4,5},{5,4},{6,7},{7,6},{8,12},{9,13},{10,... | collective-permute-start | bytes 245768 | tf_op jit(solution)/shard_map/ppermute | solution.py:442
  7.8 4.6 %collective-permute-start.6 = (f32[2,2,16,128]{3,2,1,0:T(8,128)S(1)}, f32[2,2,16,128]{3,2,1,0:T(8,128)S(1)}, u32[]{:S(2)}, u32[]{:S(2)}) collective-permute-start(f32[2,2,16,128]{3,2,1,0:T(8,128)S(1)} %get-tuple-element.44), channel_id=1, source_target_pairs={{0,3},{1,2},{2,1},{3,0},{4,7},{5,6},{6,5},{7,4},{8,11},{9,10},{10,... | collective-permute-start | bytes 98312 | tf_op jit(solution)/shard_map/ppermute | solution.py:551
  8.4 4.0 %collective-permute-start.7 = (f32[2,2,16,128]{3,2,1,0:T(8,128)S(1)}, f32[2,2,16,128]{3,2,1,0:T(8,128)S(1)}, u32[]{:S(2)}, u32[]{:S(2)}) collective-permute-start(f32[2,2,16,128]{3,2,1,0:T(8,128)S(1)} %get-tuple-element.45), channel_id=1, source_target_pairs={{0,2},{1,3},{2,0},{3,1},{4,6},{5,7},{6,4},{7,5},{8,10},{9,11},{10,... | collective-permute-start | bytes 98312 | tf_op jit(solution)/shard_map/ppermute | solution.py:551
  9.9 4.6 %collective-permute-start.5 = (f32[2,2,2,16,128]{4,3,2,1,0:T(8,128)S(1)}, f32[2,2,2,16,128]{4,3,2,1,0:T(8,128)S(1)}, u32[]{:S(2)}, u32[]{:S(2)}) collective-permute-start(f32[2,2,2,16,128]{4,3,2,1,0:T(8,128)S(1)} %get-tuple-element.40.mine_ref), channel_id=1, source_target_pairs={{0,4},{1,5},{2,6},{3,7},{4,0},{5,1},{6,2},{7,3},{8,9},{9,8},{10,11... | collective-permute-start | bytes 196616 | tf_op jit(solution)/shard_map/ppermute | solution.py:442
  11.9 3.0 %collective-permute-start.4 = (f32[2,2,2,16,128]{4,3,2,1,0:T(8,128)S(1)}, f32[2,2,2,16,128]{4,3,2,1,0:T(8,128)S(1)}, u32[]{:S(2)}, u32[]{:S(2)}) collective-permute-start(f32[2,2,2,16,128]{4,3,2,1,0:T(8,128)S(1)} %get-tuple-element.40.mine_ref), channel_id=1, source_target_pairs={{0,1},{1,0},{2,3},{3,2},{4,8},{5,9},{6,10},{7,11},{8,4},{9,5},{10,... | collective-permute-start | bytes 196616 | tf_op jit(solution)/shard_map/ppermute | solution.py:442
  11.9 3.2 %collective-permute-start.3 = (f32[2,2,2,16,128]{4,3,2,1,0:T(8,128)S(1)}, f32[2,2,2,16,128]{4,3,2,1,0:T(8,128)S(1)}, u32[]{:S(2)}, u32[]{:S(2)}) collective-permute-start(f32[2,2,2,16,128]{4,3,2,1,0:T(8,128)S(1)} %get-tuple-element.40.mine_ref), channel_id=1, source_target_pairs={{0,1},{1,0},{2,3},{3,2},{4,5},{5,4},{6,7},{7,6},{8,12},{9,13},{10,... | collective-permute-start | bytes 196616 | tf_op jit(solution)/shard_map/ppermute | solution.py:442
  12.4 4.5 %collective-permute-start.10 = (f32[2,2,2,16,128]{4,3,2,1,0:T(8,128)S(1)}, f32[2,2,2,16,128]{4,3,2,1,0:T(8,128)S(1)}, u32[]{:S(2)}, u32[]{:S(2)}) collective-permute-start(f32[2,2,2,16,128]{4,3,2,1,0:T(8,128)S(1)} %stack.3._others_ref.others_ref), channel_id=1, source_target_pairs={{0,4},{1,5},{2,6},{3,7},{4,0},{5,1},{6,2},{7,3},{8,9},{9,8},{10,11... | collective-permute-start | bytes 196616 | tf_op jit(solution)/shard_map/ppermute | solution.py:442
  14.4 2.6 %collective-permute-start.9 = (f32[2,2,2,16,128]{4,3,2,1,0:T(8,128)S(1)}, f32[2,2,2,16,128]{4,3,2,1,0:T(8,128)S(1)}, u32[]{:S(2)}, u32[]{:S(2)}) collective-permute-start(f32[2,2,2,16,128]{4,3,2,1,0:T(8,128)S(1)} %stack.3._others_ref.others_ref), channel_id=1, source_target_pairs={{0,1},{1,0},{2,3},{3,2},{4,8},{5,9},{6,10},{7,11},{8,4},{9,5},{10,... | collective-permute-start | bytes 196616 | tf_op jit(solution)/shard_map/ppermute | solution.py:442
  14.4 2.5 %collective-permute-start.8 = (f32[2,2,2,16,128]{4,3,2,1,0:T(8,128)S(1)}, f32[2,2,2,16,128]{4,3,2,1,0:T(8,128)S(1)}, u32[]{:S(2)}, u32[]{:S(2)}) collective-permute-start(f32[2,2,2,16,128]{4,3,2,1,0:T(8,128)S(1)} %stack.3._others_ref.others_ref), channel_id=1, source_target_pairs={{0,1},{1,0},{2,3},{3,2},{4,5},{5,4},{6,7},{7,6},{8,12},{9,13},{10,... | collective-permute-start | bytes 196616 | tf_op jit(solution)/shard_map/ppermute | solution.py:442
  14.9 2.0 %collective-permute-start.11 = (f32[2,2,2,16,128]{4,3,2,1,0:T(8,128)S(1)}, f32[2,2,2,16,128]{4,3,2,1,0:T(8,128)S(1)}, u32[]{:S(2)}, u32[]{:S(2)}) collective-permute-start(f32[2,2,2,16,128]{4,3,2,1,0:T(8,128)S(1)} %stack.4), channel_id=1, source_target_pairs={{0,1},{1,0},{2,3},{3,2},{4,5},{5,4},{6,7},{7,6},{8,9},{9,8},{10,11... | collective-permute-start | bytes 196616 | tf_op jit(solution)/shard_map/ppermute | solution.py:551
  15.1 1.9 %collective-permute-start.12 = (f32[2,2,2,16,128]{4,3,2,1,0:T(8,128)S(1)}, f32[2,2,2,16,128]{4,3,2,1,0:T(8,128)S(1)}, u32[]{:S(2)}, u32[]{:S(2)}) collective-permute-start(f32[2,2,2,16,128]{4,3,2,1,0:T(8,128)S(1)} %stack.5), channel_id=1, source_target_pairs={{0,1},{1,0},{2,3},{3,2},{4,5},{5,4},{6,7},{7,6},{8,9},{9,8},{10,11... | collective-permute-start | bytes 196616 | tf_op jit(solution)/shard_map/ppermute | solution.py:551

commit v26 on v25

--- a/solution.py
+++ b/solution.py
@@ -90,22 +90,22 @@
     *rest,
 ):
     sent_refs, rest = rest[:ROUNDS], rest[ROUNDS:]
-    table, spots_ref, traces_ref, edges, sems = rest
+    table, spots_ref, traces_ref, edges, sums, sems = rest
     levels, extent, across = ids_ref.shape
     regions = table_hbm.shape[1]
     end = LEAD + extent
     rows = pl.ds(LEAD, extent)
-    moves = [(table_hbm, table), (spots_hbm, spots_ref), (traces_hbm, traces_ref)]
-    for begin in range(0, levels, levels // 2):
-        part = pl.ds(begin, levels // 2)
-        moves += [
-            (src_now.at[0, part], wide.at[0, part, rows, :]),
-            (rec_now.at[0, part], wide.at[1, part, rows, :]),
-            (ids_hbm.at[part], ids_ref.at[part]),
-            (src_prev.at[0, part], prev_ref.at[0, part]),
-            (rec_prev.at[0, part], prev_ref.at[1, part]),
-        ]
-    moves.append((amps_hbm, amps_ref))
+    moves = [
+        (src_now.at[0], wide.at[0, :, rows, :]),
+        (rec_now.at[0], wide.at[1, :, rows, :]),
+        (ids_hbm, ids_ref),
+        (src_prev.at[0], prev_ref.at[0]),
+        (rec_prev.at[0], prev_ref.at[1]),
+        (table_hbm, table),
+        (spots_hbm, spots_ref),
+        (traces_hbm, traces_ref),
+        (amps_hbm, amps_ref),
+    ]
     copies = [
         pltpu.make_async_copy(here, there, sems.at[i]) for i, (here, there) in enumerate(moves)
     ]
@@ -119,7 +119,22 @@
     weights = lane_weights((8, across))
     low_half = is_low(across)
     my_round = lax.rem(lax.axis_index("tile"), ROUNDS)
-    for copy in copies:
+    for copy in copies[:2]:
+        copy.wait()
+    for field in range(2):
+        for level in range(levels):
+            edges[field, level] = jnp.where(
+                low_half, wide[field, level, LEAD : LEAD + 8, :], wide[field, level, end - 8 : end, :]
+            )
+    for field in range(2):
+        for level in range(levels):
+            total = lane_sum(edges[field, level], weights) + jnp.where(
+                low_half,
+                beside_sum(wide, field, level, LEAD, 8),
+                beside_sum(wide, field, level, end - 8, 8),
+            )
+            sums[field, level] = depth_sum(lambda near: edges[field, near], level, levels, total)
+    for copy in copies[2:]:
         copy.wait()
 
     spots = spots_ref[...]
@@ -167,18 +182,7 @@
 
     for field in range(2):
         for level in range(levels):
-            edges[field, level] = jnp.where(
-                low_half, wide[field, level, LEAD : LEAD + 8, :], wide[field, level, end - 8 : end, :]
-            )
-    for field in range(2):
-        for level in range(levels):
-            now = edges[field, level]
-            total = lane_sum(now, weights) + jnp.where(
-                low_half,
-                beside_sum(wide, field, level, LEAD, 8),
-                beside_sum(wide, field, level, end - 8, 8),
-            )
-            total = depth_sum(lambda near: edges[field, near], level, levels, total)
+            now, total = edges[field, level], sums[field, level]
             value = 2.0 * now - halves(prev_ref, field, level) + coefs[level] * total
             if field == 1 and level == 0:
                 value = value + jnp.where(low_half, planes[0:8, :], planes[extent - 8 : extent, :])
@@ -496,7 +500,8 @@
             scratch(*receiver_cell.shape, dtype=jnp.int32),
             scratch(*receiver_data.shape),
             scratch(2, levels, 8, across),
-            pltpu.SemaphoreType.DMA((14,)),
+            scratch(2, levels, 8, across),
+            pltpu.SemaphoreType.DMA((9,)),
         ],
         compiler_params=params,
         name="own_edges",

time: 18.1 us -> 18.1 us (level)
  no operation moved by 1% of the time
where the time goes in v26:
time: 18.1 us; the launch traced here: 18 us
  starting transfers between devices  11.3 us (62%)
  Pallas kernels  4.02 us (22%)
  between operations  1.37 us (8%)
  waiting for transfers between devices  1.28 us (7%)
    ppermute x9, starting transfers between devices, swap_tiles(): return lax.ppermute(value, ('tile', 'shot'), pairs)  8.6 us
    ppermute x4, starting transfers between devices, swap_shots(): lax.ppermute(value, 'shot', [(shot, shot ^ number) for shot in range(shot...  2.7 us
    pallas_call x1, Pallas kernels, per_device(): pl.pallas_call(own_edges, out_shape=(struct(*wavelet.shape), struct(*wide...  1.41 us
    ppermute x9, waiting for transfers between devices, swap_tiles(): return lax.ppermute(value, ('tile', 'shot'), pairs)  1.27 us
    pallas_call x1, Pallas kernels, per_device(): pl.pallas_call(functools.partial(image_products, weight), out_shape=struc...  0.92 us
    pallas_call x1, Pallas kernels, per_device(): pl.pallas_call(functools.partial(own_steps, width), out_shape=(struct(lev...  0.72 us
    pallas_call x1, Pallas kernels, per_device(): pl.pallas_call(functools.partial(early_products, weight), out_shape=(stru...  0.67 us
  transfers between devices with their start and end apart: 13, of which 2 were waited for; matrix products, arithmetic and copies ran while one was open for 0% of the time, Pallas kernels for 8%

profile of v26, /device:TPU:0, one launch (start us, length us, event | category | flops | bytes accessed | tf_op | source)
XLA Modules:
  0.0 18.0 jit_solution(868379887111580823)
XLA Ops:
  0.6 1.4 %own_edges.1 = (f32[1,2]{1,0:T(1,128)S(1)}, f32[2,8,32,128]{3,2,1,0:T(8,128)S(1)}, f32[2,8,16,128]{3,2,1,0:T(8,128)S(1)}, s32[8,16,128]{2,1,0:T(8,128)S(1)}, f32...) custom-call(f32[1,16]{1,0:T(1,128)} %bitcast.9, ...), custom_call_target="tpu_custom_call" | custom-call | tf_op jit(solution)/shard_map/own_edges/pallas_call | solution.py:485
  2.0 3.1 %collective-permute-start = (f32[20,8,128]{2,1,0:T(8,128)S(1)}, f32[20,8,128]{2,1,0:T(8,128)S(1)}, u32[]{:S(2)}, u32[]{:S(2)}) collective-permute-start(f32[20,8,128]{2,1,0:T(8,128)S(1)} %get-tuple-element.37), channel_id=1, source_target_pairs={{0,4},{1,5},{2,6},{3,7},{4,0},{5,1},{6,2},{7,3},{8,9},{9,8},{10,11... | collective-permute-start | bytes 245768 | tf_op jit(solution)/shard_map/ppermute | solution.py:446
  5.1 0.0 collective-permute-start.1
  5.1 0.5 %collective-permute-start.2 = (f32[20,8,128]{2,1,0:T(8,128)S(1)}, f32[20,8,128]{2,1,0:T(8,128)S(1)}, u32[]{:S(2)}, u32[]{:S(2)}) collective-permute-start(f32[20,8,128]{2,1,0:T(8,128)S(1)} %get-tuple-element.39), channel_id=1, source_target_pairs={{0,1},{1,0},{2,3},{3,2},{4,5},{5,4},{6,7},{7,6},{8,12},{9,13},{10,... | collective-permute-start | bytes 245768 | tf_op jit(solution)/shard_map/ppermute | solution.py:446
  6.3 0.7 %own_steps.1 = (f32[8,16,128]{2,1,0:T(8,128)S(1)}, f32[2,8,16,128]{3,2,1,0:T(8,128)S(1)}, f32[2,8,8,128]{3,2,1,0:T(8,128)S(1)}, f32[8,32,128]{2,1,0:T(8,128)S(1)...) custom-call(s32[1]{0:T(128)S(6)} %copy.13.cell_ref, f32[1,2]{1,0:T(1,128)S(1)} %get-tuple-element.25.amps_ref, ...), custom_call_target="tpu_custom_call" | custom-call | tf_op jit(solution)/shard_map/own_steps/pallas_call | solution.py:525
  7.0 0.6 %collective-permute-done.rest_0_ = f32[20,8,128]{2,1,0:T(8,128)S(1)} collective-permute-done((f32[20,8,128]{2,1,0:T(8,128)S(1)}, f32[20,8,128]{2,1,0:T(8,128)S(1)}, u32[]{:S(2)}, u32[]{:S(2)}) %collective-permute-start) | collective-permute-done | bytes 81952 | tf_op jit(solution)/shard_map/ppermute | solution.py:446
  7.6 0.0 collective-permute-done.1.rest_1_
  7.6 0.0 collective-permute-done.2.rest_2_
  7.6 0.3 %neighbours_part.1 = (f32[2,8,16,128]{3,2,1,0:T(8,128)S(1)}, f32[2,2,2,16,128]{4,3,2,1,0:T(8,128)S(1)}, f32[2,2,16,128]{3,2,1,0:T(8,128)S(1)}, f32[2,2,16,128]{3,2,1,0:T(8,128)S(1)}) custom-call(s32[4,8,128]{2,1,0:T(8,128)S(1)} %get-tuple-element.31.sides_ref, s32[2,8,128]{2,1,0:T(8,128)S(1)} %get-tuple-element.32.bits_ref, ...), custom_call_target="tpu_custom_call" | custom-call | tf_op jit(solution)/shard_map/neighbours_part/pallas_call | solution.py:542
  7.9 0.6 %collective-permute-start.6 = (f32[2,2,16,128]{3,2,1,0:T(8,128)S(1)}, f32[2,2,16,128]{3,2,1,0:T(8,128)S(1)}, u32[]{:S(2)}, u32[]{:S(2)}) collective-permute-start(f32[2,2,16,128]{3,2,1,0:T(8,128)S(1)} %get-tuple-element.44), channel_id=1, source_target_pairs={{0,3},{1,2},{2,1},{3,0},{4,7},{5,6},{6,5},{7,4},{8,11},{9,10},{10,... | collective-permute-start | bytes 98312 | tf_op jit(solution)/shard_map/ppermute | solution.py:556
  8.5 1.4 %collective-permute-start.7 = (f32[2,2,16,128]{3,2,1,0:T(8,128)S(1)}, f32[2,2,16,128]{3,2,1,0:T(8,128)S(1)}, u32[]{:S(2)}, u32[]{:S(2)}) collective-permute-start(f32[2,2,16,128]{3,2,1,0:T(8,128)S(1)} %get-tuple-element.45), channel_id=1, source_target_pairs={{0,2},{1,3},{2,0},{3,1},{4,6},{5,7},{6,4},{7,5},{8,10},{9,11},{10,... | collective-permute-start | bytes 98312 | tf_op jit(solution)/shard_map/ppermute | solution.py:556
  9.9 2.0 %collective-permute-start.5 = (f32[2,2,2,16,128]{4,3,2,1,0:T(8,128)S(1)}, f32[2,2,2,16,128]{4,3,2,1,0:T(8,128)S(1)}, u32[]{:S(2)}, u32[]{:S(2)}) collective-permute-start(f32[2,2,2,16,128]{4,3,2,1,0:T(8,128)S(1)} %get-tuple-element.40.mine_ref), channel_id=1, source_target_pairs={{0,4},{1,5},{2,6},{3,7},{4,0},{5,1},{6,2},{7,3},{8,9},{9,8},{10,11... | collective-permute-start | bytes 196616 | tf_op jit(solution)/shard_map/ppermute | solution.py:446
  12.0 0.0 collective-permute-start.4
  12.0 0.5 %collective-permute-start.3 = (f32[2,2,2,16,128]{4,3,2,1,0:T(8,128)S(1)}, f32[2,2,2,16,128]{4,3,2,1,0:T(8,128)S(1)}, u32[]{:S(2)}, u32[]{:S(2)}) collective-permute-start(f32[2,2,2,16,128]{4,3,2,1,0:T(8,128)S(1)} %get-tuple-element.40.mine_ref), channel_id=1, source_target_pairs={{0,1},{1,0},{2,3},{3,2},{4,5},{5,4},{6,7},{7,6},{8,12},{9,13},{10,... | collective-permute-start | bytes 196616 | tf_op jit(solution)/shard_map/ppermute | solution.py:446
  12.5 0.0 collective-permute-done.6.refs_0_
  12.5 0.0 collective-permute-done.7.refs_1_
  12.5 1.9 %collective-permute-start.10 = (f32[2,2,2,16,128]{4,3,2,1,0:T(8,128)S(1)}, f32[2,2,2,16,128]{4,3,2,1,0:T(8,128)S(1)}, u32[]{:S(2)}, u32[]{:S(2)}) collective-permute-start(f32[2,2,2,16,128]{4,3,2,1,0:T(8,128)S(1)} %stack.3._others_ref.others_ref), channel_id=1, source_target_pairs={{0,4},{1,5},{2,6},{3,7},{4,0},{5,1},{6,2},{7,3},{8,9},{9,8},{10,11... | collective-permute-start | bytes 196616 | tf_op jit(solution)/shard_map/ppermute | solution.py:446
  14.4 0.0 collective-permute-start.9
  14.5 0.0 collective-permute-done.5.first_ref
  14.5 0.5 %collective-permute-start.8 = (f32[2,2,2,16,128]{4,3,2,1,0:T(8,128)S(1)}, f32[2,2,2,16,128]{4,3,2,1,0:T(8,128)S(1)}, u32[]{:S(2)}, u32[]{:S(2)}) collective-permute-start(f32[2,2,2,16,128]{4,3,2,1,0:T(8,128)S(1)} %stack.3._others_ref.others_ref), channel_id=1, source_target_pairs={{0,1},{1,0},{2,3},{3,2},{4,5},{5,4},{6,7},{7,6},{8,12},{9,13},{10,... | collective-permute-start | bytes 196616 | tf_op jit(solution)/shard_map/ppermute | solution.py:446
  15.0 0.0 collective-permute-done.4.second_ref
  15.0 0.2 collective-permute-start.11
  15.1 0.0 collective-permute-done.3.third_ref
  15.2 0.5 %collective-permute-start.12 = (f32[2,2,2,16,128]{4,3,2,1,0:T(8,128)S(1)}, f32[2,2,2,16,128]{4,3,2,1,0:T(8,128)S(1)}, u32[]{:S(2)}, u32[]{:S(2)}) collective-permute-start(f32[2,2,2,16,128]{4,3,2,1,0:T(8,128)S(1)} %stack.5), channel_id=1, source_target_pairs={{0,1},{1,0},{2,3},{3,2},{4,5},{5,4},{6,7},{7,6},{8,9},{9,8},{10,11... | collective-permute-start | bytes 196616 | tf_op jit(solution)/shard_map/ppermute | solution.py:556
  15.7 0.7 %early_products.1 = (f32[1,8,16,128]{3,2,1,0:T(8,128)}, f32[1,8,16,128]{3,2,1,0:T(8,128)}, f32[33,2,16,128]{3,2,1,0:T(8,128)S(1)}) custom-call(s32[4,8,128]{2,1,0:T(8,128)S(1)} %get-tuple-element.31.sides_ref, f32[2,2,2,16,128]{4,3,2,1,0:T(8,128)S(1)} %get-tuple-element.40.mine_ref, f32[2,2,2,16,128]{4,3,2,1,0:T(8,128)S(1)} %collective-permute-done.3.third_ref, ...), custom_call_target="tpu_custom_call" | custom-call | tf_op jit(solution)/shard_map/early_products/pallas_call | solution.py:587
  16.3 0.7 %collective-permute-done.10.rest_2_ = f32[2,2,2,16,128]{4,3,2,1,0:T(8,128)S(1)} collective-permute-done((f32[2,2,2,16,128]{4,3,2,1,0:T(8,128)S(1)}, f32[2,2,2,16,128]{4,3,2,1,0:T(8,128)S(1)}, u32[]{:S(2)}, u32[]{:S(2)}) %collective-permute-start.10) | collective-permute-done | bytes 65568 | tf_op jit(solution)/shard_map/ppermute | solution.py:446
  17.0 0.0 collective-permute-done.9.rest_1_
  17.0 0.0 collective-permute-done.8.rest_0_
  17.0 0.0 collective-permute-done.11.rest_3_
  17.0 0.0 collective-permute-done.12.rest_4_
  17.0 0.9 %image_products.1 = f32[33,2,16,128]{3,2,1,0:T(8,128)} custom-call(s32[4,8,128]{2,1,0:T(8,128)S(1)} %get-tuple-element.31.sides_ref, f32[2,2,2,16,128]{4,3,2,1,0:T(8,128)S(1)} %stack.3._others_ref.others_ref, f32[2,2,2,16,128]{4,3,2,1,0:T(8,128)S(1)} %collective-permute-done.8.rest_0_, f32[2,2,2,16,128]{4,3,2,1,0:T(8,128)S(1)} %collective-permute-done.9.rest_1_, ...), custom_call_target="tpu_custom_call" | custom-call | tf_op jit(solution)/shard_map/image_products/pallas_call | solution.py:604
  (8 shorter events, 0.0 us)
Async XLA Ops:
  2.0 5.5 %collective-permute-start = (f32[20,8,128]{2,1,0:T(8,128)S(1)}, f32[20,8,128]{2,1,0:T(8,128)S(1)}, u32[]{:S(2)}, u32[]{:S(2)}) collective-permute-start(f32[20,8,128]{2,1,0:T(8,128)S(1)} %get-tuple-element.37), channel_id=1, source_target_pairs={{0,4},{1,5},{2,6},{3,7},{4,0},{5,1},{6,2},{7,3},{8,9},{9,8},{10,11... | collective-permute-start | bytes 245768 | tf_op jit(solution)/shard_map/ppermute | solution.py:446
  5.1 2.4 %collective-permute-start.1 = (f32[20,8,128]{2,1,0:T(8,128)S(1)}, f32[20,8,128]{2,1,0:T(8,128)S(1)}, u32[]{:S(2)}, u32[]{:S(2)}) collective-permute-start(f32[20,8,128]{2,1,0:T(8,128)S(1)} %get-tuple-element.38), channel_id=1, source_target_pairs={{0,1},{1,0},{2,3},{3,2},{4,8},{5,9},{6,10},{7,11},{8,4},{9,5},{10,... | collective-permute-start | bytes 245768 | tf_op jit(solution)/shard_map/ppermute | solution.py:446
  5.1 2.4 %collective-permute-start.2 = (f32[20,8,128]{2,1,0:T(8,128)S(1)}, f32[20,8,128]{2,1,0:T(8,128)S(1)}, u32[]{:S(2)}, u32[]{:S(2)}) collective-permute-start(f32[20,8,128]{2,1,0:T(8,128)S(1)} %get-tuple-element.39), channel_id=1, source_target_pairs={{0,1},{1,0},{2,3},{3,2},{4,5},{5,4},{6,7},{7,6},{8,12},{9,13},{10,... | collective-permute-start | bytes 245768 | tf_op jit(solution)/shard_map/ppermute | solution.py:446
  7.9 4.6 %collective-permute-start.6 = (f32[2,2,16,128]{3,2,1,0:T(8,128)S(1)}, f32[2,2,16,128]{3,2,1,0:T(8,128)S(1)}, u32[]{:S(2)}, u32[]{:S(2)}) collective-permute-start(f32[2,2,16,128]{3,2,1,0:T(8,128)S(1)} %get-tuple-element.44), channel_id=1, source_target_pairs={{0,3},{1,2},{2,1},{3,0},{4,7},{5,6},{6,5},{7,4},{8,11},{9,10},{10,... | collective-permute-start | bytes 98312 | tf_op jit(solution)/shard_map/ppermute | solution.py:556
  8.5 4.0 %collective-permute-start.7 = (f32[2,2,16,128]{3,2,1,0:T(8,128)S(1)}, f32[2,2,16,128]{3,2,1,0:T(8,128)S(1)}, u32[]{:S(2)}, u32[]{:S(2)}) collective-permute-start(f32[2,2,16,128]{3,2,1,0:T(8,128)S(1)} %get-tuple-element.45), channel_id=1, source_target_pairs={{0,2},{1,3},{2,0},{3,1},{4,6},{5,7},{6,4},{7,5},{8,10},{9,11},{10,... | collective-permute-start | bytes 98312 | tf_op jit(solution)/shard_map/ppermute | solution.py:556
  9.9 4.6 %collective-permute-start.5 = (f32[2,2,2,16,128]{4,3,2,1,0:T(8,128)S(1)}, f32[2,2,2,16,128]{4,3,2,1,0:T(8,128)S(1)}, u32[]{:S(2)}, u32[]{:S(2)}) collective-permute-start(f32[2,2,2,16,128]{4,3,2,1,0:T(8,128)S(1)} %get-tuple-element.40.mine_ref), channel_id=1, source_target_pairs={{0,4},{1,5},{2,6},{3,7},{4,0},{5,1},{6,2},{7,3},{8,9},{9,8},{10,11... | collective-permute-start | bytes 196616 | tf_op jit(solution)/shard_map/ppermute | solution.py:446
  12.0 3.0 %collective-permute-start.4 = (f32[2,2,2,16,128]{4,3,2,1,0:T(8,128)S(1)}, f32[2,2,2,16,128]{4,3,2,1,0:T(8,128)S(1)}, u32[]{:S(2)}, u32[]{:S(2)}) collective-permute-start(f32[2,2,2,16,128]{4,3,2,1,0:T(8,128)S(1)} %get-tuple-element.40.mine_ref), channel_id=1, source_target_pairs={{0,1},{1,0},{2,3},{3,2},{4,8},{5,9},{6,10},{7,11},{8,4},{9,5},{10,... | collective-permute-start | bytes 196616 | tf_op jit(solution)/shard_map/ppermute | solution.py:446
  12.0 3.2 %collective-permute-start.3 = (f32[2,2,2,16,128]{4,3,2,1,0:T(8,128)S(1)}, f32[2,2,2,16,128]{4,3,2,1,0:T(8,128)S(1)}, u32[]{:S(2)}, u32[]{:S(2)}) collective-permute-start(f32[2,2,2,16,128]{4,3,2,1,0:T(8,128)S(1)} %get-tuple-element.40.mine_ref), channel_id=1, source_target_pairs={{0,1},{1,0},{2,3},{3,2},{4,5},{5,4},{6,7},{7,6},{8,12},{9,13},{10,... | collective-permute-start | bytes 196616 | tf_op jit(solution)/shard_map/ppermute | solution.py:446
  12.5 4.5 %collective-permute-start.10 = (f32[2,2,2,16,128]{4,3,2,1,0:T(8,128)S(1)}, f32[2,2,2,16,128]{4,3,2,1,0:T(8,128)S(1)}, u32[]{:S(2)}, u32[]{:S(2)}) collective-permute-start(f32[2,2,2,16,128]{4,3,2,1,0:T(8,128)S(1)} %stack.3._others_ref.others_ref), channel_id=1, source_target_pairs={{0,4},{1,5},{2,6},{3,7},{4,0},{5,1},{6,2},{7,3},{8,9},{9,8},{10,11... | collective-permute-start | bytes 196616 | tf_op jit(solution)/shard_map/ppermute | solution.py:446
  14.4 2.6 %collective-permute-start.9 = (f32[2,2,2,16,128]{4,3,2,1,0:T(8,128)S(1)}, f32[2,2,2,16,128]{4,3,2,1,0:T(8,128)S(1)}, u32[]{:S(2)}, u32[]{:S(2)}) collective-permute-start(f32[2,2,2,16,128]{4,3,2,1,0:T(8,128)S(1)} %stack.3._others_ref.others_ref), channel_id=1, source_target_pairs={{0,1},{1,0},{2,3},{3,2},{4,8},{5,9},{6,10},{7,11},{8,4},{9,5},{10,... | collective-permute-start | bytes 196616 | tf_op jit(solution)/shard_map/ppermute | solution.py:446
  14.5 2.5 %collective-permute-start.8 = (f32[2,2,2,16,128]{4,3,2,1,0:T(8,128)S(1)}, f32[2,2,2,16,128]{4,3,2,1,0:T(8,128)S(1)}, u32[]{:S(2)}, u32[]{:S(2)}) collective-permute-start(f32[2,2,2,16,128]{4,3,2,1,0:T(8,128)S(1)} %stack.3._others_ref.others_ref), channel_id=1, source_target_pairs={{0,1},{1,0},{2,3},{3,2},{4,5},{5,4},{6,7},{7,6},{8,12},{9,13},{10,... | collective-permute-start | bytes 196616 | tf_op jit(solution)/shard_map/ppermute | solution.py:446
  15.0 2.0 %collective-permute-start.11 = (f32[2,2,2,16,128]{4,3,2,1,0:T(8,128)S(1)}, f32[2,2,2,16,128]{4,3,2,1,0:T(8,128)S(1)}, u32[]{:S(2)}, u32[]{:S(2)}) collective-permute-start(f32[2,2,2,16,128]{4,3,2,1,0:T(8,128)S(1)} %stack.4), channel_id=1, source_target_pairs={{0,1},{1,0},{2,3},{3,2},{4,5},{5,4},{6,7},{7,6},{8,9},{9,8},{10,11... | collective-permute-start | bytes 196616 | tf_op jit(solution)/shard_map/ppermute | solution.py:556
  15.2 1.9 %collective-permute-start.12 = (f32[2,2,2,16,128]{4,3,2,1,0:T(8,128)S(1)}, f32[2,2,2,16,128]{4,3,2,1,0:T(8,128)S(1)}, u32[]{:S(2)}, u32[]{:S(2)}) collective-permute-start(f32[2,2,2,16,128]{4,3,2,1,0:T(8,128)S(1)} %stack.5), channel_id=1, source_target_pairs={{0,1},{1,0},{2,3},{3,2},{4,5},{5,4},{6,7},{7,6},{8,9},{9,8},{10,11... | collective-permute-start | bytes 196616 | tf_op jit(solution)/shard_map/ppermute | solution.py:556

commit v27 on v24

--- a/solution.py
+++ b/solution.py
@@ -585,7 +585,7 @@
             scratch(shots, 2, share, 3 * extent, across),
             scratch(*image_shape),
             pltpu.SemaphoreType.DMA((2,)),
-            pltpu.SemaphoreType.DMA((11,)),
+            pltpu.SemaphoreType.DMA((OFFS,)),
         ],
         compiler_params=params,
         name="image_products",

time: 18.2 us -> 18.4 us (1.011)
  Pallas kernels: 3.33 us -> 3.54 us
    pallas_call x1, Pallas kernels: 0.97 us -> 1.18 us  [per_device(): pl.pallas_call(functools.partial(image_products, weight), out_shape=(stru...]
where the time goes in v27:
time: 18.4 us; the launch traced here: 18.2 us
  starting transfers between devices  11.3 us (61%)
  Pallas kernels  3.54 us (19%)
  waiting for transfers between devices  1.95 us (11%)
  between operations  1.36 us (7%)
    ppermute x9, starting transfers between devices, swap_tiles(): return lax.ppermute(value, ('tile', 'shot'), pairs)  8.6 us
    ppermute x4, starting transfers between devices, swap_shots(): lax.ppermute(value, 'shot', [(shot, shot ^ number) for shot in range(shot...  2.7 us
    ppermute x9, waiting for transfers between devices, swap_tiles(): return lax.ppermute(value, ('tile', 'shot'), pairs)  1.94 us
    pallas_call x1, Pallas kernels, per_device(): pl.pallas_call(own_edges, out_shape=(struct(*wavelet.shape), struct(*wide...  1.33 us
    pallas_call x1, Pallas kernels, per_device(): pl.pallas_call(functools.partial(image_products, weight), out_shape=(stru...  1.18 us
    pallas_call x1, Pallas kernels, per_device(): pl.pallas_call(functools.partial(own_steps, width), out_shape=(struct(lev...  0.72 us
  transfers between devices with their start and end apart: 13, of which 2 were waited for; matrix products, arithmetic and copies ran while one was open for 0% of the time, Pallas kernels for 4%

profile of v27, /device:TPU:0, one launch (start us, length us, event | category | flops | bytes accessed | tf_op | source)
XLA Modules:
  0.0 18.2 jit_solution(8677074996477798276)
XLA Ops:
  0.6 1.3 %own_edges.1 = (f32[1,2]{1,0:T(1,128)S(1)}, f32[2,8,32,128]{3,2,1,0:T(8,128)S(1)}, f32[2,8,16,128]{3,2,1,0:T(8,128)S(1)}, s32[8,16,128]{2,1,0:T(8,128)S(1)}, f32...) custom-call(f32[1,16]{1,0:T(1,128)} %bitcast.9, ...), custom_call_target="tpu_custom_call" | custom-call | tf_op jit(solution)/shard_map/own_edges/pallas_call | solution.py:473
  2.0 3.1 %collective-permute-start = (f32[20,8,128]{2,1,0:T(8,128)S(1)}, f32[20,8,128]{2,1,0:T(8,128)S(1)}, u32[]{:S(2)}, u32[]{:S(2)}) collective-permute-start(f32[20,8,128]{2,1,0:T(8,128)S(1)} %get-tuple-element.34), channel_id=1, source_target_pairs={{0,4},{1,5},{2,6},{3,7},{4,0},{5,1},{6,2},{7,3},{8,9},{9,8},{10,11... | collective-permute-start | bytes 245768 | tf_op jit(solution)/shard_map/ppermute | solution.py:434
  5.1 0.0 collective-permute-start.1
  5.1 0.5 %collective-permute-start.2 = (f32[20,8,128]{2,1,0:T(8,128)S(1)}, f32[20,8,128]{2,1,0:T(8,128)S(1)}, u32[]{:S(2)}, u32[]{:S(2)}) collective-permute-start(f32[20,8,128]{2,1,0:T(8,128)S(1)} %get-tuple-element.36), channel_id=1, source_target_pairs={{0,1},{1,0},{2,3},{3,2},{4,5},{5,4},{6,7},{7,6},{8,12},{9,13},{10,... | collective-permute-start | bytes 245768 | tf_op jit(solution)/shard_map/ppermute | solution.py:434
  6.2 0.7 %own_steps.1 = (f32[8,16,128]{2,1,0:T(8,128)S(1)}, f32[2,8,16,128]{3,2,1,0:T(8,128)S(1)}, f32[2,8,8,128]{3,2,1,0:T(8,128)S(1)}, f32[8,32,128]{2,1,0:T(8,128)S(1)...) custom-call(s32[1]{0:T(128)S(6)} %copy.13.cell_ref, f32[1,2]{1,0:T(1,128)S(1)} %get-tuple-element.22.amps_ref, ...), custom_call_target="tpu_custom_call" | custom-call | tf_op jit(solution)/shard_map/own_steps/pallas_call | solution.py:512
  6.9 0.6 %collective-permute-done.rest_0_ = f32[20,8,128]{2,1,0:T(8,128)S(1)} collective-permute-done((f32[20,8,128]{2,1,0:T(8,128)S(1)}, f32[20,8,128]{2,1,0:T(8,128)S(1)}, u32[]{:S(2)}, u32[]{:S(2)}) %collective-permute-start) | collective-permute-done | bytes 81952 | tf_op jit(solution)/shard_map/ppermute | solution.py:434
  7.5 0.0 collective-permute-done.1.rest_1_
  7.5 0.0 collective-permute-done.2.rest_2_
  7.5 0.3 %neighbours_part.1 = (f32[2,8,16,128]{3,2,1,0:T(8,128)S(1)}, f32[2,2,2,16,128]{4,3,2,1,0:T(8,128)S(1)}, f32[2,2,16,128]{3,2,1,0:T(8,128)S(1)}, f32[2,2,16,128]{3,2,1,0:T(8,128)S(1)}) custom-call(s32[4,8,128]{2,1,0:T(8,128)S(1)} %get-tuple-element.28.sides_ref, s32[2,8,128]{2,1,0:T(8,128)S(1)} %get-tuple-element.29.bits_ref, ...), custom_call_target="tpu_custom_call" | custom-call | tf_op jit(solution)/shard_map/neighbours_part/pallas_call | solution.py:529
  7.8 0.6 %collective-permute-start.3 = (f32[2,2,16,128]{3,2,1,0:T(8,128)S(1)}, f32[2,2,16,128]{3,2,1,0:T(8,128)S(1)}, u32[]{:S(2)}, u32[]{:S(2)}) collective-permute-start(f32[2,2,16,128]{3,2,1,0:T(8,128)S(1)} %get-tuple-element.37), channel_id=1, source_target_pairs={{0,3},{1,2},{2,1},{3,0},{4,7},{5,6},{6,5},{7,4},{8,11},{9,10},{10,... | collective-permute-start | bytes 98312 | tf_op jit(solution)/shard_map/ppermute | solution.py:543
  8.4 1.4 %collective-permute-start.4 = (f32[2,2,16,128]{3,2,1,0:T(8,128)S(1)}, f32[2,2,16,128]{3,2,1,0:T(8,128)S(1)}, u32[]{:S(2)}, u32[]{:S(2)}) collective-permute-start(f32[2,2,16,128]{3,2,1,0:T(8,128)S(1)} %get-tuple-element.38), channel_id=1, source_target_pairs={{0,2},{1,3},{2,0},{3,1},{4,6},{5,7},{6,4},{7,5},{8,10},{9,11},{10,... | collective-permute-start | bytes 98312 | tf_op jit(solution)/shard_map/ppermute | solution.py:543
  9.9 2.0 %collective-permute-start.10 = (f32[2,2,2,16,128]{4,3,2,1,0:T(8,128)S(1)}, f32[2,2,2,16,128]{4,3,2,1,0:T(8,128)S(1)}, u32[]{:S(2)}, u32[]{:S(2)}) collective-permute-start(f32[2,2,2,16,128]{4,3,2,1,0:T(8,128)S(1)} %get-tuple-element.39.rest_3_), channel_id=1, source_target_pairs={{0,4},{1,5},{2,6},{3,7},{4,0},{5,1},{6,2},{7,3},{8,9},{9,8},{10,11... | collective-permute-start | bytes 196616 | tf_op jit(solution)/shard_map/ppermute | solution.py:434
  11.9 0.0 collective-permute-start.9
  11.9 0.5 %collective-permute-start.8 = (f32[2,2,2,16,128]{4,3,2,1,0:T(8,128)S(1)}, f32[2,2,2,16,128]{4,3,2,1,0:T(8,128)S(1)}, u32[]{:S(2)}, u32[]{:S(2)}) collective-permute-start(f32[2,2,2,16,128]{4,3,2,1,0:T(8,128)S(1)} %get-tuple-element.39.rest_3_), channel_id=1, source_target_pairs={{0,1},{1,0},{2,3},{3,2},{4,5},{5,4},{6,7},{7,6},{8,12},{9,13},{10,... | collective-permute-start | bytes 196616 | tf_op jit(solution)/shard_map/ppermute | solution.py:434
  12.4 0.0 collective-permute-done.3.refs_0_
  12.4 0.0 collective-permute-done.4.refs_1_
  12.4 1.9 %collective-permute-start.7 = (f32[2,2,2,16,128]{4,3,2,1,0:T(8,128)S(1)}, f32[2,2,2,16,128]{4,3,2,1,0:T(8,128)S(1)}, u32[]{:S(2)}, u32[]{:S(2)}) collective-permute-start(f32[2,2,2,16,128]{4,3,2,1,0:T(8,128)S(1)} %stack.3._others_ref.others_ref), channel_id=1, source_target_pairs={{0,4},{1,5},{2,6},{3,7},{4,0},{5,1},{6,2},{7,3},{8,9},{9,8},{10,11... | collective-permute-start | bytes 196616 | tf_op jit(solution)/shard_map/ppermute | solution.py:434
  14.4 0.0 collective-permute-start.6
  14.4 0.0 collective-permute-done.10.rest_6_
  14.4 0.5 %collective-permute-start.5 = (f32[2,2,2,16,128]{4,3,2,1,0:T(8,128)S(1)}, f32[2,2,2,16,128]{4,3,2,1,0:T(8,128)S(1)}, u32[]{:S(2)}, u32[]{:S(2)}) collective-permute-start(f32[2,2,2,16,128]{4,3,2,1,0:T(8,128)S(1)} %stack.3._others_ref.others_ref), channel_id=1, source_target_pairs={{0,1},{1,0},{2,3},{3,2},{4,5},{5,4},{6,7},{7,6},{8,12},{9,13},{10,... | collective-permute-start | bytes 196616 | tf_op jit(solution)/shard_map/ppermute | solution.py:434
  14.9 0.0 collective-permute-done.9.rest_5_
  14.9 0.2 collective-permute-start.11
  15.1 0.0 collective-permute-done.8.rest_4_
  15.1 0.5 %collective-permute-start.12 = (f32[2,2,2,16,128]{4,3,2,1,0:T(8,128)S(1)}, f32[2,2,2,16,128]{4,3,2,1,0:T(8,128)S(1)}, u32[]{:S(2)}, u32[]{:S(2)}) collective-permute-start(f32[2,2,2,16,128]{4,3,2,1,0:T(8,128)S(1)} %stack.5), channel_id=1, source_target_pairs={{0,1},{1,0},{2,3},{3,2},{4,5},{5,4},{6,7},{7,6},{8,9},{9,8},{10,11... | collective-permute-start | bytes 196616 | tf_op jit(solution)/shard_map/ppermute | solution.py:543
  15.6 1.4 %collective-permute-done.7.rest_2_ = f32[2,2,2,16,128]{4,3,2,1,0:T(8,128)S(1)} collective-permute-done((f32[2,2,2,16,128]{4,3,2,1,0:T(8,128)S(1)}, f32[2,2,2,16,128]{4,3,2,1,0:T(8,128)S(1)}, u32[]{:S(2)}, u32[]{:S(2)}) %collective-permute-start.7) | collective-permute-done | bytes 65568 | tf_op jit(solution)/shard_map/ppermute | solution.py:434
  16.9 0.0 collective-permute-done.6.rest_1_
  16.9 0.0 collective-permute-done.5.rest_0_
  17.0 0.0 collective-permute-done.11.rest_7_
  17.0 0.0 collective-permute-done.12.rest_8_
  17.0 1.2 %image_products.1 = (f32[1,8,16,128]{3,2,1,0:T(8,128)}, f32[1,8,16,128]{3,2,1,0:T(8,128)}, f32[33,2,16,128]{3,2,1,0:T(8,128)}) custom-call(s32[4,8,128]{2,1,0:T(8,128)S(1)} %get-tuple-element.28.sides_ref, f32[2,2,2,16,128]{4,3,2,1,0:T(8,128)S(1)} %stack.3._others_ref.others_ref, f32[2,2,2,16,128]{4,3,2,1,0:T(8,128)S(1)} %collective-permute-done.5.rest_0_, ...), custom_call_target="tpu_custom_call" | custom-call | tf_op jit(solution)/shard_map/image_products/pallas_call | solution.py:575
  (8 shorter events, 0.0 us)
Async XLA Ops:
  2.0 5.5 %collective-permute-start = (f32[20,8,128]{2,1,0:T(8,128)S(1)}, f32[20,8,128]{2,1,0:T(8,128)S(1)}, u32[]{:S(2)}, u32[]{:S(2)}) collective-permute-start(f32[20,8,128]{2,1,0:T(8,128)S(1)} %get-tuple-element.34), channel_id=1, source_target_pairs={{0,4},{1,5},{2,6},{3,7},{4,0},{5,1},{6,2},{7,3},{8,9},{9,8},{10,11... | collective-permute-start | bytes 245768 | tf_op jit(solution)/shard_map/ppermute | solution.py:434
  5.1 2.4 %collective-permute-start.1 = (f32[20,8,128]{2,1,0:T(8,128)S(1)}, f32[20,8,128]{2,1,0:T(8,128)S(1)}, u32[]{:S(2)}, u32[]{:S(2)}) collective-permute-start(f32[20,8,128]{2,1,0:T(8,128)S(1)} %get-tuple-element.35), channel_id=1, source_target_pairs={{0,1},{1,0},{2,3},{3,2},{4,8},{5,9},{6,10},{7,11},{8,4},{9,5},{10,... | collective-permute-start | bytes 245768 | tf_op jit(solution)/shard_map/ppermute | solution.py:434
  5.1 2.4 %collective-permute-start.2 = (f32[20,8,128]{2,1,0:T(8,128)S(1)}, f32[20,8,128]{2,1,0:T(8,128)S(1)}, u32[]{:S(2)}, u32[]{:S(2)}) collective-permute-start(f32[20,8,128]{2,1,0:T(8,128)S(1)} %get-tuple-element.36), channel_id=1, source_target_pairs={{0,1},{1,0},{2,3},{3,2},{4,5},{5,4},{6,7},{7,6},{8,12},{9,13},{10,... | collective-permute-start | bytes 245768 | tf_op jit(solution)/shard_map/ppermute | solution.py:434
  7.8 4.6 %collective-permute-start.3 = (f32[2,2,16,128]{3,2,1,0:T(8,128)S(1)}, f32[2,2,16,128]{3,2,1,0:T(8,128)S(1)}, u32[]{:S(2)}, u32[]{:S(2)}) collective-permute-start(f32[2,2,16,128]{3,2,1,0:T(8,128)S(1)} %get-tuple-element.37), channel_id=1, source_target_pairs={{0,3},{1,2},{2,1},{3,0},{4,7},{5,6},{6,5},{7,4},{8,11},{9,10},{10,... | collective-permute-start | bytes 98312 | tf_op jit(solution)/shard_map/ppermute | solution.py:543
  8.4 4.0 %collective-permute-start.4 = (f32[2,2,16,128]{3,2,1,0:T(8,128)S(1)}, f32[2,2,16,128]{3,2,1,0:T(8,128)S(1)}, u32[]{:S(2)}, u32[]{:S(2)}) collective-permute-start(f32[2,2,16,128]{3,2,1,0:T(8,128)S(1)} %get-tuple-element.38), channel_id=1, source_target_pairs={{0,2},{1,3},{2,0},{3,1},{4,6},{5,7},{6,4},{7,5},{8,10},{9,11},{10,... | collective-permute-start | bytes 98312 | tf_op jit(solution)/shard_map/ppermute | solution.py:543
  9.9 4.6 %collective-permute-start.10 = (f32[2,2,2,16,128]{4,3,2,1,0:T(8,128)S(1)}, f32[2,2,2,16,128]{4,3,2,1,0:T(8,128)S(1)}, u32[]{:S(2)}, u32[]{:S(2)}) collective-permute-start(f32[2,2,2,16,128]{4,3,2,1,0:T(8,128)S(1)} %get-tuple-element.39.rest_3_), channel_id=1, source_target_pairs={{0,4},{1,5},{2,6},{3,7},{4,0},{5,1},{6,2},{7,3},{8,9},{9,8},{10,11... | collective-permute-start | bytes 196616 | tf_op jit(solution)/shard_map/ppermute | solution.py:434
  11.9 3.0 %collective-permute-start.9 = (f32[2,2,2,16,128]{4,3,2,1,0:T(8,128)S(1)}, f32[2,2,2,16,128]{4,3,2,1,0:T(8,128)S(1)}, u32[]{:S(2)}, u32[]{:S(2)}) collective-permute-start(f32[2,2,2,16,128]{4,3,2,1,0:T(8,128)S(1)} %get-tuple-element.39.rest_3_), channel_id=1, source_target_pairs={{0,1},{1,0},{2,3},{3,2},{4,8},{5,9},{6,10},{7,11},{8,4},{9,5},{10,... | collective-permute-start | bytes 196616 | tf_op jit(solution)/shard_map/ppermute | solution.py:434
  11.9 3.2 %collective-permute-start.8 = (f32[2,2,2,16,128]{4,3,2,1,0:T(8,128)S(1)}, f32[2,2,2,16,128]{4,3,2,1,0:T(8,128)S(1)}, u32[]{:S(2)}, u32[]{:S(2)}) collective-permute-start(f32[2,2,2,16,128]{4,3,2,1,0:T(8,128)S(1)} %get-tuple-element.39.rest_3_), channel_id=1, source_target_pairs={{0,1},{1,0},{2,3},{3,2},{4,5},{5,4},{6,7},{7,6},{8,12},{9,13},{10,... | collective-permute-start | bytes 196616 | tf_op jit(solution)/shard_map/ppermute | solution.py:434
  12.4 4.5 %collective-permute-start.7 = (f32[2,2,2,16,128]{4,3,2,1,0:T(8,128)S(1)}, f32[2,2,2,16,128]{4,3,2,1,0:T(8,128)S(1)}, u32[]{:S(2)}, u32[]{:S(2)}) collective-permute-start(f32[2,2,2,16,128]{4,3,2,1,0:T(8,128)S(1)} %stack.3._others_ref.others_ref), channel_id=1, source_target_pairs={{0,4},{1,5},{2,6},{3,7},{4,0},{5,1},{6,2},{7,3},{8,9},{9,8},{10,11... | collective-permute-start | bytes 196616 | tf_op jit(solution)/shard_map/ppermute | solution.py:434
  14.4 2.6 %collective-permute-start.6 = (f32[2,2,2,16,128]{4,3,2,1,0:T(8,128)S(1)}, f32[2,2,2,16,128]{4,3,2,1,0:T(8,128)S(1)}, u32[]{:S(2)}, u32[]{:S(2)}) collective-permute-start(f32[2,2,2,16,128]{4,3,2,1,0:T(8,128)S(1)} %stack.3._others_ref.others_ref), channel_id=1, source_target_pairs={{0,1},{1,0},{2,3},{3,2},{4,8},{5,9},{6,10},{7,11},{8,4},{9,5},{10,... | collective-permute-start | bytes 196616 | tf_op jit(solution)/shard_map/ppermute | solution.py:434
  14.4 2.5 %collective-permute-start.5 = (f32[2,2,2,16,128]{4,3,2,1,0:T(8,128)S(1)}, f32[2,2,2,16,128]{4,3,2,1,0:T(8,128)S(1)}, u32[]{:S(2)}, u32[]{:S(2)}) collective-permute-start(f32[2,2,2,16,128]{4,3,2,1,0:T(8,128)S(1)} %stack.3._others_ref.others_ref), channel_id=1, source_target_pairs={{0,1},{1,0},{2,3},{3,2},{4,5},{5,4},{6,7},{7,6},{8,12},{9,13},{10,... | collective-permute-start | bytes 196616 | tf_op jit(solution)/shard_map/ppermute | solution.py:434
  14.9 2.0 %collective-permute-start.11 = (f32[2,2,2,16,128]{4,3,2,1,0:T(8,128)S(1)}, f32[2,2,2,16,128]{4,3,2,1,0:T(8,128)S(1)}, u32[]{:S(2)}, u32[]{:S(2)}) collective-permute-start(f32[2,2,2,16,128]{4,3,2,1,0:T(8,128)S(1)} %stack.4), channel_id=1, source_target_pairs={{0,1},{1,0},{2,3},{3,2},{4,5},{5,4},{6,7},{7,6},{8,9},{9,8},{10,11... | collective-permute-start | bytes 196616 | tf_op jit(solution)/shard_map/ppermute | solution.py:543
  15.1 1.9 %collective-permute-start.12 = (f32[2,2,2,16,128]{4,3,2,1,0:T(8,128)S(1)}, f32[2,2,2,16,128]{4,3,2,1,0:T(8,128)S(1)}, u32[]{:S(2)}, u32[]{:S(2)}) collective-permute-start(f32[2,2,2,16,128]{4,3,2,1,0:T(8,128)S(1)} %stack.5), channel_id=1, source_target_pairs={{0,1},{1,0},{2,3},{3,2},{4,5},{5,4},{6,7},{7,6},{8,9},{9,8},{10,11... | collective-permute-start | bytes 196616 | tf_op jit(solution)/shard_map/ppermute | solution.py:543
